TPU v7x, 256 devices: a whole 4x4x8 slice. The times are simulated.
256 devices in a mesh: patch: 128 (over z_hi, y, x, core), cfg: 2 (over z_lo).
Axes of the slice: x: 4, y: 4, z: 8 (z_hi: 4, z_lo: 2; z = z_hi * 2 + z_lo), core: 2. Of those that a mesh axis runs over, the one named last changes fastest.
Arguments:
- tokens: bfloat16 [2, 32768, 1280], P('cfg', 'patch'), may hold values from -12 to 12
- stale_keys: bfloat16 [2, 2048, 2560], P('cfg', 'patch'), may hold values from -64 to 64
- norm_gain: float32 [1280], replicated, may hold values from 0.25 to 1.75
- norm_bias: float32 [1280], replicated, may hold values from -3 to 3
- query_weight: bfloat16 [1280, 1280], replicated, may hold values from -0.15625 to 0.15625
- pair_weight: bfloat16 [1280, 2560], replicated, may hold values from -0.15625 to 0.15625
Outputs:
- attended: bfloat16 [2, 32768, 1280], P('cfg', 'patch')
- fresh_keys: bfloat16 [2, 2048, 2560], P('cfg', 'patch')
All inputs are finite; a program needn't handle non-finite values.
Results may differ from a plain program's by a relative error of at most 0.008.
The roundings to bfloat16 on the way count: a program that leaves them out, or rounds other values in their place, can miss the bound.
Values may be sent and summed in bfloat16 or wider, within the bound.
No kernel may reach another device: no remote copies, remote signals or barrier semaphores. Data moves between devices by JAX's collectives and lax.ppermute only.
A program may use at most 128 MiB of HBM per device.

v0:
```python
import jax
import jax.numpy as jnp
from jax import lax
from jax.sharding import PartitionSpec as P

HEADS = 20
HEAD_DIM = 64
GROUPS = 32
POOL = 4


epsilon = 1e-05


def head_partials(queries, table):
    model_width = queries.shape[1]
    score_scale = HEAD_DIM ** (-0.5)
    maxima = []
    totals = []
    partial_sums = []
    for first_head in range(0, HEADS, 4):
        head_count = min(4, HEADS - first_head)
        column_low = first_head * HEAD_DIM
        column_high = column_low + head_count * HEAD_DIM
        heads_query = queries[:, column_low:column_high].reshape(
            queries.shape[0], head_count, HEAD_DIM
        )
        heads_key = table[:, column_low:column_high].reshape(table.shape[0], head_count, HEAD_DIM)
        heads_value = table[:, model_width + column_low : model_width + column_high].reshape(
            table.shape[0], head_count, HEAD_DIM
        )
        scores = (
            jnp.einsum("thd,khd->htk", heads_query, heads_key, preferred_element_type=jnp.float32)
            * score_scale
        )
        largest = jnp.max(scores, axis=2)
        weights = jnp.exp(scores - largest[:, :, None])
        maxima.append(largest)
        totals.append(jnp.sum(weights, axis=2))
        partial_sums.append(
            jnp.einsum(
                "htk,khd->thd",
                weights.astype(jnp.bfloat16),
                heads_value,
                preferred_element_type=jnp.float32,
            )
        )
    return (
        jnp.concatenate(maxima, axis=0),
        jnp.concatenate(totals, axis=0),
        jnp.concatenate(partial_sums, axis=1),
    )


def finish(totals, partial_sums):
    summed = partial_sums / jnp.transpose(totals)[:, :, None]
    return summed.reshape(summed.shape[0], summed.shape[1] * summed.shape[2]).astype(jnp.bfloat16)


def per_device(tokens, stale_keys, norm_gain, norm_bias, query_weight, pair_weight):
    features = tokens[0]
    cell_rows, model_width = features.shape
    values = features.astype(jnp.float32).reshape(cell_rows, GROUPS, model_width // GROUPS)
    entries = cell_rows * lax.axis_size("patch") * (model_width // GROUPS)
    center = lax.psum(jnp.sum(values, axis=(0, 2)), "patch") / entries
    shifted = values - center[None, :, None]
    spread = lax.psum(jnp.sum(shifted * shifted, axis=(0, 2)), "patch") / entries
    scaled = shifted * lax.rsqrt(spread + epsilon)[None, :, None]
    normed = (scaled.reshape(cell_rows, model_width) * norm_gain + norm_bias).astype(jnp.bfloat16)
    row_cells = cell_rows // POOL
    squares = normed.astype(jnp.float32).reshape(POOL, row_cells // POOL, POOL, model_width)
    pooled = jnp.mean(squares, axis=(0, 2)).astype(jnp.bfloat16)
    pooled_rows = pooled.shape[0]
    queries = jnp.dot(normed, query_weight, preferred_element_type=jnp.float32).astype(jnp.bfloat16)
    fresh_pairs = jnp.dot(pooled, pair_weight, preferred_element_type=jnp.float32).astype(
        jnp.bfloat16
    )
    own_start = lax.axis_index("patch") * pooled_rows
    gathered = lax.all_gather(stale_keys[0], "patch", axis=0, tiled=True)
    table = lax.dynamic_update_slice_in_dim(gathered, fresh_pairs, own_start, 0)
    maxima, totals, partial_sums = head_partials(queries, table)
    attended = finish(totals, partial_sums)
    return (attended[None], fresh_pairs[None])


def solution(mesh):
    return jax.shard_map(
        per_device,
        mesh=mesh,
        in_specs=(P("cfg", "patch", None), P("cfg", "patch", None), P(), P(), P(), P()),
        out_specs=(P("cfg", "patch", None), P("cfg", "patch", None)),
        check_vma=False,
    )
```

profile of v0, /device:TPU:32, one launch (start us, length us, event | category | flops | bytes accessed | tf_op | source)
XLA Modules:
  0.0 788.5 jit_solution(393151616912245722)
XLA Ops:
  7.9 2.8 reshape.138
  12.1 356.1 %psum.14 = f32[32]{0:T(128)S(1)} all-reduce(f32[32]{0:T(128)S(1)} %reduce_sum.88), channel_id=1, replica_groups=mesh['patch'=128,'cfg'=2] {'patch'}, use_global_device_ids=true, to_apply=%region_2.0 | all-reduce | flops 32 | bytes 256 | tf_op jit(solution)/shard_map/psum | solution.py:65
  368.3 1.3 multiply_reduce_fusion.5
  369.8 343.1 %psum.15 = f32[32]{0:T(128)S(1)} all-reduce(f32[32]{0:T(128)S(1)} %reduce_sum.91), channel_id=1, replica_groups=mesh['patch'=128,'cfg'=2] {'patch'}, use_global_device_ids=true, to_apply=%region_5.0 | all-reduce | flops 32 | bytes 256 | tf_op jit(solution)/shard_map/psum | solution.py:67
  713.1 2.2 convolution_convert_fusion.1
  717.1 2.0 convert_reduce_fusion
  719.2 4.5 constant_dynamic-update-slice_fusion
  723.7 7.7 fusion.66
  731.3 1.5 copy.54
  732.8 1.4 copy.52
  734.9 1.5 copy.49
  736.4 2.3 copy.48
  738.7 2.3 copy.46
  741.0 2.3 copy.45
  743.3 2.3 copy.43
  745.6 2.3 copy.42
  747.8 2.3 copy.40
  750.1 2.8 multiply_reduce_fusion.4
  753.0 1.4 multiply_reduce_fusion.3
  754.3 1.9 fusion.27
  756.3 3.0 fusion
  759.3 2.1 fusion.33
  761.4 1.4 multiply_reduce_fusion.2
  762.8 1.4 multiply_reduce_fusion.1
  764.2 1.9 fusion.39
  766.1 3.0 fusion.4
  769.1 1.9 fusion.45
  771.1 1.4 multiply_reduce_fusion
  772.5 1.6 fusion.8
  774.1 1.9 fusion.51
  777.2 2.3 divide_convert_fusion
  779.5 2.2 copy.55
  (42 shorter events, 6.3 us)
Async XLA Ops:
  7.2 705.9 %copy-start = (bf16[1280,1280]{1,0:T(8,128)(2,1)S(1)}, bf16[1280,1280]{1,0:T(8,128)(2,1)}, u32[]{:S(2)}) copy-start(bf16[1280,1280]{1,0:T(8,128)(2,1)} %param.10) | copy-start | bytes 9830404
  7.2 712.0 %all-gather.3.cloned.1.call-start = ((), (), s32[]{:S(2)}) async-start(), calls=%async_computation | async-start | bytes 10567680 | tf_op jit(solution)/shard_map/all_gather | solution.py:79
  750.1 2.8 copy-start.6
  750.1 2.8 copy-start.9
  750.1 4.2 copy-start.7
  756.3 3.0 copy-start.5
  759.3 2.1 copy-start.4
  761.4 2.8 copy-start.3
  771.1 3.0 copy-start.2
  772.5 9.2 %copy-start.1 = (bf16[1280,1280]{1,0:T(8,128)(2,1)S(1)}, bf16[1280,1280]{1,0:T(8,128)(2,1)}, u32[]{:S(2)}) copy-start(bf16[1280,1280]{1,0:T(8,128)(2,1)} %param.10) | copy-start | bytes 9830404
  776.0 1.1 copy-start.8
Sparse Core Ops, SparseCore 0:
  11.6 97.3 all-gather.2
where the time goes:
time: 790 us; the launch traced here: 788 us
  blocking collectives  699 us (88%)
  local copies, waits for them, and re-layouts  34.8 us (4%)
  matrix products  24.7 us (3%)
  other arithmetic  14.7 us (2%)
  between operations  14.3 us (2%)
    psum x1, blocking collectives, per_device(): center = lax.psum(jnp.sum(values, axis=(0, 2)), 'patch') / entries  356 us
    psum x1, blocking collectives, per_device(): lax.psum(jnp.sum(shifted * shifted, axis=(0, 2)), 'patch') / entries  343 us
    slice x6, local copies, waits for them, and re-layouts, head_partials(): table[:, column_low:column_high]  16.7 us
  transfers between devices with their start and end apart: 1, of which 0 were waited for; matrix products, arithmetic and copies ran while one was open for 2% of the time, Pallas kernels for 0%

commit v1 on v0

v1 whole, which is shorter than its diff:
```python
import functools

import jax
import jax.numpy as jnp
from jax import lax
from jax.experimental import pallas as pl
from jax.experimental.pallas import tpu as pltpu
from jax.sharding import PartitionSpec as P

HEADS = 20
HEAD_DIM = 64
GROUPS = 32
POOL = 4
WIDTH = 1280
CELLS = 256
ROWS = 16
GROUP_WIDTH = WIDTH // GROUPS
LANES = 128
SET_TILES = 5
TABLE_WIDTH = SET_TILES * LANES
QUERY_WIDTH = 3 * LANES
epsilon = 1e-05

f32 = jnp.float32
bf16 = jnp.bfloat16
HIGHEST = lax.Precision.HIGHEST
VMEM = pl.BlockSpec(memory_space=pltpu.VMEM)
SMEM = pl.BlockSpec(memory_space=pltpu.SMEM)


def iota(shape, axis):
    return lax.broadcasted_iota(jnp.int32, shape, axis)


def group_of_channel():
    low = iota((WIDTH, LANES), 1) * GROUP_WIDTH
    channel = iota((WIDTH, LANES), 0)
    return ((channel >= low) & (channel < low + GROUP_WIDTH)).astype(f32)


def channel_of_group():
    low = iota((LANES, WIDTH), 0) * GROUP_WIDTH
    channel = iota((LANES, WIDTH), 1)
    return ((channel >= low) & (channel < low + GROUP_WIDTH)).astype(f32)


def exact_dot(left, right):
    return jnp.dot(left, right, precision=HIGHEST, preferred_element_type=f32)


def combine(parts, entries):
    mean = sum(part[0:1] for part in parts) / len(parts)
    squares = sum(part[1:2] for part in parts)
    apart = sum((part[0:1] - mean) * (part[0:1] - mean) for part in parts)
    return mean, squares + entries * apart


def stack_stats(mean, squares):
    row = iota((8, LANES), 0)
    return jnp.where(row == 0, mean, jnp.where(row == 1, squares, 0.0))


def encode(stats):
    high = stats.astype(bf16).astype(f32)
    rest = stats - high
    middle = rest.astype(bf16).astype(f32)
    low = rest - middle
    row = jnp.concatenate([high, middle, low], axis=1)
    return jnp.concatenate([row, jnp.zeros_like(row)], axis=0).astype(bf16)


def decode(rows):
    parts = rows.astype(f32)
    return (
        parts[0:8, 0:LANES] + parts[0:8, LANES : 2 * LANES] + parts[0:8, 2 * LANES : 3 * LANES]
    )


def head_tiles(pairs):
    lane = iota((ROWS, LANES), 1)
    even, odd = [], []
    for t in range(WIDTH // LANES):
        keys = pairs[:, t * LANES : (t + 1) * LANES].astype(f32)
        values = pairs[:, WIDTH + t * LANES : WIDTH + (t + 1) * LANES].astype(f32)
        turned = pltpu.roll(values, HEAD_DIM, 1)
        even.append(jnp.where(lane < HEAD_DIM, keys, turned).astype(bf16))
        odd.append(jnp.where(lane < HEAD_DIM, turned, keys).astype(bf16))
    sets = []
    for j in range(4):
        last = (even if j % 2 == 0 else odd)[8 + j // 2]
        sets.append(
            jnp.concatenate(
                [even[2 * j], odd[2 * j], even[2 * j + 1], odd[2 * j + 1], last], axis=1
            )
        )
    return sets


def local_kernel(tokens_ref, stale_ref, stats_ref, sets_ref):
    values = tokens_ref[...].astype(f32)
    to_group = group_of_channel()
    sums = jnp.broadcast_to(jnp.sum(values, axis=0, keepdims=True), (8, WIDTH))
    mean = exact_dot(sums, to_group) / (CELLS * GROUP_WIDTH)
    center = exact_dot(mean, channel_of_group())
    shifted = values - center[0:1]
    squares = jnp.broadcast_to(jnp.sum(shifted * shifted, axis=0, keepdims=True), (8, WIDTH))
    squares = exact_dot(squares, to_group)
    stats_ref[...] = stack_stats(mean, squares)
    for j, block in enumerate(head_tiles(stale_ref[...])):
        sets_ref[j] = block


def x_kernel(place_ref, own_ref, other_ref, sets_ref, *out_refs):
    mean, squares = combine([own_ref[...], other_ref[...]], CELLS * GROUP_WIDTH)
    coded = encode(stack_stats(mean, squares))
    place = place_ref[0]
    for k, out_ref in enumerate(out_refs):
        out_ref[0:ROWS, :] = sets_ref[lax.rem(place + k, 4)]
        out_ref[ROWS : 2 * ROWS, 0:QUERY_WIDTH] = coded
        out_ref[ROWS : 2 * ROWS, QUERY_WIDTH:] = jnp.zeros(
            (ROWS, TABLE_WIDTH - QUERY_WIDTH), bf16
        )


def z_kernel(*refs):
    *in_refs, out_ref = refs
    stats = [decode(ref[ROWS : 2 * ROWS, 0:QUERY_WIDTH]) for ref in in_refs]
    mean, squares = combine(stats, 2 * CELLS * GROUP_WIDTH)
    for k, ref in enumerate(in_refs):
        out_ref[k * ROWS : (k + 1) * ROWS, :] = ref[0:ROWS, :]
    out_ref[4 * ROWS : 5 * ROWS, 0:QUERY_WIDTH] = encode(stack_stats(mean, squares))
    out_ref[4 * ROWS : 5 * ROWS, QUERY_WIDTH:] = jnp.zeros(
        (ROWS, TABLE_WIDTH - QUERY_WIDTH), bf16
    )


def y_kernel(*refs):
    *in_refs, stats_ref, out_ref = refs
    stats = [decode(ref[4 * ROWS : 5 * ROWS, 0:QUERY_WIDTH]) for ref in in_refs]
    mean, squares = combine(stats, 8 * CELLS * GROUP_WIDTH)
    stats_ref[...] = stack_stats(mean, squares)
    for k, ref in enumerate(in_refs):
        out_ref[k * 4 * ROWS : (k + 1) * 4 * ROWS, :] = ref[0 : 4 * ROWS, :]


def project_kernel(
    place_ref, tokens_ref, s0, s1, s2, s3, gain_ref, bias_ref, query_ref, pair_ref, *refs
):
    *message_refs, fresh_ref, sets_ref, last_ref = refs
    mean, squares = combine([s0[...], s1[...], s2[...], s3[...]], 32 * CELLS * GROUP_WIDTH)
    spread = squares / (128 * CELLS * GROUP_WIDTH)
    row = iota((8, LANES), 0)
    both = jnp.where(row == 0, mean, lax.rsqrt(spread + epsilon))
    channels = exact_dot(both, channel_of_group())
    scaled = (tokens_ref[...].astype(f32) - channels[0:1]) * channels[1:2]
    normed = (scaled * gain_ref[...] + bias_ref[...]).astype(bf16)

    square = iota((ROWS, CELLS), 0)
    cell = iota((ROWS, CELLS), 1)
    cell_square = lax.shift_right_logical(lax.bitwise_and(cell, 63), 2)
    pool = jnp.where(cell_square == square, 1.0 / (POOL * POOL), 0.0).astype(bf16)
    pooled = jnp.dot(pool, normed, preferred_element_type=f32).astype(bf16)

    place = place_ref[0]
    last = jnp.dot(normed, query_ref[:, 1024:], preferred_element_type=f32).astype(bf16)
    last_ref[0] = last[:, 0:LANES]
    last_ref[1] = last[:, LANES:]
    for k in (1, 3, 2, 0):
        j = lax.rem(place + k, 4)
        columns = pl.ds(pl.multiple_of(j * 256, 256), 256)
        block = jnp.dot(normed, query_ref[:, columns], preferred_element_type=f32)
        message_refs[k][0:CELLS, 0:256] = block.astype(bf16)
        message_refs[k][0:CELLS, 256:] = last_ref[lax.shift_right_logical(j, 1)]

    fresh = jnp.dot(pooled, pair_ref[...], preferred_element_type=f32).astype(bf16)
    fresh_ref[...] = fresh
    for j, block in enumerate(head_tiles(fresh)):
        sets_ref[j] = block
    for k in range(4):
        block = sets_ref[lax.rem(place + k, 4)]
        message_refs[k][CELLS : CELLS + ROWS, :] = block[:, 0:QUERY_WIDTH]
        message_refs[k][CELLS + ROWS : CELLS + 2 * ROWS, 0:256] = block[:, QUERY_WIDTH:]
        message_refs[k][CELLS + ROWS : CELLS + 2 * ROWS, 256:] = jnp.zeros((ROWS, LANES), bf16)


def attend_kernel(source, place_ref, message_ref, *refs):
    *table_refs, out_ref, first_ref = refs
    first_ref[...] = table_refs[0][...]
    low = source * ROWS
    first_ref[low : low + ROWS, 0:QUERY_WIDTH] = message_ref[CELLS : CELLS + ROWS, :]
    first_ref[low : low + ROWS, QUERY_WIDTH:] = message_ref[CELLS + ROWS : CELLS + 2 * ROWS, 0:256]
    pieces = [first_ref] + table_refs[1:]
    lane = iota((CELLS, LANES), 1)
    low_half = lane < HEAD_DIM
    parity = lax.bitwise_and(place_ref[0], 1)
    factor = HEAD_DIM ** (-0.5) * 1.4426950408889634
    results = []
    for h in range(SET_TILES):
        queries = message_ref[0:CELLS, (h // 2) * LANES : (h // 2 + 1) * LANES]
        if h < 4:
            mask = low_half if h % 2 == 0 else jnp.logical_not(low_half)
        else:
            mask = lax.shift_right_logical(lane, 6) == parity
        queries = jnp.where(mask, queries.astype(f32), 0.0).astype(bf16)
        tiles = [ref[:, h * LANES : (h + 1) * LANES] for ref in pieces]
        scores = [
            lax.dot_general(queries, tile, (((1,), (1,)), ((), ())), preferred_element_type=f32)
            for tile in tiles
        ]
        largest = scores[0]
        for part in scores[1:]:
            largest = jnp.maximum(largest, part)
        largest = jnp.max(largest, axis=1, keepdims=True)
        total = None
        summed = None
        for part, tile in zip(scores, tiles):
            weights = jnp.exp2((part - largest) * factor)
            product = jnp.dot(weights.astype(bf16), tile, preferred_element_type=f32)
            total = weights if total is None else total + weights
            summed = product if summed is None else summed + product
        total = jnp.sum(total, axis=1, keepdims=True)
        results.append(summed / total)
    for t in range(2):
        both = jnp.where(low_half, results[2 * t + 1], results[2 * t])
        out_ref[:, t * LANES : (t + 1) * LANES] = pltpu.roll(both, HEAD_DIM, 1).astype(bf16)
    out_ref[:, 256:] = pltpu.roll(results[4], HEAD_DIM, 1).astype(bf16)


def assemble_kernel(place_ref, *refs):
    *in_refs, out_ref, pair_ref, last_ref = refs
    place = place_ref[0]
    for k, ref in enumerate(in_refs):
        j = lax.rem(place + k, 4)
        pair_ref[j] = ref[:, 0:256]
        last_ref[j] = ref[:, 256:]
    for j in range(4):
        out_ref[:, j * 256 : (j + 1) * 256] = pair_ref[j]
    low_half = iota((CELLS, LANES), 1) < HEAD_DIM
    for t in range(2):
        both = jnp.where(low_half, last_ref[2 * t].astype(f32), last_ref[2 * t + 1].astype(f32))
        out_ref[:, 1024 + t * LANES : 1024 + (t + 1) * LANES] = both.astype(bf16)


def call(kernel, ins, outs, *args, scratch=(), limit=24):
    return pl.pallas_call(
        kernel,
        in_specs=ins,
        out_specs=[VMEM] * len(outs),
        out_shape=[jax.ShapeDtypeStruct(shape, kind) for shape, kind in outs],
        scratch_shapes=list(scratch),
        compiler_params=pltpu.CompilerParams(vmem_limit_bytes=limit * 1024 * 1024),
    )(*args)


AXES = {"z": (32, 4), "y": (8, 4), "x": (2, 4), "core": (1, 2)}


def shift(array, axis, step):
    stride, size = AXES[axis]
    pairs = []
    for source in range(128):
        place = source // stride % size
        target = source + ((place + step) % size - place) * stride
        pairs.append((source, target))
    return lax.ppermute(array, "patch", pairs)


def after(array, *others):
    return lax.optimization_barrier((array, *others))[0]


def per_device(tokens, stale_keys, norm_gain, norm_bias, query_weight, pair_weight):
    tokens, stale = tokens[0], stale_keys[0]
    place = (lax.axis_index("patch") // 2 % 4).astype(jnp.int32).reshape(1)
    message = ((2 * ROWS, TABLE_WIDTH), bf16)
    stats, sets = call(
        local_kernel,
        [VMEM, VMEM],
        [((8, LANES), f32), ((4, ROWS, TABLE_WIDTH), bf16)],
        tokens,
        stale,
    )
    other = shift(stats, "core", 1)
    messages = call(
        x_kernel, [SMEM, VMEM, VMEM, VMEM], [message] * 4, place, stats, other, sets
    )
    received = [messages[0]] + [shift(messages[k], "x", k) for k in (1, 2, 3)]
    (part,) = call(z_kernel, [VMEM] * 4, [((5 * ROWS, TABLE_WIDTH), bf16)], *received)
    parts = [part] + [shift(part, "z", k) for k in (1, 2, 3)]
    stats, piece = call(
        y_kernel,
        [VMEM] * 4,
        [((8, LANES), f32), ((CELLS, TABLE_WIDTH), bf16)],
        *parts,
    )
    all_stats = [stats] + [shift(stats, "y", k) for k in (1, 2, 3)]
    pieces = [piece] + [shift(piece, "y", k) for k in (1, 3, 2)]
    pieces += [shift(block, "core", 1) for block in pieces]
    *queries, fresh = call(
        project_kernel,
        [SMEM] + [VMEM] * 9,
        [((CELLS + 2 * ROWS, QUERY_WIDTH), bf16)] * 4 + [((ROWS, 2 * WIDTH), bf16)],
        place,
        tokens,
        *all_stats,
        norm_gain.reshape(1, WIDTH),
        norm_bias.reshape(1, WIDTH),
        query_weight,
        pair_weight,
        scratch=[pltpu.VMEM((4, ROWS, TABLE_WIDTH), bf16), pltpu.VMEM((2, CELLS, LANES), bf16)],
        limit=32,
    )
    results = [None] * 4
    for k in (1, 3, 2, 0):
        asked = shift(queries[k], "x", k) if k else queries[0]
        (answer,) = call(
            functools.partial(attend_kernel, k),
            [SMEM] + [VMEM] * 9,
            [((CELLS, QUERY_WIDTH), bf16)],
            place,
            asked,
            *pieces,
            scratch=[pltpu.VMEM((CELLS, TABLE_WIDTH), bf16)],
            limit=32,
        )
        results[k] = shift(answer, "x", -k) if k else answer
    (attended,) = call(
        assemble_kernel,
        [SMEM] + [VMEM] * 4,
        [((CELLS, WIDTH), bf16)],
        place,
        *results,
        scratch=[pltpu.VMEM((4, CELLS, 256), bf16), pltpu.VMEM((4, CELLS, LANES), bf16)],
    )
    return (attended[None], fresh[None])


def solution(mesh):
    return jax.shard_map(
        per_device,
        mesh=mesh,
        in_specs=(P("cfg", "patch", None), P("cfg", "patch", None), P(), P(), P(), P()),
        out_specs=(P("cfg", "patch", None), P("cfg", "patch", None)),
        check_vma=False,
    )
```

time: 790 us -> 101 us (0.13)
  blocking collectives: 699 us -> 0 us
  starting transfers between devices: 0.04 us -> 34.9 us
  waiting for transfers between devices: 0.7 us -> 32.8 us
  local copies, waits for them, and re-layouts: 34.8 us -> 9.24 us
  matrix products: 24.7 us -> 0 us
  Pallas kernels: 0 us -> 23.4 us
  other arithmetic: 14.7 us -> 0 us
  between operations: 14.3 us -> 0.73 us
    psum x2 -> x0, blocking collectives: 699 us -> none  [the longest x1 356 us: per_device(): center = lax.psum(jnp.sum(values, axis=(0, 2)), 'patch') / entries]
    ppermute x0 -> x23, starting transfers between devices: none -> 34.9 us  [shift(): return lax.ppermute(array, 'patch', pairs)]
    ppermute x0 -> x23, waiting for transfers between devices: none -> 32.8 us  [shift(): return lax.ppermute(array, 'patch', pairs)]
    slice x17 -> x0, local copies, waits for them, and re-layouts: 28.3 us -> none  [the longest x6 16.7 us: head_partials(): table[:, column_low:column_high]]
    dot_general x12 -> x0, matrix products: 24.7 us -> none  [the longest x5 9.78 us: head_partials(): jnp.einsum('htk,khd->thd', weights.astype(jnp.bfloat16), heads_value, pre...]
    pallas_call x0 -> x10, Pallas kernels: none -> 23.4 us  [call(): pl.pallas_call(kernel, in_specs=ins, out_specs=[VMEM] * len(outs), out_sh...]
    reduce_sum x8 -> x0, other arithmetic: 12.4 us -> none  [the longest x3 7.67 us: head_partials(): totals.append(jnp.sum(weights, axis=2))]
  transfers between devices with their start and end apart: 1 -> 23, of which waited for: 0 -> 10; matrix products, arithmetic and copies ran while one was open for 2% -> 1% of each run, Pallas kernels for 0% -> 21%
where the time goes in v1:
time: 101 us
  starting transfers between devices  34.9 us (35%)
  waiting for transfers between devices  32.8 us (32%)
  Pallas kernels  23.4 us (23%)
  local copies, waits for them, and re-layouts  9.24 us (9%)
    ppermute x23, starting transfers between devices, shift(): return lax.ppermute(array, 'patch', pairs)  34.9 us
    ppermute x23, waiting for transfers between devices, shift(): return lax.ppermute(array, 'patch', pairs)  32.8 us
    pallas_call x10, Pallas kernels, call(): pl.pallas_call(kernel, in_specs=ins, out_specs=[VMEM] * len(outs), out_sh...  23.4 us
    unnamed x10, local copies, waits for them, and re-layouts  7.84 us
  transfers between devices with their start and end apart: 23, of which 10 were waited for; matrix products, arithmetic and copies ran while one was open for 1% of the time, Pallas kernels for 21%

profile of v1, /device:TPU:32, one launch (start us, length us, event | category | flops | bytes accessed | tf_op | source)
XLA Modules:
  0.0 101.1 jit_solution(3655660099981540862)
XLA Ops:
  0.6 1.1 %copy-done.2 = bf16[1,256,1280]{2,1,0:T(8,128)(2,1)S(1)} copy-done((bf16[1,256,1280]{2,1,0:T(8,128)(2,1)S(1)}, bf16[1,256,1280]{2,1,0:T(8,128)(2,1)}, u32[]{:S(2)}) %copy-start.2) | copy-done | bytes 655384
  2.6 1.4 %shard_map.77 = (f32[8,128]{1,0:T(8,128)S(1)}, bf16[4,16,640]{2,1,0:T(8,128)(2,1)S(1)}) custom-call(bf16[256,1280]{1,0:T(8,128)(2,1)S(1)} %bitcast.5, bf16[16,2560]{1,0:T(8,128)(2,1)S(1)} %bitcast.7), custom_call_target="tpu_custom_call" | custom-call | tf_op jit(solution)/shard_map/pallas_call | solution.py:245
  4.1 1.1 %collective-permute-done.other_ref = f32[8,128]{1,0:T(8,128)S(1)} collective-permute-done((f32[8,128]{1,0:T(8,128)S(1)}, f32[8,128]{1,0:T(8,128)S(1)}, u32[]{:S(2)}, u32[]{:S(2)}) %collective-permute-start) | collective-permute-done | bytes 4128 | tf_op jit(solution)/shard_map/ppermute | solution.py:265
  5.2 1.6 %collective-permute-start.1 = (bf16[32,640]{1,0:T(8,128)(2,1)S(1)}, bf16[32,640]{1,0:T(8,128)(2,1)S(1)}, u32[]{:S(2)}, u32[]{:S(2)}) collective-permute-start(bf16[32,640]{1,0:T(8,128)(2,1)S(1)} %get-tuple-element.18), channel_id=1, source_target_pairs={{0,4},{2,6},{4,8},{6,10},{8,12},{10,14},{12,0},{14,2},{16,20},{18,... | collective-permute-start | bytes 122888 | tf_op jit(solution)/shard_map/ppermute | solution.py:265
  6.8 2.7 %collective-permute-start.2 = (bf16[32,640]{1,0:T(8,128)(2,1)S(1)}, bf16[32,640]{1,0:T(8,128)(2,1)S(1)}, u32[]{:S(2)}, u32[]{:S(2)}) collective-permute-start(bf16[32,640]{1,0:T(8,128)(2,1)S(1)} %get-tuple-element.19), channel_id=1, source_target_pairs={{0,8},{2,10},{4,12},{6,14},{8,0},{10,2},{12,4},{14,6},{16,24},{18,... | collective-permute-start | bytes 122888 | tf_op jit(solution)/shard_map/ppermute | solution.py:265
  9.5 1.4 %collective-permute-start.3 = (bf16[32,640]{1,0:T(8,128)(2,1)S(1)}, bf16[32,640]{1,0:T(8,128)(2,1)S(1)}, u32[]{:S(2)}, u32[]{:S(2)}) collective-permute-start(bf16[32,640]{1,0:T(8,128)(2,1)S(1)} %get-tuple-element.20), channel_id=1, source_target_pairs={{0,12},{2,14},{4,0},{6,2},{8,4},{10,6},{12,8},{14,10},{16,28},{18,... | collective-permute-start | bytes 122888 | tf_op jit(solution)/shard_map/ppermute | solution.py:265
  11.0 1.3 %collective-permute-done.2.refs_2_ = bf16[32,640]{1,0:T(8,128)(2,1)S(1)} collective-permute-done((bf16[32,640]{1,0:T(8,128)(2,1)S(1)}, bf16[32,640]{1,0:T(8,128)(2,1)S(1)}, u32[]{:S(2)}, u32[]{:S(2)}) %collective-permute-start.2) | collective-permute-done | bytes 40992 | tf_op jit(solution)/shard_map/ppermute | solution.py:265
  12.3 1.2 %collective-permute-done.3.refs_3_ = bf16[32,640]{1,0:T(8,128)(2,1)S(1)} collective-permute-done((bf16[32,640]{1,0:T(8,128)(2,1)S(1)}, bf16[32,640]{1,0:T(8,128)(2,1)S(1)}, u32[]{:S(2)}, u32[]{:S(2)}) %collective-permute-start.3) | collective-permute-done | bytes 40992 | tf_op jit(solution)/shard_map/ppermute | solution.py:265
  13.6 5.5 %collective-permute-start.6 = (bf16[80,640]{1,0:T(8,128)(2,1)S(1)}, bf16[80,640]{1,0:T(8,128)(2,1)S(1)}, u32[]{:S(2)}, u32[]{:S(2)}) collective-permute-start(bf16[80,640]{1,0:T(8,128)(2,1)S(1)} %shard_map.79.refs_0_), channel_id=1, source_target_pairs={{0,192},{2,194},{4,196},{6,198},{8,200},{10,202},{12,204},{14,206}... | collective-permute-start | bytes 307208 | tf_op jit(solution)/shard_map/ppermute | solution.py:265
  19.1 1.4 %collective-permute-start.5 = (bf16[80,640]{1,0:T(8,128)(2,1)S(1)}, bf16[80,640]{1,0:T(8,128)(2,1)S(1)}, u32[]{:S(2)}, u32[]{:S(2)}) collective-permute-start(bf16[80,640]{1,0:T(8,128)(2,1)S(1)} %shard_map.79.refs_0_), channel_id=1, source_target_pairs={{0,128},{2,130},{4,132},{6,134},{8,136},{10,138},{12,140},{14,142}... | collective-permute-start | bytes 307208 | tf_op jit(solution)/shard_map/ppermute | solution.py:265
  20.5 2.4 %collective-permute-start.4 = (bf16[80,640]{1,0:T(8,128)(2,1)S(1)}, bf16[80,640]{1,0:T(8,128)(2,1)S(1)}, u32[]{:S(2)}, u32[]{:S(2)}) collective-permute-start(bf16[80,640]{1,0:T(8,128)(2,1)S(1)} %shard_map.79.refs_0_), channel_id=1, source_target_pairs={{0,64},{2,66},{4,68},{6,70},{8,72},{10,74},{12,76},{14,78},{16,80}... | collective-permute-start | bytes 307208 | tf_op jit(solution)/shard_map/ppermute | solution.py:265
  22.9 6.3 %collective-permute-done.5.refs_2_ = bf16[80,640]{1,0:T(8,128)(2,1)S(1)} collective-permute-done((bf16[80,640]{1,0:T(8,128)(2,1)S(1)}, bf16[80,640]{1,0:T(8,128)(2,1)S(1)}, u32[]{:S(2)}, u32[]{:S(2)}) %collective-permute-start.5) | collective-permute-done | bytes 102432 | tf_op jit(solution)/shard_map/ppermute | solution.py:265
  30.1 3.3 %collective-permute-start.12 = (bf16[256,640]{1,0:T(8,128)(2,1)S(1)}, bf16[256,640]{1,0:T(8,128)(2,1)S(1)}, u32[]{:S(2)}, u32[]{:S(2)}) collective-permute-start(bf16[256,640]{1,0:T(8,128)(2,1)S(1)} %get-tuple-element.23.refs_0_), channel_id=1, source_target_pairs={{0,32},{2,34},{4,36},{6,38},{8,40},{10,42},{12,44},{14,46},{16,48}... | collective-permute-start | bytes 983048 | tf_op jit(solution)/shard_map/ppermute | solution.py:265
  35.4 2.3 %collective-permute-start.9 = (f32[8,128]{1,0:T(8,128)S(1)}, f32[8,128]{1,0:T(8,128)S(1)}, u32[]{:S(2)}, u32[]{:S(2)}) collective-permute-start(f32[8,128]{1,0:T(8,128)S(1)} %get-tuple-element.21.s0), channel_id=1, source_target_pairs={{0,48},{2,50},{4,52},{6,54},{8,56},{10,58},{12,60},{14,62},{16,0},... | collective-permute-start | bytes 12296 | tf_op jit(solution)/shard_map/ppermute | solution.py:265
  37.6 10.1 %collective-permute-done.9.s3 = f32[8,128]{1,0:T(8,128)S(1)} collective-permute-done((f32[8,128]{1,0:T(8,128)S(1)}, f32[8,128]{1,0:T(8,128)S(1)}, u32[]{:S(2)}, u32[]{:S(2)}) %collective-permute-start.9) | collective-permute-done | bytes 4128 | tf_op jit(solution)/shard_map/ppermute | solution.py:265
  47.8 1.8 %collective-permute-start.8 = (f32[8,128]{1,0:T(8,128)S(1)}, f32[8,128]{1,0:T(8,128)S(1)}, u32[]{:S(2)}, u32[]{:S(2)}) collective-permute-start(f32[8,128]{1,0:T(8,128)S(1)} %get-tuple-element.21.s0), channel_id=1, source_target_pairs={{0,32},{2,34},{4,36},{6,38},{8,40},{10,42},{12,44},{14,46},{16,48}... | collective-permute-start | bytes 12296 | tf_op jit(solution)/shard_map/ppermute | solution.py:265
  49.6 3.3 %collective-permute-done.8.s2 = f32[8,128]{1,0:T(8,128)S(1)} collective-permute-done((f32[8,128]{1,0:T(8,128)S(1)}, f32[8,128]{1,0:T(8,128)S(1)}, u32[]{:S(2)}, u32[]{:S(2)}) %collective-permute-start.8) | collective-permute-done | bytes 4128 | tf_op jit(solution)/shard_map/ppermute | solution.py:265
  52.9 1.2 %collective-permute-start.7 = (f32[8,128]{1,0:T(8,128)S(1)}, f32[8,128]{1,0:T(8,128)S(1)}, u32[]{:S(2)}, u32[]{:S(2)}) collective-permute-start(f32[8,128]{1,0:T(8,128)S(1)} %get-tuple-element.21.s0), channel_id=1, source_target_pairs={{0,16},{2,18},{4,20},{6,22},{8,24},{10,26},{12,28},{14,30},{16,32}... | collective-permute-start | bytes 12296 | tf_op jit(solution)/shard_map/ppermute | solution.py:265
  55.5 2.2 %collective-permute-done.7.s1 = f32[8,128]{1,0:T(8,128)S(1)} collective-permute-done((f32[8,128]{1,0:T(8,128)S(1)}, f32[8,128]{1,0:T(8,128)S(1)}, u32[]{:S(2)}, u32[]{:S(2)}) %collective-permute-start.7) | collective-permute-done | bytes 4128 | tf_op jit(solution)/shard_map/ppermute | solution.py:265
  57.7 2.9 %copy-done = bf16[1280,2560]{1,0:T(8,128)(2,1)S(1)} copy-done((bf16[1280,2560]{1,0:T(8,128)(2,1)S(1)}, bf16[1280,2560]{1,0:T(8,128)(2,1)}, u32[]{:S(2)}) %copy-start) | copy-done | bytes 6553624
  60.6 1.9 %copy-done.1 = bf16[1280,1280]{1,0:T(8,128)(2,1)S(1)} copy-done((bf16[1280,1280]{1,0:T(8,128)(2,1)S(1)}, bf16[1280,1280]{1,0:T(8,128)(2,1)}, u32[]{:S(2)}) %copy-start.1) | copy-done | bytes 3276824
  62.5 1.1 %copy-done.3 = bf16[1,256,1280]{2,1,0:T(8,128)(2,1)S(1)} copy-done((bf16[1,256,1280]{2,1,0:T(8,128)(2,1)S(1)}, bf16[1,256,1280]{2,1,0:T(8,128)(2,1)}, u32[]{:S(2)}) %copy-start.3) | copy-done | bytes 655384
  63.6 3.3 %shard_map.81 = (bf16[288,384]{1,0:T(8,128)(2,1)S(1)}, bf16[288,384]{1,0:T(8,128)(2,1)S(1)}, bf16[288,384]{1,0:T(8,128)(2,1)S(1)}, bf16[288,384]{1,0:T(8,128)(2,1)S(1)}, bf16[16,2560]{1,0:T(8,128)(2,1)}) custom-call(s32[1]{0:T(128)} %bitcast.place_ref, bf16[256,1280]{1,0:T(8,128)(2,1)S(1)} %bitcast.6, f32[8,128]{1,0:T(8,128)S(1)} %get-tuple-element.21.s0, ...), custom_call_target="tpu_custom_call" | custom-call | tf_op jit(solution)/shard_map/pallas_call | solution.py:245
  67.9 6.1 %collective-permute-done.17.message_ref = bf16[288,384]{1,0:T(8,128)(2,1)S(1)} collective-permute-done((bf16[288,384]{1,0:T(8,128)(2,1)S(1)}, bf16[288,384]{1,0:T(8,128)(2,1)S(1)}, u32[]{:S(2)}, u32[]{:S(2)}) %collective-permute-start.17) | collective-permute-done | bytes 221216 | tf_op jit(solution)/shard_map/ppermute | solution.py:265
  74.0 1.1 %collective-permute-start.19 = (bf16[288,384]{1,0:T(8,128)(2,1)S(1)}, bf16[288,384]{1,0:T(8,128)(2,1)S(1)}, u32[]{:S(2)}, u32[]{:S(2)}) collective-permute-start(bf16[288,384]{1,0:T(8,128)(2,1)S(1)} %get-tuple-element.25), channel_id=1, source_target_pairs={{0,8},{2,10},{4,12},{6,14},{8,0},{10,2},{12,4},{14,6},{16,24},{18,... | collective-permute-start | bytes 663560 | tf_op jit(solution)/shard_map/ppermute | solution.py:265
  76.1 4.4 %shard_map.83 = bf16[256,384]{1,0:T(8,128)(2,1)S(1)} custom-call(s32[1]{0:T(128)} %bitcast.place_ref, bf16[288,384]{1,0:T(8,128)(2,1)S(1)} %collective-permute-done.17.message_ref, bf16[256,640]{1,0:T(8,128)(2,1)S(1)} %get-tuple-element.23.refs_0_, bf16[256,640]{1,0:T(8,128)(2,1)S(1)} %collective-permute-done.10.refs_1_, ...), custom_call_target="tpu_custom_call" | custom-call | tf_op jit(solution)/shard_map/pallas_call | solution.py:245
  80.6 2.3 %collective-permute-start.18 = (bf16[256,384]{1,0:T(8,128)(2,1)S(1)}, bf16[256,384]{1,0:T(8,128)(2,1)S(1)}, u32[]{:S(2)}, u32[]{:S(2)}) collective-permute-start(bf16[256,384]{1,0:T(8,128)(2,1)S(1)} %shard_map.83), channel_id=1, source_target_pairs={{0,12},{2,14},{4,0},{6,2},{8,4},{10,6},{12,8},{14,10},{16,28},{18,... | collective-permute-start | bytes 589832 | tf_op jit(solution)/shard_map/ppermute | solution.py:265
  82.8 4.4 %shard_map.84 = bf16[256,384]{1,0:T(8,128)(2,1)S(1)} custom-call(s32[1]{0:T(128)} %bitcast.place_ref, bf16[288,384]{1,0:T(8,128)(2,1)S(1)} %collective-permute-done.19.message_ref, bf16[256,640]{1,0:T(8,128)(2,1)S(1)} %get-tuple-element.23.refs_0_, bf16[256,640]{1,0:T(8,128)(2,1)S(1)} %collective-permute-done.10.refs_1_, ...), custom_call_target="tpu_custom_call" | custom-call | tf_op jit(solution)/shard_map/pallas_call | solution.py:245
  87.2 1.2 %collective-permute-start.20 = (bf16[256,384]{1,0:T(8,128)(2,1)S(1)}, bf16[256,384]{1,0:T(8,128)(2,1)S(1)}, u32[]{:S(2)}, u32[]{:S(2)}) collective-permute-start(bf16[256,384]{1,0:T(8,128)(2,1)S(1)} %shard_map.84), channel_id=1, source_target_pairs={{0,8},{2,10},{4,12},{6,14},{8,0},{10,2},{12,4},{14,6},{16,24},{18,... | collective-permute-start | bytes 589832 | tf_op jit(solution)/shard_map/ppermute | solution.py:265
  88.4 4.4 %shard_map.85 = bf16[256,384]{1,0:T(8,128)(2,1)S(1)} custom-call(s32[1]{0:T(128)} %bitcast.place_ref, bf16[288,384]{1,0:T(8,128)(2,1)S(1)} %collective-permute-done.21.message_ref, bf16[256,640]{1,0:T(8,128)(2,1)S(1)} %get-tuple-element.23.refs_0_, bf16[256,640]{1,0:T(8,128)(2,1)S(1)} %collective-permute-done.10.refs_1_, ...), custom_call_target="tpu_custom_call" | custom-call | tf_op jit(solution)/shard_map/pallas_call | solution.py:245
  92.9 2.6 %collective-permute-start.22 = (bf16[256,384]{1,0:T(8,128)(2,1)S(1)}, bf16[256,384]{1,0:T(8,128)(2,1)S(1)}, u32[]{:S(2)}, u32[]{:S(2)}) collective-permute-start(bf16[256,384]{1,0:T(8,128)(2,1)S(1)} %shard_map.85), channel_id=1, source_target_pairs={{0,4},{2,6},{4,8},{6,10},{8,12},{10,14},{12,0},{14,2},{16,20},{18,... | collective-permute-start | bytes 589832 | tf_op jit(solution)/shard_map/ppermute | solution.py:265
  95.4 4.4 %shard_map.82.refs_0_ = bf16[256,384]{1,0:T(8,128)(2,1)S(1)} custom-call(s32[1]{0:T(128)} %bitcast.place_ref, bf16[288,384]{1,0:T(8,128)(2,1)S(1)} %get-tuple-element.22.message_ref, bf16[256,640]{1,0:T(8,128)(2,1)S(1)} %get-tuple-element.23.refs_0_, bf16[256,640]{1,0:T(8,128)(2,1)S(1)} %collective-permute-done.10.refs_1_, ...), custom_call_target="tpu_custom_call" | custom-call | tf_op jit(solution)/shard_map/pallas_call | solution.py:245
  (36 shorter events, 8.6 us)
Async XLA Ops:
  0.6 1.1 %copy-start.2 = (bf16[1,256,1280]{2,1,0:T(8,128)(2,1)S(1)}, bf16[1,256,1280]{2,1,0:T(8,128)(2,1)}, u32[]{:S(2)}) copy-start(bf16[1,256,1280]{2,1,0:T(8,128)(2,1)} %param.6) | copy-start | bytes 1966084
  1.7 0.9 copy-start.4
  4.0 1.2 %collective-permute-start = (f32[8,128]{1,0:T(8,128)S(1)}, f32[8,128]{1,0:T(8,128)S(1)}, u32[]{:S(2)}, u32[]{:S(2)}) collective-permute-start(f32[8,128]{1,0:T(8,128)S(1)} %get-tuple-element.15.own_ref), channel_id=1, source_target_pairs={{0,2},{2,0},{4,6},{6,4},{8,10},{10,8},{12,14},{14,12},{16,18},{18,... | collective-permute-start | bytes 12296 | tf_op jit(solution)/shard_map/ppermute | solution.py:265
  5.2 5.7 %collective-permute-start.1 = (bf16[32,640]{1,0:T(8,128)(2,1)S(1)}, bf16[32,640]{1,0:T(8,128)(2,1)S(1)}, u32[]{:S(2)}, u32[]{:S(2)}) collective-permute-start(bf16[32,640]{1,0:T(8,128)(2,1)S(1)} %get-tuple-element.18), channel_id=1, source_target_pairs={{0,4},{2,6},{4,8},{6,10},{8,12},{10,14},{12,0},{14,2},{16,20},{18,... | collective-permute-start | bytes 122888 | tf_op jit(solution)/shard_map/ppermute | solution.py:265
  6.8 5.5 %collective-permute-start.2 = (bf16[32,640]{1,0:T(8,128)(2,1)S(1)}, bf16[32,640]{1,0:T(8,128)(2,1)S(1)}, u32[]{:S(2)}, u32[]{:S(2)}) collective-permute-start(bf16[32,640]{1,0:T(8,128)(2,1)S(1)} %get-tuple-element.19), channel_id=1, source_target_pairs={{0,8},{2,10},{4,12},{6,14},{8,0},{10,2},{12,4},{14,6},{16,24},{18,... | collective-permute-start | bytes 122888 | tf_op jit(solution)/shard_map/ppermute | solution.py:265
  9.5 4.0 %collective-permute-start.3 = (bf16[32,640]{1,0:T(8,128)(2,1)S(1)}, bf16[32,640]{1,0:T(8,128)(2,1)S(1)}, u32[]{:S(2)}, u32[]{:S(2)}) collective-permute-start(bf16[32,640]{1,0:T(8,128)(2,1)S(1)} %get-tuple-element.20), channel_id=1, source_target_pairs={{0,12},{2,14},{4,0},{6,2},{8,4},{10,6},{12,8},{14,10},{16,28},{18,... | collective-permute-start | bytes 122888 | tf_op jit(solution)/shard_map/ppermute | solution.py:265
  13.6 9.3 %collective-permute-start.6 = (bf16[80,640]{1,0:T(8,128)(2,1)S(1)}, bf16[80,640]{1,0:T(8,128)(2,1)S(1)}, u32[]{:S(2)}, u32[]{:S(2)}) collective-permute-start(bf16[80,640]{1,0:T(8,128)(2,1)S(1)} %shard_map.79.refs_0_), channel_id=1, source_target_pairs={{0,192},{2,194},{4,196},{6,198},{8,200},{10,202},{12,204},{14,206}... | collective-permute-start | bytes 307208 | tf_op jit(solution)/shard_map/ppermute | solution.py:265
  19.1 10.1 %collective-permute-start.5 = (bf16[80,640]{1,0:T(8,128)(2,1)S(1)}, bf16[80,640]{1,0:T(8,128)(2,1)S(1)}, u32[]{:S(2)}, u32[]{:S(2)}) collective-permute-start(bf16[80,640]{1,0:T(8,128)(2,1)S(1)} %shard_map.79.refs_0_), channel_id=1, source_target_pairs={{0,128},{2,130},{4,132},{6,134},{8,136},{10,138},{12,140},{14,142}... | collective-permute-start | bytes 307208 | tf_op jit(solution)/shard_map/ppermute | solution.py:265
  20.5 9.5 %collective-permute-start.4 = (bf16[80,640]{1,0:T(8,128)(2,1)S(1)}, bf16[80,640]{1,0:T(8,128)(2,1)S(1)}, u32[]{:S(2)}, u32[]{:S(2)}) collective-permute-start(bf16[80,640]{1,0:T(8,128)(2,1)S(1)} %shard_map.79.refs_0_), channel_id=1, source_target_pairs={{0,64},{2,66},{4,68},{6,70},{8,72},{10,74},{12,76},{14,78},{16,80}... | collective-permute-start | bytes 307208 | tf_op jit(solution)/shard_map/ppermute | solution.py:265
  30.1 37.2 %collective-permute-start.12 = (bf16[256,640]{1,0:T(8,128)(2,1)S(1)}, bf16[256,640]{1,0:T(8,128)(2,1)S(1)}, u32[]{:S(2)}, u32[]{:S(2)}) collective-permute-start(bf16[256,640]{1,0:T(8,128)(2,1)S(1)} %get-tuple-element.23.refs_0_), channel_id=1, source_target_pairs={{0,32},{2,34},{4,36},{6,38},{8,40},{10,42},{12,44},{14,46},{16,48}... | collective-permute-start | bytes 983048 | tf_op jit(solution)/shard_map/ppermute | solution.py:265
  33.3 34.0 %collective-permute-start.11 = (bf16[256,640]{1,0:T(8,128)(2,1)S(1)}, bf16[256,640]{1,0:T(8,128)(2,1)S(1)}, u32[]{:S(2)}, u32[]{:S(2)}) collective-permute-start(bf16[256,640]{1,0:T(8,128)(2,1)S(1)} %get-tuple-element.23.refs_0_), channel_id=1, source_target_pairs={{0,48},{2,50},{4,52},{6,54},{8,56},{10,58},{12,60},{14,62},{16,0},... | collective-permute-start | bytes 983048 | tf_op jit(solution)/shard_map/ppermute | solution.py:265
  34.4 33.4 %collective-permute-start.10 = (bf16[256,640]{1,0:T(8,128)(2,1)S(1)}, bf16[256,640]{1,0:T(8,128)(2,1)S(1)}, u32[]{:S(2)}, u32[]{:S(2)}) collective-permute-start(bf16[256,640]{1,0:T(8,128)(2,1)S(1)} %get-tuple-element.23.refs_0_), channel_id=1, source_target_pairs={{0,16},{2,18},{4,20},{6,22},{8,24},{10,26},{12,28},{14,30},{16,32}... | collective-permute-start | bytes 983048 | tf_op jit(solution)/shard_map/ppermute | solution.py:265
  35.4 39.7 %collective-permute-start.13 = (bf16[256,640]{1,0:T(8,128)(2,1)S(1)}, bf16[256,640]{1,0:T(8,128)(2,1)S(1)}, u32[]{:S(2)}, u32[]{:S(2)}) collective-permute-start(bf16[256,640]{1,0:T(8,128)(2,1)S(1)} %get-tuple-element.23.refs_0_), channel_id=1, source_target_pairs={{0,2},{2,0},{4,6},{6,4},{8,10},{10,8},{12,14},{14,12},{16,18},{18,... | collective-permute-start | bytes 983048 | tf_op jit(solution)/shard_map/ppermute | solution.py:265
  35.4 12.4 %collective-permute-start.9 = (f32[8,128]{1,0:T(8,128)S(1)}, f32[8,128]{1,0:T(8,128)S(1)}, u32[]{:S(2)}, u32[]{:S(2)}) collective-permute-start(f32[8,128]{1,0:T(8,128)S(1)} %get-tuple-element.21.s0), channel_id=1, source_target_pairs={{0,48},{2,50},{4,52},{6,54},{8,56},{10,58},{12,60},{14,62},{16,0},... | collective-permute-start | bytes 12296 | tf_op jit(solution)/shard_map/ppermute | solution.py:265
  47.8 5.1 %collective-permute-start.8 = (f32[8,128]{1,0:T(8,128)S(1)}, f32[8,128]{1,0:T(8,128)S(1)}, u32[]{:S(2)}, u32[]{:S(2)}) collective-permute-start(f32[8,128]{1,0:T(8,128)S(1)} %get-tuple-element.21.s0), channel_id=1, source_target_pairs={{0,32},{2,34},{4,36},{6,38},{8,40},{10,42},{12,44},{14,46},{16,48}... | collective-permute-start | bytes 12296 | tf_op jit(solution)/shard_map/ppermute | solution.py:265
  52.9 4.8 %collective-permute-start.7 = (f32[8,128]{1,0:T(8,128)S(1)}, f32[8,128]{1,0:T(8,128)S(1)}, u32[]{:S(2)}, u32[]{:S(2)}) collective-permute-start(f32[8,128]{1,0:T(8,128)S(1)} %get-tuple-element.21.s0), channel_id=1, source_target_pairs={{0,16},{2,18},{4,20},{6,22},{8,24},{10,26},{12,28},{14,30},{16,32}... | collective-permute-start | bytes 12296 | tf_op jit(solution)/shard_map/ppermute | solution.py:265
  57.7 2.9 %copy-start = (bf16[1280,2560]{1,0:T(8,128)(2,1)S(1)}, bf16[1280,2560]{1,0:T(8,128)(2,1)}, u32[]{:S(2)}) copy-start(bf16[1280,2560]{1,0:T(8,128)(2,1)} %pair_ref.1) | copy-start | bytes 19660804
  60.6 1.9 %copy-start.1 = (bf16[1280,1280]{1,0:T(8,128)(2,1)S(1)}, bf16[1280,1280]{1,0:T(8,128)(2,1)}, u32[]{:S(2)}) copy-start(bf16[1280,1280]{1,0:T(8,128)(2,1)} %query_ref.1) | copy-start | bytes 9830404
  62.5 1.1 %copy-start.3 = (bf16[1,256,1280]{2,1,0:T(8,128)(2,1)S(1)}, bf16[1,256,1280]{2,1,0:T(8,128)(2,1)}, u32[]{:S(2)}) copy-start(bf16[1,256,1280]{2,1,0:T(8,128)(2,1)} %param.6) | copy-start | bytes 1966084
  66.9 7.1 %collective-permute-start.17 = (bf16[288,384]{1,0:T(8,128)(2,1)S(1)}, bf16[288,384]{1,0:T(8,128)(2,1)S(1)}, u32[]{:S(2)}, u32[]{:S(2)}) collective-permute-start(bf16[288,384]{1,0:T(8,128)(2,1)S(1)} %get-tuple-element.24), channel_id=1, source_target_pairs={{0,4},{2,6},{4,8},{6,10},{8,12},{10,14},{12,0},{14,2},{16,20},{18,... | collective-permute-start | bytes 663560 | tf_op jit(solution)/shard_map/ppermute | solution.py:265
  67.3 8.8 %collective-permute-start.16 = (bf16[256,640]{1,0:T(8,128)(2,1)S(1)}, bf16[256,640]{1,0:T(8,128)(2,1)S(1)}, u32[]{:S(2)}, u32[]{:S(2)}) collective-permute-start(bf16[256,640]{1,0:T(8,128)(2,1)S(1)} %collective-permute-done.12.refs_3_), channel_id=1, source_target_pairs={{0,2},{2,0},{4,6},{6,4},{8,10},{10,8},{12,14},{14,12},{16,18},{18,... | collective-permute-start | bytes 983048 | tf_op jit(solution)/shard_map/ppermute | solution.py:265
  67.3 8.8 %collective-permute-start.15 = (bf16[256,640]{1,0:T(8,128)(2,1)S(1)}, bf16[256,640]{1,0:T(8,128)(2,1)S(1)}, u32[]{:S(2)}, u32[]{:S(2)}) collective-permute-start(bf16[256,640]{1,0:T(8,128)(2,1)S(1)} %collective-permute-done.11.refs_2_), channel_id=1, source_target_pairs={{0,2},{2,0},{4,6},{6,4},{8,10},{10,8},{12,14},{14,12},{16,18},{18,... | collective-permute-start | bytes 983048 | tf_op jit(solution)/shard_map/ppermute | solution.py:265
  67.8 8.3 %collective-permute-start.14 = (bf16[256,640]{1,0:T(8,128)(2,1)S(1)}, bf16[256,640]{1,0:T(8,128)(2,1)S(1)}, u32[]{:S(2)}, u32[]{:S(2)}) collective-permute-start(bf16[256,640]{1,0:T(8,128)(2,1)S(1)} %collective-permute-done.10.refs_1_), channel_id=1, source_target_pairs={{0,2},{2,0},{4,6},{6,4},{8,10},{10,8},{12,14},{14,12},{16,18},{18,... | collective-permute-start | bytes 983048 | tf_op jit(solution)/shard_map/ppermute | solution.py:265
  74.0 8.8 %collective-permute-start.19 = (bf16[288,384]{1,0:T(8,128)(2,1)S(1)}, bf16[288,384]{1,0:T(8,128)(2,1)S(1)}, u32[]{:S(2)}, u32[]{:S(2)}) collective-permute-start(bf16[288,384]{1,0:T(8,128)(2,1)S(1)} %get-tuple-element.25), channel_id=1, source_target_pairs={{0,8},{2,10},{4,12},{6,14},{8,0},{10,2},{12,4},{14,6},{16,24},{18,... | collective-permute-start | bytes 663560 | tf_op jit(solution)/shard_map/ppermute | solution.py:265
  75.1 13.3 %collective-permute-start.21 = (bf16[288,384]{1,0:T(8,128)(2,1)S(1)}, bf16[288,384]{1,0:T(8,128)(2,1)S(1)}, u32[]{:S(2)}, u32[]{:S(2)}) collective-permute-start(bf16[288,384]{1,0:T(8,128)(2,1)S(1)} %get-tuple-element.26), channel_id=1, source_target_pairs={{0,12},{2,14},{4,0},{6,2},{8,4},{10,6},{12,8},{14,10},{16,28},{18,... | collective-permute-start | bytes 663560 | tf_op jit(solution)/shard_map/ppermute | solution.py:265
  80.6 19.3 %collective-permute-start.18 = (bf16[256,384]{1,0:T(8,128)(2,1)S(1)}, bf16[256,384]{1,0:T(8,128)(2,1)S(1)}, u32[]{:S(2)}, u32[]{:S(2)}) collective-permute-start(bf16[256,384]{1,0:T(8,128)(2,1)S(1)} %shard_map.83), channel_id=1, source_target_pairs={{0,12},{2,14},{4,0},{6,2},{8,4},{10,6},{12,8},{14,10},{16,28},{18,... | collective-permute-start | bytes 589832 | tf_op jit(solution)/shard_map/ppermute | solution.py:265
  87.2 12.6 %collective-permute-start.20 = (bf16[256,384]{1,0:T(8,128)(2,1)S(1)}, bf16[256,384]{1,0:T(8,128)(2,1)S(1)}, u32[]{:S(2)}, u32[]{:S(2)}) collective-permute-start(bf16[256,384]{1,0:T(8,128)(2,1)S(1)} %shard_map.84), channel_id=1, source_target_pairs={{0,8},{2,10},{4,12},{6,14},{8,0},{10,2},{12,4},{14,6},{16,24},{18,... | collective-permute-start | bytes 589832 | tf_op jit(solution)/shard_map/ppermute | solution.py:265
  92.9 7.2 %collective-permute-start.22 = (bf16[256,384]{1,0:T(8,128)(2,1)S(1)}, bf16[256,384]{1,0:T(8,128)(2,1)S(1)}, u32[]{:S(2)}, u32[]{:S(2)}) collective-permute-start(bf16[256,384]{1,0:T(8,128)(2,1)S(1)} %shard_map.85), channel_id=1, source_target_pairs={{0,4},{2,6},{4,8},{6,10},{8,12},{10,14},{12,0},{14,2},{16,20},{18,... | collective-permute-start | bytes 589832 | tf_op jit(solution)/shard_map/ppermute | solution.py:265

commit v2 on v1

v2 whole, which is shorter than its diff:
```python
import functools

import jax
import jax.numpy as jnp
from jax import lax
from jax.experimental import pallas as pl
from jax.experimental.pallas import tpu as pltpu
from jax.sharding import PartitionSpec as P

HEADS = 20
HEAD_DIM = 64
GROUPS = 32
POOL = 4
WIDTH = 1280
CELLS = 256
ROWS = 16
GROUP_WIDTH = WIDTH // GROUPS
LANES = 128
SET_HEADS = 5
SET_ROWS = SET_HEADS * ROWS
ANSWER_ROWS = SET_HEADS * CELLS // 2
epsilon = 1e-05

f32 = jnp.float32
bf16 = jnp.bfloat16
HIGHEST = lax.Precision.HIGHEST
VMEM = pl.BlockSpec(memory_space=pltpu.VMEM)
SMEM = pl.BlockSpec(memory_space=pltpu.SMEM)
HBM = pl.BlockSpec(memory_space=pltpu.HBM)


def iota(shape, axis):
    return lax.broadcasted_iota(jnp.int32, shape, axis)


def group_of_channel():
    low = iota((WIDTH, LANES), 1) * GROUP_WIDTH
    channel = iota((WIDTH, LANES), 0)
    return ((channel >= low) & (channel < low + GROUP_WIDTH)).astype(f32)


def channel_of_group():
    low = iota((LANES, WIDTH), 0) * GROUP_WIDTH
    channel = iota((LANES, WIDTH), 1)
    return ((channel >= low) & (channel < low + GROUP_WIDTH)).astype(f32)


def exact_dot(left, right):
    return jnp.dot(left, right, precision=HIGHEST, preferred_element_type=f32)


def combine(parts, entries):
    mean = sum(part[0:1] for part in parts) / len(parts)
    squares = sum(part[1:2] for part in parts)
    apart = sum((part[0:1] - mean) * (part[0:1] - mean) for part in parts)
    return mean, squares + entries * apart


def stack_stats(mean, squares):
    row = iota((8, LANES), 0)
    return jnp.where(row == 0, mean, jnp.where(row == 1, squares, 0.0))


def encode(mean, squares):
    row = iota((ROWS, LANES), 0)
    coded = jnp.zeros((ROWS, LANES), f32)
    for i, rest in enumerate((mean, squares)):
        for part in range(3):
            rounded = rest.astype(bf16).astype(f32)
            coded = jnp.where(row == 3 * i + part, rounded, coded)
            rest = rest - rounded
    return coded.astype(bf16)


def decode(rows):
    parts = rows.astype(f32)
    return jnp.concatenate(
        [parts[0:1] + parts[1:2] + parts[2:3], parts[3:4] + parts[4:5] + parts[5:6]], axis=0
    )


def head_tiles(pairs):
    lane = iota((ROWS, LANES), 1)
    even, odd = [], []
    for t in range(WIDTH // LANES):
        keys = pairs[:, t * LANES : (t + 1) * LANES].astype(f32)
        values = pairs[:, WIDTH + t * LANES : WIDTH + (t + 1) * LANES].astype(f32)
        turned = pltpu.roll(values, HEAD_DIM, 1)
        even.append(jnp.where(lane < HEAD_DIM, keys, turned).astype(bf16))
        odd.append(jnp.where(lane < HEAD_DIM, turned, keys).astype(bf16))
    sets = []
    for j in range(4):
        last = (even if j % 2 == 0 else odd)[8 + j // 2]
        sets.append(
            jnp.concatenate(
                [even[2 * j], odd[2 * j], even[2 * j + 1], odd[2 * j + 1], last], axis=0
            )
        )
    return sets


def turn(block):
    return pltpu.roll(block.astype(f32), HEAD_DIM, 1)


def fold(block, mask):
    half = CELLS // 2
    return jnp.where(mask, block[0:half].astype(f32), turn(block[half:])).astype(bf16)


def unfold(block):
    return jnp.concatenate([block.astype(f32), turn(block)], axis=0)


def local_kernel(tokens_hbm, stale_hbm, stats_ref, sets_ref, tokens_ref, stale_ref, arrived):
    copies = [
        pltpu.make_async_copy(tokens_hbm, tokens_ref, arrived.at[0]),
        pltpu.make_async_copy(stale_hbm, stale_ref, arrived.at[1]),
    ]
    for copy in copies:
        copy.start()
    to_group, to_channel = group_of_channel(), channel_of_group()
    copies[0].wait()
    values = tokens_ref[...].astype(f32)
    sums = jnp.broadcast_to(jnp.sum(values, axis=0, keepdims=True), (8, WIDTH))
    mean = exact_dot(sums, to_group) / (CELLS * GROUP_WIDTH)
    center = exact_dot(mean, to_channel)
    shifted = values - center[0:1]
    squares = jnp.broadcast_to(jnp.sum(shifted * shifted, axis=0, keepdims=True), (8, WIDTH))
    squares = exact_dot(squares, to_group)
    stats_ref[...] = stack_stats(mean, squares)
    copies[1].wait()
    for j, block in enumerate(head_tiles(stale_ref[...])):
        sets_ref[j] = block


def x_kernel(place_ref, own_ref, other_ref, sets_ref, *out_refs):
    mean, squares = combine([own_ref[...], other_ref[...]], CELLS * GROUP_WIDTH)
    coded = encode(mean, squares)
    place = place_ref[0]
    for k, out_ref in enumerate(out_refs):
        out_ref[0:SET_ROWS, :] = sets_ref[lax.rem(place + k, 4)]
        out_ref[SET_ROWS:, :] = coded


def z_kernel(*refs):
    *in_refs, out_ref = refs
    stats = [decode(ref[SET_ROWS:, :]) for ref in in_refs]
    mean, squares = combine(stats, 2 * CELLS * GROUP_WIDTH)
    for k, ref in enumerate(in_refs):
        for h in range(SET_HEADS):
            low = h * 4 * ROWS + k * ROWS
            out_ref[low : low + ROWS, :] = ref[h * ROWS : (h + 1) * ROWS, :]
    out_ref[4 * SET_ROWS :, :] = encode(mean, squares)


def stats_kernel(*refs):
    *in_refs, stats_ref = refs
    stats = [decode(ref[4 * SET_ROWS :, :]) for ref in in_refs]
    mean, squares = combine(stats, 8 * CELLS * GROUP_WIDTH)
    stats_ref[...] = stack_stats(mean, squares)


def piece_kernel(stats_ref, *refs):
    *in_refs, out_ref = refs
    for k, ref in enumerate(in_refs):
        for h in range(SET_HEADS):
            low = h * CELLS + k * 4 * ROWS
            out_ref[low : low + 4 * ROWS, :] = ref[h * 4 * ROWS : (h + 1) * 4 * ROWS, :]


def weights_kernel(query_hbm, pair_hbm, gain_hbm, bias_hbm, *refs):
    *out_refs, arrived = refs
    copies = [
        pltpu.make_async_copy(source, target, arrived.at[i])
        for i, (source, target) in enumerate(
            zip((query_hbm, pair_hbm, gain_hbm, bias_hbm), out_refs)
        )
    ]
    for copy in copies:
        copy.start()
    for copy in copies:
        copy.wait()


def project_kernel(
    place_ref, tokens_ref, s0, s1, s2, s3, query_ref, pair_ref, gain_ref, bias_ref, *refs
):
    *message_refs, fresh_ref, sets_ref, last_ref = refs
    mean, squares = combine([s0[...], s1[...], s2[...], s3[...]], 32 * CELLS * GROUP_WIDTH)
    spread = squares / (128 * CELLS * GROUP_WIDTH)
    row = iota((8, LANES), 0)
    both = jnp.where(row == 0, mean, lax.rsqrt(spread + epsilon))
    channels = exact_dot(both, channel_of_group())
    scaled = (tokens_ref[...].astype(f32) - channels[0:1]) * channels[1:2]
    normed = (scaled * gain_ref[...] + bias_ref[...]).astype(bf16)

    square = iota((ROWS, CELLS), 0)
    cell = iota((ROWS, CELLS), 1)
    cell_square = lax.shift_right_logical(lax.bitwise_and(cell, 63), 2)
    pool = jnp.where(cell_square == square, 1.0 / (POOL * POOL), 0.0).astype(bf16)
    pooled = jnp.dot(pool, normed, preferred_element_type=f32).astype(bf16)

    place = place_ref[0]
    last = jnp.dot(normed, query_ref[:, 1024:], preferred_element_type=f32).astype(bf16)
    last_ref[0] = last[:, 0:LANES]
    last_ref[1] = last[:, LANES:]
    lane_half = lax.shift_right_logical(iota((CELLS // 2, LANES), 1), 6)
    for k in (2, 1, 3, 0):
        j = lax.rem(place + k, 4)
        columns = pl.ds(pl.multiple_of(j * 256, 256), 256)
        block = jnp.dot(normed, query_ref[:, columns], preferred_element_type=f32).astype(bf16)
        message_refs[k][0:CELLS, :] = block[:, 0:LANES]
        message_refs[k][CELLS : 2 * CELLS, :] = block[:, LANES:]
        mask = lane_half == lax.bitwise_and(j, 1)
        message_refs[k][2 * CELLS : ANSWER_ROWS, :] = fold(
            last_ref[lax.shift_right_logical(j, 1)], mask
        )

    fresh = jnp.dot(pooled, pair_ref[...], preferred_element_type=f32).astype(bf16)
    fresh_ref[...] = fresh
    for j, block in enumerate(head_tiles(fresh)):
        sets_ref[j] = block
    for k in range(4):
        message_refs[k][ANSWER_ROWS:, :] = sets_ref[lax.rem(place + k, 4)]


def attend_kernel(sources, place_ref, *refs):
    count = len(sources)
    message_refs, table_refs = refs[:count], refs[count : count + 8]
    out_refs, first_refs = refs[count + 8 : 2 * count + 8], refs[2 * count + 8 :]
    for source, message_ref, first_ref in zip(sources, message_refs, first_refs):
        first_ref[...] = table_refs[0][...]
        for h in range(SET_HEADS):
            low = h * CELLS + source * ROWS
            fresh = message_ref[ANSWER_ROWS + h * ROWS : ANSWER_ROWS + (h + 1) * ROWS, :]
            first_ref[low : low + ROWS, :] = fresh
    lane = iota((CELLS, LANES), 1)
    low_half = lane < HEAD_DIM
    parity = lax.bitwise_and(place_ref[0], 1)
    factor = HEAD_DIM ** (-0.5) * 1.4426950408889634
    against = (((1,), (1,)), ((), ()))
    results = []
    for h in range(SET_HEADS):
        if h < 4:
            mask = low_half if h % 2 == 0 else jnp.logical_not(low_half)
        else:
            mask = lax.shift_right_logical(lane, 6) == parity
        groups = []
        for message_ref in message_refs:
            if h < 4:
                queries = message_ref[(h // 2) * CELLS : (h // 2 + 1) * CELLS, :].astype(f32)
            else:
                queries = unfold(message_ref[2 * CELLS : ANSWER_ROWS, :])
            groups.append(jnp.where(mask, queries, 0.0).astype(bf16))
        queries = jnp.concatenate(groups, axis=0) if count > 1 else groups[0]
        head = slice(h * CELLS, (h + 1) * CELLS)
        firsts = [ref[head, :] for ref in first_refs]
        tiles = [ref[head, :] for ref in table_refs[1:]]
        scores = [
            jnp.concatenate(
                [
                    lax.dot_general(group, tile, against, preferred_element_type=f32)
                    for group, tile in zip(groups, firsts)
                ],
                axis=0,
            )
        ]
        for tile in tiles:
            scores.append(lax.dot_general(queries, tile, against, preferred_element_type=f32))
        largest = scores[0]
        for part in scores[1:]:
            largest = jnp.maximum(largest, part)
        largest = jnp.max(largest, axis=1, keepdims=True)
        total = summed = None
        for index, part in enumerate(scores):
            weights = jnp.exp2((part - largest) * factor)
            total = weights if total is None else total + weights
            weights = weights.astype(bf16)
            if index == 0:
                summed = jnp.concatenate(
                    [
                        jnp.dot(
                            weights[g * CELLS : (g + 1) * CELLS],
                            tile,
                            preferred_element_type=f32,
                        )
                        for g, tile in enumerate(firsts)
                    ],
                    axis=0,
                )
            else:
                summed = summed + jnp.dot(
                    weights, tiles[index - 1], preferred_element_type=f32
                )
        results.append(summed / jnp.sum(total, axis=1, keepdims=True))
    for g, out_ref in enumerate(out_refs):
        rows = slice(g * CELLS, (g + 1) * CELLS)
        for t in range(2):
            both = jnp.where(low_half, results[2 * t + 1][rows], results[2 * t][rows])
            out_ref[t * CELLS : (t + 1) * CELLS, :] = turn(both).astype(bf16)
        half = lax.shift_right_logical(iota((CELLS // 2, LANES), 1), 6)
        out_ref[2 * CELLS :, :] = fold(turn(results[4][rows]), half == parity)


def assemble_kernel(place_ref, *refs):
    *in_refs, out_ref, sets_ref = refs
    place = place_ref[0]
    for k, ref in enumerate(in_refs):
        sets_ref[lax.rem(place + k, 4)] = ref[...]
    for j in range(4):
        for t in range(2):
            low = (2 * j + t) * LANES
            out_ref[:, low : low + LANES] = sets_ref[j, t * CELLS : (t + 1) * CELLS, :]
    low_half = iota((CELLS, LANES), 1) < HEAD_DIM
    for t in range(2):
        low = (8 + t) * LANES
        both = [unfold(sets_ref[2 * t + i, 2 * CELLS :, :]) for i in range(2)]
        out_ref[:, low : low + LANES] = jnp.where(low_half, *both).astype(bf16)


def call(kernel, ins, outs, *args, scratch=(), limit=24):
    return pl.pallas_call(
        kernel,
        in_specs=ins,
        out_specs=[VMEM] * len(outs),
        out_shape=[jax.ShapeDtypeStruct(shape, kind) for shape, kind in outs],
        scratch_shapes=list(scratch),
        compiler_params=pltpu.CompilerParams(vmem_limit_bytes=limit * 1024 * 1024),
        cost_estimate=pl.CostEstimate(flops=1, bytes_accessed=1, transcendentals=0),
    )(*args)


AXES = {"z": (32, 4), "y": (8, 4), "x": (2, 4), "core": (1, 2)}


def shift(array, axis, step):
    stride, size = AXES[axis]
    pairs = []
    for source in range(128):
        place = source // stride % size
        target = source + ((place + step) % size - place) * stride
        pairs.append((source, target))
    return lax.ppermute(array, "patch", pairs)


def after(array, *others):
    return lax.optimization_barrier((array, *others))[0]


def per_device(tokens, stale_keys, norm_gain, norm_bias, query_weight, pair_weight):
    place = (lax.axis_index("patch") // 2 % 4).astype(jnp.int32).reshape(1)
    table = ((SET_HEADS * CELLS, LANES), bf16)
    answer = ((ANSWER_ROWS, LANES), bf16)
    stats, sets, tokens = call(
        local_kernel,
        [HBM, HBM],
        [((8, LANES), f32), ((4, SET_ROWS, LANES), bf16), ((CELLS, WIDTH), bf16)],
        tokens[0],
        stale_keys[0],
        scratch=[pltpu.VMEM((ROWS, 2 * WIDTH), bf16), pltpu.SemaphoreType.DMA((2,))],
    )
    other = shift(stats, "core", 1)
    messages = call(
        x_kernel,
        [SMEM, VMEM, VMEM, VMEM],
        [((SET_ROWS + ROWS, LANES), bf16)] * 4,
        place,
        stats,
        other,
        sets,
    )
    received = [messages[0]] + [shift(messages[k], "x", k) for k in (1, 2, 3)]
    (part,) = call(z_kernel, [VMEM] * 4, [((4 * SET_ROWS + ROWS, LANES), bf16)], *received)
    parts = [part] + [shift(part, "z", k) for k in (1, 2, 3)]
    query_weight, pair_weight, norm_gain, norm_bias, _ = lax.optimization_barrier(
        (query_weight, pair_weight, norm_gain, norm_bias, part)
    )
    weights = call(
        weights_kernel,
        [HBM] * 4,
        [
            ((WIDTH, WIDTH), bf16),
            ((WIDTH, 2 * WIDTH), bf16),
            ((1, WIDTH), f32),
            ((1, WIDTH), f32),
        ],
        query_weight,
        pair_weight,
        norm_gain.reshape(1, WIDTH),
        norm_bias.reshape(1, WIDTH),
        scratch=[pltpu.SemaphoreType.DMA((4,))],
    )
    parts, weights = lax.optimization_barrier((parts, weights))
    (stats,) = call(stats_kernel, [VMEM] * 4, [((8, LANES), f32)], *parts)
    all_stats = [stats] + [shift(stats, "y", k) for k in (1, 2, 3)]
    (piece,) = call(piece_kernel, [VMEM] * 5, [table], stats, *parts)
    pieces = [piece, shift(piece, "y", 1), shift(piece, "y", 3)]
    late = after(piece, *all_stats)
    pieces.append(shift(late, "y", 2))
    *queries, fresh = call(
        project_kernel,
        [SMEM] + [VMEM] * 9,
        [((ANSWER_ROWS + SET_ROWS, LANES), bf16)] * 4 + [((ROWS, 2 * WIDTH), bf16)],
        place,
        tokens,
        *all_stats,
        *weights,
        scratch=[
            pltpu.VMEM((4, SET_ROWS, LANES), bf16),
            pltpu.VMEM((2, CELLS, LANES), bf16),
        ],
    )
    asked = {0: queries[0]}
    for k in (2, 1, 3):
        asked[k] = shift(after(queries[k], pieces[1]) if k == 3 else queries[k], "x", k)
    pieces += [shift(block, "core", 1) for block in [late] + pieces[1:]]
    results = [None] * 4
    for sources in ((1, 3, 2), (0,)):
        answers = call(
            functools.partial(attend_kernel, sources),
            [SMEM] + [VMEM] * (len(sources) + 8),
            [answer] * len(sources),
            place,
            *[asked[k] for k in sources],
            *pieces,
            scratch=[pltpu.VMEM(*table)] * len(sources),
            limit=40,
        )
        for k, block in zip(sources, answers):
            results[k] = shift(block, "x", -k) if k else block
    (attended,) = call(
        assemble_kernel,
        [SMEM] + [VMEM] * 4,
        [((CELLS, WIDTH), bf16)],
        place,
        *results,
        scratch=[pltpu.VMEM((4, ANSWER_ROWS, LANES), bf16)],
    )
    return (attended[None], fresh[None])


def solution(mesh):
    return jax.shard_map(
        per_device,
        mesh=mesh,
        in_specs=(P("cfg", "patch", None), P("cfg", "patch", None), P(), P(), P(), P()),
        out_specs=(P("cfg", "patch", None), P("cfg", "patch", None)),
        check_vma=False,
    )
```

time: 101 us -> 86.8 us (0.86)
  the two profiles are of different devices: /device:TPU:32 before, /device:TPU:1 now
where the time goes in v2:
time: 86.8 us; the launch traced here: 86.4 us
  starting transfers between devices  39.6 us (46%)
  Pallas kernels  22.6 us (26%)
  waiting for transfers between devices  15.3 us (18%)
  local copies, waits for them, and re-layouts  8.15 us (9%)
    ppermute x23, starting transfers between devices, shift(): return lax.ppermute(array, 'patch', pairs)  39.6 us
    pallas_call x10, Pallas kernels, call(): pl.pallas_call(kernel, in_specs=ins, out_specs=[VMEM] * len(outs), out_sh...  22.6 us
    ppermute x23, waiting for transfers between devices, shift(): return lax.ppermute(array, 'patch', pairs)  15.3 us
    unnamed x8, local copies, waits for them, and re-layouts  6.75 us
  transfers between devices with their start and end apart: 23, of which 10 were waited for; matrix products, arithmetic and copies ran while one was open for 2% of the time, Pallas kernels for 10%

profile of v2, /device:TPU:1, one launch (start us, length us, event | category | flops | bytes accessed | tf_op | source)
XLA Modules:
  0.0 86.4 jit_solution(4122751845417546488)
XLA Ops:
  0.6 1.1 %copy-done.2 = bf16[1,256,1280]{2,1,0:T(8,128)(2,1)S(1)} copy-done((bf16[1,256,1280]{2,1,0:T(8,128)(2,1)S(1)}, bf16[1,256,1280]{2,1,0:T(8,128)(2,1)}, u32[]{:S(2)}) %copy-start.2) | copy-done | bytes 655384
  1.7 0.9 %copy-done.3 = bf16[1,16,2560]{2,1,0:T(8,128)(2,1)S(1)} copy-done((bf16[1,16,2560]{2,1,0:T(8,128)(2,1)S(1)}, bf16[1,16,2560]{2,1,0:T(8,128)(2,1)}, u32[]{:S(2)}) %copy-start.3) | copy-done | bytes 81944
  2.6 2.1 %shard_map.77 = (f32[8,128]{1,0:T(8,128)S(1)}, bf16[4,80,128]{2,1,0:T(8,128)(2,1)S(1)}, bf16[256,1280]{1,0:T(8,128)(2,1)S(1)}) custom-call(bf16[256,1280]{1,0:T(8,128)(2,1)S(1)} %bitcast.5, bf16[16,2560]{1,0:T(8,128)(2,1)S(1)} %bitcast.6), custom_call_target="tpu_custom_call" | custom-call | flops 1 | bytes 1 | tf_op jit(solution)/shard_map/pallas_call | solution.py:323
  4.7 3.3 %collective-permute-start = (f32[8,128]{1,0:T(8,128)S(1)}, f32[8,128]{1,0:T(8,128)S(1)}, u32[]{:S(2)}, u32[]{:S(2)}) collective-permute-start(f32[8,128]{1,0:T(8,128)S(1)} %get-tuple-element.36.own_ref), channel_id=1, source_target_pairs={{0,2},{2,0},{4,6},{6,4},{8,10},{10,8},{12,14},{14,12},{16,18},{18,... | collective-permute-start | bytes 12296 | tf_op jit(solution)/shard_map/ppermute | solution.py:344
  8.0 0.8 collective-permute-done.other_ref
  9.0 1.9 %collective-permute-start.2 = (bf16[96,128]{1,0:T(8,128)(2,1)S(1)}, bf16[96,128]{1,0:T(8,128)(2,1)S(1)}, u32[]{:S(2)}, u32[]{:S(2)}) collective-permute-start(bf16[96,128]{1,0:T(8,128)(2,1)S(1)} %get-tuple-element.40), channel_id=1, source_target_pairs={{0,8},{2,10},{4,12},{6,14},{8,0},{10,2},{12,4},{14,6},{16,24},{18,... | collective-permute-start | bytes 73736 | tf_op jit(solution)/shard_map/ppermute | solution.py:344
  10.9 1.2 %collective-permute-start.3 = (bf16[96,128]{1,0:T(8,128)(2,1)S(1)}, bf16[96,128]{1,0:T(8,128)(2,1)S(1)}, u32[]{:S(2)}, u32[]{:S(2)}) collective-permute-start(bf16[96,128]{1,0:T(8,128)(2,1)S(1)} %get-tuple-element.41), channel_id=1, source_target_pairs={{0,12},{2,14},{4,0},{6,2},{8,4},{10,6},{12,8},{14,10},{16,28},{18,... | collective-permute-start | bytes 73736 | tf_op jit(solution)/shard_map/ppermute | solution.py:344
  12.0 0.8 collective-permute-done.1.refs_1_
  13.2 0.7 collective-permute-done.3.refs_3_
  14.0 6.0 %collective-permute-start.6 = (bf16[336,128]{1,0:T(8,128)(2,1)S(1)}, bf16[336,128]{1,0:T(8,128)(2,1)S(1)}, u32[]{:S(2)}, u32[]{:S(2)}) collective-permute-start(bf16[336,128]{1,0:T(8,128)(2,1)S(1)} %shard_map.79.refs_0_), channel_id=1, source_target_pairs={{0,192},{2,194},{4,196},{6,198},{8,200},{10,202},{12,204},{14,206}... | collective-permute-start | bytes 258056 | tf_op jit(solution)/shard_map/ppermute | solution.py:344
  20.0 1.0 %collective-permute-start.5 = (bf16[336,128]{1,0:T(8,128)(2,1)S(1)}, bf16[336,128]{1,0:T(8,128)(2,1)S(1)}, u32[]{:S(2)}, u32[]{:S(2)}) collective-permute-start(bf16[336,128]{1,0:T(8,128)(2,1)S(1)} %shard_map.79.refs_0_), channel_id=1, source_target_pairs={{0,128},{2,130},{4,132},{6,134},{8,136},{10,138},{12,140},{14,142}... | collective-permute-start | bytes 258056 | tf_op jit(solution)/shard_map/ppermute | solution.py:344
  21.0 2.3 %collective-permute-start.4 = (bf16[336,128]{1,0:T(8,128)(2,1)S(1)}, bf16[336,128]{1,0:T(8,128)(2,1)S(1)}, u32[]{:S(2)}, u32[]{:S(2)}) collective-permute-start(bf16[336,128]{1,0:T(8,128)(2,1)S(1)} %shard_map.79.refs_0_), channel_id=1, source_target_pairs={{0,64},{2,66},{4,68},{6,70},{8,72},{10,74},{12,76},{14,78},{16,80}... | collective-permute-start | bytes 258056 | tf_op jit(solution)/shard_map/ppermute | solution.py:344
  24.6 2.9 %copy-done = bf16[1280,2560]{1,0:T(8,128)(2,1)S(1)} copy-done((bf16[1280,2560]{1,0:T(8,128)(2,1)S(1)}, bf16[1280,2560]{1,0:T(8,128)(2,1)}, u32[]{:S(2)}) %copy-start) | copy-done | bytes 6553624
  27.5 1.9 %copy-done.1 = bf16[1280,1280]{1,0:T(8,128)(2,1)S(1)} copy-done((bf16[1280,1280]{1,0:T(8,128)(2,1)S(1)}, bf16[1280,1280]{1,0:T(8,128)(2,1)}, u32[]{:S(2)}) %copy-start.1) | copy-done | bytes 3276824
  29.4 0.9 %shard_map.80 = (bf16[1280,1280]{1,0:T(8,128)(2,1)S(1)}, bf16[1280,2560]{1,0:T(8,128)(2,1)S(1)}, f32[1,1280]{1,0:T(1,128)S(1)}, f32[1,1280]{1,0:T(1,128)S(1)}) custom-call(bf16[1280,1280]{1,0:T(8,128)(2,1)S(1)} %copy-done.1, bf16[1280,2560]{1,0:T(8,128)(2,1)S(1)} %copy-done, f32[1,1280]{1,0:T(1,128)S(1)} %reshape.14.gain_hbm, f32[1,1280]{1,0:T(1,128)S(1)} %reshape.15.bias_hbm), custom_call_target="tpu_custom_call" | custom-call | flops 1 | bytes 1 | tf_op jit(solution)/shard_map/pallas_call | solution.py:323
  30.4 2.8 %collective-permute-start.9 = (f32[8,128]{1,0:T(8,128)S(1)}, f32[8,128]{1,0:T(8,128)S(1)}, u32[]{:S(2)}, u32[]{:S(2)}) collective-permute-start(f32[8,128]{1,0:T(8,128)S(1)} %shard_map.81.s0.stats_ref), channel_id=1, source_target_pairs={{0,48},{2,50},{4,52},{6,54},{8,56},{10,58},{12,60},{14,62},{16,0},... | collective-permute-start | bytes 12296 | tf_op jit(solution)/shard_map/ppermute | solution.py:344
  34.2 2.1 %collective-permute-start.11 = (bf16[1280,128]{1,0:T(8,128)(2,1)S(1)}, bf16[1280,128]{1,0:T(8,128)(2,1)S(1)}, u32[]{:S(2)}, u32[]{:S(2)}) collective-permute-start(bf16[1280,128]{1,0:T(8,128)(2,1)S(1)} %shard_map.83.refs_1_.refs_3_), channel_id=1, source_target_pairs={{0,48},{2,50},{4,52},{6,54},{8,56},{10,58},{12,60},{14,62},{16,0},... | collective-permute-start | bytes 983048 | tf_op jit(solution)/shard_map/ppermute | solution.py:344
  36.3 0.8 collective-permute-done.8.s2
  37.2 1.4 %collective-permute-start.12 = (bf16[1280,128]{1,0:T(8,128)(2,1)S(1)}, bf16[1280,128]{1,0:T(8,128)(2,1)S(1)}, u32[]{:S(2)}, u32[]{:S(2)}) collective-permute-start(bf16[1280,128]{1,0:T(8,128)(2,1)S(1)} %shard_map.83.refs_1_.refs_3_), channel_id=1, source_target_pairs={{0,32},{2,34},{4,36},{6,38},{8,40},{10,42},{12,44},{14,46},{16,48}... | collective-permute-start | bytes 983048 | tf_op jit(solution)/shard_map/ppermute | solution.py:344
  38.6 3.2 %shard_map.82 = (bf16[720,128]{1,0:T(8,128)(2,1)S(1)}, bf16[720,128]{1,0:T(8,128)(2,1)S(1)}, bf16[720,128]{1,0:T(8,128)(2,1)S(1)}, bf16[720,128]{1,0:T(8,128)(2,1)S(1)}, bf16[16,2560]{1,0:T(8,128)(2,1)}) custom-call(s32[1]{0:T(128)} %bitcast.place_ref, bf16[256,1280]{1,0:T(8,128)(2,1)S(1)} %get-tuple-element.35.tokens_ref, ...), custom_call_target="tpu_custom_call" | custom-call | flops 1 | bytes 1 | tf_op jit(solution)/shard_map/pallas_call | solution.py:323
  41.8 3.2 %collective-permute-start.19 = (bf16[720,128]{1,0:T(8,128)(2,1)S(1)}, bf16[720,128]{1,0:T(8,128)(2,1)S(1)}, u32[]{:S(2)}, u32[]{:S(2)}) collective-permute-start(bf16[720,128]{1,0:T(8,128)(2,1)S(1)} %get-tuple-element.63), channel_id=1, source_target_pairs={{0,8},{2,10},{4,12},{6,14},{8,0},{10,2},{12,4},{14,6},{16,24},{18,... | collective-permute-start | bytes 552968 | tf_op jit(solution)/shard_map/ppermute | solution.py:344
  45.1 2.6 %collective-permute-done.17.refs_0_ = bf16[720,128]{1,0:T(8,128)(2,1)S(1)} collective-permute-done((bf16[720,128]{1,0:T(8,128)(2,1)S(1)}, bf16[720,128]{1,0:T(8,128)(2,1)S(1)}, u32[]{:S(2)}, u32[]{:S(2)}) %collective-permute-start.17) | collective-permute-done | bytes 184352 | tf_op jit(solution)/shard_map/ppermute | solution.py:344
  47.7 5.5 %collective-permute-start.13 = (bf16[1280,128]{1,0:T(8,128)(2,1)S(1)}, bf16[1280,128]{1,0:T(8,128)(2,1)S(1)}, u32[]{:S(2)}, u32[]{:S(2)}) collective-permute-start(bf16[1280,128]{1,0:T(8,128)(2,1)S(1)} %shard_map.83.refs_1_.refs_3_), channel_id=1, source_target_pairs={{0,2},{2,0},{4,6},{6,4},{8,10},{10,8},{12,14},{14,12},{16,18},{18,... | collective-permute-start | bytes 983048 | tf_op jit(solution)/shard_map/ppermute | solution.py:344
  53.3 1.5 %collective-permute-start.14 = (bf16[1280,128]{1,0:T(8,128)(2,1)S(1)}, bf16[1280,128]{1,0:T(8,128)(2,1)S(1)}, u32[]{:S(2)}, u32[]{:S(2)}) collective-permute-start(bf16[1280,128]{1,0:T(8,128)(2,1)S(1)} %collective-permute-done.10.refs_2_.refs_4_), channel_id=1, source_target_pairs={{0,2},{2,0},{4,6},{6,4},{8,10},{10,8},{12,14},{14,12},{16,18},{18,... | collective-permute-start | bytes 983048 | tf_op jit(solution)/shard_map/ppermute | solution.py:344
  54.8 2.1 %collective-permute-start.18 = (bf16[720,128]{1,0:T(8,128)(2,1)S(1)}, bf16[720,128]{1,0:T(8,128)(2,1)S(1)}, u32[]{:S(2)}, u32[]{:S(2)}) collective-permute-start(bf16[720,128]{1,0:T(8,128)(2,1)S(1)} %get-tuple-element.62), channel_id=1, source_target_pairs={{0,12},{2,14},{4,0},{6,2},{8,4},{10,6},{12,8},{14,10},{16,28},{18,... | collective-permute-start | bytes 552968 | tf_op jit(solution)/shard_map/ppermute | solution.py:344
  56.9 3.6 %collective-permute-done.18.refs_1_ = bf16[720,128]{1,0:T(8,128)(2,1)S(1)} collective-permute-done((bf16[720,128]{1,0:T(8,128)(2,1)S(1)}, bf16[720,128]{1,0:T(8,128)(2,1)S(1)}, u32[]{:S(2)}, u32[]{:S(2)}) %collective-permute-start.18) | collective-permute-done | bytes 184352 | tf_op jit(solution)/shard_map/ppermute | solution.py:344
  60.5 10.9 %shard_map.85 = (bf16[640,128]{1,0:T(8,128)(2,1)S(1)}, bf16[640,128]{1,0:T(8,128)(2,1)S(1)}, bf16[640,128]{1,0:T(8,128)(2,1)S(1)}) custom-call(s32[1]{0:T(128)} %bitcast.place_ref, bf16[720,128]{1,0:T(8,128)(2,1)S(1)} %collective-permute-done.17.refs_0_, bf16[720,128]{1,0:T(8,128)(2,1)S(1)} %collective-permute-done.18.refs_1_, ...), custom_call_target="tpu_custom_call" | custom-call | flops 1 | bytes 1 | tf_op jit(solution)/shard_map/pallas_call | solution.py:323
  71.5 3.5 %collective-permute-start.20 = (bf16[640,128]{1,0:T(8,128)(2,1)S(1)}, bf16[640,128]{1,0:T(8,128)(2,1)S(1)}, u32[]{:S(2)}, u32[]{:S(2)}) collective-permute-start(bf16[640,128]{1,0:T(8,128)(2,1)S(1)} %get-tuple-element.64), channel_id=1, source_target_pairs={{0,12},{2,14},{4,0},{6,2},{8,4},{10,6},{12,8},{14,10},{16,28},{18,... | collective-permute-start | bytes 491528 | tf_op jit(solution)/shard_map/ppermute | solution.py:344
  75.6 4.4 %shard_map.84.refs_0_ = bf16[640,128]{1,0:T(8,128)(2,1)S(1)} custom-call(s32[1]{0:T(128)} %bitcast.place_ref, bf16[720,128]{1,0:T(8,128)(2,1)S(1)} %get-tuple-element.58.refs_0_, bf16[1280,128]{1,0:T(8,128)(2,1)S(1)} %shard_map.83.refs_1_.refs_3_, bf16[1280,128]{1,0:T(8,128)(2,1)S(1)} %collective-permute-done.10.refs_2_.refs_4_, ...), custom_call_target="tpu_custom_call" | custom-call | flops 1 | bytes 1 | tf_op jit(solution)/shard_map/pallas_call | solution.py:323
  80.0 1.2 %collective-permute-done.20.refs_1_ = bf16[640,128]{1,0:T(8,128)(2,1)S(1)} collective-permute-done((bf16[640,128]{1,0:T(8,128)(2,1)S(1)}, bf16[640,128]{1,0:T(8,128)(2,1)S(1)}, u32[]{:S(2)}, u32[]{:S(2)}) %collective-permute-start.20) | collective-permute-done | bytes 163872 | tf_op jit(solution)/shard_map/ppermute | solution.py:344
  81.2 4.2 %collective-permute-done.22.refs_3_ = bf16[640,128]{1,0:T(8,128)(2,1)S(1)} collective-permute-done((bf16[640,128]{1,0:T(8,128)(2,1)S(1)}, bf16[640,128]{1,0:T(8,128)(2,1)S(1)}, u32[]{:S(2)}, u32[]{:S(2)}) %collective-permute-start.22) | collective-permute-done | bytes 163872 | tf_op jit(solution)/shard_map/ppermute | solution.py:344
  85.4 1.0 %shard_map.86 = bf16[256,1280]{1,0:T(8,128)(2,1)} custom-call(s32[1]{0:T(128)} %bitcast.place_ref, bf16[640,128]{1,0:T(8,128)(2,1)S(1)} %shard_map.84.refs_0_, bf16[640,128]{1,0:T(8,128)(2,1)S(1)} %collective-permute-done.20.refs_1_, bf16[640,128]{1,0:T(8,128)(2,1)S(1)} %collective-permute-done.21.refs_2_, bf16[640,128]{1,0:T(8,128)(2,1)S(1)} %collective-permute-done.22.refs_3_), custom_call_target="tpu_custom_call" | custom-call | flops 1 | bytes 1 | tf_op jit(solution)/shard_map/pallas_call | solution.py:323
  (34 shorter events, 3.8 us)
Async XLA Ops:
  0.6 1.1 %copy-start.2 = (bf16[1,256,1280]{2,1,0:T(8,128)(2,1)S(1)}, bf16[1,256,1280]{2,1,0:T(8,128)(2,1)}, u32[]{:S(2)}) copy-start(bf16[1,256,1280]{2,1,0:T(8,128)(2,1)} %param.6) | copy-start | bytes 1966084
  1.7 0.9 %copy-start.3 = (bf16[1,16,2560]{2,1,0:T(8,128)(2,1)S(1)}, bf16[1,16,2560]{2,1,0:T(8,128)(2,1)}, u32[]{:S(2)}) copy-start(bf16[1,16,2560]{2,1,0:T(8,128)(2,1)} %param.7) | copy-start | bytes 245764
  4.7 4.2 %collective-permute-start = (f32[8,128]{1,0:T(8,128)S(1)}, f32[8,128]{1,0:T(8,128)S(1)}, u32[]{:S(2)}, u32[]{:S(2)}) collective-permute-start(f32[8,128]{1,0:T(8,128)S(1)} %get-tuple-element.36.own_ref), channel_id=1, source_target_pairs={{0,2},{2,0},{4,6},{6,4},{8,10},{10,8},{12,14},{14,12},{16,18},{18,... | collective-permute-start | bytes 12296 | tf_op jit(solution)/shard_map/ppermute | solution.py:344
  8.9 4.0 %collective-permute-start.1 = (bf16[96,128]{1,0:T(8,128)(2,1)S(1)}, bf16[96,128]{1,0:T(8,128)(2,1)S(1)}, u32[]{:S(2)}, u32[]{:S(2)}) collective-permute-start(bf16[96,128]{1,0:T(8,128)(2,1)S(1)} %get-tuple-element.39), channel_id=1, source_target_pairs={{0,4},{2,6},{4,8},{6,10},{8,12},{10,14},{12,0},{14,2},{16,20},{18,... | collective-permute-start | bytes 73736 | tf_op jit(solution)/shard_map/ppermute | solution.py:344
  9.0 4.3 %collective-permute-start.2 = (bf16[96,128]{1,0:T(8,128)(2,1)S(1)}, bf16[96,128]{1,0:T(8,128)(2,1)S(1)}, u32[]{:S(2)}, u32[]{:S(2)}) collective-permute-start(bf16[96,128]{1,0:T(8,128)(2,1)S(1)} %get-tuple-element.40), channel_id=1, source_target_pairs={{0,8},{2,10},{4,12},{6,14},{8,0},{10,2},{12,4},{14,6},{16,24},{18,... | collective-permute-start | bytes 73736 | tf_op jit(solution)/shard_map/ppermute | solution.py:344
  10.9 3.1 %collective-permute-start.3 = (bf16[96,128]{1,0:T(8,128)(2,1)S(1)}, bf16[96,128]{1,0:T(8,128)(2,1)S(1)}, u32[]{:S(2)}, u32[]{:S(2)}) collective-permute-start(bf16[96,128]{1,0:T(8,128)(2,1)S(1)} %get-tuple-element.41), channel_id=1, source_target_pairs={{0,12},{2,14},{4,0},{6,2},{8,4},{10,6},{12,8},{14,10},{16,28},{18,... | collective-permute-start | bytes 73736 | tf_op jit(solution)/shard_map/ppermute | solution.py:344
  14.0 16.3 %collective-permute-start.6 = (bf16[336,128]{1,0:T(8,128)(2,1)S(1)}, bf16[336,128]{1,0:T(8,128)(2,1)S(1)}, u32[]{:S(2)}, u32[]{:S(2)}) collective-permute-start(bf16[336,128]{1,0:T(8,128)(2,1)S(1)} %shard_map.79.refs_0_), channel_id=1, source_target_pairs={{0,192},{2,194},{4,196},{6,198},{8,200},{10,202},{12,204},{14,206}... | collective-permute-start | bytes 258056 | tf_op jit(solution)/shard_map/ppermute | solution.py:344
  20.0 10.3 %collective-permute-start.5 = (bf16[336,128]{1,0:T(8,128)(2,1)S(1)}, bf16[336,128]{1,0:T(8,128)(2,1)S(1)}, u32[]{:S(2)}, u32[]{:S(2)}) collective-permute-start(bf16[336,128]{1,0:T(8,128)(2,1)S(1)} %shard_map.79.refs_0_), channel_id=1, source_target_pairs={{0,128},{2,130},{4,132},{6,134},{8,136},{10,138},{12,140},{14,142}... | collective-permute-start | bytes 258056 | tf_op jit(solution)/shard_map/ppermute | solution.py:344
  21.0 9.4 %collective-permute-start.4 = (bf16[336,128]{1,0:T(8,128)(2,1)S(1)}, bf16[336,128]{1,0:T(8,128)(2,1)S(1)}, u32[]{:S(2)}, u32[]{:S(2)}) collective-permute-start(bf16[336,128]{1,0:T(8,128)(2,1)S(1)} %shard_map.79.refs_0_), channel_id=1, source_target_pairs={{0,64},{2,66},{4,68},{6,70},{8,72},{10,74},{12,76},{14,78},{16,80}... | collective-permute-start | bytes 258056 | tf_op jit(solution)/shard_map/ppermute | solution.py:344
  24.6 2.9 %copy-start = (bf16[1280,2560]{1,0:T(8,128)(2,1)S(1)}, bf16[1280,2560]{1,0:T(8,128)(2,1)}, u32[]{:S(2)}) copy-start(bf16[1280,2560]{1,0:T(8,128)(2,1)} %pair_hbm) | copy-start | bytes 19660804
  27.5 1.9 %copy-start.1 = (bf16[1280,1280]{1,0:T(8,128)(2,1)S(1)}, bf16[1280,1280]{1,0:T(8,128)(2,1)}, u32[]{:S(2)}) copy-start(bf16[1280,1280]{1,0:T(8,128)(2,1)} %query_hbm) | copy-start | bytes 9830404
  30.4 5.9 %collective-permute-start.9 = (f32[8,128]{1,0:T(8,128)S(1)}, f32[8,128]{1,0:T(8,128)S(1)}, u32[]{:S(2)}, u32[]{:S(2)}) collective-permute-start(f32[8,128]{1,0:T(8,128)S(1)} %shard_map.81.s0.stats_ref), channel_id=1, source_target_pairs={{0,48},{2,50},{4,52},{6,54},{8,56},{10,58},{12,60},{14,62},{16,0},... | collective-permute-start | bytes 12296 | tf_op jit(solution)/shard_map/ppermute | solution.py:344
  33.2 4.0 %collective-permute-start.8 = (f32[8,128]{1,0:T(8,128)S(1)}, f32[8,128]{1,0:T(8,128)S(1)}, u32[]{:S(2)}, u32[]{:S(2)}) collective-permute-start(f32[8,128]{1,0:T(8,128)S(1)} %shard_map.81.s0.stats_ref), channel_id=1, source_target_pairs={{0,32},{2,34},{4,36},{6,38},{8,40},{10,42},{12,44},{14,46},{16,48}... | collective-permute-start | bytes 12296 | tf_op jit(solution)/shard_map/ppermute | solution.py:344
  33.5 3.7 %collective-permute-start.7 = (f32[8,128]{1,0:T(8,128)S(1)}, f32[8,128]{1,0:T(8,128)S(1)}, u32[]{:S(2)}, u32[]{:S(2)}) collective-permute-start(f32[8,128]{1,0:T(8,128)S(1)} %shard_map.81.s0.stats_ref), channel_id=1, source_target_pairs={{0,16},{2,18},{4,20},{6,22},{8,24},{10,26},{12,28},{14,30},{16,32}... | collective-permute-start | bytes 12296 | tf_op jit(solution)/shard_map/ppermute | solution.py:344
  34.2 19.0 %collective-permute-start.11 = (bf16[1280,128]{1,0:T(8,128)(2,1)S(1)}, bf16[1280,128]{1,0:T(8,128)(2,1)S(1)}, u32[]{:S(2)}, u32[]{:S(2)}) collective-permute-start(bf16[1280,128]{1,0:T(8,128)(2,1)S(1)} %shard_map.83.refs_1_.refs_3_), channel_id=1, source_target_pairs={{0,48},{2,50},{4,52},{6,54},{8,56},{10,58},{12,60},{14,62},{16,0},... | collective-permute-start | bytes 983048 | tf_op jit(solution)/shard_map/ppermute | solution.py:344
  36.3 17.0 %collective-permute-start.10 = (bf16[1280,128]{1,0:T(8,128)(2,1)S(1)}, bf16[1280,128]{1,0:T(8,128)(2,1)S(1)}, u32[]{:S(2)}, u32[]{:S(2)}) collective-permute-start(bf16[1280,128]{1,0:T(8,128)(2,1)S(1)} %shard_map.83.refs_1_.refs_3_), channel_id=1, source_target_pairs={{0,16},{2,18},{4,20},{6,22},{8,24},{10,26},{12,28},{14,30},{16,32}... | collective-permute-start | bytes 983048 | tf_op jit(solution)/shard_map/ppermute | solution.py:344
  37.2 17.6 %collective-permute-start.12 = (bf16[1280,128]{1,0:T(8,128)(2,1)S(1)}, bf16[1280,128]{1,0:T(8,128)(2,1)S(1)}, u32[]{:S(2)}, u32[]{:S(2)}) collective-permute-start(bf16[1280,128]{1,0:T(8,128)(2,1)S(1)} %shard_map.83.refs_1_.refs_3_), channel_id=1, source_target_pairs={{0,32},{2,34},{4,36},{6,38},{8,40},{10,42},{12,44},{14,46},{16,48}... | collective-permute-start | bytes 983048 | tf_op jit(solution)/shard_map/ppermute | solution.py:344
  41.8 5.9 %collective-permute-start.17 = (bf16[720,128]{1,0:T(8,128)(2,1)S(1)}, bf16[720,128]{1,0:T(8,128)(2,1)S(1)}, u32[]{:S(2)}, u32[]{:S(2)}) collective-permute-start(bf16[720,128]{1,0:T(8,128)(2,1)S(1)} %get-tuple-element.60), channel_id=1, source_target_pairs={{0,4},{2,6},{4,8},{6,10},{8,12},{10,14},{12,0},{14,2},{16,20},{18,... | collective-permute-start | bytes 552968 | tf_op jit(solution)/shard_map/ppermute | solution.py:344
  41.8 13.0 %collective-permute-start.19 = (bf16[720,128]{1,0:T(8,128)(2,1)S(1)}, bf16[720,128]{1,0:T(8,128)(2,1)S(1)}, u32[]{:S(2)}, u32[]{:S(2)}) collective-permute-start(bf16[720,128]{1,0:T(8,128)(2,1)S(1)} %get-tuple-element.63), channel_id=1, source_target_pairs={{0,8},{2,10},{4,12},{6,14},{8,0},{10,2},{12,4},{14,6},{16,24},{18,... | collective-permute-start | bytes 552968 | tf_op jit(solution)/shard_map/ppermute | solution.py:344
  47.7 9.2 %collective-permute-start.13 = (bf16[1280,128]{1,0:T(8,128)(2,1)S(1)}, bf16[1280,128]{1,0:T(8,128)(2,1)S(1)}, u32[]{:S(2)}, u32[]{:S(2)}) collective-permute-start(bf16[1280,128]{1,0:T(8,128)(2,1)S(1)} %shard_map.83.refs_1_.refs_3_), channel_id=1, source_target_pairs={{0,2},{2,0},{4,6},{6,4},{8,10},{10,8},{12,14},{14,12},{16,18},{18,... | collective-permute-start | bytes 983048 | tf_op jit(solution)/shard_map/ppermute | solution.py:344
  53.3 7.3 %collective-permute-start.15 = (bf16[1280,128]{1,0:T(8,128)(2,1)S(1)}, bf16[1280,128]{1,0:T(8,128)(2,1)S(1)}, u32[]{:S(2)}, u32[]{:S(2)}) collective-permute-start(bf16[1280,128]{1,0:T(8,128)(2,1)S(1)} %collective-permute-done.11.refs_3_.refs_5_), channel_id=1, source_target_pairs={{0,2},{2,0},{4,6},{6,4},{8,10},{10,8},{12,14},{14,12},{16,18},{18,... | collective-permute-start | bytes 983048 | tf_op jit(solution)/shard_map/ppermute | solution.py:344
  53.3 7.2 %collective-permute-start.14 = (bf16[1280,128]{1,0:T(8,128)(2,1)S(1)}, bf16[1280,128]{1,0:T(8,128)(2,1)S(1)}, u32[]{:S(2)}, u32[]{:S(2)}) collective-permute-start(bf16[1280,128]{1,0:T(8,128)(2,1)S(1)} %collective-permute-done.10.refs_2_.refs_4_), channel_id=1, source_target_pairs={{0,2},{2,0},{4,6},{6,4},{8,10},{10,8},{12,14},{14,12},{16,18},{18,... | collective-permute-start | bytes 983048 | tf_op jit(solution)/shard_map/ppermute | solution.py:344
  54.8 5.8 %collective-permute-start.16 = (bf16[1280,128]{1,0:T(8,128)(2,1)S(1)}, bf16[1280,128]{1,0:T(8,128)(2,1)S(1)}, u32[]{:S(2)}, u32[]{:S(2)}) collective-permute-start(bf16[1280,128]{1,0:T(8,128)(2,1)S(1)} %collective-permute-done.12.refs_4_.refs_6_), channel_id=1, source_target_pairs={{0,2},{2,0},{4,6},{6,4},{8,10},{10,8},{12,14},{14,12},{16,18},{18,... | collective-permute-start | bytes 983048 | tf_op jit(solution)/shard_map/ppermute | solution.py:344
  54.8 5.7 %collective-permute-start.18 = (bf16[720,128]{1,0:T(8,128)(2,1)S(1)}, bf16[720,128]{1,0:T(8,128)(2,1)S(1)}, u32[]{:S(2)}, u32[]{:S(2)}) collective-permute-start(bf16[720,128]{1,0:T(8,128)(2,1)S(1)} %get-tuple-element.62), channel_id=1, source_target_pairs={{0,12},{2,14},{4,0},{6,2},{8,4},{10,6},{12,8},{14,10},{16,28},{18,... | collective-permute-start | bytes 552968 | tf_op jit(solution)/shard_map/ppermute | solution.py:344
  71.5 9.8 %collective-permute-start.20 = (bf16[640,128]{1,0:T(8,128)(2,1)S(1)}, bf16[640,128]{1,0:T(8,128)(2,1)S(1)}, u32[]{:S(2)}, u32[]{:S(2)}) collective-permute-start(bf16[640,128]{1,0:T(8,128)(2,1)S(1)} %get-tuple-element.64), channel_id=1, source_target_pairs={{0,12},{2,14},{4,0},{6,2},{8,4},{10,6},{12,8},{14,10},{16,28},{18,... | collective-permute-start | bytes 491528 | tf_op jit(solution)/shard_map/ppermute | solution.py:344
  74.9 6.3 %collective-permute-start.21 = (bf16[640,128]{1,0:T(8,128)(2,1)S(1)}, bf16[640,128]{1,0:T(8,128)(2,1)S(1)}, u32[]{:S(2)}, u32[]{:S(2)}) collective-permute-start(bf16[640,128]{1,0:T(8,128)(2,1)S(1)} %get-tuple-element.65), channel_id=1, source_target_pairs={{0,8},{2,10},{4,12},{6,14},{8,0},{10,2},{12,4},{14,6},{16,24},{18,... | collective-permute-start | bytes 491528 | tf_op jit(solution)/shard_map/ppermute | solution.py:344
  74.9 10.5 %collective-permute-start.22 = (bf16[640,128]{1,0:T(8,128)(2,1)S(1)}, bf16[640,128]{1,0:T(8,128)(2,1)S(1)}, u32[]{:S(2)}, u32[]{:S(2)}) collective-permute-start(bf16[640,128]{1,0:T(8,128)(2,1)S(1)} %get-tuple-element.66), channel_id=1, source_target_pairs={{0,4},{2,6},{4,8},{6,10},{8,12},{10,14},{12,0},{14,2},{16,20},{18,... | collective-permute-start | bytes 491528 | tf_op jit(solution)/shard_map/ppermute | solution.py:344

commit v3 on v2

--- a/solution.py
+++ b/solution.py
@@ -112,24 +112,20 @@
     return jnp.concatenate([block.astype(f32), turn(block)], axis=0)
 
 
-def local_kernel(tokens_hbm, stale_hbm, stats_ref, sets_ref, tokens_ref, stale_ref, arrived):
-    copies = [
-        pltpu.make_async_copy(tokens_hbm, tokens_ref, arrived.at[0]),
-        pltpu.make_async_copy(stale_hbm, stale_ref, arrived.at[1]),
-    ]
-    for copy in copies:
-        copy.start()
-    to_group, to_channel = group_of_channel(), channel_of_group()
-    copies[0].wait()
-    values = tokens_ref[...].astype(f32)
+def local_kernel(tokens_ref, stats_ref, kept_ref):
+    tokens = tokens_ref[...]
+    kept_ref[...] = tokens
+    values = tokens.astype(f32)
     sums = jnp.broadcast_to(jnp.sum(values, axis=0, keepdims=True), (8, WIDTH))
-    mean = exact_dot(sums, to_group) / (CELLS * GROUP_WIDTH)
-    center = exact_dot(mean, to_channel)
+    mean = exact_dot(sums, group_of_channel()) / (CELLS * GROUP_WIDTH)
+    center = exact_dot(mean, channel_of_group())
     shifted = values - center[0:1]
     squares = jnp.broadcast_to(jnp.sum(shifted * shifted, axis=0, keepdims=True), (8, WIDTH))
-    squares = exact_dot(squares, to_group)
+    squares = exact_dot(squares, group_of_channel())
     stats_ref[...] = stack_stats(mean, squares)
-    copies[1].wait()
+
+
+def sets_kernel(stats_ref, stale_ref, sets_ref):
     for j, block in enumerate(head_tiles(stale_ref[...])):
         sets_ref[j] = block
 
@@ -193,7 +189,9 @@
     both = jnp.where(row == 0, mean, lax.rsqrt(spread + epsilon))
     channels = exact_dot(both, channel_of_group())
     scaled = (tokens_ref[...].astype(f32) - channels[0:1]) * channels[1:2]
-    normed = (scaled * gain_ref[...] + bias_ref[...]).astype(bf16)
+    gain = gain_ref[...].reshape(1, WIDTH)
+    bias = bias_ref[...].reshape(1, WIDTH)
+    normed = (scaled * gain + bias).astype(bf16)
 
     square = iota((ROWS, CELLS), 0)
     cell = iota((ROWS, CELLS), 1)
@@ -240,8 +238,9 @@
     parity = lax.bitwise_and(place_ref[0], 1)
     factor = HEAD_DIM ** (-0.5) * 1.4426950408889634
     against = (((1,), (1,)), ((), ()))
-    results = []
-    for h in range(SET_HEADS):
+    ones = jnp.ones((CELLS, LANES), bf16)
+
+    def head_scores(h):
         if h < 4:
             mask = low_half if h % 2 == 0 else jnp.logical_not(low_half)
         else:
@@ -255,45 +254,43 @@
             groups.append(jnp.where(mask, queries, 0.0).astype(bf16))
         queries = jnp.concatenate(groups, axis=0) if count > 1 else groups[0]
         head = slice(h * CELLS, (h + 1) * CELLS)
-        firsts = [ref[head, :] for ref in first_refs]
-        tiles = [ref[head, :] for ref in table_refs[1:]]
-        scores = [
-            jnp.concatenate(
-                [
-                    lax.dot_general(group, tile, against, preferred_element_type=f32)
-                    for group, tile in zip(groups, firsts)
-                ],
-                axis=0,
-            )
+        firsts = [
+            lax.dot_general(group, ref[head, :], against, preferred_element_type=f32)
+            for group, ref in zip(groups, first_refs)
         ]
-        for tile in tiles:
-            scores.append(lax.dot_general(queries, tile, against, preferred_element_type=f32))
+        scores = [jnp.concatenate(firsts, axis=0)]
+        for ref in table_refs[1:]:
+            keys = ref[head, :]
+            scores.append(lax.dot_general(queries, keys, against, preferred_element_type=f32))
+        return scores
+
+    def head_result(h, scores):
+        head = slice(h * CELLS, (h + 1) * CELLS)
         largest = scores[0]
         for part in scores[1:]:
             largest = jnp.maximum(largest, part)
         largest = jnp.max(largest, axis=1, keepdims=True)
-        total = summed = None
+        summed = None
         for index, part in enumerate(scores):
-            weights = jnp.exp2((part - largest) * factor)
-            total = weights if total is None else total + weights
-            weights = weights.astype(bf16)
+            weights = jnp.exp2((part - largest) * factor).astype(bf16)
             if index == 0:
-                summed = jnp.concatenate(
-                    [
-                        jnp.dot(
-                            weights[g * CELLS : (g + 1) * CELLS],
-                            tile,
-                            preferred_element_type=f32,
-                        )
-                        for g, tile in enumerate(firsts)
-                    ],
-                    axis=0,
-                )
+                products = []
+                for g, ref in enumerate(first_refs):
+                    values = jnp.concatenate([ref[head, :], ones], axis=1)
+                    rows = weights[g * CELLS : (g + 1) * CELLS]
+                    products.append(jnp.dot(rows, values, preferred_element_type=f32))
+                summed = jnp.concatenate(products, axis=0)
             else:
-                summed = summed + jnp.dot(
-                    weights, tiles[index - 1], preferred_element_type=f32
-                )
-        results.append(summed / jnp.sum(total, axis=1, keepdims=True))
+                values = jnp.concatenate([table_refs[index][head, :], ones], axis=1)
+                summed = summed + jnp.dot(weights, values, preferred_element_type=f32)
+        return summed[:, 0:LANES] / summed[:, LANES:]
+
+    results = []
+    scores = head_scores(0)
+    for h in range(SET_HEADS):
+        following = head_scores(h + 1) if h + 1 < SET_HEADS else None
+        results.append(head_result(h, scores))
+        scores = following
     for g, out_ref in enumerate(out_refs):
         rows = slice(g * CELLS, (g + 1) * CELLS)
         for t in range(2):
@@ -331,17 +328,19 @@
     )(*args)
 
 
-AXES = {"z": (32, 4), "y": (8, 4), "x": (2, 4), "core": (1, 2)}
-
-
-def shift(array, axis, step):
-    stride, size = AXES[axis]
+def permute(array, place):
     pairs = []
     for source in range(128):
-        place = source // stride % size
-        target = source + ((place + step) % size - place) * stride
-        pairs.append((source, target))
+        z, y, x, core = place(source // 32, source // 8 % 4, source // 2 % 4, source % 2)
+        pairs.append((source, z % 4 * 32 + y % 4 * 8 + x % 4 * 2 + core % 2))
     return lax.ppermute(array, "patch", pairs)
+
+
+def shift(array, axis, step):
+    def place(*places):
+        return [at + step * (name == axis) for at, name in zip(places, ("z", "y", "x", "core"))]
+
+    return permute(array, place)
 
 
 def after(array, *others):
@@ -352,13 +351,14 @@
     place = (lax.axis_index("patch") // 2 % 4).astype(jnp.int32).reshape(1)
     table = ((SET_HEADS * CELLS, LANES), bf16)
     answer = ((ANSWER_ROWS, LANES), bf16)
-    stats, sets, tokens = call(
+    stats, tokens = call(
         local_kernel,
-        [HBM, HBM],
-        [((8, LANES), f32), ((4, SET_ROWS, LANES), bf16), ((CELLS, WIDTH), bf16)],
+        [VMEM],
+        [((8, LANES), f32), ((CELLS, WIDTH), bf16)],
         tokens[0],
-        stale_keys[0],
-        scratch=[pltpu.VMEM((ROWS, 2 * WIDTH), bf16), pltpu.SemaphoreType.DMA((2,))],
+    )
+    (sets,) = call(
+        sets_kernel, [VMEM, VMEM], [((4, SET_ROWS, LANES), bf16)], stats, stale_keys[0]
     )
     other = shift(stats, "core", 1)
     messages = call(
@@ -382,13 +382,13 @@
         [
             ((WIDTH, WIDTH), bf16),
             ((WIDTH, 2 * WIDTH), bf16),
-            ((1, WIDTH), f32),
-            ((1, WIDTH), f32),
+            ((WIDTH,), f32),
+            ((WIDTH,), f32),
         ],
         query_weight,
         pair_weight,
-        norm_gain.reshape(1, WIDTH),
-        norm_bias.reshape(1, WIDTH),
+        norm_gain,
+        norm_bias,
         scratch=[pltpu.SemaphoreType.DMA((4,))],
     )
     parts, weights = lax.optimization_barrier((parts, weights))
@@ -396,8 +396,7 @@
     all_stats = [stats] + [shift(stats, "y", k) for k in (1, 2, 3)]
     (piece,) = call(piece_kernel, [VMEM] * 5, [table], stats, *parts)
     pieces = [piece, shift(piece, "y", 1), shift(piece, "y", 3)]
-    late = after(piece, *all_stats)
-    pieces.append(shift(late, "y", 2))
+    pieces.append(shift(after(piece, *all_stats), "y", 2))
     *queries, fresh = call(
         project_kernel,
         [SMEM] + [VMEM] * 9,
@@ -414,16 +413,16 @@
     asked = {0: queries[0]}
     for k in (2, 1, 3):
         asked[k] = shift(after(queries[k], pieces[1]) if k == 3 else queries[k], "x", k)
-    pieces += [shift(block, "core", 1) for block in [late] + pieces[1:]]
+    tables = pieces + [shift(after(block, asked[2]), "core", 1) for block in pieces]
     results = [None] * 4
-    for sources in ((1, 3, 2), (0,)):
+    for sources in ((2, 1), (3,), (0,)):
         answers = call(
             functools.partial(attend_kernel, sources),
             [SMEM] + [VMEM] * (len(sources) + 8),
             [answer] * len(sources),
             place,
             *[asked[k] for k in sources],
-            *pieces,
+            *tables,
             scratch=[pltpu.VMEM(*table)] * len(sources),
             limit=40,
         )

time: 86.8 us -> 75 us (0.86)
  the two profiles are of different devices: /device:TPU:1 before, /device:TPU:32 now
where the time goes in v3:
time: 75 us; the launch traced here: 74.1 us
  starting transfers between devices  33.7 us (45%)
  Pallas kernels  20.3 us (27%)
  waiting for transfers between devices  11.2 us (15%)
  local copies, waits for them, and re-layouts  8.14 us (11%)
  between operations  0.8 us (1%)
    ppermute x23, starting transfers between devices, permute(): return lax.ppermute(array, 'patch', pairs)  33.7 us
    pallas_call x12, Pallas kernels, call(): pl.pallas_call(kernel, in_specs=ins, out_specs=[VMEM] * len(outs), out_sh...  20.3 us
    ppermute x23, waiting for transfers between devices, permute(): return lax.ppermute(array, 'patch', pairs)  11.2 us
    unnamed x12, local copies, waits for them, and re-layouts  8.14 us
  transfers between devices with their start and end apart: 23, of which 9 were waited for; matrix products, arithmetic and copies ran while one was open for 0% of the time, Pallas kernels for 24%

profile of v3, /device:TPU:32, one launch (start us, length us, event | category | flops | bytes accessed | tf_op | source)
XLA Modules:
  0.0 74.1 jit_solution(187184092807437427)
XLA Ops:
  0.6 1.1 %copy-done.2 = bf16[1,256,1280]{2,1,0:T(8,128)(2,1)S(1)} copy-done((bf16[1,256,1280]{2,1,0:T(8,128)(2,1)S(1)}, bf16[1,256,1280]{2,1,0:T(8,128)(2,1)}, u32[]{:S(2)}) %copy-start.2) | copy-done | bytes 655384
  1.7 1.4 %shard_map.77 = (f32[8,128]{1,0:T(8,128)S(1)}, bf16[256,1280]{1,0:T(8,128)(2,1)S(1)}) custom-call(bf16[256,1280]{1,0:T(8,128)(2,1)S(1)} %bitcast.5), custom_call_target="tpu_custom_call" | custom-call | flops 1 | bytes 1 | tf_op jit(solution)/shard_map/pallas_call | solution.py:320
  3.2 0.9 %copy-done.3 = bf16[1,16,2560]{2,1,0:T(8,128)(2,1)S(1)} copy-done((bf16[1,16,2560]{2,1,0:T(8,128)(2,1)S(1)}, bf16[1,16,2560]{2,1,0:T(8,128)(2,1)}, u32[]{:S(2)}) %copy-start.3) | copy-done | bytes 81944
  4.4 1.6 %collective-permute-start.1 = (bf16[96,128]{1,0:T(8,128)(2,1)S(1)}, bf16[96,128]{1,0:T(8,128)(2,1)S(1)}, u32[]{:S(2)}, u32[]{:S(2)}) collective-permute-start(bf16[96,128]{1,0:T(8,128)(2,1)S(1)} %get-tuple-element.40), channel_id=1, source_target_pairs={{0,4},{2,6},{4,8},{6,10},{8,12},{10,14},{12,0},{14,2},{16,20},{18,... | collective-permute-start | bytes 73736 | tf_op jit(solution)/shard_map/ppermute | solution.py:336
  6.0 2.7 %collective-permute-start.2 = (bf16[96,128]{1,0:T(8,128)(2,1)S(1)}, bf16[96,128]{1,0:T(8,128)(2,1)S(1)}, u32[]{:S(2)}, u32[]{:S(2)}) collective-permute-start(bf16[96,128]{1,0:T(8,128)(2,1)S(1)} %get-tuple-element.41), channel_id=1, source_target_pairs={{0,8},{2,10},{4,12},{6,14},{8,0},{10,2},{12,4},{14,6},{16,24},{18,... | collective-permute-start | bytes 73736 | tf_op jit(solution)/shard_map/ppermute | solution.py:336
  8.7 1.4 %collective-permute-start.3 = (bf16[96,128]{1,0:T(8,128)(2,1)S(1)}, bf16[96,128]{1,0:T(8,128)(2,1)S(1)}, u32[]{:S(2)}, u32[]{:S(2)}) collective-permute-start(bf16[96,128]{1,0:T(8,128)(2,1)S(1)} %get-tuple-element.42), channel_id=1, source_target_pairs={{0,12},{2,14},{4,0},{6,2},{8,4},{10,6},{12,8},{14,10},{16,28},{18,... | collective-permute-start | bytes 73736 | tf_op jit(solution)/shard_map/ppermute | solution.py:336
  10.1 1.2 %collective-permute-done.2.refs_2_ = bf16[96,128]{1,0:T(8,128)(2,1)S(1)} collective-permute-done((bf16[96,128]{1,0:T(8,128)(2,1)S(1)}, bf16[96,128]{1,0:T(8,128)(2,1)S(1)}, u32[]{:S(2)}, u32[]{:S(2)}) %collective-permute-start.2) | collective-permute-done | bytes 24608 | tf_op jit(solution)/shard_map/ppermute | solution.py:336
  11.3 1.2 %collective-permute-done.3.refs_3_ = bf16[96,128]{1,0:T(8,128)(2,1)S(1)} collective-permute-done((bf16[96,128]{1,0:T(8,128)(2,1)S(1)}, bf16[96,128]{1,0:T(8,128)(2,1)S(1)}, u32[]{:S(2)}, u32[]{:S(2)}) %collective-permute-start.3) | collective-permute-done | bytes 24608 | tf_op jit(solution)/shard_map/ppermute | solution.py:336
  12.6 5.5 %collective-permute-start.6 = (bf16[336,128]{1,0:T(8,128)(2,1)S(1)}, bf16[336,128]{1,0:T(8,128)(2,1)S(1)}, u32[]{:S(2)}, u32[]{:S(2)}) collective-permute-start(bf16[336,128]{1,0:T(8,128)(2,1)S(1)} %shard_map.80.refs_0_), channel_id=1, source_target_pairs={{0,192},{2,194},{4,196},{6,198},{8,200},{10,202},{12,204},{14,206}... | collective-permute-start | bytes 258056 | tf_op jit(solution)/shard_map/ppermute | solution.py:336
  18.0 1.4 %collective-permute-start.5 = (bf16[336,128]{1,0:T(8,128)(2,1)S(1)}, bf16[336,128]{1,0:T(8,128)(2,1)S(1)}, u32[]{:S(2)}, u32[]{:S(2)}) collective-permute-start(bf16[336,128]{1,0:T(8,128)(2,1)S(1)} %shard_map.80.refs_0_), channel_id=1, source_target_pairs={{0,128},{2,130},{4,132},{6,134},{8,136},{10,138},{12,140},{14,142}... | collective-permute-start | bytes 258056 | tf_op jit(solution)/shard_map/ppermute | solution.py:336
  19.5 2.4 %collective-permute-start.4 = (bf16[336,128]{1,0:T(8,128)(2,1)S(1)}, bf16[336,128]{1,0:T(8,128)(2,1)S(1)}, u32[]{:S(2)}, u32[]{:S(2)}) collective-permute-start(bf16[336,128]{1,0:T(8,128)(2,1)S(1)} %shard_map.80.refs_0_), channel_id=1, source_target_pairs={{0,64},{2,66},{4,68},{6,70},{8,72},{10,74},{12,76},{14,78},{16,80}... | collective-permute-start | bytes 258056 | tf_op jit(solution)/shard_map/ppermute | solution.py:336
  21.9 2.9 %copy-done = bf16[1280,2560]{1,0:T(8,128)(2,1)S(1)} copy-done((bf16[1280,2560]{1,0:T(8,128)(2,1)S(1)}, bf16[1280,2560]{1,0:T(8,128)(2,1)}, u32[]{:S(2)}) %copy-start) | copy-done | bytes 6553624
  24.7 1.9 %copy-done.1 = bf16[1280,1280]{1,0:T(8,128)(2,1)S(1)} copy-done((bf16[1280,1280]{1,0:T(8,128)(2,1)S(1)}, bf16[1280,1280]{1,0:T(8,128)(2,1)}, u32[]{:S(2)}) %copy-start.1) | copy-done | bytes 3276824
  28.0 0.9 %shard_map.81 = (bf16[1280,1280]{1,0:T(8,128)(2,1)S(1)}, bf16[1280,2560]{1,0:T(8,128)(2,1)S(1)}, f32[1280]{0:T(1024)S(1)}, f32[1280]{0:T(1024)S(1)}) custom-call(bf16[1280,1280]{1,0:T(8,128)(2,1)S(1)} %copy-done.1, bf16[1280,2560]{1,0:T(8,128)(2,1)S(1)} %copy-done, f32[1280]{0:T(1024)S(1)} %copy-done.4, f32[1280]{0:T(1024)S(1)} %copy-done.5), custom_call_target="tpu_custom_call" | custom-call | flops 1 | bytes 1 | tf_op jit(solution)/shard_map/pallas_call | solution.py:320
  29.0 3.1 %collective-permute-start.9 = (f32[8,128]{1,0:T(8,128)S(1)}, f32[8,128]{1,0:T(8,128)S(1)}, u32[]{:S(2)}, u32[]{:S(2)}) collective-permute-start(f32[8,128]{1,0:T(8,128)S(1)} %shard_map.82.s0.stats_ref), channel_id=1, source_target_pairs={{0,48},{2,50},{4,52},{6,54},{8,56},{10,58},{12,60},{14,62},{16,0},... | collective-permute-start | bytes 12296 | tf_op jit(solution)/shard_map/ppermute | solution.py:336
  32.7 1.0 %collective-permute-start.7 = (f32[8,128]{1,0:T(8,128)S(1)}, f32[8,128]{1,0:T(8,128)S(1)}, u32[]{:S(2)}, u32[]{:S(2)}) collective-permute-start(f32[8,128]{1,0:T(8,128)S(1)} %shard_map.82.s0.stats_ref), channel_id=1, source_target_pairs={{0,16},{2,18},{4,20},{6,22},{8,24},{10,26},{12,28},{14,30},{16,32}... | collective-permute-start | bytes 12296 | tf_op jit(solution)/shard_map/ppermute | solution.py:336
  33.7 2.3 %collective-permute-start.11 = (bf16[1280,128]{1,0:T(8,128)(2,1)S(1)}, bf16[1280,128]{1,0:T(8,128)(2,1)S(1)}, u32[]{:S(2)}, u32[]{:S(2)}) collective-permute-start(bf16[1280,128]{1,0:T(8,128)(2,1)S(1)} %shard_map.84.refs_1_.refs_2_), channel_id=1, source_target_pairs={{0,48},{2,50},{4,52},{6,54},{8,56},{10,58},{12,60},{14,62},{16,0},... | collective-permute-start | bytes 983048 | tf_op jit(solution)/shard_map/ppermute | solution.py:336
  36.0 1.2 %collective-permute-done.8.s2 = f32[8,128]{1,0:T(8,128)S(1)} collective-permute-done((f32[8,128]{1,0:T(8,128)S(1)}, f32[8,128]{1,0:T(8,128)S(1)}, u32[]{:S(2)}, u32[]{:S(2)}) %collective-permute-start.8) | collective-permute-done | bytes 4128 | tf_op jit(solution)/shard_map/ppermute | solution.py:336
  37.5 1.8 %collective-permute-start.12 = (bf16[1280,128]{1,0:T(8,128)(2,1)S(1)}, bf16[1280,128]{1,0:T(8,128)(2,1)S(1)}, u32[]{:S(2)}, u32[]{:S(2)}) collective-permute-start(bf16[1280,128]{1,0:T(8,128)(2,1)S(1)} %shard_map.84.refs_1_.refs_2_), channel_id=1, source_target_pairs={{0,32},{2,34},{4,36},{6,38},{8,40},{10,42},{12,44},{14,46},{16,48}... | collective-permute-start | bytes 983048 | tf_op jit(solution)/shard_map/ppermute | solution.py:336
  39.3 3.2 %shard_map.83 = (bf16[720,128]{1,0:T(8,128)(2,1)S(1)}, bf16[720,128]{1,0:T(8,128)(2,1)S(1)}, bf16[720,128]{1,0:T(8,128)(2,1)S(1)}, bf16[720,128]{1,0:T(8,128)(2,1)S(1)}, bf16[16,2560]{1,0:T(8,128)(2,1)}) custom-call(s32[1]{0:T(128)} %bitcast.place_ref, bf16[256,1280]{1,0:T(8,128)(2,1)S(1)} %get-tuple-element.37.tokens_ref, ...), custom_call_target="tpu_custom_call" | custom-call | flops 1 | bytes 1 | tf_op jit(solution)/shard_map/pallas_call | solution.py:320
  42.5 1.5 %collective-permute-start.13 = (bf16[720,128]{1,0:T(8,128)(2,1)S(1)}, bf16[720,128]{1,0:T(8,128)(2,1)S(1)}, u32[]{:S(2)}, u32[]{:S(2)}) collective-permute-start(bf16[720,128]{1,0:T(8,128)(2,1)S(1)} %get-tuple-element.61), channel_id=1, source_target_pairs={{0,8},{2,10},{4,12},{6,14},{8,0},{10,2},{12,4},{14,6},{16,24},{18,... | collective-permute-start | bytes 552968 | tf_op jit(solution)/shard_map/ppermute | solution.py:336
  44.0 2.0 %collective-permute-start.18 = (bf16[720,128]{1,0:T(8,128)(2,1)S(1)}, bf16[720,128]{1,0:T(8,128)(2,1)S(1)}, u32[]{:S(2)}, u32[]{:S(2)}) collective-permute-start(bf16[720,128]{1,0:T(8,128)(2,1)S(1)} %get-tuple-element.66), channel_id=1, source_target_pairs={{0,4},{2,6},{4,8},{6,10},{8,12},{10,14},{12,0},{14,2},{16,20},{18,... | collective-permute-start | bytes 552968 | tf_op jit(solution)/shard_map/ppermute | solution.py:336
  46.0 3.6 %collective-permute-done.13.refs_0_ = bf16[720,128]{1,0:T(8,128)(2,1)S(1)} collective-permute-done((bf16[720,128]{1,0:T(8,128)(2,1)S(1)}, bf16[720,128]{1,0:T(8,128)(2,1)S(1)}, u32[]{:S(2)}, u32[]{:S(2)}) %collective-permute-start.13) | collective-permute-done | bytes 184352 | tf_op jit(solution)/shard_map/ppermute | solution.py:336
  50.1 0.8 %collective-permute-done.10.refs_2_.refs_3_ = bf16[1280,128]{1,0:T(8,128)(2,1)S(1)} collective-permute-done((bf16[1280,128]{1,0:T(8,128)(2,1)S(1)}, bf16[1280,128]{1,0:T(8,128)(2,1)S(1)}, u32[]{:S(2)}, u32[]{:S(2)}) %collective-permute-start.10) | collective-permute-done | bytes 327712 | tf_op jit(solution)/shard_map/ppermute | solution.py:336
  51.5 2.3 %collective-permute-start.21 = (bf16[720,128]{1,0:T(8,128)(2,1)S(1)}, bf16[720,128]{1,0:T(8,128)(2,1)S(1)}, u32[]{:S(2)}, u32[]{:S(2)}) collective-permute-start(bf16[720,128]{1,0:T(8,128)(2,1)S(1)} %get-tuple-element.70), channel_id=1, source_target_pairs={{0,12},{2,14},{4,0},{6,2},{8,4},{10,6},{12,8},{14,10},{16,28},{18,... | collective-permute-start | bytes 552968 | tf_op jit(solution)/shard_map/ppermute | solution.py:336
  53.8 6.6 %shard_map.86 = (bf16[640,128]{1,0:T(8,128)(2,1)S(1)}, bf16[640,128]{1,0:T(8,128)(2,1)S(1)}) custom-call(s32[1]{0:T(128)} %bitcast.place_ref, bf16[720,128]{1,0:T(8,128)(2,1)S(1)} %collective-permute-done.13.refs_0_, bf16[720,128]{1,0:T(8,128)(2,1)S(1)} %collective-permute-done.18.refs_1_, bf16[1280,128]{1,0:T(8,128)(2,1)S(1)} %shard_map.84.refs_1_.refs_2_, ...), custom_call_target="tpu_custom_call" | custom-call | flops 1 | bytes 1 | tf_op jit(solution)/shard_map/pallas_call | solution.py:320
  60.4 1.6 %collective-permute-start.19 = (bf16[640,128]{1,0:T(8,128)(2,1)S(1)}, bf16[640,128]{1,0:T(8,128)(2,1)S(1)}, u32[]{:S(2)}, u32[]{:S(2)}) collective-permute-start(bf16[640,128]{1,0:T(8,128)(2,1)S(1)} %get-tuple-element.67), channel_id=1, source_target_pairs={{0,12},{2,14},{4,0},{6,2},{8,4},{10,6},{12,8},{14,10},{16,28},{18,... | collective-permute-start | bytes 491528 | tf_op jit(solution)/shard_map/ppermute | solution.py:336
  62.3 3.5 %shard_map.87 = bf16[640,128]{1,0:T(8,128)(2,1)S(1)} custom-call(s32[1]{0:T(128)} %bitcast.place_ref, bf16[720,128]{1,0:T(8,128)(2,1)S(1)} %collective-permute-done.21.refs_0_, bf16[1280,128]{1,0:T(8,128)(2,1)S(1)} %shard_map.84.refs_1_.refs_2_, bf16[1280,128]{1,0:T(8,128)(2,1)S(1)} %collective-permute-done.10.refs_2_.refs_3_, ...), custom_call_target="tpu_custom_call" | custom-call | flops 1 | bytes 1 | tf_op jit(solution)/shard_map/pallas_call | solution.py:320
  65.8 1.0 %collective-permute-start.22 = (bf16[640,128]{1,0:T(8,128)(2,1)S(1)}, bf16[640,128]{1,0:T(8,128)(2,1)S(1)}, u32[]{:S(2)}, u32[]{:S(2)}) collective-permute-start(bf16[640,128]{1,0:T(8,128)(2,1)S(1)} %shard_map.87), channel_id=1, source_target_pairs={{0,4},{2,6},{4,8},{6,10},{8,12},{10,14},{12,0},{14,2},{16,20},{18,... | collective-permute-start | bytes 491528 | tf_op jit(solution)/shard_map/ppermute | solution.py:336
  66.9 3.5 %shard_map.85.refs_0_ = bf16[640,128]{1,0:T(8,128)(2,1)S(1)} custom-call(s32[1]{0:T(128)} %bitcast.place_ref, bf16[720,128]{1,0:T(8,128)(2,1)S(1)} %get-tuple-element.59.refs_0_, bf16[1280,128]{1,0:T(8,128)(2,1)S(1)} %shard_map.84.refs_1_.refs_2_, bf16[1280,128]{1,0:T(8,128)(2,1)S(1)} %collective-permute-done.10.refs_2_.refs_3_, ...), custom_call_target="tpu_custom_call" | custom-call | flops 1 | bytes 1 | tf_op jit(solution)/shard_map/pallas_call | solution.py:320
  70.4 2.7 %collective-permute-done.22.refs_3_ = bf16[640,128]{1,0:T(8,128)(2,1)S(1)} collective-permute-done((bf16[640,128]{1,0:T(8,128)(2,1)S(1)}, bf16[640,128]{1,0:T(8,128)(2,1)S(1)}, u32[]{:S(2)}, u32[]{:S(2)}) %collective-permute-start.22) | collective-permute-done | bytes 163872 | tf_op jit(solution)/shard_map/ppermute | solution.py:336
  73.1 1.0 %shard_map.88 = bf16[256,1280]{1,0:T(8,128)(2,1)} custom-call(s32[1]{0:T(128)} %bitcast.place_ref, bf16[640,128]{1,0:T(8,128)(2,1)S(1)} %shard_map.85.refs_0_, bf16[640,128]{1,0:T(8,128)(2,1)S(1)} %collective-permute-done.19.refs_1_, bf16[640,128]{1,0:T(8,128)(2,1)S(1)} %collective-permute-done.20.refs_2_, bf16[640,128]{1,0:T(8,128)(2,1)S(1)} %collective-permute-done.22.refs_3_), custom_call_target="tpu_custom_call" | custom-call | flops 1 | bytes 1 | tf_op jit(solution)/shard_map/pallas_call | solution.py:320
  (38 shorter events, 4.1 us)
Async XLA Ops:
  0.6 1.1 %copy-start.2 = (bf16[1,256,1280]{2,1,0:T(8,128)(2,1)S(1)}, bf16[1,256,1280]{2,1,0:T(8,128)(2,1)}, u32[]{:S(2)}) copy-start(bf16[1,256,1280]{2,1,0:T(8,128)(2,1)} %param.6) | copy-start | bytes 1966084
  3.1 1.2 %collective-permute-start = (f32[8,128]{1,0:T(8,128)S(1)}, f32[8,128]{1,0:T(8,128)S(1)}, u32[]{:S(2)}, u32[]{:S(2)}) collective-permute-start(f32[8,128]{1,0:T(8,128)S(1)} %get-tuple-element.38.stats_ref.own_ref), channel_id=1, source_target_pairs={{0,2},{2,0},{4,6},{6,4},{8,10},{10,8},{12,14},{14,12},{16,18},{18,... | collective-permute-start | bytes 12296 | tf_op jit(solution)/shard_map/ppermute | solution.py:336
  3.2 0.9 %copy-start.3 = (bf16[1,16,2560]{2,1,0:T(8,128)(2,1)S(1)}, bf16[1,16,2560]{2,1,0:T(8,128)(2,1)}, u32[]{:S(2)}) copy-start(bf16[1,16,2560]{2,1,0:T(8,128)(2,1)} %param.7) | copy-start | bytes 245764
  4.4 5.8 %collective-permute-start.1 = (bf16[96,128]{1,0:T(8,128)(2,1)S(1)}, bf16[96,128]{1,0:T(8,128)(2,1)S(1)}, u32[]{:S(2)}, u32[]{:S(2)}) collective-permute-start(bf16[96,128]{1,0:T(8,128)(2,1)S(1)} %get-tuple-element.40), channel_id=1, source_target_pairs={{0,4},{2,6},{4,8},{6,10},{8,12},{10,14},{12,0},{14,2},{16,20},{18,... | collective-permute-start | bytes 73736 | tf_op jit(solution)/shard_map/ppermute | solution.py:336
  6.0 5.3 %collective-permute-start.2 = (bf16[96,128]{1,0:T(8,128)(2,1)S(1)}, bf16[96,128]{1,0:T(8,128)(2,1)S(1)}, u32[]{:S(2)}, u32[]{:S(2)}) collective-permute-start(bf16[96,128]{1,0:T(8,128)(2,1)S(1)} %get-tuple-element.41), channel_id=1, source_target_pairs={{0,8},{2,10},{4,12},{6,14},{8,0},{10,2},{12,4},{14,6},{16,24},{18,... | collective-permute-start | bytes 73736 | tf_op jit(solution)/shard_map/ppermute | solution.py:336
  8.7 3.8 %collective-permute-start.3 = (bf16[96,128]{1,0:T(8,128)(2,1)S(1)}, bf16[96,128]{1,0:T(8,128)(2,1)S(1)}, u32[]{:S(2)}, u32[]{:S(2)}) collective-permute-start(bf16[96,128]{1,0:T(8,128)(2,1)S(1)} %get-tuple-element.42), channel_id=1, source_target_pairs={{0,12},{2,14},{4,0},{6,2},{8,4},{10,6},{12,8},{14,10},{16,28},{18,... | collective-permute-start | bytes 73736 | tf_op jit(solution)/shard_map/ppermute | solution.py:336
  12.6 16.3 %collective-permute-start.6 = (bf16[336,128]{1,0:T(8,128)(2,1)S(1)}, bf16[336,128]{1,0:T(8,128)(2,1)S(1)}, u32[]{:S(2)}, u32[]{:S(2)}) collective-permute-start(bf16[336,128]{1,0:T(8,128)(2,1)S(1)} %shard_map.80.refs_0_), channel_id=1, source_target_pairs={{0,192},{2,194},{4,196},{6,198},{8,200},{10,202},{12,204},{14,206}... | collective-permute-start | bytes 258056 | tf_op jit(solution)/shard_map/ppermute | solution.py:336
  18.0 10.9 %collective-permute-start.5 = (bf16[336,128]{1,0:T(8,128)(2,1)S(1)}, bf16[336,128]{1,0:T(8,128)(2,1)S(1)}, u32[]{:S(2)}, u32[]{:S(2)}) collective-permute-start(bf16[336,128]{1,0:T(8,128)(2,1)S(1)} %shard_map.80.refs_0_), channel_id=1, source_target_pairs={{0,128},{2,130},{4,132},{6,134},{8,136},{10,138},{12,140},{14,142}... | collective-permute-start | bytes 258056 | tf_op jit(solution)/shard_map/ppermute | solution.py:336
  19.5 9.5 %collective-permute-start.4 = (bf16[336,128]{1,0:T(8,128)(2,1)S(1)}, bf16[336,128]{1,0:T(8,128)(2,1)S(1)}, u32[]{:S(2)}, u32[]{:S(2)}) collective-permute-start(bf16[336,128]{1,0:T(8,128)(2,1)S(1)} %shard_map.80.refs_0_), channel_id=1, source_target_pairs={{0,64},{2,66},{4,68},{6,70},{8,72},{10,74},{12,76},{14,78},{16,80}... | collective-permute-start | bytes 258056 | tf_op jit(solution)/shard_map/ppermute | solution.py:336
  21.9 2.9 %copy-start = (bf16[1280,2560]{1,0:T(8,128)(2,1)S(1)}, bf16[1280,2560]{1,0:T(8,128)(2,1)}, u32[]{:S(2)}) copy-start(bf16[1280,2560]{1,0:T(8,128)(2,1)} %pair_hbm) | copy-start | bytes 19660804
  24.7 1.9 %copy-start.1 = (bf16[1280,1280]{1,0:T(8,128)(2,1)S(1)}, bf16[1280,1280]{1,0:T(8,128)(2,1)}, u32[]{:S(2)}) copy-start(bf16[1280,1280]{1,0:T(8,128)(2,1)} %query_hbm) | copy-start | bytes 9830404
  26.6 0.7 copy-start.4
  27.3 0.7 copy-start.5
  29.0 7.1 %collective-permute-start.9 = (f32[8,128]{1,0:T(8,128)S(1)}, f32[8,128]{1,0:T(8,128)S(1)}, u32[]{:S(2)}, u32[]{:S(2)}) collective-permute-start(f32[8,128]{1,0:T(8,128)S(1)} %shard_map.82.s0.stats_ref), channel_id=1, source_target_pairs={{0,48},{2,50},{4,52},{6,54},{8,56},{10,58},{12,60},{14,62},{16,0},... | collective-permute-start | bytes 12296 | tf_op jit(solution)/shard_map/ppermute | solution.py:336
  32.1 5.2 %collective-permute-start.8 = (f32[8,128]{1,0:T(8,128)S(1)}, f32[8,128]{1,0:T(8,128)S(1)}, u32[]{:S(2)}, u32[]{:S(2)}) collective-permute-start(f32[8,128]{1,0:T(8,128)S(1)} %shard_map.82.s0.stats_ref), channel_id=1, source_target_pairs={{0,32},{2,34},{4,36},{6,38},{8,40},{10,42},{12,44},{14,46},{16,48}... | collective-permute-start | bytes 12296 | tf_op jit(solution)/shard_map/ppermute | solution.py:336
  32.7 4.8 %collective-permute-start.7 = (f32[8,128]{1,0:T(8,128)S(1)}, f32[8,128]{1,0:T(8,128)S(1)}, u32[]{:S(2)}, u32[]{:S(2)}) collective-permute-start(f32[8,128]{1,0:T(8,128)S(1)} %shard_map.82.s0.stats_ref), channel_id=1, source_target_pairs={{0,16},{2,18},{4,20},{6,22},{8,24},{10,26},{12,28},{14,30},{16,32}... | collective-permute-start | bytes 12296 | tf_op jit(solution)/shard_map/ppermute | solution.py:336
  33.7 15.9 %collective-permute-start.11 = (bf16[1280,128]{1,0:T(8,128)(2,1)S(1)}, bf16[1280,128]{1,0:T(8,128)(2,1)S(1)}, u32[]{:S(2)}, u32[]{:S(2)}) collective-permute-start(bf16[1280,128]{1,0:T(8,128)(2,1)S(1)} %shard_map.84.refs_1_.refs_2_), channel_id=1, source_target_pairs={{0,48},{2,50},{4,52},{6,54},{8,56},{10,58},{12,60},{14,62},{16,0},... | collective-permute-start | bytes 983048 | tf_op jit(solution)/shard_map/ppermute | solution.py:336
  36.0 14.9 %collective-permute-start.10 = (bf16[1280,128]{1,0:T(8,128)(2,1)S(1)}, bf16[1280,128]{1,0:T(8,128)(2,1)S(1)}, u32[]{:S(2)}, u32[]{:S(2)}) collective-permute-start(bf16[1280,128]{1,0:T(8,128)(2,1)S(1)} %shard_map.84.refs_1_.refs_2_), channel_id=1, source_target_pairs={{0,16},{2,18},{4,20},{6,22},{8,24},{10,26},{12,28},{14,30},{16,32}... | collective-permute-start | bytes 983048 | tf_op jit(solution)/shard_map/ppermute | solution.py:336
  37.5 13.4 %collective-permute-start.12 = (bf16[1280,128]{1,0:T(8,128)(2,1)S(1)}, bf16[1280,128]{1,0:T(8,128)(2,1)S(1)}, u32[]{:S(2)}, u32[]{:S(2)}) collective-permute-start(bf16[1280,128]{1,0:T(8,128)(2,1)S(1)} %shard_map.84.refs_1_.refs_2_), channel_id=1, source_target_pairs={{0,32},{2,34},{4,36},{6,38},{8,40},{10,42},{12,44},{14,46},{16,48}... | collective-permute-start | bytes 983048 | tf_op jit(solution)/shard_map/ppermute | solution.py:336
  42.5 7.1 %collective-permute-start.13 = (bf16[720,128]{1,0:T(8,128)(2,1)S(1)}, bf16[720,128]{1,0:T(8,128)(2,1)S(1)}, u32[]{:S(2)}, u32[]{:S(2)}) collective-permute-start(bf16[720,128]{1,0:T(8,128)(2,1)S(1)} %get-tuple-element.61), channel_id=1, source_target_pairs={{0,8},{2,10},{4,12},{6,14},{8,0},{10,2},{12,4},{14,6},{16,24},{18,... | collective-permute-start | bytes 552968 | tf_op jit(solution)/shard_map/ppermute | solution.py:336
  44.0 7.5 %collective-permute-start.18 = (bf16[720,128]{1,0:T(8,128)(2,1)S(1)}, bf16[720,128]{1,0:T(8,128)(2,1)S(1)}, u32[]{:S(2)}, u32[]{:S(2)}) collective-permute-start(bf16[720,128]{1,0:T(8,128)(2,1)S(1)} %get-tuple-element.66), channel_id=1, source_target_pairs={{0,4},{2,6},{4,8},{6,10},{8,12},{10,14},{12,0},{14,2},{16,20},{18,... | collective-permute-start | bytes 552968 | tf_op jit(solution)/shard_map/ppermute | solution.py:336
  49.6 4.2 %collective-permute-start.14 = (bf16[1280,128]{1,0:T(8,128)(2,1)S(1)}, bf16[1280,128]{1,0:T(8,128)(2,1)S(1)}, u32[]{:S(2)}, u32[]{:S(2)}) collective-permute-start(bf16[1280,128]{1,0:T(8,128)(2,1)S(1)} %shard_map.84.refs_1_.refs_2_), channel_id=1, source_target_pairs={{0,2},{2,0},{4,6},{6,4},{8,10},{10,8},{12,14},{14,12},{16,18},{18,... | collective-permute-start | bytes 983048 | tf_op jit(solution)/shard_map/ppermute | solution.py:336
  49.6 4.2 %collective-permute-start.16 = (bf16[1280,128]{1,0:T(8,128)(2,1)S(1)}, bf16[1280,128]{1,0:T(8,128)(2,1)S(1)}, u32[]{:S(2)}, u32[]{:S(2)}) collective-permute-start(bf16[1280,128]{1,0:T(8,128)(2,1)S(1)} %collective-permute-done.11.refs_3_.refs_4_), channel_id=1, source_target_pairs={{0,2},{2,0},{4,6},{6,4},{8,10},{10,8},{12,14},{14,12},{16,18},{18,... | collective-permute-start | bytes 983048 | tf_op jit(solution)/shard_map/ppermute | solution.py:336
  50.9 2.9 %collective-permute-start.15 = (bf16[1280,128]{1,0:T(8,128)(2,1)S(1)}, bf16[1280,128]{1,0:T(8,128)(2,1)S(1)}, u32[]{:S(2)}, u32[]{:S(2)}) collective-permute-start(bf16[1280,128]{1,0:T(8,128)(2,1)S(1)} %collective-permute-done.10.refs_2_.refs_3_), channel_id=1, source_target_pairs={{0,2},{2,0},{4,6},{6,4},{8,10},{10,8},{12,14},{14,12},{16,18},{18,... | collective-permute-start | bytes 983048 | tf_op jit(solution)/shard_map/ppermute | solution.py:336
  50.9 2.9 %collective-permute-start.17 = (bf16[1280,128]{1,0:T(8,128)(2,1)S(1)}, bf16[1280,128]{1,0:T(8,128)(2,1)S(1)}, u32[]{:S(2)}, u32[]{:S(2)}) collective-permute-start(bf16[1280,128]{1,0:T(8,128)(2,1)S(1)} %collective-permute-done.12.refs_4_.refs_5_), channel_id=1, source_target_pairs={{0,2},{2,0},{4,6},{6,4},{8,10},{10,8},{12,14},{14,12},{16,18},{18,... | collective-permute-start | bytes 983048 | tf_op jit(solution)/shard_map/ppermute | solution.py:336
  51.5 10.8 %collective-permute-start.21 = (bf16[720,128]{1,0:T(8,128)(2,1)S(1)}, bf16[720,128]{1,0:T(8,128)(2,1)S(1)}, u32[]{:S(2)}, u32[]{:S(2)}) collective-permute-start(bf16[720,128]{1,0:T(8,128)(2,1)S(1)} %get-tuple-element.70), channel_id=1, source_target_pairs={{0,12},{2,14},{4,0},{6,2},{8,4},{10,6},{12,8},{14,10},{16,28},{18,... | collective-permute-start | bytes 552968 | tf_op jit(solution)/shard_map/ppermute | solution.py:336
  60.4 10.0 %collective-permute-start.19 = (bf16[640,128]{1,0:T(8,128)(2,1)S(1)}, bf16[640,128]{1,0:T(8,128)(2,1)S(1)}, u32[]{:S(2)}, u32[]{:S(2)}) collective-permute-start(bf16[640,128]{1,0:T(8,128)(2,1)S(1)} %get-tuple-element.67), channel_id=1, source_target_pairs={{0,12},{2,14},{4,0},{6,2},{8,4},{10,6},{12,8},{14,10},{16,28},{18,... | collective-permute-start | bytes 491528 | tf_op jit(solution)/shard_map/ppermute | solution.py:336
  62.1 8.4 %collective-permute-start.20 = (bf16[640,128]{1,0:T(8,128)(2,1)S(1)}, bf16[640,128]{1,0:T(8,128)(2,1)S(1)}, u32[]{:S(2)}, u32[]{:S(2)}) collective-permute-start(bf16[640,128]{1,0:T(8,128)(2,1)S(1)} %get-tuple-element.68), channel_id=1, source_target_pairs={{0,8},{2,10},{4,12},{6,14},{8,0},{10,2},{12,4},{14,6},{16,24},{18,... | collective-permute-start | bytes 491528 | tf_op jit(solution)/shard_map/ppermute | solution.py:336
  65.8 7.3 %collective-permute-start.22 = (bf16[640,128]{1,0:T(8,128)(2,1)S(1)}, bf16[640,128]{1,0:T(8,128)(2,1)S(1)}, u32[]{:S(2)}, u32[]{:S(2)}) collective-permute-start(bf16[640,128]{1,0:T(8,128)(2,1)S(1)} %shard_map.87), channel_id=1, source_target_pairs={{0,4},{2,6},{4,8},{6,10},{8,12},{10,14},{12,0},{14,2},{16,20},{18,... | collective-permute-start | bytes 491528 | tf_op jit(solution)/shard_map/ppermute | solution.py:336

commit v4 on v3

--- a/solution.py
+++ b/solution.py
@@ -139,6 +139,11 @@
         out_ref[SET_ROWS:, :] = coded
 
 
+def affine_kernel(gain_ref, bias_ref, out_ref):
+    out_ref[0:1, :] = gain_ref[...].reshape(1, WIDTH)
+    out_ref[1:2, :] = bias_ref[...].reshape(1, WIDTH)
+
+
 def z_kernel(*refs):
     *in_refs, out_ref = refs
     stats = [decode(ref[SET_ROWS:, :]) for ref in in_refs]
@@ -165,22 +170,14 @@
             out_ref[low : low + 4 * ROWS, :] = ref[h * 4 * ROWS : (h + 1) * 4 * ROWS, :]
 
 
-def weights_kernel(query_hbm, pair_hbm, gain_hbm, bias_hbm, *refs):
-    *out_refs, arrived = refs
-    copies = [
-        pltpu.make_async_copy(source, target, arrived.at[i])
-        for i, (source, target) in enumerate(
-            zip((query_hbm, pair_hbm, gain_hbm, bias_hbm), out_refs)
-        )
-    ]
-    for copy in copies:
-        copy.start()
-    for copy in copies:
-        copy.wait()
+def load_kernel(source_hbm, target_ref, arrived):
+    copy = pltpu.make_async_copy(source_hbm, target_ref, arrived)
+    copy.start()
+    copy.wait()
 
 
 def project_kernel(
-    place_ref, tokens_ref, s0, s1, s2, s3, query_ref, pair_ref, gain_ref, bias_ref, *refs
+    place_ref, tokens_ref, s0, s1, s2, s3, affine_ref, query_ref, pair_ref, *refs
 ):
     *message_refs, fresh_ref, sets_ref, last_ref = refs
     mean, squares = combine([s0[...], s1[...], s2[...], s3[...]], 32 * CELLS * GROUP_WIDTH)
@@ -189,9 +186,7 @@
     both = jnp.where(row == 0, mean, lax.rsqrt(spread + epsilon))
     channels = exact_dot(both, channel_of_group())
     scaled = (tokens_ref[...].astype(f32) - channels[0:1]) * channels[1:2]
-    gain = gain_ref[...].reshape(1, WIDTH)
-    bias = bias_ref[...].reshape(1, WIDTH)
-    normed = (scaled * gain + bias).astype(bf16)
+    normed = (scaled * affine_ref[0:1] + affine_ref[1:2]).astype(bf16)
 
     square = iota((ROWS, CELLS), 0)
     cell = iota((ROWS, CELLS), 1)
@@ -371,26 +366,23 @@
         sets,
     )
     received = [messages[0]] + [shift(messages[k], "x", k) for k in (1, 2, 3)]
+    norm_gain, norm_bias, _ = lax.optimization_barrier((norm_gain, norm_bias, messages[0]))
+    (affine,) = call(affine_kernel, [VMEM] * 2, [((2, WIDTH), f32)], norm_gain, norm_bias)
+    received, affine = lax.optimization_barrier((received, affine))
     (part,) = call(z_kernel, [VMEM] * 4, [((4 * SET_ROWS + ROWS, LANES), bf16)], *received)
     parts = [part] + [shift(part, "z", k) for k in (1, 2, 3)]
-    query_weight, pair_weight, norm_gain, norm_bias, _ = lax.optimization_barrier(
-        (query_weight, pair_weight, norm_gain, norm_bias, part)
-    )
-    weights = call(
-        weights_kernel,
-        [HBM] * 4,
-        [
-            ((WIDTH, WIDTH), bf16),
-            ((WIDTH, 2 * WIDTH), bf16),
-            ((WIDTH,), f32),
-            ((WIDTH,), f32),
-        ],
-        query_weight,
-        pair_weight,
-        norm_gain,
-        norm_bias,
-        scratch=[pltpu.SemaphoreType.DMA((4,))],
-    )
+    weights = [part]
+    for weight, limit in ((query_weight, 49), (pair_weight, 43)):
+        weight = after(weight, weights[0])
+        weights = list(call(
+            load_kernel,
+            [HBM],
+            [(weight.shape, bf16)],
+            weight,
+            scratch=[pltpu.SemaphoreType.DMA],
+            limit=limit,
+        )) + weights
+    weights = weights[1::-1]
     parts, weights = lax.optimization_barrier((parts, weights))
     (stats,) = call(stats_kernel, [VMEM] * 4, [((8, LANES), f32)], *parts)
     all_stats = [stats] + [shift(stats, "y", k) for k in (1, 2, 3)]
@@ -399,11 +391,12 @@
     pieces.append(shift(after(piece, *all_stats), "y", 2))
     *queries, fresh = call(
         project_kernel,
-        [SMEM] + [VMEM] * 9,
+        [SMEM] + [VMEM] * 8,
         [((ANSWER_ROWS + SET_ROWS, LANES), bf16)] * 4 + [((ROWS, 2 * WIDTH), bf16)],
         place,
         tokens,
         *all_stats,
+        affine,
         *weights,
         scratch=[
             pltpu.VMEM((4, SET_ROWS, LANES), bf16),

time: 75 us -> 74.7 us (level)
  local copies, waits for them, and re-layouts: 8.14 us -> 3.36 us
  Pallas kernels: 20.3 us -> 24 us
    unnamed x12 -> x8, local copies, waits for them, and re-layouts: 8.14 us -> 3.36 us
    pallas_call x12 -> x14, Pallas kernels: 20.3 us -> 24 us  [call(): pl.pallas_call(kernel, in_specs=ins, out_specs=[VMEM] * len(outs), out_sh...]
  transfers between devices with their start and end apart: 23 -> 23, of which waited for: 9 -> 8; matrix products, arithmetic and copies ran while one was open for 0% -> 0% of each run, Pallas kernels for 24% -> 29%
where the time goes in v4:
time: 74.7 us; the launch traced here: 73.4 us
  starting transfers between devices  34 us (46%)
  Pallas kernels  24 us (32%)
  waiting for transfers between devices  11.2 us (15%)
  local copies, waits for them, and re-layouts  3.36 us (4%)
  between operations  0.79 us (1%)
    ppermute x23, starting transfers between devices, permute(): return lax.ppermute(array, 'patch', pairs)  34 us
    pallas_call x14, Pallas kernels, call(): pl.pallas_call(kernel, in_specs=ins, out_specs=[VMEM] * len(outs), out_sh...  24 us
    ppermute x23, waiting for transfers between devices, permute(): return lax.ppermute(array, 'patch', pairs)  11.2 us
    unnamed x8, local copies, waits for them, and re-layouts  3.36 us
  transfers between devices with their start and end apart: 23, of which 8 were waited for; matrix products, arithmetic and copies ran while one was open for 0% of the time, Pallas kernels for 29%

profile of v4, /device:TPU:32, one launch (start us, length us, event | category | flops | bytes accessed | tf_op | source)
XLA Modules:
  0.0 73.4 jit_solution(1674904925944707588)
XLA Ops:
  0.6 1.1 %copy-done = bf16[1,256,1280]{2,1,0:T(8,128)(2,1)S(1)} copy-done((bf16[1,256,1280]{2,1,0:T(8,128)(2,1)S(1)}, bf16[1,256,1280]{2,1,0:T(8,128)(2,1)}, u32[]{:S(2)}) %copy-start) | copy-done | bytes 655384
  1.7 1.4 %shard_map.77 = (f32[8,128]{1,0:T(8,128)S(1)}, bf16[256,1280]{1,0:T(8,128)(2,1)S(1)}) custom-call(bf16[256,1280]{1,0:T(8,128)(2,1)S(1)} %bitcast.5), custom_call_target="tpu_custom_call" | custom-call | flops 1 | bytes 1 | tf_op jit(solution)/shard_map/pallas_call | solution.py:315
  3.2 0.9 %copy-done.1 = bf16[1,16,2560]{2,1,0:T(8,128)(2,1)S(1)} copy-done((bf16[1,16,2560]{2,1,0:T(8,128)(2,1)S(1)}, bf16[1,16,2560]{2,1,0:T(8,128)(2,1)}, u32[]{:S(2)}) %copy-start.1) | copy-done | bytes 81944
  4.4 1.6 %collective-permute-start.1 = (bf16[96,128]{1,0:T(8,128)(2,1)S(1)}, bf16[96,128]{1,0:T(8,128)(2,1)S(1)}, u32[]{:S(2)}, u32[]{:S(2)}) collective-permute-start(bf16[96,128]{1,0:T(8,128)(2,1)S(1)} %get-tuple-element.39), channel_id=1, source_target_pairs={{0,4},{2,6},{4,8},{6,10},{8,12},{10,14},{12,0},{14,2},{16,20},{18,... | collective-permute-start | bytes 73736 | tf_op jit(solution)/shard_map/ppermute | solution.py:331
  6.0 2.7 %collective-permute-start.2 = (bf16[96,128]{1,0:T(8,128)(2,1)S(1)}, bf16[96,128]{1,0:T(8,128)(2,1)S(1)}, u32[]{:S(2)}, u32[]{:S(2)}) collective-permute-start(bf16[96,128]{1,0:T(8,128)(2,1)S(1)} %get-tuple-element.40), channel_id=1, source_target_pairs={{0,8},{2,10},{4,12},{6,14},{8,0},{10,2},{12,4},{14,6},{16,24},{18,... | collective-permute-start | bytes 73736 | tf_op jit(solution)/shard_map/ppermute | solution.py:331
  8.7 1.4 %collective-permute-start.3 = (bf16[96,128]{1,0:T(8,128)(2,1)S(1)}, bf16[96,128]{1,0:T(8,128)(2,1)S(1)}, u32[]{:S(2)}, u32[]{:S(2)}) collective-permute-start(bf16[96,128]{1,0:T(8,128)(2,1)S(1)} %get-tuple-element.41), channel_id=1, source_target_pairs={{0,12},{2,14},{4,0},{6,2},{8,4},{10,6},{12,8},{14,10},{16,28},{18,... | collective-permute-start | bytes 73736 | tf_op jit(solution)/shard_map/ppermute | solution.py:331
  10.8 0.7 copy-done.3
  11.5 1.0 %collective-permute-done.3.refs_3_ = bf16[96,128]{1,0:T(8,128)(2,1)S(1)} collective-permute-done((bf16[96,128]{1,0:T(8,128)(2,1)S(1)}, bf16[96,128]{1,0:T(8,128)(2,1)S(1)}, u32[]{:S(2)}, u32[]{:S(2)}) %collective-permute-start.3) | collective-permute-done | bytes 24608 | tf_op jit(solution)/shard_map/ppermute | solution.py:331
  12.6 5.5 %collective-permute-start.6 = (bf16[336,128]{1,0:T(8,128)(2,1)S(1)}, bf16[336,128]{1,0:T(8,128)(2,1)S(1)}, u32[]{:S(2)}, u32[]{:S(2)}) collective-permute-start(bf16[336,128]{1,0:T(8,128)(2,1)S(1)} %shard_map.81.refs_0_), channel_id=1, source_target_pairs={{0,192},{2,194},{4,196},{6,198},{8,200},{10,202},{12,204},{14,206}... | collective-permute-start | bytes 258056 | tf_op jit(solution)/shard_map/ppermute | solution.py:331
  18.0 1.4 %collective-permute-start.5 = (bf16[336,128]{1,0:T(8,128)(2,1)S(1)}, bf16[336,128]{1,0:T(8,128)(2,1)S(1)}, u32[]{:S(2)}, u32[]{:S(2)}) collective-permute-start(bf16[336,128]{1,0:T(8,128)(2,1)S(1)} %shard_map.81.refs_0_), channel_id=1, source_target_pairs={{0,128},{2,130},{4,132},{6,134},{8,136},{10,138},{12,140},{14,142}... | collective-permute-start | bytes 258056 | tf_op jit(solution)/shard_map/ppermute | solution.py:331
  19.5 2.4 %collective-permute-start.4 = (bf16[336,128]{1,0:T(8,128)(2,1)S(1)}, bf16[336,128]{1,0:T(8,128)(2,1)S(1)}, u32[]{:S(2)}, u32[]{:S(2)}) collective-permute-start(bf16[336,128]{1,0:T(8,128)(2,1)S(1)} %shard_map.81.refs_0_), channel_id=1, source_target_pairs={{0,64},{2,66},{4,68},{6,70},{8,72},{10,74},{12,76},{14,78},{16,80}... | collective-permute-start | bytes 258056 | tf_op jit(solution)/shard_map/ppermute | solution.py:331
  21.9 1.9 %shard_map.82.query_ref = bf16[1280,1280]{1,0:T(8,128)(2,1)S(1)} custom-call(bf16[1280,1280]{1,0:T(8,128)(2,1)} %source_hbm), custom_call_target="tpu_custom_call" | custom-call | flops 1 | bytes 1 | tf_op jit(solution)/shard_map/pallas_call | solution.py:315
  23.8 2.9 %shard_map.83.pair_ref = bf16[1280,2560]{1,0:T(8,128)(2,1)S(1)} custom-call(bf16[1280,2560]{1,0:T(8,128)(2,1)} %source_hbm.1), custom_call_target="tpu_custom_call" | custom-call | flops 1 | bytes 1 | tf_op jit(solution)/shard_map/pallas_call | solution.py:315
  26.7 1.0 %collective-permute-done.5.refs_2_ = bf16[336,128]{1,0:T(8,128)(2,1)S(1)} collective-permute-done((bf16[336,128]{1,0:T(8,128)(2,1)S(1)}, bf16[336,128]{1,0:T(8,128)(2,1)S(1)}, u32[]{:S(2)}, u32[]{:S(2)}) %collective-permute-start.5) | collective-permute-done | bytes 86048 | tf_op jit(solution)/shard_map/ppermute | solution.py:331
  27.7 3.1 %collective-permute-start.9 = (f32[8,128]{1,0:T(8,128)S(1)}, f32[8,128]{1,0:T(8,128)S(1)}, u32[]{:S(2)}, u32[]{:S(2)}) collective-permute-start(f32[8,128]{1,0:T(8,128)S(1)} %shard_map.84.s0.stats_ref), channel_id=1, source_target_pairs={{0,48},{2,50},{4,52},{6,54},{8,56},{10,58},{12,60},{14,62},{16,0},... | collective-permute-start | bytes 12296 | tf_op jit(solution)/shard_map/ppermute | solution.py:331
  31.5 1.0 %collective-permute-start.7 = (f32[8,128]{1,0:T(8,128)S(1)}, f32[8,128]{1,0:T(8,128)S(1)}, u32[]{:S(2)}, u32[]{:S(2)}) collective-permute-start(f32[8,128]{1,0:T(8,128)S(1)} %shard_map.84.s0.stats_ref), channel_id=1, source_target_pairs={{0,16},{2,18},{4,20},{6,22},{8,24},{10,26},{12,28},{14,30},{16,32}... | collective-permute-start | bytes 12296 | tf_op jit(solution)/shard_map/ppermute | solution.py:331
  32.5 2.3 %collective-permute-start.11 = (bf16[1280,128]{1,0:T(8,128)(2,1)S(1)}, bf16[1280,128]{1,0:T(8,128)(2,1)S(1)}, u32[]{:S(2)}, u32[]{:S(2)}) collective-permute-start(bf16[1280,128]{1,0:T(8,128)(2,1)S(1)} %shard_map.86.refs_1_.refs_2_), channel_id=1, source_target_pairs={{0,48},{2,50},{4,52},{6,54},{8,56},{10,58},{12,60},{14,62},{16,0},... | collective-permute-start | bytes 983048 | tf_op jit(solution)/shard_map/ppermute | solution.py:331
  34.8 1.2 %collective-permute-done.8.s2 = f32[8,128]{1,0:T(8,128)S(1)} collective-permute-done((f32[8,128]{1,0:T(8,128)S(1)}, f32[8,128]{1,0:T(8,128)S(1)}, u32[]{:S(2)}, u32[]{:S(2)}) %collective-permute-start.8) | collective-permute-done | bytes 4128 | tf_op jit(solution)/shard_map/ppermute | solution.py:331
  36.3 1.7 %collective-permute-start.12 = (bf16[1280,128]{1,0:T(8,128)(2,1)S(1)}, bf16[1280,128]{1,0:T(8,128)(2,1)S(1)}, u32[]{:S(2)}, u32[]{:S(2)}) collective-permute-start(bf16[1280,128]{1,0:T(8,128)(2,1)S(1)} %shard_map.86.refs_1_.refs_2_), channel_id=1, source_target_pairs={{0,32},{2,34},{4,36},{6,38},{8,40},{10,42},{12,44},{14,46},{16,48}... | collective-permute-start | bytes 983048 | tf_op jit(solution)/shard_map/ppermute | solution.py:331
  38.0 3.2 %shard_map.85 = (bf16[720,128]{1,0:T(8,128)(2,1)S(1)}, bf16[720,128]{1,0:T(8,128)(2,1)S(1)}, bf16[720,128]{1,0:T(8,128)(2,1)S(1)}, bf16[720,128]{1,0:T(8,128)(2,1)S(1)}, bf16[16,2560]{1,0:T(8,128)(2,1)}) custom-call(s32[1]{0:T(128)} %bitcast.place_ref, bf16[256,1280]{1,0:T(8,128)(2,1)S(1)} %get-tuple-element.36.tokens_ref, ...), custom_call_target="tpu_custom_call" | custom-call | flops 1 | bytes 1 | tf_op jit(solution)/shard_map/pallas_call | solution.py:315
  41.2 1.5 %collective-permute-start.13 = (bf16[720,128]{1,0:T(8,128)(2,1)S(1)}, bf16[720,128]{1,0:T(8,128)(2,1)S(1)}, u32[]{:S(2)}, u32[]{:S(2)}) collective-permute-start(bf16[720,128]{1,0:T(8,128)(2,1)S(1)} %get-tuple-element.59), channel_id=1, source_target_pairs={{0,8},{2,10},{4,12},{6,14},{8,0},{10,2},{12,4},{14,6},{16,24},{18,... | collective-permute-start | bytes 552968 | tf_op jit(solution)/shard_map/ppermute | solution.py:331
  42.8 2.2 %collective-permute-start.18 = (bf16[720,128]{1,0:T(8,128)(2,1)S(1)}, bf16[720,128]{1,0:T(8,128)(2,1)S(1)}, u32[]{:S(2)}, u32[]{:S(2)}) collective-permute-start(bf16[720,128]{1,0:T(8,128)(2,1)S(1)} %get-tuple-element.64), channel_id=1, source_target_pairs={{0,4},{2,6},{4,8},{6,10},{8,12},{10,14},{12,0},{14,2},{16,20},{18,... | collective-permute-start | bytes 552968 | tf_op jit(solution)/shard_map/ppermute | solution.py:331
  45.0 3.4 %collective-permute-done.13.refs_0_ = bf16[720,128]{1,0:T(8,128)(2,1)S(1)} collective-permute-done((bf16[720,128]{1,0:T(8,128)(2,1)S(1)}, bf16[720,128]{1,0:T(8,128)(2,1)S(1)}, u32[]{:S(2)}, u32[]{:S(2)}) %collective-permute-start.13) | collective-permute-done | bytes 184352 | tf_op jit(solution)/shard_map/ppermute | solution.py:331
  48.9 1.4 %collective-permute-done.10.refs_2_.refs_3_ = bf16[1280,128]{1,0:T(8,128)(2,1)S(1)} collective-permute-done((bf16[1280,128]{1,0:T(8,128)(2,1)S(1)}, bf16[1280,128]{1,0:T(8,128)(2,1)S(1)}, u32[]{:S(2)}, u32[]{:S(2)}) %collective-permute-start.10) | collective-permute-done | bytes 327712 | tf_op jit(solution)/shard_map/ppermute | solution.py:331
  50.8 2.5 %collective-permute-start.21 = (bf16[720,128]{1,0:T(8,128)(2,1)S(1)}, bf16[720,128]{1,0:T(8,128)(2,1)S(1)}, u32[]{:S(2)}, u32[]{:S(2)}) collective-permute-start(bf16[720,128]{1,0:T(8,128)(2,1)S(1)} %get-tuple-element.68), channel_id=1, source_target_pairs={{0,12},{2,14},{4,0},{6,2},{8,4},{10,6},{12,8},{14,10},{16,28},{18,... | collective-permute-start | bytes 552968 | tf_op jit(solution)/shard_map/ppermute | solution.py:331
  53.3 6.5 %shard_map.88 = (bf16[640,128]{1,0:T(8,128)(2,1)S(1)}, bf16[640,128]{1,0:T(8,128)(2,1)S(1)}) custom-call(s32[1]{0:T(128)} %bitcast.place_ref, bf16[720,128]{1,0:T(8,128)(2,1)S(1)} %collective-permute-done.13.refs_0_, bf16[720,128]{1,0:T(8,128)(2,1)S(1)} %collective-permute-done.18.refs_1_, bf16[1280,128]{1,0:T(8,128)(2,1)S(1)} %shard_map.86.refs_1_.refs_2_, ...), custom_call_target="tpu_custom_call" | custom-call | flops 1 | bytes 1 | tf_op jit(solution)/shard_map/pallas_call | solution.py:315
  59.8 1.6 %collective-permute-start.19 = (bf16[640,128]{1,0:T(8,128)(2,1)S(1)}, bf16[640,128]{1,0:T(8,128)(2,1)S(1)}, u32[]{:S(2)}, u32[]{:S(2)}) collective-permute-start(bf16[640,128]{1,0:T(8,128)(2,1)S(1)} %get-tuple-element.65), channel_id=1, source_target_pairs={{0,12},{2,14},{4,0},{6,2},{8,4},{10,6},{12,8},{14,10},{16,28},{18,... | collective-permute-start | bytes 491528 | tf_op jit(solution)/shard_map/ppermute | solution.py:331
  61.5 3.4 %shard_map.89 = bf16[640,128]{1,0:T(8,128)(2,1)S(1)} custom-call(s32[1]{0:T(128)} %bitcast.place_ref, bf16[720,128]{1,0:T(8,128)(2,1)S(1)} %collective-permute-done.21.refs_0_, bf16[1280,128]{1,0:T(8,128)(2,1)S(1)} %shard_map.86.refs_1_.refs_2_, bf16[1280,128]{1,0:T(8,128)(2,1)S(1)} %collective-permute-done.10.refs_2_.refs_3_, ...), custom_call_target="tpu_custom_call" | custom-call | flops 1 | bytes 1 | tf_op jit(solution)/shard_map/pallas_call | solution.py:315
  65.0 1.2 %collective-permute-start.22 = (bf16[640,128]{1,0:T(8,128)(2,1)S(1)}, bf16[640,128]{1,0:T(8,128)(2,1)S(1)}, u32[]{:S(2)}, u32[]{:S(2)}) collective-permute-start(bf16[640,128]{1,0:T(8,128)(2,1)S(1)} %shard_map.89), channel_id=1, source_target_pairs={{0,4},{2,6},{4,8},{6,10},{8,12},{10,14},{12,0},{14,2},{16,20},{18,... | collective-permute-start | bytes 491528 | tf_op jit(solution)/shard_map/ppermute | solution.py:331
  66.2 3.5 %shard_map.87.refs_0_ = bf16[640,128]{1,0:T(8,128)(2,1)S(1)} custom-call(s32[1]{0:T(128)} %bitcast.place_ref, bf16[720,128]{1,0:T(8,128)(2,1)S(1)} %get-tuple-element.57.refs_0_, bf16[1280,128]{1,0:T(8,128)(2,1)S(1)} %shard_map.86.refs_1_.refs_2_, bf16[1280,128]{1,0:T(8,128)(2,1)S(1)} %collective-permute-done.10.refs_2_.refs_3_, ...), custom_call_target="tpu_custom_call" | custom-call | flops 1 | bytes 1 | tf_op jit(solution)/shard_map/pallas_call | solution.py:315
  69.7 2.7 %collective-permute-done.22.refs_3_ = bf16[640,128]{1,0:T(8,128)(2,1)S(1)} collective-permute-done((bf16[640,128]{1,0:T(8,128)(2,1)S(1)}, bf16[640,128]{1,0:T(8,128)(2,1)S(1)}, u32[]{:S(2)}, u32[]{:S(2)}) %collective-permute-start.22) | collective-permute-done | bytes 163872 | tf_op jit(solution)/shard_map/ppermute | solution.py:331
  72.4 1.0 %shard_map.90 = bf16[256,1280]{1,0:T(8,128)(2,1)} custom-call(s32[1]{0:T(128)} %bitcast.place_ref, bf16[640,128]{1,0:T(8,128)(2,1)S(1)} %shard_map.87.refs_0_, bf16[640,128]{1,0:T(8,128)(2,1)S(1)} %collective-permute-done.19.refs_1_, bf16[640,128]{1,0:T(8,128)(2,1)S(1)} %collective-permute-done.20.refs_2_, bf16[640,128]{1,0:T(8,128)(2,1)S(1)} %collective-permute-done.22.refs_3_), custom_call_target="tpu_custom_call" | custom-call | flops 1 | bytes 1 | tf_op jit(solution)/shard_map/pallas_call | solution.py:315
  (36 shorter events, 3.2 us)
Async XLA Ops:
  0.6 1.1 %copy-start = (bf16[1,256,1280]{2,1,0:T(8,128)(2,1)S(1)}, bf16[1,256,1280]{2,1,0:T(8,128)(2,1)}, u32[]{:S(2)}) copy-start(bf16[1,256,1280]{2,1,0:T(8,128)(2,1)} %param.6) | copy-start | bytes 1966084
  3.1 1.2 %collective-permute-start = (f32[8,128]{1,0:T(8,128)S(1)}, f32[8,128]{1,0:T(8,128)S(1)}, u32[]{:S(2)}, u32[]{:S(2)}) collective-permute-start(f32[8,128]{1,0:T(8,128)S(1)} %get-tuple-element.37.stats_ref.own_ref), channel_id=1, source_target_pairs={{0,2},{2,0},{4,6},{6,4},{8,10},{10,8},{12,14},{14,12},{16,18},{18,... | collective-permute-start | bytes 12296 | tf_op jit(solution)/shard_map/ppermute | solution.py:331
  3.2 0.9 %copy-start.1 = (bf16[1,16,2560]{2,1,0:T(8,128)(2,1)S(1)}, bf16[1,16,2560]{2,1,0:T(8,128)(2,1)}, u32[]{:S(2)}) copy-start(bf16[1,16,2560]{2,1,0:T(8,128)(2,1)} %param.7) | copy-start | bytes 245764
  4.4 7.1 %collective-permute-start.1 = (bf16[96,128]{1,0:T(8,128)(2,1)S(1)}, bf16[96,128]{1,0:T(8,128)(2,1)S(1)}, u32[]{:S(2)}, u32[]{:S(2)}) collective-permute-start(bf16[96,128]{1,0:T(8,128)(2,1)S(1)} %get-tuple-element.39), channel_id=1, source_target_pairs={{0,4},{2,6},{4,8},{6,10},{8,12},{10,14},{12,0},{14,2},{16,20},{18,... | collective-permute-start | bytes 73736 | tf_op jit(solution)/shard_map/ppermute | solution.py:331
  6.0 5.6 %collective-permute-start.2 = (bf16[96,128]{1,0:T(8,128)(2,1)S(1)}, bf16[96,128]{1,0:T(8,128)(2,1)S(1)}, u32[]{:S(2)}, u32[]{:S(2)}) collective-permute-start(bf16[96,128]{1,0:T(8,128)(2,1)S(1)} %get-tuple-element.40), channel_id=1, source_target_pairs={{0,8},{2,10},{4,12},{6,14},{8,0},{10,2},{12,4},{14,6},{16,24},{18,... | collective-permute-start | bytes 73736 | tf_op jit(solution)/shard_map/ppermute | solution.py:331
  8.7 3.8 %collective-permute-start.3 = (bf16[96,128]{1,0:T(8,128)(2,1)S(1)}, bf16[96,128]{1,0:T(8,128)(2,1)S(1)}, u32[]{:S(2)}, u32[]{:S(2)}) collective-permute-start(bf16[96,128]{1,0:T(8,128)(2,1)S(1)} %get-tuple-element.41), channel_id=1, source_target_pairs={{0,12},{2,14},{4,0},{6,2},{8,4},{10,6},{12,8},{14,10},{16,28},{18,... | collective-permute-start | bytes 73736 | tf_op jit(solution)/shard_map/ppermute | solution.py:331
  10.1 0.7 copy-start.2
  10.8 0.7 copy-start.3
  12.6 14.1 %collective-permute-start.6 = (bf16[336,128]{1,0:T(8,128)(2,1)S(1)}, bf16[336,128]{1,0:T(8,128)(2,1)S(1)}, u32[]{:S(2)}, u32[]{:S(2)}) collective-permute-start(bf16[336,128]{1,0:T(8,128)(2,1)S(1)} %shard_map.81.refs_0_), channel_id=1, source_target_pairs={{0,192},{2,194},{4,196},{6,198},{8,200},{10,202},{12,204},{14,206}... | collective-permute-start | bytes 258056 | tf_op jit(solution)/shard_map/ppermute | solution.py:331
  18.0 9.7 %collective-permute-start.5 = (bf16[336,128]{1,0:T(8,128)(2,1)S(1)}, bf16[336,128]{1,0:T(8,128)(2,1)S(1)}, u32[]{:S(2)}, u32[]{:S(2)}) collective-permute-start(bf16[336,128]{1,0:T(8,128)(2,1)S(1)} %shard_map.81.refs_0_), channel_id=1, source_target_pairs={{0,128},{2,130},{4,132},{6,134},{8,136},{10,138},{12,140},{14,142}... | collective-permute-start | bytes 258056 | tf_op jit(solution)/shard_map/ppermute | solution.py:331
  19.5 8.2 %collective-permute-start.4 = (bf16[336,128]{1,0:T(8,128)(2,1)S(1)}, bf16[336,128]{1,0:T(8,128)(2,1)S(1)}, u32[]{:S(2)}, u32[]{:S(2)}) collective-permute-start(bf16[336,128]{1,0:T(8,128)(2,1)S(1)} %shard_map.81.refs_0_), channel_id=1, source_target_pairs={{0,64},{2,66},{4,68},{6,70},{8,72},{10,74},{12,76},{14,78},{16,80}... | collective-permute-start | bytes 258056 | tf_op jit(solution)/shard_map/ppermute | solution.py:331
  27.7 7.1 %collective-permute-start.9 = (f32[8,128]{1,0:T(8,128)S(1)}, f32[8,128]{1,0:T(8,128)S(1)}, u32[]{:S(2)}, u32[]{:S(2)}) collective-permute-start(f32[8,128]{1,0:T(8,128)S(1)} %shard_map.84.s0.stats_ref), channel_id=1, source_target_pairs={{0,48},{2,50},{4,52},{6,54},{8,56},{10,58},{12,60},{14,62},{16,0},... | collective-permute-start | bytes 12296 | tf_op jit(solution)/shard_map/ppermute | solution.py:331
  30.8 5.1 %collective-permute-start.8 = (f32[8,128]{1,0:T(8,128)S(1)}, f32[8,128]{1,0:T(8,128)S(1)}, u32[]{:S(2)}, u32[]{:S(2)}) collective-permute-start(f32[8,128]{1,0:T(8,128)S(1)} %shard_map.84.s0.stats_ref), channel_id=1, source_target_pairs={{0,32},{2,34},{4,36},{6,38},{8,40},{10,42},{12,44},{14,46},{16,48}... | collective-permute-start | bytes 12296 | tf_op jit(solution)/shard_map/ppermute | solution.py:331
  31.5 4.9 %collective-permute-start.7 = (f32[8,128]{1,0:T(8,128)S(1)}, f32[8,128]{1,0:T(8,128)S(1)}, u32[]{:S(2)}, u32[]{:S(2)}) collective-permute-start(f32[8,128]{1,0:T(8,128)S(1)} %shard_map.84.s0.stats_ref), channel_id=1, source_target_pairs={{0,16},{2,18},{4,20},{6,22},{8,24},{10,26},{12,28},{14,30},{16,32}... | collective-permute-start | bytes 12296 | tf_op jit(solution)/shard_map/ppermute | solution.py:331
  32.5 15.9 %collective-permute-start.11 = (bf16[1280,128]{1,0:T(8,128)(2,1)S(1)}, bf16[1280,128]{1,0:T(8,128)(2,1)S(1)}, u32[]{:S(2)}, u32[]{:S(2)}) collective-permute-start(bf16[1280,128]{1,0:T(8,128)(2,1)S(1)} %shard_map.86.refs_1_.refs_2_), channel_id=1, source_target_pairs={{0,48},{2,50},{4,52},{6,54},{8,56},{10,58},{12,60},{14,62},{16,0},... | collective-permute-start | bytes 983048 | tf_op jit(solution)/shard_map/ppermute | solution.py:331
  34.8 15.5 %collective-permute-start.10 = (bf16[1280,128]{1,0:T(8,128)(2,1)S(1)}, bf16[1280,128]{1,0:T(8,128)(2,1)S(1)}, u32[]{:S(2)}, u32[]{:S(2)}) collective-permute-start(bf16[1280,128]{1,0:T(8,128)(2,1)S(1)} %shard_map.86.refs_1_.refs_2_), channel_id=1, source_target_pairs={{0,16},{2,18},{4,20},{6,22},{8,24},{10,26},{12,28},{14,30},{16,32}... | collective-permute-start | bytes 983048 | tf_op jit(solution)/shard_map/ppermute | solution.py:331
  36.3 14.0 %collective-permute-start.12 = (bf16[1280,128]{1,0:T(8,128)(2,1)S(1)}, bf16[1280,128]{1,0:T(8,128)(2,1)S(1)}, u32[]{:S(2)}, u32[]{:S(2)}) collective-permute-start(bf16[1280,128]{1,0:T(8,128)(2,1)S(1)} %shard_map.86.refs_1_.refs_2_), channel_id=1, source_target_pairs={{0,32},{2,34},{4,36},{6,38},{8,40},{10,42},{12,44},{14,46},{16,48}... | collective-permute-start | bytes 983048 | tf_op jit(solution)/shard_map/ppermute | solution.py:331
  41.2 7.1 %collective-permute-start.13 = (bf16[720,128]{1,0:T(8,128)(2,1)S(1)}, bf16[720,128]{1,0:T(8,128)(2,1)S(1)}, u32[]{:S(2)}, u32[]{:S(2)}) collective-permute-start(bf16[720,128]{1,0:T(8,128)(2,1)S(1)} %get-tuple-element.59), channel_id=1, source_target_pairs={{0,8},{2,10},{4,12},{6,14},{8,0},{10,2},{12,4},{14,6},{16,24},{18,... | collective-permute-start | bytes 552968 | tf_op jit(solution)/shard_map/ppermute | solution.py:331
  42.8 8.0 %collective-permute-start.18 = (bf16[720,128]{1,0:T(8,128)(2,1)S(1)}, bf16[720,128]{1,0:T(8,128)(2,1)S(1)}, u32[]{:S(2)}, u32[]{:S(2)}) collective-permute-start(bf16[720,128]{1,0:T(8,128)(2,1)S(1)} %get-tuple-element.64), channel_id=1, source_target_pairs={{0,4},{2,6},{4,8},{6,10},{8,12},{10,14},{12,0},{14,2},{16,20},{18,... | collective-permute-start | bytes 552968 | tf_op jit(solution)/shard_map/ppermute | solution.py:331
  48.4 4.9 %collective-permute-start.14 = (bf16[1280,128]{1,0:T(8,128)(2,1)S(1)}, bf16[1280,128]{1,0:T(8,128)(2,1)S(1)}, u32[]{:S(2)}, u32[]{:S(2)}) collective-permute-start(bf16[1280,128]{1,0:T(8,128)(2,1)S(1)} %shard_map.86.refs_1_.refs_2_), channel_id=1, source_target_pairs={{0,2},{2,0},{4,6},{6,4},{8,10},{10,8},{12,14},{14,12},{16,18},{18,... | collective-permute-start | bytes 983048 | tf_op jit(solution)/shard_map/ppermute | solution.py:331
  48.4 4.9 %collective-permute-start.16 = (bf16[1280,128]{1,0:T(8,128)(2,1)S(1)}, bf16[1280,128]{1,0:T(8,128)(2,1)S(1)}, u32[]{:S(2)}, u32[]{:S(2)}) collective-permute-start(bf16[1280,128]{1,0:T(8,128)(2,1)S(1)} %collective-permute-done.11.refs_3_.refs_4_), channel_id=1, source_target_pairs={{0,2},{2,0},{4,6},{6,4},{8,10},{10,8},{12,14},{14,12},{16,18},{18,... | collective-permute-start | bytes 983048 | tf_op jit(solution)/shard_map/ppermute | solution.py:331
  50.3 3.0 %collective-permute-start.15 = (bf16[1280,128]{1,0:T(8,128)(2,1)S(1)}, bf16[1280,128]{1,0:T(8,128)(2,1)S(1)}, u32[]{:S(2)}, u32[]{:S(2)}) collective-permute-start(bf16[1280,128]{1,0:T(8,128)(2,1)S(1)} %collective-permute-done.10.refs_2_.refs_3_), channel_id=1, source_target_pairs={{0,2},{2,0},{4,6},{6,4},{8,10},{10,8},{12,14},{14,12},{16,18},{18,... | collective-permute-start | bytes 983048 | tf_op jit(solution)/shard_map/ppermute | solution.py:331
  50.3 3.0 %collective-permute-start.17 = (bf16[1280,128]{1,0:T(8,128)(2,1)S(1)}, bf16[1280,128]{1,0:T(8,128)(2,1)S(1)}, u32[]{:S(2)}, u32[]{:S(2)}) collective-permute-start(bf16[1280,128]{1,0:T(8,128)(2,1)S(1)} %collective-permute-done.12.refs_4_.refs_5_), channel_id=1, source_target_pairs={{0,2},{2,0},{4,6},{6,4},{8,10},{10,8},{12,14},{14,12},{16,18},{18,... | collective-permute-start | bytes 983048 | tf_op jit(solution)/shard_map/ppermute | solution.py:331
  50.8 10.7 %collective-permute-start.21 = (bf16[720,128]{1,0:T(8,128)(2,1)S(1)}, bf16[720,128]{1,0:T(8,128)(2,1)S(1)}, u32[]{:S(2)}, u32[]{:S(2)}) collective-permute-start(bf16[720,128]{1,0:T(8,128)(2,1)S(1)} %get-tuple-element.68), channel_id=1, source_target_pairs={{0,12},{2,14},{4,0},{6,2},{8,4},{10,6},{12,8},{14,10},{16,28},{18,... | collective-permute-start | bytes 552968 | tf_op jit(solution)/shard_map/ppermute | solution.py:331
  59.8 9.9 %collective-permute-start.19 = (bf16[640,128]{1,0:T(8,128)(2,1)S(1)}, bf16[640,128]{1,0:T(8,128)(2,1)S(1)}, u32[]{:S(2)}, u32[]{:S(2)}) collective-permute-start(bf16[640,128]{1,0:T(8,128)(2,1)S(1)} %get-tuple-element.65), channel_id=1, source_target_pairs={{0,12},{2,14},{4,0},{6,2},{8,4},{10,6},{12,8},{14,10},{16,28},{18,... | collective-permute-start | bytes 491528 | tf_op jit(solution)/shard_map/ppermute | solution.py:331
  61.4 8.2 %collective-permute-start.20 = (bf16[640,128]{1,0:T(8,128)(2,1)S(1)}, bf16[640,128]{1,0:T(8,128)(2,1)S(1)}, u32[]{:S(2)}, u32[]{:S(2)}) collective-permute-start(bf16[640,128]{1,0:T(8,128)(2,1)S(1)} %get-tuple-element.66), channel_id=1, source_target_pairs={{0,8},{2,10},{4,12},{6,14},{8,0},{10,2},{12,4},{14,6},{16,24},{18,... | collective-permute-start | bytes 491528 | tf_op jit(solution)/shard_map/ppermute | solution.py:331
  65.0 7.5 %collective-permute-start.22 = (bf16[640,128]{1,0:T(8,128)(2,1)S(1)}, bf16[640,128]{1,0:T(8,128)(2,1)S(1)}, u32[]{:S(2)}, u32[]{:S(2)}) collective-permute-start(bf16[640,128]{1,0:T(8,128)(2,1)S(1)} %shard_map.89), channel_id=1, source_target_pairs={{0,4},{2,6},{4,8},{6,10},{8,12},{10,14},{12,0},{14,2},{16,20},{18,... | collective-permute-start | bytes 491528 | tf_op jit(solution)/shard_map/ppermute | solution.py:331

commit v5 on v4

--- a/solution.py
+++ b/solution.py
@@ -23,7 +23,6 @@
 
 f32 = jnp.float32
 bf16 = jnp.bfloat16
-HIGHEST = lax.Precision.HIGHEST
 VMEM = pl.BlockSpec(memory_space=pltpu.VMEM)
 SMEM = pl.BlockSpec(memory_space=pltpu.SMEM)
 HBM = pl.BlockSpec(memory_space=pltpu.HBM)
@@ -36,17 +35,35 @@
 def group_of_channel():
     low = iota((WIDTH, LANES), 1) * GROUP_WIDTH
     channel = iota((WIDTH, LANES), 0)
-    return ((channel >= low) & (channel < low + GROUP_WIDTH)).astype(f32)
+    return ((channel >= low) & (channel < low + GROUP_WIDTH)).astype(f32).astype(bf16)
 
 
 def channel_of_group():
     low = iota((LANES, WIDTH), 0) * GROUP_WIDTH
     channel = iota((LANES, WIDTH), 1)
-    return ((channel >= low) & (channel < low + GROUP_WIDTH)).astype(f32)
-
-
-def exact_dot(left, right):
-    return jnp.dot(left, right, precision=HIGHEST, preferred_element_type=f32)
+    return ((channel >= low) & (channel < low + GROUP_WIDTH)).astype(f32).astype(bf16)
+
+
+def split_rows(*rows):
+    width = rows[0].shape[1]
+    row = iota((ROWS, width), 0)
+    split = jnp.zeros((ROWS, width), f32)
+    for i, rest in enumerate(rows):
+        for part in range(3):
+            rounded = rest.astype(bf16).astype(f32)
+            split = jnp.where(row == 3 * i + part, rounded, split)
+            rest = rest - rounded
+    return split.astype(bf16)
+
+
+def join_rows(split, i):
+    parts = split[3 * i : 3 * i + 3].astype(f32)
+    return parts[0:1] + parts[1:2] + parts[2:3]
+
+
+def select_dot(matrix, *rows):
+    products = jnp.dot(split_rows(*rows), matrix, preferred_element_type=f32)
+    return [join_rows(products, i) for i in range(len(rows))]
 
 
 def combine(parts, entries):
@@ -61,22 +78,9 @@
     return jnp.where(row == 0, mean, jnp.where(row == 1, squares, 0.0))
 
 
-def encode(mean, squares):
-    row = iota((ROWS, LANES), 0)
-    coded = jnp.zeros((ROWS, LANES), f32)
-    for i, rest in enumerate((mean, squares)):
-        for part in range(3):
-            rounded = rest.astype(bf16).astype(f32)
-            coded = jnp.where(row == 3 * i + part, rounded, coded)
-            rest = rest - rounded
-    return coded.astype(bf16)
-
-
 def decode(rows):
-    parts = rows.astype(f32)
-    return jnp.concatenate(
-        [parts[0:1] + parts[1:2] + parts[2:3], parts[3:4] + parts[4:5] + parts[5:6]], axis=0
-    )
+    split = rows.astype(f32)
+    return jnp.concatenate([join_rows(split, 0), join_rows(split, 1)], axis=0)
 
 
 def head_tiles(pairs):
@@ -116,12 +120,13 @@
     tokens = tokens_ref[...]
     kept_ref[...] = tokens
     values = tokens.astype(f32)
-    sums = jnp.broadcast_to(jnp.sum(values, axis=0, keepdims=True), (8, WIDTH))
-    mean = exact_dot(sums, group_of_channel()) / (CELLS * GROUP_WIDTH)
-    center = exact_dot(mean, channel_of_group())
-    shifted = values - center[0:1]
-    squares = jnp.broadcast_to(jnp.sum(shifted * shifted, axis=0, keepdims=True), (8, WIDTH))
-    squares = exact_dot(squares, group_of_channel())
+    (mean,) = select_dot(group_of_channel(), jnp.sum(values, axis=0, keepdims=True))
+    mean = mean / (CELLS * GROUP_WIDTH)
+    (center,) = select_dot(channel_of_group(), mean)
+    shifted = values - center
+    (squares,) = select_dot(
+        group_of_channel(), jnp.sum(shifted * shifted, axis=0, keepdims=True)
+    )
     stats_ref[...] = stack_stats(mean, squares)
 
 
@@ -132,7 +137,7 @@
 
 def x_kernel(place_ref, own_ref, other_ref, sets_ref, *out_refs):
     mean, squares = combine([own_ref[...], other_ref[...]], CELLS * GROUP_WIDTH)
-    coded = encode(mean, squares)
+    coded = split_rows(mean, squares)
     place = place_ref[0]
     for k, out_ref in enumerate(out_refs):
         out_ref[0:SET_ROWS, :] = sets_ref[lax.rem(place + k, 4)]
@@ -152,7 +157,7 @@
         for h in range(SET_HEADS):
             low = h * 4 * ROWS + k * ROWS
             out_ref[low : low + ROWS, :] = ref[h * ROWS : (h + 1) * ROWS, :]
-    out_ref[4 * SET_ROWS :, :] = encode(mean, squares)
+    out_ref[4 * SET_ROWS :, :] = split_rows(mean, squares)
 
 
 def stats_kernel(*refs):
@@ -182,10 +187,8 @@
     *message_refs, fresh_ref, sets_ref, last_ref = refs
     mean, squares = combine([s0[...], s1[...], s2[...], s3[...]], 32 * CELLS * GROUP_WIDTH)
     spread = squares / (128 * CELLS * GROUP_WIDTH)
-    row = iota((8, LANES), 0)
-    both = jnp.where(row == 0, mean, lax.rsqrt(spread + epsilon))
-    channels = exact_dot(both, channel_of_group())
-    scaled = (tokens_ref[...].astype(f32) - channels[0:1]) * channels[1:2]
+    center, inverse = select_dot(channel_of_group(), mean, lax.rsqrt(spread + epsilon))
+    scaled = (tokens_ref[...].astype(f32) - center) * inverse
     normed = (scaled * affine_ref[0:1] + affine_ref[1:2]).astype(bf16)
 
     square = iota((ROWS, CELLS), 0)
@@ -370,18 +373,19 @@
     (affine,) = call(affine_kernel, [VMEM] * 2, [((2, WIDTH), f32)], norm_gain, norm_bias)
     received, affine = lax.optimization_barrier((received, affine))
     (part,) = call(z_kernel, [VMEM] * 4, [((4 * SET_ROWS + ROWS, LANES), bf16)], *received)
-    parts = [part] + [shift(part, "z", k) for k in (1, 2, 3)]
+    parts = [part] + [shift(part, "z", k) for k in (2, 3, 1)]
     weights = [part]
     for weight, limit in ((query_weight, 49), (pair_weight, 43)):
         weight = after(weight, weights[0])
-        weights = list(call(
+        loaded = call(
             load_kernel,
             [HBM],
             [(weight.shape, bf16)],
             weight,
             scratch=[pltpu.SemaphoreType.DMA],
             limit=limit,
-        )) + weights
+        )
+        weights = [*loaded, *weights]
     weights = weights[1::-1]
     parts, weights = lax.optimization_barrier((parts, weights))
     (stats,) = call(stats_kernel, [VMEM] * 4, [((8, LANES), f32)], *parts)
@@ -404,9 +408,9 @@
         ],
     )
     asked = {0: queries[0]}
-    for k in (2, 1, 3):
+    for k in (1, 2, 3):
         asked[k] = shift(after(queries[k], pieces[1]) if k == 3 else queries[k], "x", k)
-    tables = pieces + [shift(after(block, asked[2]), "core", 1) for block in pieces]
+    tables = pieces + [shift(after(block, asked[1]), "core", 1) for block in pieces]
     results = [None] * 4
     for sources in ((2, 1), (3,), (0,)):
         answers = call(

time: 74.7 us -> 73.5 us (0.984); the launches traced: 73.4 us -> 73.1 us
  transfers between devices with their start and end apart: 23 -> 23, of which waited for: 8 -> 9; matrix products, arithmetic and copies ran while one was open for 0% -> 0% of each run, Pallas kernels for 29% -> 29%
where the time goes in v5:
time: 73.5 us; the launch traced here: 73.1 us
  starting transfers between devices  34.2 us (47%)
  Pallas kernels  23.4 us (32%)
  waiting for transfers between devices  11.3 us (15%)
  local copies, waits for them, and re-layouts  3.36 us (5%)
  between operations  0.8 us (1%)
    ppermute x23, starting transfers between devices, permute(): return lax.ppermute(array, 'patch', pairs)  34.2 us
    pallas_call x14, Pallas kernels, call(): pl.pallas_call(kernel, in_specs=ins, out_specs=[VMEM] * len(outs), out_sh...  23.4 us
    ppermute x23, waiting for transfers between devices, permute(): return lax.ppermute(array, 'patch', pairs)  11.3 us
    unnamed x8, local copies, waits for them, and re-layouts  3.36 us
  transfers between devices with their start and end apart: 23, of which 9 were waited for; matrix products, arithmetic and copies ran while one was open for 0% of the time, Pallas kernels for 29%

profile of v5, /device:TPU:32, one launch (start us, length us, event | category | flops | bytes accessed | tf_op | source)
XLA Modules:
  0.0 73.1 jit_solution(222490811257141112)
XLA Ops:
  0.6 1.1 %copy-done = bf16[1,256,1280]{2,1,0:T(8,128)(2,1)S(1)} copy-done((bf16[1,256,1280]{2,1,0:T(8,128)(2,1)S(1)}, bf16[1,256,1280]{2,1,0:T(8,128)(2,1)}, u32[]{:S(2)}) %copy-start) | copy-done | bytes 655384
  1.7 1.0 %shard_map.77 = (f32[8,128]{1,0:T(8,128)S(1)}, bf16[256,1280]{1,0:T(8,128)(2,1)S(1)}) custom-call(bf16[256,1280]{1,0:T(8,128)(2,1)S(1)} %bitcast.5), custom_call_target="tpu_custom_call" | custom-call | flops 1 | bytes 1 | tf_op jit(solution)/shard_map/pallas_call | solution.py:318
  2.8 0.9 %copy-done.1 = bf16[1,16,2560]{2,1,0:T(8,128)(2,1)S(1)} copy-done((bf16[1,16,2560]{2,1,0:T(8,128)(2,1)S(1)}, bf16[1,16,2560]{2,1,0:T(8,128)(2,1)}, u32[]{:S(2)}) %copy-start.1) | copy-done | bytes 81944
  4.0 1.6 %collective-permute-start.1 = (bf16[96,128]{1,0:T(8,128)(2,1)S(1)}, bf16[96,128]{1,0:T(8,128)(2,1)S(1)}, u32[]{:S(2)}, u32[]{:S(2)}) collective-permute-start(bf16[96,128]{1,0:T(8,128)(2,1)S(1)} %get-tuple-element.39), channel_id=1, source_target_pairs={{0,4},{2,6},{4,8},{6,10},{8,12},{10,14},{12,0},{14,2},{16,20},{18,... | collective-permute-start | bytes 73736 | tf_op jit(solution)/shard_map/ppermute | solution.py:334
  5.5 2.7 %collective-permute-start.2 = (bf16[96,128]{1,0:T(8,128)(2,1)S(1)}, bf16[96,128]{1,0:T(8,128)(2,1)S(1)}, u32[]{:S(2)}, u32[]{:S(2)}) collective-permute-start(bf16[96,128]{1,0:T(8,128)(2,1)S(1)} %get-tuple-element.40), channel_id=1, source_target_pairs={{0,8},{2,10},{4,12},{6,14},{8,0},{10,2},{12,4},{14,6},{16,24},{18,... | collective-permute-start | bytes 73736 | tf_op jit(solution)/shard_map/ppermute | solution.py:334
  8.3 1.4 %collective-permute-start.3 = (bf16[96,128]{1,0:T(8,128)(2,1)S(1)}, bf16[96,128]{1,0:T(8,128)(2,1)S(1)}, u32[]{:S(2)}, u32[]{:S(2)}) collective-permute-start(bf16[96,128]{1,0:T(8,128)(2,1)S(1)} %get-tuple-element.41), channel_id=1, source_target_pairs={{0,12},{2,14},{4,0},{6,2},{8,4},{10,6},{12,8},{14,10},{16,28},{18,... | collective-permute-start | bytes 73736 | tf_op jit(solution)/shard_map/ppermute | solution.py:334
  9.7 0.7 copy-done.2
  11.1 1.0 %collective-permute-done.3.refs_3_ = bf16[96,128]{1,0:T(8,128)(2,1)S(1)} collective-permute-done((bf16[96,128]{1,0:T(8,128)(2,1)S(1)}, bf16[96,128]{1,0:T(8,128)(2,1)S(1)}, u32[]{:S(2)}, u32[]{:S(2)}) %collective-permute-start.3) | collective-permute-done | bytes 24608 | tf_op jit(solution)/shard_map/ppermute | solution.py:334
  12.1 3.3 %collective-permute-start.6 = (bf16[336,128]{1,0:T(8,128)(2,1)S(1)}, bf16[336,128]{1,0:T(8,128)(2,1)S(1)}, u32[]{:S(2)}, u32[]{:S(2)}) collective-permute-start(bf16[336,128]{1,0:T(8,128)(2,1)S(1)} %shard_map.81.refs_0_), channel_id=1, source_target_pairs={{0,64},{2,66},{4,68},{6,70},{8,72},{10,74},{12,76},{14,78},{16,80}... | collective-permute-start | bytes 258056 | tf_op jit(solution)/shard_map/ppermute | solution.py:334
  15.5 2.2 %collective-permute-start.5 = (bf16[336,128]{1,0:T(8,128)(2,1)S(1)}, bf16[336,128]{1,0:T(8,128)(2,1)S(1)}, u32[]{:S(2)}, u32[]{:S(2)}) collective-permute-start(bf16[336,128]{1,0:T(8,128)(2,1)S(1)} %shard_map.81.refs_0_), channel_id=1, source_target_pairs={{0,192},{2,194},{4,196},{6,198},{8,200},{10,202},{12,204},{14,206}... | collective-permute-start | bytes 258056 | tf_op jit(solution)/shard_map/ppermute | solution.py:334
  17.7 4.9 %collective-permute-start.4 = (bf16[336,128]{1,0:T(8,128)(2,1)S(1)}, bf16[336,128]{1,0:T(8,128)(2,1)S(1)}, u32[]{:S(2)}, u32[]{:S(2)}) collective-permute-start(bf16[336,128]{1,0:T(8,128)(2,1)S(1)} %shard_map.81.refs_0_), channel_id=1, source_target_pairs={{0,128},{2,130},{4,132},{6,134},{8,136},{10,138},{12,140},{14,142}... | collective-permute-start | bytes 258056 | tf_op jit(solution)/shard_map/ppermute | solution.py:334
  22.6 1.9 %shard_map.82.query_ref = bf16[1280,1280]{1,0:T(8,128)(2,1)S(1)} custom-call(bf16[1280,1280]{1,0:T(8,128)(2,1)} %source_hbm), custom_call_target="tpu_custom_call" | custom-call | flops 1 | bytes 1 | tf_op jit(solution)/shard_map/pallas_call | solution.py:318
  24.6 2.9 %shard_map.83.pair_ref = bf16[1280,2560]{1,0:T(8,128)(2,1)S(1)} custom-call(bf16[1280,2560]{1,0:T(8,128)(2,1)} %source_hbm.1), custom_call_target="tpu_custom_call" | custom-call | flops 1 | bytes 1 | tf_op jit(solution)/shard_map/pallas_call | solution.py:318
  27.5 1.2 %collective-permute-done.4.refs_1_ = bf16[336,128]{1,0:T(8,128)(2,1)S(1)} collective-permute-done((bf16[336,128]{1,0:T(8,128)(2,1)S(1)}, bf16[336,128]{1,0:T(8,128)(2,1)S(1)}, u32[]{:S(2)}, u32[]{:S(2)}) %collective-permute-start.4) | collective-permute-done | bytes 86048 | tf_op jit(solution)/shard_map/ppermute | solution.py:334
  28.7 3.1 %collective-permute-start.9 = (f32[8,128]{1,0:T(8,128)S(1)}, f32[8,128]{1,0:T(8,128)S(1)}, u32[]{:S(2)}, u32[]{:S(2)}) collective-permute-start(f32[8,128]{1,0:T(8,128)S(1)} %shard_map.84.s0.stats_ref), channel_id=1, source_target_pairs={{0,48},{2,50},{4,52},{6,54},{8,56},{10,58},{12,60},{14,62},{16,0},... | collective-permute-start | bytes 12296 | tf_op jit(solution)/shard_map/ppermute | solution.py:334
  32.4 1.0 %collective-permute-start.7 = (f32[8,128]{1,0:T(8,128)S(1)}, f32[8,128]{1,0:T(8,128)S(1)}, u32[]{:S(2)}, u32[]{:S(2)}) collective-permute-start(f32[8,128]{1,0:T(8,128)S(1)} %shard_map.84.s0.stats_ref), channel_id=1, source_target_pairs={{0,16},{2,18},{4,20},{6,22},{8,24},{10,26},{12,28},{14,30},{16,32}... | collective-permute-start | bytes 12296 | tf_op jit(solution)/shard_map/ppermute | solution.py:334
  33.4 2.3 %collective-permute-start.11 = (bf16[1280,128]{1,0:T(8,128)(2,1)S(1)}, bf16[1280,128]{1,0:T(8,128)(2,1)S(1)}, u32[]{:S(2)}, u32[]{:S(2)}) collective-permute-start(bf16[1280,128]{1,0:T(8,128)(2,1)S(1)} %shard_map.86.refs_1_.refs_2_), channel_id=1, source_target_pairs={{0,48},{2,50},{4,52},{6,54},{8,56},{10,58},{12,60},{14,62},{16,0},... | collective-permute-start | bytes 983048 | tf_op jit(solution)/shard_map/ppermute | solution.py:334
  35.7 1.2 %collective-permute-done.8.s2 = f32[8,128]{1,0:T(8,128)S(1)} collective-permute-done((f32[8,128]{1,0:T(8,128)S(1)}, f32[8,128]{1,0:T(8,128)S(1)}, u32[]{:S(2)}, u32[]{:S(2)}) %collective-permute-start.8) | collective-permute-done | bytes 4128 | tf_op jit(solution)/shard_map/ppermute | solution.py:334
  37.3 1.7 %collective-permute-start.12 = (bf16[1280,128]{1,0:T(8,128)(2,1)S(1)}, bf16[1280,128]{1,0:T(8,128)(2,1)S(1)}, u32[]{:S(2)}, u32[]{:S(2)}) collective-permute-start(bf16[1280,128]{1,0:T(8,128)(2,1)S(1)} %shard_map.86.refs_1_.refs_2_), channel_id=1, source_target_pairs={{0,32},{2,34},{4,36},{6,38},{8,40},{10,42},{12,44},{14,46},{16,48}... | collective-permute-start | bytes 983048 | tf_op jit(solution)/shard_map/ppermute | solution.py:334
  39.0 3.0 %shard_map.85 = (bf16[720,128]{1,0:T(8,128)(2,1)S(1)}, bf16[720,128]{1,0:T(8,128)(2,1)S(1)}, bf16[720,128]{1,0:T(8,128)(2,1)S(1)}, bf16[720,128]{1,0:T(8,128)(2,1)S(1)}, bf16[16,2560]{1,0:T(8,128)(2,1)}) custom-call(s32[1]{0:T(128)} %bitcast.place_ref, bf16[256,1280]{1,0:T(8,128)(2,1)S(1)} %get-tuple-element.36.tokens_ref, ...), custom_call_target="tpu_custom_call" | custom-call | flops 1 | bytes 1 | tf_op jit(solution)/shard_map/pallas_call | solution.py:318
  42.2 3.6 %collective-permute-start.18 = (bf16[720,128]{1,0:T(8,128)(2,1)S(1)}, bf16[720,128]{1,0:T(8,128)(2,1)S(1)}, u32[]{:S(2)}, u32[]{:S(2)}) collective-permute-start(bf16[720,128]{1,0:T(8,128)(2,1)S(1)} %get-tuple-element.64), channel_id=1, source_target_pairs={{0,8},{2,10},{4,12},{6,14},{8,0},{10,2},{12,4},{14,6},{16,24},{18,... | collective-permute-start | bytes 552968 | tf_op jit(solution)/shard_map/ppermute | solution.py:334
  45.8 2.9 %collective-permute-done.13.refs_1_ = bf16[720,128]{1,0:T(8,128)(2,1)S(1)} collective-permute-done((bf16[720,128]{1,0:T(8,128)(2,1)S(1)}, bf16[720,128]{1,0:T(8,128)(2,1)S(1)}, u32[]{:S(2)}, u32[]{:S(2)}) %collective-permute-start.13) | collective-permute-done | bytes 184352 | tf_op jit(solution)/shard_map/ppermute | solution.py:334
  49.2 0.8 %collective-permute-done.10.refs_2_.refs_3_ = bf16[1280,128]{1,0:T(8,128)(2,1)S(1)} collective-permute-done((bf16[1280,128]{1,0:T(8,128)(2,1)S(1)}, bf16[1280,128]{1,0:T(8,128)(2,1)S(1)}, u32[]{:S(2)}, u32[]{:S(2)}) %collective-permute-start.10) | collective-permute-done | bytes 327712 | tf_op jit(solution)/shard_map/ppermute | solution.py:334
  50.5 0.8 %collective-permute-done.18.refs_0_ = bf16[720,128]{1,0:T(8,128)(2,1)S(1)} collective-permute-done((bf16[720,128]{1,0:T(8,128)(2,1)S(1)}, bf16[720,128]{1,0:T(8,128)(2,1)S(1)}, u32[]{:S(2)}, u32[]{:S(2)}) %collective-permute-start.18) | collective-permute-done | bytes 184352 | tf_op jit(solution)/shard_map/ppermute | solution.py:334
  51.3 1.4 %collective-permute-start.21 = (bf16[720,128]{1,0:T(8,128)(2,1)S(1)}, bf16[720,128]{1,0:T(8,128)(2,1)S(1)}, u32[]{:S(2)}, u32[]{:S(2)}) collective-permute-start(bf16[720,128]{1,0:T(8,128)(2,1)S(1)} %get-tuple-element.68), channel_id=1, source_target_pairs={{0,12},{2,14},{4,0},{6,2},{8,4},{10,6},{12,8},{14,10},{16,28},{18,... | collective-permute-start | bytes 552968 | tf_op jit(solution)/shard_map/ppermute | solution.py:334
  52.7 6.5 %shard_map.88 = (bf16[640,128]{1,0:T(8,128)(2,1)S(1)}, bf16[640,128]{1,0:T(8,128)(2,1)S(1)}) custom-call(s32[1]{0:T(128)} %bitcast.place_ref, bf16[720,128]{1,0:T(8,128)(2,1)S(1)} %collective-permute-done.18.refs_0_, bf16[720,128]{1,0:T(8,128)(2,1)S(1)} %collective-permute-done.13.refs_1_, bf16[1280,128]{1,0:T(8,128)(2,1)S(1)} %shard_map.86.refs_1_.refs_2_, ...), custom_call_target="tpu_custom_call" | custom-call | flops 1 | bytes 1 | tf_op jit(solution)/shard_map/pallas_call | solution.py:318
  59.2 1.6 %collective-permute-start.19 = (bf16[640,128]{1,0:T(8,128)(2,1)S(1)}, bf16[640,128]{1,0:T(8,128)(2,1)S(1)}, u32[]{:S(2)}, u32[]{:S(2)}) collective-permute-start(bf16[640,128]{1,0:T(8,128)(2,1)S(1)} %get-tuple-element.65), channel_id=1, source_target_pairs={{0,12},{2,14},{4,0},{6,2},{8,4},{10,6},{12,8},{14,10},{16,28},{18,... | collective-permute-start | bytes 491528 | tf_op jit(solution)/shard_map/ppermute | solution.py:334
  60.9 1.2 %collective-permute-start.20 = (bf16[640,128]{1,0:T(8,128)(2,1)S(1)}, bf16[640,128]{1,0:T(8,128)(2,1)S(1)}, u32[]{:S(2)}, u32[]{:S(2)}) collective-permute-start(bf16[640,128]{1,0:T(8,128)(2,1)S(1)} %get-tuple-element.66), channel_id=1, source_target_pairs={{0,8},{2,10},{4,12},{6,14},{8,0},{10,2},{12,4},{14,6},{16,24},{18,... | collective-permute-start | bytes 491528 | tf_op jit(solution)/shard_map/ppermute | solution.py:334
  62.1 3.5 %shard_map.89 = bf16[640,128]{1,0:T(8,128)(2,1)S(1)} custom-call(s32[1]{0:T(128)} %bitcast.place_ref, bf16[720,128]{1,0:T(8,128)(2,1)S(1)} %collective-permute-done.21.refs_0_, bf16[1280,128]{1,0:T(8,128)(2,1)S(1)} %shard_map.86.refs_1_.refs_2_, bf16[1280,128]{1,0:T(8,128)(2,1)S(1)} %collective-permute-done.10.refs_2_.refs_3_, ...), custom_call_target="tpu_custom_call" | custom-call | flops 1 | bytes 1 | tf_op jit(solution)/shard_map/pallas_call | solution.py:318
  65.6 3.5 %shard_map.87.refs_0_ = bf16[640,128]{1,0:T(8,128)(2,1)S(1)} custom-call(s32[1]{0:T(128)} %bitcast.place_ref, bf16[720,128]{1,0:T(8,128)(2,1)S(1)} %get-tuple-element.57.refs_0_, bf16[1280,128]{1,0:T(8,128)(2,1)S(1)} %shard_map.86.refs_1_.refs_2_, bf16[1280,128]{1,0:T(8,128)(2,1)S(1)} %collective-permute-done.10.refs_2_.refs_3_, ...), custom_call_target="tpu_custom_call" | custom-call | flops 1 | bytes 1 | tf_op jit(solution)/shard_map/pallas_call | solution.py:318
  69.1 3.0 %collective-permute-done.22.refs_3_ = bf16[640,128]{1,0:T(8,128)(2,1)S(1)} collective-permute-done((bf16[640,128]{1,0:T(8,128)(2,1)S(1)}, bf16[640,128]{1,0:T(8,128)(2,1)S(1)}, u32[]{:S(2)}, u32[]{:S(2)}) %collective-permute-start.22) | collective-permute-done | bytes 163872 | tf_op jit(solution)/shard_map/ppermute | solution.py:334
  72.1 1.0 %shard_map.90 = bf16[256,1280]{1,0:T(8,128)(2,1)} custom-call(s32[1]{0:T(128)} %bitcast.place_ref, bf16[640,128]{1,0:T(8,128)(2,1)S(1)} %shard_map.87.refs_0_, bf16[640,128]{1,0:T(8,128)(2,1)S(1)} %collective-permute-done.19.refs_1_, bf16[640,128]{1,0:T(8,128)(2,1)S(1)} %collective-permute-done.20.refs_2_, bf16[640,128]{1,0:T(8,128)(2,1)S(1)} %collective-permute-done.22.refs_3_), custom_call_target="tpu_custom_call" | custom-call | flops 1 | bytes 1 | tf_op jit(solution)/shard_map/pallas_call | solution.py:318
  (36 shorter events, 3.5 us)
Async XLA Ops:
  0.6 1.1 %copy-start = (bf16[1,256,1280]{2,1,0:T(8,128)(2,1)S(1)}, bf16[1,256,1280]{2,1,0:T(8,128)(2,1)}, u32[]{:S(2)}) copy-start(bf16[1,256,1280]{2,1,0:T(8,128)(2,1)} %param.6) | copy-start | bytes 1966084
  2.7 1.2 %collective-permute-start = (f32[8,128]{1,0:T(8,128)S(1)}, f32[8,128]{1,0:T(8,128)S(1)}, u32[]{:S(2)}, u32[]{:S(2)}) collective-permute-start(f32[8,128]{1,0:T(8,128)S(1)} %get-tuple-element.37.stats_ref.own_ref), channel_id=1, source_target_pairs={{0,2},{2,0},{4,6},{6,4},{8,10},{10,8},{12,14},{14,12},{16,18},{18,... | collective-permute-start | bytes 12296 | tf_op jit(solution)/shard_map/ppermute | solution.py:334
  2.8 0.9 %copy-start.1 = (bf16[1,16,2560]{2,1,0:T(8,128)(2,1)S(1)}, bf16[1,16,2560]{2,1,0:T(8,128)(2,1)}, u32[]{:S(2)}) copy-start(bf16[1,16,2560]{2,1,0:T(8,128)(2,1)} %param.7) | copy-start | bytes 245764
  4.0 7.1 %collective-permute-start.1 = (bf16[96,128]{1,0:T(8,128)(2,1)S(1)}, bf16[96,128]{1,0:T(8,128)(2,1)S(1)}, u32[]{:S(2)}, u32[]{:S(2)}) collective-permute-start(bf16[96,128]{1,0:T(8,128)(2,1)S(1)} %get-tuple-element.39), channel_id=1, source_target_pairs={{0,4},{2,6},{4,8},{6,10},{8,12},{10,14},{12,0},{14,2},{16,20},{18,... | collective-permute-start | bytes 73736 | tf_op jit(solution)/shard_map/ppermute | solution.py:334
  5.5 5.6 %collective-permute-start.2 = (bf16[96,128]{1,0:T(8,128)(2,1)S(1)}, bf16[96,128]{1,0:T(8,128)(2,1)S(1)}, u32[]{:S(2)}, u32[]{:S(2)}) collective-permute-start(bf16[96,128]{1,0:T(8,128)(2,1)S(1)} %get-tuple-element.40), channel_id=1, source_target_pairs={{0,8},{2,10},{4,12},{6,14},{8,0},{10,2},{12,4},{14,6},{16,24},{18,... | collective-permute-start | bytes 73736 | tf_op jit(solution)/shard_map/ppermute | solution.py:334
  8.3 3.8 %collective-permute-start.3 = (bf16[96,128]{1,0:T(8,128)(2,1)S(1)}, bf16[96,128]{1,0:T(8,128)(2,1)S(1)}, u32[]{:S(2)}, u32[]{:S(2)}) collective-permute-start(bf16[96,128]{1,0:T(8,128)(2,1)S(1)} %get-tuple-element.41), channel_id=1, source_target_pairs={{0,12},{2,14},{4,0},{6,2},{8,4},{10,6},{12,8},{14,10},{16,28},{18,... | collective-permute-start | bytes 73736 | tf_op jit(solution)/shard_map/ppermute | solution.py:334
  9.7 0.7 copy-start.2
  10.4 0.7 copy-start.3
  12.1 15.3 %collective-permute-start.6 = (bf16[336,128]{1,0:T(8,128)(2,1)S(1)}, bf16[336,128]{1,0:T(8,128)(2,1)S(1)}, u32[]{:S(2)}, u32[]{:S(2)}) collective-permute-start(bf16[336,128]{1,0:T(8,128)(2,1)S(1)} %shard_map.81.refs_0_), channel_id=1, source_target_pairs={{0,64},{2,66},{4,68},{6,70},{8,72},{10,74},{12,76},{14,78},{16,80}... | collective-permute-start | bytes 258056 | tf_op jit(solution)/shard_map/ppermute | solution.py:334
  15.5 12.0 %collective-permute-start.5 = (bf16[336,128]{1,0:T(8,128)(2,1)S(1)}, bf16[336,128]{1,0:T(8,128)(2,1)S(1)}, u32[]{:S(2)}, u32[]{:S(2)}) collective-permute-start(bf16[336,128]{1,0:T(8,128)(2,1)S(1)} %shard_map.81.refs_0_), channel_id=1, source_target_pairs={{0,192},{2,194},{4,196},{6,198},{8,200},{10,202},{12,204},{14,206}... | collective-permute-start | bytes 258056 | tf_op jit(solution)/shard_map/ppermute | solution.py:334
  17.7 10.9 %collective-permute-start.4 = (bf16[336,128]{1,0:T(8,128)(2,1)S(1)}, bf16[336,128]{1,0:T(8,128)(2,1)S(1)}, u32[]{:S(2)}, u32[]{:S(2)}) collective-permute-start(bf16[336,128]{1,0:T(8,128)(2,1)S(1)} %shard_map.81.refs_0_), channel_id=1, source_target_pairs={{0,128},{2,130},{4,132},{6,134},{8,136},{10,138},{12,140},{14,142}... | collective-permute-start | bytes 258056 | tf_op jit(solution)/shard_map/ppermute | solution.py:334
  28.7 7.1 %collective-permute-start.9 = (f32[8,128]{1,0:T(8,128)S(1)}, f32[8,128]{1,0:T(8,128)S(1)}, u32[]{:S(2)}, u32[]{:S(2)}) collective-permute-start(f32[8,128]{1,0:T(8,128)S(1)} %shard_map.84.s0.stats_ref), channel_id=1, source_target_pairs={{0,48},{2,50},{4,52},{6,54},{8,56},{10,58},{12,60},{14,62},{16,0},... | collective-permute-start | bytes 12296 | tf_op jit(solution)/shard_map/ppermute | solution.py:334
  31.7 5.2 %collective-permute-start.8 = (f32[8,128]{1,0:T(8,128)S(1)}, f32[8,128]{1,0:T(8,128)S(1)}, u32[]{:S(2)}, u32[]{:S(2)}) collective-permute-start(f32[8,128]{1,0:T(8,128)S(1)} %shard_map.84.s0.stats_ref), channel_id=1, source_target_pairs={{0,32},{2,34},{4,36},{6,38},{8,40},{10,42},{12,44},{14,46},{16,48}... | collective-permute-start | bytes 12296 | tf_op jit(solution)/shard_map/ppermute | solution.py:334
  32.4 4.9 %collective-permute-start.7 = (f32[8,128]{1,0:T(8,128)S(1)}, f32[8,128]{1,0:T(8,128)S(1)}, u32[]{:S(2)}, u32[]{:S(2)}) collective-permute-start(f32[8,128]{1,0:T(8,128)S(1)} %shard_map.84.s0.stats_ref), channel_id=1, source_target_pairs={{0,16},{2,18},{4,20},{6,22},{8,24},{10,26},{12,28},{14,30},{16,32}... | collective-permute-start | bytes 12296 | tf_op jit(solution)/shard_map/ppermute | solution.py:334
  33.4 15.3 %collective-permute-start.11 = (bf16[1280,128]{1,0:T(8,128)(2,1)S(1)}, bf16[1280,128]{1,0:T(8,128)(2,1)S(1)}, u32[]{:S(2)}, u32[]{:S(2)}) collective-permute-start(bf16[1280,128]{1,0:T(8,128)(2,1)S(1)} %shard_map.86.refs_1_.refs_2_), channel_id=1, source_target_pairs={{0,48},{2,50},{4,52},{6,54},{8,56},{10,58},{12,60},{14,62},{16,0},... | collective-permute-start | bytes 983048 | tf_op jit(solution)/shard_map/ppermute | solution.py:334
  35.7 14.3 %collective-permute-start.10 = (bf16[1280,128]{1,0:T(8,128)(2,1)S(1)}, bf16[1280,128]{1,0:T(8,128)(2,1)S(1)}, u32[]{:S(2)}, u32[]{:S(2)}) collective-permute-start(bf16[1280,128]{1,0:T(8,128)(2,1)S(1)} %shard_map.86.refs_1_.refs_2_), channel_id=1, source_target_pairs={{0,16},{2,18},{4,20},{6,22},{8,24},{10,26},{12,28},{14,30},{16,32}... | collective-permute-start | bytes 983048 | tf_op jit(solution)/shard_map/ppermute | solution.py:334
  37.3 12.8 %collective-permute-start.12 = (bf16[1280,128]{1,0:T(8,128)(2,1)S(1)}, bf16[1280,128]{1,0:T(8,128)(2,1)S(1)}, u32[]{:S(2)}, u32[]{:S(2)}) collective-permute-start(bf16[1280,128]{1,0:T(8,128)(2,1)S(1)} %shard_map.86.refs_1_.refs_2_), channel_id=1, source_target_pairs={{0,32},{2,34},{4,36},{6,38},{8,40},{10,42},{12,44},{14,46},{16,48}... | collective-permute-start | bytes 983048 | tf_op jit(solution)/shard_map/ppermute | solution.py:334
  41.9 6.7 %collective-permute-start.13 = (bf16[720,128]{1,0:T(8,128)(2,1)S(1)}, bf16[720,128]{1,0:T(8,128)(2,1)S(1)}, u32[]{:S(2)}, u32[]{:S(2)}) collective-permute-start(bf16[720,128]{1,0:T(8,128)(2,1)S(1)} %get-tuple-element.59), channel_id=1, source_target_pairs={{0,4},{2,6},{4,8},{6,10},{8,12},{10,14},{12,0},{14,2},{16,20},{18,... | collective-permute-start | bytes 552968 | tf_op jit(solution)/shard_map/ppermute | solution.py:334
  42.2 9.1 %collective-permute-start.18 = (bf16[720,128]{1,0:T(8,128)(2,1)S(1)}, bf16[720,128]{1,0:T(8,128)(2,1)S(1)}, u32[]{:S(2)}, u32[]{:S(2)}) collective-permute-start(bf16[720,128]{1,0:T(8,128)(2,1)S(1)} %get-tuple-element.64), channel_id=1, source_target_pairs={{0,8},{2,10},{4,12},{6,14},{8,0},{10,2},{12,4},{14,6},{16,24},{18,... | collective-permute-start | bytes 552968 | tf_op jit(solution)/shard_map/ppermute | solution.py:334
  48.7 4.0 %collective-permute-start.14 = (bf16[1280,128]{1,0:T(8,128)(2,1)S(1)}, bf16[1280,128]{1,0:T(8,128)(2,1)S(1)}, u32[]{:S(2)}, u32[]{:S(2)}) collective-permute-start(bf16[1280,128]{1,0:T(8,128)(2,1)S(1)} %shard_map.86.refs_1_.refs_2_), channel_id=1, source_target_pairs={{0,2},{2,0},{4,6},{6,4},{8,10},{10,8},{12,14},{14,12},{16,18},{18,... | collective-permute-start | bytes 983048 | tf_op jit(solution)/shard_map/ppermute | solution.py:334
  48.7 4.0 %collective-permute-start.16 = (bf16[1280,128]{1,0:T(8,128)(2,1)S(1)}, bf16[1280,128]{1,0:T(8,128)(2,1)S(1)}, u32[]{:S(2)}, u32[]{:S(2)}) collective-permute-start(bf16[1280,128]{1,0:T(8,128)(2,1)S(1)} %collective-permute-done.11.refs_3_.refs_4_), channel_id=1, source_target_pairs={{0,2},{2,0},{4,6},{6,4},{8,10},{10,8},{12,14},{14,12},{16,18},{18,... | collective-permute-start | bytes 983048 | tf_op jit(solution)/shard_map/ppermute | solution.py:334
  50.0 2.7 %collective-permute-start.15 = (bf16[1280,128]{1,0:T(8,128)(2,1)S(1)}, bf16[1280,128]{1,0:T(8,128)(2,1)S(1)}, u32[]{:S(2)}, u32[]{:S(2)}) collective-permute-start(bf16[1280,128]{1,0:T(8,128)(2,1)S(1)} %collective-permute-done.10.refs_2_.refs_3_), channel_id=1, source_target_pairs={{0,2},{2,0},{4,6},{6,4},{8,10},{10,8},{12,14},{14,12},{16,18},{18,... | collective-permute-start | bytes 983048 | tf_op jit(solution)/shard_map/ppermute | solution.py:334
  50.0 2.7 %collective-permute-start.17 = (bf16[1280,128]{1,0:T(8,128)(2,1)S(1)}, bf16[1280,128]{1,0:T(8,128)(2,1)S(1)}, u32[]{:S(2)}, u32[]{:S(2)}) collective-permute-start(bf16[1280,128]{1,0:T(8,128)(2,1)S(1)} %collective-permute-done.12.refs_4_.refs_5_), channel_id=1, source_target_pairs={{0,2},{2,0},{4,6},{6,4},{8,10},{10,8},{12,14},{14,12},{16,18},{18,... | collective-permute-start | bytes 983048 | tf_op jit(solution)/shard_map/ppermute | solution.py:334
  51.3 10.7 %collective-permute-start.21 = (bf16[720,128]{1,0:T(8,128)(2,1)S(1)}, bf16[720,128]{1,0:T(8,128)(2,1)S(1)}, u32[]{:S(2)}, u32[]{:S(2)}) collective-permute-start(bf16[720,128]{1,0:T(8,128)(2,1)S(1)} %get-tuple-element.68), channel_id=1, source_target_pairs={{0,12},{2,14},{4,0},{6,2},{8,4},{10,6},{12,8},{14,10},{16,28},{18,... | collective-permute-start | bytes 552968 | tf_op jit(solution)/shard_map/ppermute | solution.py:334
  59.2 9.9 %collective-permute-start.19 = (bf16[640,128]{1,0:T(8,128)(2,1)S(1)}, bf16[640,128]{1,0:T(8,128)(2,1)S(1)}, u32[]{:S(2)}, u32[]{:S(2)}) collective-permute-start(bf16[640,128]{1,0:T(8,128)(2,1)S(1)} %get-tuple-element.65), channel_id=1, source_target_pairs={{0,12},{2,14},{4,0},{6,2},{8,4},{10,6},{12,8},{14,10},{16,28},{18,... | collective-permute-start | bytes 491528 | tf_op jit(solution)/shard_map/ppermute | solution.py:334
  60.9 8.2 %collective-permute-start.20 = (bf16[640,128]{1,0:T(8,128)(2,1)S(1)}, bf16[640,128]{1,0:T(8,128)(2,1)S(1)}, u32[]{:S(2)}, u32[]{:S(2)}) collective-permute-start(bf16[640,128]{1,0:T(8,128)(2,1)S(1)} %get-tuple-element.66), channel_id=1, source_target_pairs={{0,8},{2,10},{4,12},{6,14},{8,0},{10,2},{12,4},{14,6},{16,24},{18,... | collective-permute-start | bytes 491528 | tf_op jit(solution)/shard_map/ppermute | solution.py:334
  65.5 6.6 %collective-permute-start.22 = (bf16[640,128]{1,0:T(8,128)(2,1)S(1)}, bf16[640,128]{1,0:T(8,128)(2,1)S(1)}, u32[]{:S(2)}, u32[]{:S(2)}) collective-permute-start(bf16[640,128]{1,0:T(8,128)(2,1)S(1)} %shard_map.89), channel_id=1, source_target_pairs={{0,4},{2,6},{4,8},{6,10},{8,12},{10,14},{12,0},{14,2},{16,20},{18,... | collective-permute-start | bytes 491528 | tf_op jit(solution)/shard_map/ppermute | solution.py:334

commit v6 on v5

--- a/solution.py
+++ b/solution.py
@@ -30,6 +30,10 @@
 
 def iota(shape, axis):
     return lax.broadcasted_iota(jnp.int32, shape, axis)
+
+
+def x_place(place_ref):
+    return lax.bitwise_and(lax.shift_right_logical(place_ref[0], 1), 3)
 
 
 def group_of_channel():
@@ -138,7 +142,7 @@
 def x_kernel(place_ref, own_ref, other_ref, sets_ref, *out_refs):
     mean, squares = combine([own_ref[...], other_ref[...]], CELLS * GROUP_WIDTH)
     coded = split_rows(mean, squares)
-    place = place_ref[0]
+    place = x_place(place_ref)
     for k, out_ref in enumerate(out_refs):
         out_ref[0:SET_ROWS, :] = sets_ref[lax.rem(place + k, 4)]
         out_ref[SET_ROWS:, :] = coded
@@ -167,6 +171,11 @@
     stats_ref[...] = stack_stats(mean, squares)
 
 
+def all_stats_kernel(s0, s1, s2, s3, stats_ref):
+    mean, squares = combine([s0[...], s1[...], s2[...], s3[...]], 32 * CELLS * GROUP_WIDTH)
+    stats_ref[...] = stack_stats(mean, squares)
+
+
 def piece_kernel(stats_ref, *refs):
     *in_refs, out_ref = refs
     for k, ref in enumerate(in_refs):
@@ -182,10 +191,11 @@
 
 
 def project_kernel(
-    place_ref, tokens_ref, s0, s1, s2, s3, affine_ref, query_ref, pair_ref, *refs
+    place_ref, tokens_ref, own_ref, other_ref, affine_ref, query_ref, pair_ref, *refs
 ):
     *message_refs, fresh_ref, sets_ref, last_ref = refs
-    mean, squares = combine([s0[...], s1[...], s2[...], s3[...]], 32 * CELLS * GROUP_WIDTH)
+    stats = jnp.where(lax.bitwise_and(place_ref[0], 1) == 1, own_ref[...], other_ref[...])
+    mean, squares = stats[0:1], stats[1:2]
     spread = squares / (128 * CELLS * GROUP_WIDTH)
     center, inverse = select_dot(channel_of_group(), mean, lax.rsqrt(spread + epsilon))
     scaled = (tokens_ref[...].astype(f32) - center) * inverse
@@ -197,7 +207,7 @@
     pool = jnp.where(cell_square == square, 1.0 / (POOL * POOL), 0.0).astype(bf16)
     pooled = jnp.dot(pool, normed, preferred_element_type=f32).astype(bf16)
 
-    place = place_ref[0]
+    place = x_place(place_ref)
     last = jnp.dot(normed, query_ref[:, 1024:], preferred_element_type=f32).astype(bf16)
     last_ref[0] = last[:, 0:LANES]
     last_ref[1] = last[:, LANES:]
@@ -233,7 +243,7 @@
             first_ref[low : low + ROWS, :] = fresh
     lane = iota((CELLS, LANES), 1)
     low_half = lane < HEAD_DIM
-    parity = lax.bitwise_and(place_ref[0], 1)
+    parity = lax.bitwise_and(x_place(place_ref), 1)
     factor = HEAD_DIM ** (-0.5) * 1.4426950408889634
     against = (((1,), (1,)), ((), ()))
     ones = jnp.ones((CELLS, LANES), bf16)
@@ -300,7 +310,7 @@
 
 def assemble_kernel(place_ref, *refs):
     *in_refs, out_ref, sets_ref = refs
-    place = place_ref[0]
+    place = x_place(place_ref)
     for k, ref in enumerate(in_refs):
         sets_ref[lax.rem(place + k, 4)] = ref[...]
     for j in range(4):
@@ -326,19 +336,17 @@
     )(*args)
 
 
-def permute(array, place):
+AXES = {"z": (32, 4), "y": (8, 4), "x": (2, 4), "core": (1, 2)}
+
+
+def shift(array, axis, step, cores=(0, 1)):
+    stride, size = AXES[axis]
     pairs = []
     for source in range(128):
-        z, y, x, core = place(source // 32, source // 8 % 4, source // 2 % 4, source % 2)
-        pairs.append((source, z % 4 * 32 + y % 4 * 8 + x % 4 * 2 + core % 2))
+        place = source // stride % size
+        if source % 2 in cores:
+            pairs.append((source, source + ((place + step) % size - place) * stride))
     return lax.ppermute(array, "patch", pairs)
-
-
-def shift(array, axis, step):
-    def place(*places):
-        return [at + step * (name == axis) for at, name in zip(places, ("z", "y", "x", "core"))]
-
-    return permute(array, place)
 
 
 def after(array, *others):
@@ -346,7 +354,7 @@
 
 
 def per_device(tokens, stale_keys, norm_gain, norm_bias, query_weight, pair_weight):
-    place = (lax.axis_index("patch") // 2 % 4).astype(jnp.int32).reshape(1)
+    place = lax.axis_index("patch").astype(jnp.int32).reshape(1)
     table = ((SET_HEADS * CELLS, LANES), bf16)
     answer = ((ANSWER_ROWS, LANES), bf16)
     stats, tokens = call(
@@ -389,17 +397,19 @@
     weights = weights[1::-1]
     parts, weights = lax.optimization_barrier((parts, weights))
     (stats,) = call(stats_kernel, [VMEM] * 4, [((8, LANES), f32)], *parts)
-    all_stats = [stats] + [shift(stats, "y", k) for k in (1, 2, 3)]
+    y_stats = [stats] + [shift(stats, "y", k, cores=(1,)) for k in (1, 2, 3)]
     (piece,) = call(piece_kernel, [VMEM] * 5, [table], stats, *parts)
     pieces = [piece, shift(piece, "y", 1), shift(piece, "y", 3)]
-    pieces.append(shift(after(piece, *all_stats), "y", 2))
+    (stats,) = call(all_stats_kernel, [VMEM] * 4, [((8, LANES), f32)], *y_stats)
+    pieces.append(shift(after(piece, stats), "y", 2))
+    both_stats = [stats, shift(stats, "core", 1, cores=(1,))]
     *queries, fresh = call(
         project_kernel,
-        [SMEM] + [VMEM] * 8,
+        [SMEM] + [VMEM] * 6,
         [((ANSWER_ROWS + SET_ROWS, LANES), bf16)] * 4 + [((ROWS, 2 * WIDTH), bf16)],
         place,
         tokens,
-        *all_stats,
+        *both_stats,
         affine,
         *weights,
         scratch=[

time: 73.5 us -> 79.9 us (1.087)
  waiting for transfers between devices: 11.3 us -> 18 us
    ppermute x23 -> x24, waiting for transfers between devices: 11.3 us -> 18 us  [shift(): return lax.ppermute(array, 'patch', pairs)]
    ppermute x23 -> x24, starting transfers between devices: 34.2 us -> 33.8 us  [shift(): return lax.ppermute(array, 'patch', pairs)]
    pallas_call x14 -> x15, Pallas kernels: 23.4 us -> 23.4 us  [call(): pl.pallas_call(kernel, in_specs=ins, out_specs=[VMEM] * len(outs), out_sh...]
  transfers between devices with their start and end apart: 23 -> 24, of which waited for: 9 -> 7; matrix products, arithmetic and copies ran while one was open for 0% -> 0% of each run, Pallas kernels for 29% -> 27%
where the time goes in v6:
time: 79.9 us; the launch traced here: 79.4 us
  starting transfers between devices  33.8 us (42%)
  Pallas kernels  23.4 us (29%)
  waiting for transfers between devices  18 us (23%)
  local copies, waits for them, and re-layouts  3.36 us (4%)
  between operations  0.84 us (1%)
    ppermute x24, starting transfers between devices, shift(): return lax.ppermute(array, 'patch', pairs)  33.8 us
    pallas_call x15, Pallas kernels, call(): pl.pallas_call(kernel, in_specs=ins, out_specs=[VMEM] * len(outs), out_sh...  23.4 us
    ppermute x24, waiting for transfers between devices, shift(): return lax.ppermute(array, 'patch', pairs)  18 us
    unnamed x8, local copies, waits for them, and re-layouts  3.36 us
  transfers between devices with their start and end apart: 24, of which 7 were waited for; matrix products, arithmetic and copies ran while one was open for 0% of the time, Pallas kernels for 27%

profile of v6, /device:TPU:32, one launch (start us, length us, event | category | flops | bytes accessed | tf_op | source)
XLA Modules:
  0.0 79.4 jit_solution(4981881229421917217)
XLA Ops:
  0.6 1.1 %copy-done = bf16[1,256,1280]{2,1,0:T(8,128)(2,1)S(1)} copy-done((bf16[1,256,1280]{2,1,0:T(8,128)(2,1)S(1)}, bf16[1,256,1280]{2,1,0:T(8,128)(2,1)}, u32[]{:S(2)}) %copy-start) | copy-done | bytes 655384
  1.7 1.0 %shard_map.77 = (f32[8,128]{1,0:T(8,128)S(1)}, bf16[256,1280]{1,0:T(8,128)(2,1)S(1)}) custom-call(bf16[256,1280]{1,0:T(8,128)(2,1)S(1)} %bitcast.5), custom_call_target="tpu_custom_call" | custom-call | flops 1 | bytes 1 | tf_op jit(solution)/shard_map/pallas_call | solution.py:328
  2.8 0.9 %copy-done.1 = bf16[1,16,2560]{2,1,0:T(8,128)(2,1)S(1)} copy-done((bf16[1,16,2560]{2,1,0:T(8,128)(2,1)S(1)}, bf16[1,16,2560]{2,1,0:T(8,128)(2,1)}, u32[]{:S(2)}) %copy-start.1) | copy-done | bytes 81944
  4.0 1.6 %collective-permute-start.1 = (bf16[96,128]{1,0:T(8,128)(2,1)S(1)}, bf16[96,128]{1,0:T(8,128)(2,1)S(1)}, u32[]{:S(2)}, u32[]{:S(2)}) collective-permute-start(bf16[96,128]{1,0:T(8,128)(2,1)S(1)} %get-tuple-element.39), channel_id=1, source_target_pairs={{0,4},{2,6},{4,8},{6,10},{8,12},{10,14},{12,0},{14,2},{16,20},{18,... | collective-permute-start | bytes 73736 | tf_op jit(solution)/shard_map/ppermute | solution.py:349
  5.5 2.7 %collective-permute-start.2 = (bf16[96,128]{1,0:T(8,128)(2,1)S(1)}, bf16[96,128]{1,0:T(8,128)(2,1)S(1)}, u32[]{:S(2)}, u32[]{:S(2)}) collective-permute-start(bf16[96,128]{1,0:T(8,128)(2,1)S(1)} %get-tuple-element.40), channel_id=1, source_target_pairs={{0,8},{2,10},{4,12},{6,14},{8,0},{10,2},{12,4},{14,6},{16,24},{18,... | collective-permute-start | bytes 73736 | tf_op jit(solution)/shard_map/ppermute | solution.py:349
  8.3 1.4 %collective-permute-start.3 = (bf16[96,128]{1,0:T(8,128)(2,1)S(1)}, bf16[96,128]{1,0:T(8,128)(2,1)S(1)}, u32[]{:S(2)}, u32[]{:S(2)}) collective-permute-start(bf16[96,128]{1,0:T(8,128)(2,1)S(1)} %get-tuple-element.41), channel_id=1, source_target_pairs={{0,12},{2,14},{4,0},{6,2},{8,4},{10,6},{12,8},{14,10},{16,28},{18,... | collective-permute-start | bytes 73736 | tf_op jit(solution)/shard_map/ppermute | solution.py:349
  9.7 0.7 copy-done.2
  10.4 0.7 copy-done.3
  11.1 1.0 %collective-permute-done.3.refs_3_ = bf16[96,128]{1,0:T(8,128)(2,1)S(1)} collective-permute-done((bf16[96,128]{1,0:T(8,128)(2,1)S(1)}, bf16[96,128]{1,0:T(8,128)(2,1)S(1)}, u32[]{:S(2)}, u32[]{:S(2)}) %collective-permute-start.3) | collective-permute-done | bytes 24608 | tf_op jit(solution)/shard_map/ppermute | solution.py:349
  12.1 3.3 %collective-permute-start.6 = (bf16[336,128]{1,0:T(8,128)(2,1)S(1)}, bf16[336,128]{1,0:T(8,128)(2,1)S(1)}, u32[]{:S(2)}, u32[]{:S(2)}) collective-permute-start(bf16[336,128]{1,0:T(8,128)(2,1)S(1)} %shard_map.81.refs_0_), channel_id=1, source_target_pairs={{0,64},{2,66},{4,68},{6,70},{8,72},{10,74},{12,76},{14,78},{16,80}... | collective-permute-start | bytes 258056 | tf_op jit(solution)/shard_map/ppermute | solution.py:349
  15.5 2.2 %collective-permute-start.5 = (bf16[336,128]{1,0:T(8,128)(2,1)S(1)}, bf16[336,128]{1,0:T(8,128)(2,1)S(1)}, u32[]{:S(2)}, u32[]{:S(2)}) collective-permute-start(bf16[336,128]{1,0:T(8,128)(2,1)S(1)} %shard_map.81.refs_0_), channel_id=1, source_target_pairs={{0,192},{2,194},{4,196},{6,198},{8,200},{10,202},{12,204},{14,206}... | collective-permute-start | bytes 258056 | tf_op jit(solution)/shard_map/ppermute | solution.py:349
  17.7 4.9 %collective-permute-start.4 = (bf16[336,128]{1,0:T(8,128)(2,1)S(1)}, bf16[336,128]{1,0:T(8,128)(2,1)S(1)}, u32[]{:S(2)}, u32[]{:S(2)}) collective-permute-start(bf16[336,128]{1,0:T(8,128)(2,1)S(1)} %shard_map.81.refs_0_), channel_id=1, source_target_pairs={{0,128},{2,130},{4,132},{6,134},{8,136},{10,138},{12,140},{14,142}... | collective-permute-start | bytes 258056 | tf_op jit(solution)/shard_map/ppermute | solution.py:349
  22.6 1.9 %shard_map.82.query_ref = bf16[1280,1280]{1,0:T(8,128)(2,1)S(1)} custom-call(bf16[1280,1280]{1,0:T(8,128)(2,1)} %source_hbm), custom_call_target="tpu_custom_call" | custom-call | flops 1 | bytes 1 | tf_op jit(solution)/shard_map/pallas_call | solution.py:328
  24.6 2.9 %shard_map.83.pair_ref = bf16[1280,2560]{1,0:T(8,128)(2,1)S(1)} custom-call(bf16[1280,2560]{1,0:T(8,128)(2,1)} %source_hbm.1), custom_call_target="tpu_custom_call" | custom-call | flops 1 | bytes 1 | tf_op jit(solution)/shard_map/pallas_call | solution.py:328
  27.5 1.2 %collective-permute-done.4.refs_1_ = bf16[336,128]{1,0:T(8,128)(2,1)S(1)} collective-permute-done((bf16[336,128]{1,0:T(8,128)(2,1)S(1)}, bf16[336,128]{1,0:T(8,128)(2,1)S(1)}, u32[]{:S(2)}, u32[]{:S(2)}) %collective-permute-start.4) | collective-permute-done | bytes 86048 | tf_op jit(solution)/shard_map/ppermute | solution.py:349
  29.3 0.7 collective-permute-start.8
  30.0 0.7 collective-permute-start.7
  30.7 3.1 %collective-permute-start.12 = (bf16[1280,128]{1,0:T(8,128)(2,1)S(1)}, bf16[1280,128]{1,0:T(8,128)(2,1)S(1)}, u32[]{:S(2)}, u32[]{:S(2)}) collective-permute-start(bf16[1280,128]{1,0:T(8,128)(2,1)S(1)} %shard_map.87.refs_1_.refs_2_), channel_id=1, source_target_pairs={{0,48},{2,50},{4,52},{6,54},{8,56},{10,58},{12,60},{14,62},{16,0},... | collective-permute-start | bytes 983048 | tf_op jit(solution)/shard_map/ppermute | solution.py:349
  33.8 2.3 %collective-permute-start.13 = (bf16[1280,128]{1,0:T(8,128)(2,1)S(1)}, bf16[1280,128]{1,0:T(8,128)(2,1)S(1)}, u32[]{:S(2)}, u32[]{:S(2)}) collective-permute-start(bf16[1280,128]{1,0:T(8,128)(2,1)S(1)} %shard_map.87.refs_1_.refs_2_), channel_id=1, source_target_pairs={{0,32},{2,34},{4,36},{6,38},{8,40},{10,42},{12,44},{14,46},{16,48}... | collective-permute-start | bytes 983048 | tf_op jit(solution)/shard_map/ppermute | solution.py:349
  36.1 1.3 %collective-permute-start.10 = (f32[8,128]{1,0:T(8,128)S(1)}, f32[8,128]{1,0:T(8,128)S(1)}, u32[]{:S(2)}, u32[]{:S(2)}) collective-permute-start(f32[8,128]{1,0:T(8,128)S(1)} %shard_map.85.own_ref), channel_id=1, source_target_pairs={{2,0},{6,4},{10,8},{14,12},{18,16},{22,20},{26,24},{30,28},{34,32}... | collective-permute-start | bytes 12296 | tf_op jit(solution)/shard_map/ppermute | solution.py:349
  37.4 5.1 %collective-permute-done.10.other_ref = f32[8,128]{1,0:T(8,128)S(1)} collective-permute-done((f32[8,128]{1,0:T(8,128)S(1)}, f32[8,128]{1,0:T(8,128)S(1)}, u32[]{:S(2)}, u32[]{:S(2)}) %collective-permute-start.10) | collective-permute-done | bytes 4128 | tf_op jit(solution)/shard_map/ppermute | solution.py:349
  42.4 2.9 %shard_map.86 = (bf16[720,128]{1,0:T(8,128)(2,1)S(1)}, bf16[720,128]{1,0:T(8,128)(2,1)S(1)}, bf16[720,128]{1,0:T(8,128)(2,1)S(1)}, bf16[720,128]{1,0:T(8,128)(2,1)S(1)}, bf16[16,2560]{1,0:T(8,128)(2,1)}) custom-call(s32[1]{0:T(128)} %bitcast.place_ref, bf16[256,1280]{1,0:T(8,128)(2,1)S(1)} %get-tuple-element.36.tokens_ref, f32[8,128]{1,0:T(8,128)S(1)} %shard_map.85.own_ref, ...), custom_call_target="tpu_custom_call" | custom-call | flops 1 | bytes 1 | tf_op jit(solution)/shard_map/pallas_call | solution.py:328
  45.7 3.3 %collective-permute-start.19 = (bf16[720,128]{1,0:T(8,128)(2,1)S(1)}, bf16[720,128]{1,0:T(8,128)(2,1)S(1)}, u32[]{:S(2)}, u32[]{:S(2)}) collective-permute-start(bf16[720,128]{1,0:T(8,128)(2,1)S(1)} %get-tuple-element.64), channel_id=1, source_target_pairs={{0,8},{2,10},{4,12},{6,14},{8,0},{10,2},{12,4},{14,6},{16,24},{18,... | collective-permute-start | bytes 552968 | tf_op jit(solution)/shard_map/ppermute | solution.py:349
  49.0 4.7 %collective-permute-done.14.refs_1_ = bf16[720,128]{1,0:T(8,128)(2,1)S(1)} collective-permute-done((bf16[720,128]{1,0:T(8,128)(2,1)S(1)}, bf16[720,128]{1,0:T(8,128)(2,1)S(1)}, u32[]{:S(2)}, u32[]{:S(2)}) %collective-permute-start.14) | collective-permute-done | bytes 184352 | tf_op jit(solution)/shard_map/ppermute | solution.py:349
  54.7 2.9 %collective-permute-done.19.refs_0_ = bf16[720,128]{1,0:T(8,128)(2,1)S(1)} collective-permute-done((bf16[720,128]{1,0:T(8,128)(2,1)S(1)}, bf16[720,128]{1,0:T(8,128)(2,1)S(1)}, u32[]{:S(2)}, u32[]{:S(2)}) %collective-permute-start.19) | collective-permute-done | bytes 184352 | tf_op jit(solution)/shard_map/ppermute | solution.py:349
  57.6 6.5 %shard_map.89 = (bf16[640,128]{1,0:T(8,128)(2,1)S(1)}, bf16[640,128]{1,0:T(8,128)(2,1)S(1)}) custom-call(s32[1]{0:T(128)} %bitcast.place_ref, bf16[720,128]{1,0:T(8,128)(2,1)S(1)} %collective-permute-done.19.refs_0_, bf16[720,128]{1,0:T(8,128)(2,1)S(1)} %collective-permute-done.14.refs_1_, bf16[1280,128]{1,0:T(8,128)(2,1)S(1)} %shard_map.87.refs_1_.refs_2_, ...), custom_call_target="tpu_custom_call" | custom-call | flops 1 | bytes 1 | tf_op jit(solution)/shard_map/pallas_call | solution.py:328
  64.2 0.9 %collective-permute-start.20 = (bf16[640,128]{1,0:T(8,128)(2,1)S(1)}, bf16[640,128]{1,0:T(8,128)(2,1)S(1)}, u32[]{:S(2)}, u32[]{:S(2)}) collective-permute-start(bf16[640,128]{1,0:T(8,128)(2,1)S(1)} %get-tuple-element.65), channel_id=1, source_target_pairs={{0,12},{2,14},{4,0},{6,2},{8,4},{10,6},{12,8},{14,10},{16,28},{18,... | collective-permute-start | bytes 491528 | tf_op jit(solution)/shard_map/ppermute | solution.py:349
  65.1 3.3 %collective-permute-start.21 = (bf16[640,128]{1,0:T(8,128)(2,1)S(1)}, bf16[640,128]{1,0:T(8,128)(2,1)S(1)}, u32[]{:S(2)}, u32[]{:S(2)}) collective-permute-start(bf16[640,128]{1,0:T(8,128)(2,1)S(1)} %get-tuple-element.66), channel_id=1, source_target_pairs={{0,8},{2,10},{4,12},{6,14},{8,0},{10,2},{12,4},{14,6},{16,24},{18,... | collective-permute-start | bytes 491528 | tf_op jit(solution)/shard_map/ppermute | solution.py:349
  68.4 3.5 %shard_map.90 = bf16[640,128]{1,0:T(8,128)(2,1)S(1)} custom-call(s32[1]{0:T(128)} %bitcast.place_ref, bf16[720,128]{1,0:T(8,128)(2,1)S(1)} %collective-permute-done.22.refs_0_, bf16[1280,128]{1,0:T(8,128)(2,1)S(1)} %shard_map.87.refs_1_.refs_2_, bf16[1280,128]{1,0:T(8,128)(2,1)S(1)} %collective-permute-done.11.refs_2_.refs_3_, ...), custom_call_target="tpu_custom_call" | custom-call | flops 1 | bytes 1 | tf_op jit(solution)/shard_map/pallas_call | solution.py:328
  71.9 3.5 %shard_map.88.refs_0_ = bf16[640,128]{1,0:T(8,128)(2,1)S(1)} custom-call(s32[1]{0:T(128)} %bitcast.place_ref, bf16[720,128]{1,0:T(8,128)(2,1)S(1)} %get-tuple-element.57.refs_0_, bf16[1280,128]{1,0:T(8,128)(2,1)S(1)} %shard_map.87.refs_1_.refs_2_, bf16[1280,128]{1,0:T(8,128)(2,1)S(1)} %collective-permute-done.11.refs_2_.refs_3_, ...), custom_call_target="tpu_custom_call" | custom-call | flops 1 | bytes 1 | tf_op jit(solution)/shard_map/pallas_call | solution.py:328
  75.4 3.0 %collective-permute-done.23.refs_3_ = bf16[640,128]{1,0:T(8,128)(2,1)S(1)} collective-permute-done((bf16[640,128]{1,0:T(8,128)(2,1)S(1)}, bf16[640,128]{1,0:T(8,128)(2,1)S(1)}, u32[]{:S(2)}, u32[]{:S(2)}) %collective-permute-start.23) | collective-permute-done | bytes 163872 | tf_op jit(solution)/shard_map/ppermute | solution.py:349
  78.4 1.0 %shard_map.91 = bf16[256,1280]{1,0:T(8,128)(2,1)} custom-call(s32[1]{0:T(128)} %bitcast.place_ref, bf16[640,128]{1,0:T(8,128)(2,1)S(1)} %shard_map.88.refs_0_, bf16[640,128]{1,0:T(8,128)(2,1)S(1)} %collective-permute-done.20.refs_1_, bf16[640,128]{1,0:T(8,128)(2,1)S(1)} %collective-permute-done.21.refs_2_, bf16[640,128]{1,0:T(8,128)(2,1)S(1)} %collective-permute-done.23.refs_3_), custom_call_target="tpu_custom_call" | custom-call | flops 1 | bytes 1 | tf_op jit(solution)/shard_map/pallas_call | solution.py:328
  (39 shorter events, 2.6 us)
Async XLA Ops:
  0.6 1.1 %copy-start = (bf16[1,256,1280]{2,1,0:T(8,128)(2,1)S(1)}, bf16[1,256,1280]{2,1,0:T(8,128)(2,1)}, u32[]{:S(2)}) copy-start(bf16[1,256,1280]{2,1,0:T(8,128)(2,1)} %param.6) | copy-start | bytes 1966084
  2.7 1.2 %collective-permute-start = (f32[8,128]{1,0:T(8,128)S(1)}, f32[8,128]{1,0:T(8,128)S(1)}, u32[]{:S(2)}, u32[]{:S(2)}) collective-permute-start(f32[8,128]{1,0:T(8,128)S(1)} %get-tuple-element.37.stats_ref.own_ref), channel_id=1, source_target_pairs={{0,2},{2,0},{4,6},{6,4},{8,10},{10,8},{12,14},{14,12},{16,18},{18,... | collective-permute-start | bytes 12296 | tf_op jit(solution)/shard_map/ppermute | solution.py:349
  2.8 0.9 %copy-start.1 = (bf16[1,16,2560]{2,1,0:T(8,128)(2,1)S(1)}, bf16[1,16,2560]{2,1,0:T(8,128)(2,1)}, u32[]{:S(2)}) copy-start(bf16[1,16,2560]{2,1,0:T(8,128)(2,1)} %param.7) | copy-start | bytes 245764
  4.0 7.1 %collective-permute-start.1 = (bf16[96,128]{1,0:T(8,128)(2,1)S(1)}, bf16[96,128]{1,0:T(8,128)(2,1)S(1)}, u32[]{:S(2)}, u32[]{:S(2)}) collective-permute-start(bf16[96,128]{1,0:T(8,128)(2,1)S(1)} %get-tuple-element.39), channel_id=1, source_target_pairs={{0,4},{2,6},{4,8},{6,10},{8,12},{10,14},{12,0},{14,2},{16,20},{18,... | collective-permute-start | bytes 73736 | tf_op jit(solution)/shard_map/ppermute | solution.py:349
  5.5 5.6 %collective-permute-start.2 = (bf16[96,128]{1,0:T(8,128)(2,1)S(1)}, bf16[96,128]{1,0:T(8,128)(2,1)S(1)}, u32[]{:S(2)}, u32[]{:S(2)}) collective-permute-start(bf16[96,128]{1,0:T(8,128)(2,1)S(1)} %get-tuple-element.40), channel_id=1, source_target_pairs={{0,8},{2,10},{4,12},{6,14},{8,0},{10,2},{12,4},{14,6},{16,24},{18,... | collective-permute-start | bytes 73736 | tf_op jit(solution)/shard_map/ppermute | solution.py:349
  8.3 3.8 %collective-permute-start.3 = (bf16[96,128]{1,0:T(8,128)(2,1)S(1)}, bf16[96,128]{1,0:T(8,128)(2,1)S(1)}, u32[]{:S(2)}, u32[]{:S(2)}) collective-permute-start(bf16[96,128]{1,0:T(8,128)(2,1)S(1)} %get-tuple-element.41), channel_id=1, source_target_pairs={{0,12},{2,14},{4,0},{6,2},{8,4},{10,6},{12,8},{14,10},{16,28},{18,... | collective-permute-start | bytes 73736 | tf_op jit(solution)/shard_map/ppermute | solution.py:349
  9.7 0.7 copy-start.2
  10.4 0.7 copy-start.3
  12.1 15.3 %collective-permute-start.6 = (bf16[336,128]{1,0:T(8,128)(2,1)S(1)}, bf16[336,128]{1,0:T(8,128)(2,1)S(1)}, u32[]{:S(2)}, u32[]{:S(2)}) collective-permute-start(bf16[336,128]{1,0:T(8,128)(2,1)S(1)} %shard_map.81.refs_0_), channel_id=1, source_target_pairs={{0,64},{2,66},{4,68},{6,70},{8,72},{10,74},{12,76},{14,78},{16,80}... | collective-permute-start | bytes 258056 | tf_op jit(solution)/shard_map/ppermute | solution.py:349
  15.5 12.0 %collective-permute-start.5 = (bf16[336,128]{1,0:T(8,128)(2,1)S(1)}, bf16[336,128]{1,0:T(8,128)(2,1)S(1)}, u32[]{:S(2)}, u32[]{:S(2)}) collective-permute-start(bf16[336,128]{1,0:T(8,128)(2,1)S(1)} %shard_map.81.refs_0_), channel_id=1, source_target_pairs={{0,192},{2,194},{4,196},{6,198},{8,200},{10,202},{12,204},{14,206}... | collective-permute-start | bytes 258056 | tf_op jit(solution)/shard_map/ppermute | solution.py:349
  17.7 10.9 %collective-permute-start.4 = (bf16[336,128]{1,0:T(8,128)(2,1)S(1)}, bf16[336,128]{1,0:T(8,128)(2,1)S(1)}, u32[]{:S(2)}, u32[]{:S(2)}) collective-permute-start(bf16[336,128]{1,0:T(8,128)(2,1)S(1)} %shard_map.81.refs_0_), channel_id=1, source_target_pairs={{0,128},{2,130},{4,132},{6,134},{8,136},{10,138},{12,140},{14,142}... | collective-permute-start | bytes 258056 | tf_op jit(solution)/shard_map/ppermute | solution.py:349
  28.6 5.1 %collective-permute-start.9 = (f32[8,128]{1,0:T(8,128)S(1)}, f32[8,128]{1,0:T(8,128)S(1)}, u32[]{:S(2)}, u32[]{:S(2)}) collective-permute-start(f32[8,128]{1,0:T(8,128)S(1)} %shard_map.84.s0.stats_ref), channel_id=1, source_target_pairs={{2,50},{6,54},{10,58},{14,62},{18,2},{22,6},{26,10},{30,14},{34,18... | collective-permute-start | bytes 12296 | tf_op jit(solution)/shard_map/ppermute | solution.py:349
  29.3 4.5 %collective-permute-start.8 = (f32[8,128]{1,0:T(8,128)S(1)}, f32[8,128]{1,0:T(8,128)S(1)}, u32[]{:S(2)}, u32[]{:S(2)}) collective-permute-start(f32[8,128]{1,0:T(8,128)S(1)} %shard_map.84.s0.stats_ref), channel_id=1, source_target_pairs={{2,34},{6,38},{10,42},{14,46},{18,50},{22,54},{26,58},{30,62},{34,... | collective-permute-start | bytes 12296 | tf_op jit(solution)/shard_map/ppermute | solution.py:349
  30.0 3.8 %collective-permute-start.7 = (f32[8,128]{1,0:T(8,128)S(1)}, f32[8,128]{1,0:T(8,128)S(1)}, u32[]{:S(2)}, u32[]{:S(2)}) collective-permute-start(f32[8,128]{1,0:T(8,128)S(1)} %shard_map.84.s0.stats_ref), channel_id=1, source_target_pairs={{2,18},{6,22},{10,26},{14,30},{18,34},{22,38},{26,42},{30,46},{34,... | collective-permute-start | bytes 12296 | tf_op jit(solution)/shard_map/ppermute | solution.py:349
  30.7 23.0 %collective-permute-start.12 = (bf16[1280,128]{1,0:T(8,128)(2,1)S(1)}, bf16[1280,128]{1,0:T(8,128)(2,1)S(1)}, u32[]{:S(2)}, u32[]{:S(2)}) collective-permute-start(bf16[1280,128]{1,0:T(8,128)(2,1)S(1)} %shard_map.87.refs_1_.refs_2_), channel_id=1, source_target_pairs={{0,48},{2,50},{4,52},{6,54},{8,56},{10,58},{12,60},{14,62},{16,0},... | collective-permute-start | bytes 983048 | tf_op jit(solution)/shard_map/ppermute | solution.py:349
  33.8 20.5 %collective-permute-start.11 = (bf16[1280,128]{1,0:T(8,128)(2,1)S(1)}, bf16[1280,128]{1,0:T(8,128)(2,1)S(1)}, u32[]{:S(2)}, u32[]{:S(2)}) collective-permute-start(bf16[1280,128]{1,0:T(8,128)(2,1)S(1)} %shard_map.87.refs_1_.refs_2_), channel_id=1, source_target_pairs={{0,16},{2,18},{4,20},{6,22},{8,24},{10,26},{12,28},{14,30},{16,32}... | collective-permute-start | bytes 983048 | tf_op jit(solution)/shard_map/ppermute | solution.py:349
  33.8 20.5 %collective-permute-start.13 = (bf16[1280,128]{1,0:T(8,128)(2,1)S(1)}, bf16[1280,128]{1,0:T(8,128)(2,1)S(1)}, u32[]{:S(2)}, u32[]{:S(2)}) collective-permute-start(bf16[1280,128]{1,0:T(8,128)(2,1)S(1)} %shard_map.87.refs_1_.refs_2_), channel_id=1, source_target_pairs={{0,32},{2,34},{4,36},{6,38},{8,40},{10,42},{12,44},{14,46},{16,48}... | collective-permute-start | bytes 983048 | tf_op jit(solution)/shard_map/ppermute | solution.py:349
  36.1 6.3 %collective-permute-start.10 = (f32[8,128]{1,0:T(8,128)S(1)}, f32[8,128]{1,0:T(8,128)S(1)}, u32[]{:S(2)}, u32[]{:S(2)}) collective-permute-start(f32[8,128]{1,0:T(8,128)S(1)} %shard_map.85.own_ref), channel_id=1, source_target_pairs={{2,0},{6,4},{10,8},{14,12},{18,16},{22,20},{26,24},{30,28},{34,32}... | collective-permute-start | bytes 12296 | tf_op jit(solution)/shard_map/ppermute | solution.py:349
  45.4 8.3 %collective-permute-start.14 = (bf16[720,128]{1,0:T(8,128)(2,1)S(1)}, bf16[720,128]{1,0:T(8,128)(2,1)S(1)}, u32[]{:S(2)}, u32[]{:S(2)}) collective-permute-start(bf16[720,128]{1,0:T(8,128)(2,1)S(1)} %get-tuple-element.59), channel_id=1, source_target_pairs={{0,4},{2,6},{4,8},{6,10},{8,12},{10,14},{12,0},{14,2},{16,20},{18,... | collective-permute-start | bytes 552968 | tf_op jit(solution)/shard_map/ppermute | solution.py:349
  45.7 11.9 %collective-permute-start.19 = (bf16[720,128]{1,0:T(8,128)(2,1)S(1)}, bf16[720,128]{1,0:T(8,128)(2,1)S(1)}, u32[]{:S(2)}, u32[]{:S(2)}) collective-permute-start(bf16[720,128]{1,0:T(8,128)(2,1)S(1)} %get-tuple-element.64), channel_id=1, source_target_pairs={{0,8},{2,10},{4,12},{6,14},{8,0},{10,2},{12,4},{14,6},{16,24},{18,... | collective-permute-start | bytes 552968 | tf_op jit(solution)/shard_map/ppermute | solution.py:349
  53.7 3.9 %collective-permute-start.15 = (bf16[1280,128]{1,0:T(8,128)(2,1)S(1)}, bf16[1280,128]{1,0:T(8,128)(2,1)S(1)}, u32[]{:S(2)}, u32[]{:S(2)}) collective-permute-start(bf16[1280,128]{1,0:T(8,128)(2,1)S(1)} %shard_map.87.refs_1_.refs_2_), channel_id=1, source_target_pairs={{0,2},{2,0},{4,6},{6,4},{8,10},{10,8},{12,14},{14,12},{16,18},{18,... | collective-permute-start | bytes 983048 | tf_op jit(solution)/shard_map/ppermute | solution.py:349
  53.7 3.9 %collective-permute-start.17 = (bf16[1280,128]{1,0:T(8,128)(2,1)S(1)}, bf16[1280,128]{1,0:T(8,128)(2,1)S(1)}, u32[]{:S(2)}, u32[]{:S(2)}) collective-permute-start(bf16[1280,128]{1,0:T(8,128)(2,1)S(1)} %collective-permute-done.12.refs_3_.refs_4_), channel_id=1, source_target_pairs={{0,2},{2,0},{4,6},{6,4},{8,10},{10,8},{12,14},{14,12},{16,18},{18,... | collective-permute-start | bytes 983048 | tf_op jit(solution)/shard_map/ppermute | solution.py:349
  54.2 3.4 %collective-permute-start.16 = (bf16[1280,128]{1,0:T(8,128)(2,1)S(1)}, bf16[1280,128]{1,0:T(8,128)(2,1)S(1)}, u32[]{:S(2)}, u32[]{:S(2)}) collective-permute-start(bf16[1280,128]{1,0:T(8,128)(2,1)S(1)} %collective-permute-done.11.refs_2_.refs_3_), channel_id=1, source_target_pairs={{0,2},{2,0},{4,6},{6,4},{8,10},{10,8},{12,14},{14,12},{16,18},{18,... | collective-permute-start | bytes 983048 | tf_op jit(solution)/shard_map/ppermute | solution.py:349
  54.3 3.3 %collective-permute-start.18 = (bf16[1280,128]{1,0:T(8,128)(2,1)S(1)}, bf16[1280,128]{1,0:T(8,128)(2,1)S(1)}, u32[]{:S(2)}, u32[]{:S(2)}) collective-permute-start(bf16[1280,128]{1,0:T(8,128)(2,1)S(1)} %collective-permute-done.13.refs_4_.refs_5_), channel_id=1, source_target_pairs={{0,2},{2,0},{4,6},{6,4},{8,10},{10,8},{12,14},{14,12},{16,18},{18,... | collective-permute-start | bytes 983048 | tf_op jit(solution)/shard_map/ppermute | solution.py:349
  57.6 10.7 %collective-permute-start.22 = (bf16[720,128]{1,0:T(8,128)(2,1)S(1)}, bf16[720,128]{1,0:T(8,128)(2,1)S(1)}, u32[]{:S(2)}, u32[]{:S(2)}) collective-permute-start(bf16[720,128]{1,0:T(8,128)(2,1)S(1)} %get-tuple-element.68), channel_id=1, source_target_pairs={{0,12},{2,14},{4,0},{6,2},{8,4},{10,6},{12,8},{14,10},{16,28},{18,... | collective-permute-start | bytes 552968 | tf_op jit(solution)/shard_map/ppermute | solution.py:349
  64.2 11.2 %collective-permute-start.20 = (bf16[640,128]{1,0:T(8,128)(2,1)S(1)}, bf16[640,128]{1,0:T(8,128)(2,1)S(1)}, u32[]{:S(2)}, u32[]{:S(2)}) collective-permute-start(bf16[640,128]{1,0:T(8,128)(2,1)S(1)} %get-tuple-element.65), channel_id=1, source_target_pairs={{0,12},{2,14},{4,0},{6,2},{8,4},{10,6},{12,8},{14,10},{16,28},{18,... | collective-permute-start | bytes 491528 | tf_op jit(solution)/shard_map/ppermute | solution.py:349
  65.1 10.4 %collective-permute-start.21 = (bf16[640,128]{1,0:T(8,128)(2,1)S(1)}, bf16[640,128]{1,0:T(8,128)(2,1)S(1)}, u32[]{:S(2)}, u32[]{:S(2)}) collective-permute-start(bf16[640,128]{1,0:T(8,128)(2,1)S(1)} %get-tuple-element.66), channel_id=1, source_target_pairs={{0,8},{2,10},{4,12},{6,14},{8,0},{10,2},{12,4},{14,6},{16,24},{18,... | collective-permute-start | bytes 491528 | tf_op jit(solution)/shard_map/ppermute | solution.py:349
  71.8 6.6 %collective-permute-start.23 = (bf16[640,128]{1,0:T(8,128)(2,1)S(1)}, bf16[640,128]{1,0:T(8,128)(2,1)S(1)}, u32[]{:S(2)}, u32[]{:S(2)}) collective-permute-start(bf16[640,128]{1,0:T(8,128)(2,1)S(1)} %shard_map.90), channel_id=1, source_target_pairs={{0,4},{2,6},{4,8},{6,10},{8,12},{10,14},{12,0},{14,2},{16,20},{18,... | collective-permute-start | bytes 491528 | tf_op jit(solution)/shard_map/ppermute | solution.py:349

commit v7 on v5

--- a/solution.py
+++ b/solution.py
@@ -30,6 +30,12 @@
 
 def iota(shape, axis):
     return lax.broadcasted_iota(jnp.int32, shape, axis)
+
+
+def x_peer(place_ref, k):
+    place = place_ref[0]
+    step = k * (1 - 2 * lax.bitwise_and(place, 1))
+    return lax.bitwise_and(lax.shift_right_logical(place, 1) + step, 3)
 
 
 def group_of_channel():
@@ -138,9 +144,8 @@
 def x_kernel(place_ref, own_ref, other_ref, sets_ref, *out_refs):
     mean, squares = combine([own_ref[...], other_ref[...]], CELLS * GROUP_WIDTH)
     coded = split_rows(mean, squares)
-    place = place_ref[0]
     for k, out_ref in enumerate(out_refs):
-        out_ref[0:SET_ROWS, :] = sets_ref[lax.rem(place + k, 4)]
+        out_ref[0:SET_ROWS, :] = sets_ref[x_peer(place_ref, k)]
         out_ref[SET_ROWS:, :] = coded
 
 
@@ -197,13 +202,12 @@
     pool = jnp.where(cell_square == square, 1.0 / (POOL * POOL), 0.0).astype(bf16)
     pooled = jnp.dot(pool, normed, preferred_element_type=f32).astype(bf16)
 
-    place = place_ref[0]
     last = jnp.dot(normed, query_ref[:, 1024:], preferred_element_type=f32).astype(bf16)
     last_ref[0] = last[:, 0:LANES]
     last_ref[1] = last[:, LANES:]
     lane_half = lax.shift_right_logical(iota((CELLS // 2, LANES), 1), 6)
     for k in (2, 1, 3, 0):
-        j = lax.rem(place + k, 4)
+        j = x_peer(place_ref, k)
         columns = pl.ds(pl.multiple_of(j * 256, 256), 256)
         block = jnp.dot(normed, query_ref[:, columns], preferred_element_type=f32).astype(bf16)
         message_refs[k][0:CELLS, :] = block[:, 0:LANES]
@@ -218,7 +222,7 @@
     for j, block in enumerate(head_tiles(fresh)):
         sets_ref[j] = block
     for k in range(4):
-        message_refs[k][ANSWER_ROWS:, :] = sets_ref[lax.rem(place + k, 4)]
+        message_refs[k][ANSWER_ROWS:, :] = sets_ref[x_peer(place_ref, k)]
 
 
 def attend_kernel(sources, place_ref, *refs):
@@ -233,7 +237,7 @@
             first_ref[low : low + ROWS, :] = fresh
     lane = iota((CELLS, LANES), 1)
     low_half = lane < HEAD_DIM
-    parity = lax.bitwise_and(place_ref[0], 1)
+    parity = lax.bitwise_and(x_peer(place_ref, 0), 1)
     factor = HEAD_DIM ** (-0.5) * 1.4426950408889634
     against = (((1,), (1,)), ((), ()))
     ones = jnp.ones((CELLS, LANES), bf16)
@@ -300,9 +304,8 @@
 
 def assemble_kernel(place_ref, *refs):
     *in_refs, out_ref, sets_ref = refs
-    place = place_ref[0]
     for k, ref in enumerate(in_refs):
-        sets_ref[lax.rem(place + k, 4)] = ref[...]
+        sets_ref[x_peer(place_ref, k)] = ref[...]
     for j in range(4):
         for t in range(2):
             low = (2 * j + t) * LANES
@@ -326,19 +329,17 @@
     )(*args)
 
 
-def permute(array, place):
+AXES = {"z": (32, 4), "y": (8, 4), "x": (2, 4), "core": (1, 2)}
+
+
+def shift(array, axis, step):
+    stride, size = AXES[axis]
     pairs = []
     for source in range(128):
-        z, y, x, core = place(source // 32, source // 8 % 4, source // 2 % 4, source % 2)
-        pairs.append((source, z % 4 * 32 + y % 4 * 8 + x % 4 * 2 + core % 2))
+        place = source // stride % size
+        target = (place + step * (1 - 2 * (source % 2))) % size
+        pairs.append((source, source + (target - place) * stride))
     return lax.ppermute(array, "patch", pairs)
-
-
-def shift(array, axis, step):
-    def place(*places):
-        return [at + step * (name == axis) for at, name in zip(places, ("z", "y", "x", "core"))]
-
-    return permute(array, place)
 
 
 def after(array, *others):
@@ -346,7 +347,7 @@
 
 
 def per_device(tokens, stale_keys, norm_gain, norm_bias, query_weight, pair_weight):
-    place = (lax.axis_index("patch") // 2 % 4).astype(jnp.int32).reshape(1)
+    place = lax.axis_index("patch").astype(jnp.int32).reshape(1)
     table = ((SET_HEADS * CELLS, LANES), bf16)
     answer = ((ANSWER_ROWS, LANES), bf16)
     stats, tokens = call(

time: 73.5 us -> 74.2 us (level)
  the two profiles are of different devices: /device:TPU:32 before, /device:TPU:16 now
where the time goes in v7:
time: 74.2 us; the launch traced here: 73.9 us
  starting transfers between devices  36.1 us (49%)
  Pallas kernels  23.4 us (32%)
  waiting for transfers between devices  10.2 us (14%)
  local copies, waits for them, and re-layouts  3.36 us (5%)
  between operations  0.79 us (1%)
    ppermute x23, starting transfers between devices, shift(): return lax.ppermute(array, 'patch', pairs)  36.1 us
    pallas_call x14, Pallas kernels, call(): pl.pallas_call(kernel, in_specs=ins, out_specs=[VMEM] * len(outs), out_sh...  23.4 us
    ppermute x23, waiting for transfers between devices, shift(): return lax.ppermute(array, 'patch', pairs)  10.2 us
    unnamed x8, local copies, waits for them, and re-layouts  3.36 us
  transfers between devices with their start and end apart: 23, of which 7 were waited for; matrix products, arithmetic and copies ran while one was open for 0% of the time, Pallas kernels for 29%

profile of v7, /device:TPU:16, one launch (start us, length us, event | category | flops | bytes accessed | tf_op | source)
XLA Modules:
  0.0 73.9 jit_solution(10180093025371321585)
XLA Ops:
  0.6 1.1 %copy-done = bf16[1,256,1280]{2,1,0:T(8,128)(2,1)S(1)} copy-done((bf16[1,256,1280]{2,1,0:T(8,128)(2,1)S(1)}, bf16[1,256,1280]{2,1,0:T(8,128)(2,1)}, u32[]{:S(2)}) %copy-start) | copy-done | bytes 655384
  1.7 1.0 %shard_map.77 = (f32[8,128]{1,0:T(8,128)S(1)}, bf16[256,1280]{1,0:T(8,128)(2,1)S(1)}) custom-call(bf16[256,1280]{1,0:T(8,128)(2,1)S(1)} %bitcast.5), custom_call_target="tpu_custom_call" | custom-call | flops 1 | bytes 1 | tf_op jit(solution)/shard_map/pallas_call | solution.py:321
  2.8 0.9 %copy-done.1 = bf16[1,16,2560]{2,1,0:T(8,128)(2,1)S(1)} copy-done((bf16[1,16,2560]{2,1,0:T(8,128)(2,1)S(1)}, bf16[1,16,2560]{2,1,0:T(8,128)(2,1)}, u32[]{:S(2)}) %copy-start.1) | copy-done | bytes 81944
  4.0 1.6 %collective-permute-start.1 = (bf16[96,128]{1,0:T(8,128)(2,1)S(1)}, bf16[96,128]{1,0:T(8,128)(2,1)S(1)}, u32[]{:S(2)}, u32[]{:S(2)}) collective-permute-start(bf16[96,128]{1,0:T(8,128)(2,1)S(1)} %get-tuple-element.39), channel_id=1, source_target_pairs={{0,4},{2,14},{4,8},{6,2},{8,12},{10,6},{12,0},{14,10},{16,20},{18,... | collective-permute-start | bytes 73736 | tf_op jit(solution)/shard_map/ppermute | solution.py:342
  5.5 2.7 %collective-permute-start.2 = (bf16[96,128]{1,0:T(8,128)(2,1)S(1)}, bf16[96,128]{1,0:T(8,128)(2,1)S(1)}, u32[]{:S(2)}, u32[]{:S(2)}) collective-permute-start(bf16[96,128]{1,0:T(8,128)(2,1)S(1)} %get-tuple-element.40), channel_id=1, source_target_pairs={{0,8},{2,10},{4,12},{6,14},{8,0},{10,2},{12,4},{14,6},{16,24},{18,... | collective-permute-start | bytes 73736 | tf_op jit(solution)/shard_map/ppermute | solution.py:342
  8.3 1.4 %collective-permute-start.3 = (bf16[96,128]{1,0:T(8,128)(2,1)S(1)}, bf16[96,128]{1,0:T(8,128)(2,1)S(1)}, u32[]{:S(2)}, u32[]{:S(2)}) collective-permute-start(bf16[96,128]{1,0:T(8,128)(2,1)S(1)} %get-tuple-element.41), channel_id=1, source_target_pairs={{0,12},{2,6},{4,0},{6,10},{8,4},{10,14},{12,8},{14,2},{16,28},{18,... | collective-permute-start | bytes 73736 | tf_op jit(solution)/shard_map/ppermute | solution.py:342
  9.7 0.7 copy-done.2
  10.4 0.7 copy-done.3
  11.1 1.0 %collective-permute-done.3.refs_3_ = bf16[96,128]{1,0:T(8,128)(2,1)S(1)} collective-permute-done((bf16[96,128]{1,0:T(8,128)(2,1)S(1)}, bf16[96,128]{1,0:T(8,128)(2,1)S(1)}, u32[]{:S(2)}, u32[]{:S(2)}) %collective-permute-start.3) | collective-permute-done | bytes 24608 | tf_op jit(solution)/shard_map/ppermute | solution.py:342
  12.1 3.3 %collective-permute-start.6 = (bf16[336,128]{1,0:T(8,128)(2,1)S(1)}, bf16[336,128]{1,0:T(8,128)(2,1)S(1)}, u32[]{:S(2)}, u32[]{:S(2)}) collective-permute-start(bf16[336,128]{1,0:T(8,128)(2,1)S(1)} %shard_map.81.refs_0_), channel_id=1, source_target_pairs={{0,64},{2,194},{4,68},{6,198},{8,72},{10,202},{12,76},{14,206},{16... | collective-permute-start | bytes 258056 | tf_op jit(solution)/shard_map/ppermute | solution.py:342
  15.5 3.1 %collective-permute-start.5 = (bf16[336,128]{1,0:T(8,128)(2,1)S(1)}, bf16[336,128]{1,0:T(8,128)(2,1)S(1)}, u32[]{:S(2)}, u32[]{:S(2)}) collective-permute-start(bf16[336,128]{1,0:T(8,128)(2,1)S(1)} %shard_map.81.refs_0_), channel_id=1, source_target_pairs={{0,192},{2,66},{4,196},{6,70},{8,200},{10,74},{12,204},{14,78},{16... | collective-permute-start | bytes 258056 | tf_op jit(solution)/shard_map/ppermute | solution.py:342
  18.6 4.9 %collective-permute-start.4 = (bf16[336,128]{1,0:T(8,128)(2,1)S(1)}, bf16[336,128]{1,0:T(8,128)(2,1)S(1)}, u32[]{:S(2)}, u32[]{:S(2)}) collective-permute-start(bf16[336,128]{1,0:T(8,128)(2,1)S(1)} %shard_map.81.refs_0_), channel_id=1, source_target_pairs={{0,128},{2,130},{4,132},{6,134},{8,136},{10,138},{12,140},{14,142}... | collective-permute-start | bytes 258056 | tf_op jit(solution)/shard_map/ppermute | solution.py:342
  23.5 1.9 %shard_map.82.query_ref = bf16[1280,1280]{1,0:T(8,128)(2,1)S(1)} custom-call(bf16[1280,1280]{1,0:T(8,128)(2,1)} %source_hbm), custom_call_target="tpu_custom_call" | custom-call | flops 1 | bytes 1 | tf_op jit(solution)/shard_map/pallas_call | solution.py:321
  25.5 2.9 %shard_map.83.pair_ref = bf16[1280,2560]{1,0:T(8,128)(2,1)S(1)} custom-call(bf16[1280,2560]{1,0:T(8,128)(2,1)} %source_hbm.1), custom_call_target="tpu_custom_call" | custom-call | flops 1 | bytes 1 | tf_op jit(solution)/shard_map/pallas_call | solution.py:321
  28.4 0.5 collective-permute-start.9
  28.9 2.9 %collective-permute-start.8 = (f32[8,128]{1,0:T(8,128)S(1)}, f32[8,128]{1,0:T(8,128)S(1)}, u32[]{:S(2)}, u32[]{:S(2)}) collective-permute-start(f32[8,128]{1,0:T(8,128)S(1)} %shard_map.84.s0.stats_ref), channel_id=1, source_target_pairs={{0,32},{2,34},{4,36},{6,38},{8,40},{10,42},{12,44},{14,46},{16,48}... | collective-permute-start | bytes 12296 | tf_op jit(solution)/shard_map/ppermute | solution.py:342
  31.9 2.1 %collective-permute-start.11 = (bf16[1280,128]{1,0:T(8,128)(2,1)S(1)}, bf16[1280,128]{1,0:T(8,128)(2,1)S(1)}, u32[]{:S(2)}, u32[]{:S(2)}) collective-permute-start(bf16[1280,128]{1,0:T(8,128)(2,1)S(1)} %shard_map.86.refs_1_.refs_2_), channel_id=1, source_target_pairs={{0,48},{2,18},{4,52},{6,22},{8,56},{10,26},{12,60},{14,30},{16,0},... | collective-permute-start | bytes 983048 | tf_op jit(solution)/shard_map/ppermute | solution.py:342
  34.1 1.4 %collective-permute-done.7.s1 = f32[8,128]{1,0:T(8,128)S(1)} collective-permute-done((f32[8,128]{1,0:T(8,128)S(1)}, f32[8,128]{1,0:T(8,128)S(1)}, u32[]{:S(2)}, u32[]{:S(2)}) %collective-permute-start.7) | collective-permute-done | bytes 4128 | tf_op jit(solution)/shard_map/ppermute | solution.py:342
  35.5 1.8 %collective-permute-start.12 = (bf16[1280,128]{1,0:T(8,128)(2,1)S(1)}, bf16[1280,128]{1,0:T(8,128)(2,1)S(1)}, u32[]{:S(2)}, u32[]{:S(2)}) collective-permute-start(bf16[1280,128]{1,0:T(8,128)(2,1)S(1)} %shard_map.86.refs_1_.refs_2_), channel_id=1, source_target_pairs={{0,32},{2,34},{4,36},{6,38},{8,40},{10,42},{12,44},{14,46},{16,48}... | collective-permute-start | bytes 983048 | tf_op jit(solution)/shard_map/ppermute | solution.py:342
  37.3 3.0 %shard_map.85 = (bf16[720,128]{1,0:T(8,128)(2,1)S(1)}, bf16[720,128]{1,0:T(8,128)(2,1)S(1)}, bf16[720,128]{1,0:T(8,128)(2,1)S(1)}, bf16[720,128]{1,0:T(8,128)(2,1)S(1)}, bf16[16,2560]{1,0:T(8,128)(2,1)}) custom-call(s32[1]{0:T(128)} %bitcast.place_ref, bf16[256,1280]{1,0:T(8,128)(2,1)S(1)} %get-tuple-element.36.tokens_ref, ...), custom_call_target="tpu_custom_call" | custom-call | flops 1 | bytes 1 | tf_op jit(solution)/shard_map/pallas_call | solution.py:321
  40.6 6.0 %collective-permute-start.18 = (bf16[720,128]{1,0:T(8,128)(2,1)S(1)}, bf16[720,128]{1,0:T(8,128)(2,1)S(1)}, u32[]{:S(2)}, u32[]{:S(2)}) collective-permute-start(bf16[720,128]{1,0:T(8,128)(2,1)S(1)} %get-tuple-element.64), channel_id=1, source_target_pairs={{0,8},{2,10},{4,12},{6,14},{8,0},{10,2},{12,4},{14,6},{16,24},{18,... | collective-permute-start | bytes 552968 | tf_op jit(solution)/shard_map/ppermute | solution.py:342
  46.6 2.1 %collective-permute-done.13.refs_1_ = bf16[720,128]{1,0:T(8,128)(2,1)S(1)} collective-permute-done((bf16[720,128]{1,0:T(8,128)(2,1)S(1)}, bf16[720,128]{1,0:T(8,128)(2,1)S(1)}, u32[]{:S(2)}, u32[]{:S(2)}) %collective-permute-start.13) | collective-permute-done | bytes 184352 | tf_op jit(solution)/shard_map/ppermute | solution.py:342
  48.6 0.5 collective-permute-start.16
  49.2 0.4 collective-permute-start.17
  49.7 2.4 %collective-permute-done.18.refs_0_ = bf16[720,128]{1,0:T(8,128)(2,1)S(1)} collective-permute-done((bf16[720,128]{1,0:T(8,128)(2,1)S(1)}, bf16[720,128]{1,0:T(8,128)(2,1)S(1)}, u32[]{:S(2)}, u32[]{:S(2)}) %collective-permute-start.18) | collective-permute-done | bytes 184352 | tf_op jit(solution)/shard_map/ppermute | solution.py:342
  52.2 6.5 %shard_map.88 = (bf16[640,128]{1,0:T(8,128)(2,1)S(1)}, bf16[640,128]{1,0:T(8,128)(2,1)S(1)}) custom-call(s32[1]{0:T(128)} %bitcast.place_ref, bf16[720,128]{1,0:T(8,128)(2,1)S(1)} %collective-permute-done.18.refs_0_, bf16[720,128]{1,0:T(8,128)(2,1)S(1)} %collective-permute-done.13.refs_1_, bf16[1280,128]{1,0:T(8,128)(2,1)S(1)} %shard_map.86.refs_1_.refs_2_, ...), custom_call_target="tpu_custom_call" | custom-call | flops 1 | bytes 1 | tf_op jit(solution)/shard_map/pallas_call | solution.py:321
  58.7 2.1 %collective-permute-start.19 = (bf16[640,128]{1,0:T(8,128)(2,1)S(1)}, bf16[640,128]{1,0:T(8,128)(2,1)S(1)}, u32[]{:S(2)}, u32[]{:S(2)}) collective-permute-start(bf16[640,128]{1,0:T(8,128)(2,1)S(1)} %get-tuple-element.65), channel_id=1, source_target_pairs={{0,12},{2,6},{4,0},{6,10},{8,4},{10,14},{12,8},{14,2},{16,28},{18,... | collective-permute-start | bytes 491528 | tf_op jit(solution)/shard_map/ppermute | solution.py:342
  60.8 1.9 %collective-permute-start.20 = (bf16[640,128]{1,0:T(8,128)(2,1)S(1)}, bf16[640,128]{1,0:T(8,128)(2,1)S(1)}, u32[]{:S(2)}, u32[]{:S(2)}) collective-permute-start(bf16[640,128]{1,0:T(8,128)(2,1)S(1)} %get-tuple-element.66), channel_id=1, source_target_pairs={{0,8},{2,10},{4,12},{6,14},{8,0},{10,2},{12,4},{14,6},{16,24},{18,... | collective-permute-start | bytes 491528 | tf_op jit(solution)/shard_map/ppermute | solution.py:342
  62.8 3.5 %shard_map.89 = bf16[640,128]{1,0:T(8,128)(2,1)S(1)} custom-call(s32[1]{0:T(128)} %bitcast.place_ref, bf16[720,128]{1,0:T(8,128)(2,1)S(1)} %collective-permute-done.21.refs_0_, bf16[1280,128]{1,0:T(8,128)(2,1)S(1)} %shard_map.86.refs_1_.refs_2_, bf16[1280,128]{1,0:T(8,128)(2,1)S(1)} %collective-permute-done.10.refs_2_.refs_3_, ...), custom_call_target="tpu_custom_call" | custom-call | flops 1 | bytes 1 | tf_op jit(solution)/shard_map/pallas_call | solution.py:321
  66.4 3.5 %shard_map.87.refs_0_ = bf16[640,128]{1,0:T(8,128)(2,1)S(1)} custom-call(s32[1]{0:T(128)} %bitcast.place_ref, bf16[720,128]{1,0:T(8,128)(2,1)S(1)} %get-tuple-element.57.refs_0_, bf16[1280,128]{1,0:T(8,128)(2,1)S(1)} %shard_map.86.refs_1_.refs_2_, bf16[1280,128]{1,0:T(8,128)(2,1)S(1)} %collective-permute-done.10.refs_2_.refs_3_, ...), custom_call_target="tpu_custom_call" | custom-call | flops 1 | bytes 1 | tf_op jit(solution)/shard_map/pallas_call | solution.py:321
  69.9 3.0 %collective-permute-done.22.refs_3_ = bf16[640,128]{1,0:T(8,128)(2,1)S(1)} collective-permute-done((bf16[640,128]{1,0:T(8,128)(2,1)S(1)}, bf16[640,128]{1,0:T(8,128)(2,1)S(1)}, u32[]{:S(2)}, u32[]{:S(2)}) %collective-permute-start.22) | collective-permute-done | bytes 163872 | tf_op jit(solution)/shard_map/ppermute | solution.py:342
  72.9 1.0 %shard_map.90 = bf16[256,1280]{1,0:T(8,128)(2,1)} custom-call(s32[1]{0:T(128)} %bitcast.place_ref, bf16[640,128]{1,0:T(8,128)(2,1)S(1)} %shard_map.87.refs_0_, bf16[640,128]{1,0:T(8,128)(2,1)S(1)} %collective-permute-done.19.refs_1_, bf16[640,128]{1,0:T(8,128)(2,1)S(1)} %collective-permute-done.20.refs_2_, bf16[640,128]{1,0:T(8,128)(2,1)S(1)} %collective-permute-done.22.refs_3_), custom_call_target="tpu_custom_call" | custom-call | flops 1 | bytes 1 | tf_op jit(solution)/shard_map/pallas_call | solution.py:321
  (36 shorter events, 1.3 us)
Async XLA Ops:
  0.6 1.1 %copy-start = (bf16[1,256,1280]{2,1,0:T(8,128)(2,1)S(1)}, bf16[1,256,1280]{2,1,0:T(8,128)(2,1)}, u32[]{:S(2)}) copy-start(bf16[1,256,1280]{2,1,0:T(8,128)(2,1)} %param.6) | copy-start | bytes 1966084
  2.7 1.2 %collective-permute-start = (f32[8,128]{1,0:T(8,128)S(1)}, f32[8,128]{1,0:T(8,128)S(1)}, u32[]{:S(2)}, u32[]{:S(2)}) collective-permute-start(f32[8,128]{1,0:T(8,128)S(1)} %get-tuple-element.37.stats_ref.own_ref), channel_id=1, source_target_pairs={{0,2},{2,0},{4,6},{6,4},{8,10},{10,8},{12,14},{14,12},{16,18},{18,... | collective-permute-start | bytes 12296 | tf_op jit(solution)/shard_map/ppermute | solution.py:342
  2.8 0.9 %copy-start.1 = (bf16[1,16,2560]{2,1,0:T(8,128)(2,1)S(1)}, bf16[1,16,2560]{2,1,0:T(8,128)(2,1)}, u32[]{:S(2)}) copy-start(bf16[1,16,2560]{2,1,0:T(8,128)(2,1)} %param.7) | copy-start | bytes 245764
  4.0 7.1 %collective-permute-start.1 = (bf16[96,128]{1,0:T(8,128)(2,1)S(1)}, bf16[96,128]{1,0:T(8,128)(2,1)S(1)}, u32[]{:S(2)}, u32[]{:S(2)}) collective-permute-start(bf16[96,128]{1,0:T(8,128)(2,1)S(1)} %get-tuple-element.39), channel_id=1, source_target_pairs={{0,4},{2,14},{4,8},{6,2},{8,12},{10,6},{12,0},{14,10},{16,20},{18,... | collective-permute-start | bytes 73736 | tf_op jit(solution)/shard_map/ppermute | solution.py:342
  5.5 5.6 %collective-permute-start.2 = (bf16[96,128]{1,0:T(8,128)(2,1)S(1)}, bf16[96,128]{1,0:T(8,128)(2,1)S(1)}, u32[]{:S(2)}, u32[]{:S(2)}) collective-permute-start(bf16[96,128]{1,0:T(8,128)(2,1)S(1)} %get-tuple-element.40), channel_id=1, source_target_pairs={{0,8},{2,10},{4,12},{6,14},{8,0},{10,2},{12,4},{14,6},{16,24},{18,... | collective-permute-start | bytes 73736 | tf_op jit(solution)/shard_map/ppermute | solution.py:342
  8.3 3.8 %collective-permute-start.3 = (bf16[96,128]{1,0:T(8,128)(2,1)S(1)}, bf16[96,128]{1,0:T(8,128)(2,1)S(1)}, u32[]{:S(2)}, u32[]{:S(2)}) collective-permute-start(bf16[96,128]{1,0:T(8,128)(2,1)S(1)} %get-tuple-element.41), channel_id=1, source_target_pairs={{0,12},{2,6},{4,0},{6,10},{8,4},{10,14},{12,8},{14,2},{16,28},{18,... | collective-permute-start | bytes 73736 | tf_op jit(solution)/shard_map/ppermute | solution.py:342
  9.7 0.7 copy-start.2
  10.4 0.7 copy-start.3
  12.1 16.2 %collective-permute-start.6 = (bf16[336,128]{1,0:T(8,128)(2,1)S(1)}, bf16[336,128]{1,0:T(8,128)(2,1)S(1)}, u32[]{:S(2)}, u32[]{:S(2)}) collective-permute-start(bf16[336,128]{1,0:T(8,128)(2,1)S(1)} %shard_map.81.refs_0_), channel_id=1, source_target_pairs={{0,64},{2,194},{4,68},{6,198},{8,72},{10,202},{12,76},{14,206},{16... | collective-permute-start | bytes 258056 | tf_op jit(solution)/shard_map/ppermute | solution.py:342
  15.5 12.9 %collective-permute-start.5 = (bf16[336,128]{1,0:T(8,128)(2,1)S(1)}, bf16[336,128]{1,0:T(8,128)(2,1)S(1)}, u32[]{:S(2)}, u32[]{:S(2)}) collective-permute-start(bf16[336,128]{1,0:T(8,128)(2,1)S(1)} %shard_map.81.refs_0_), channel_id=1, source_target_pairs={{0,192},{2,66},{4,196},{6,70},{8,200},{10,74},{12,204},{14,78},{16... | collective-permute-start | bytes 258056 | tf_op jit(solution)/shard_map/ppermute | solution.py:342
  18.6 9.8 %collective-permute-start.4 = (bf16[336,128]{1,0:T(8,128)(2,1)S(1)}, bf16[336,128]{1,0:T(8,128)(2,1)S(1)}, u32[]{:S(2)}, u32[]{:S(2)}) collective-permute-start(bf16[336,128]{1,0:T(8,128)(2,1)S(1)} %shard_map.81.refs_0_), channel_id=1, source_target_pairs={{0,128},{2,130},{4,132},{6,134},{8,136},{10,138},{12,140},{14,142}... | collective-permute-start | bytes 258056 | tf_op jit(solution)/shard_map/ppermute | solution.py:342
  28.4 5.6 %collective-permute-start.9 = (f32[8,128]{1,0:T(8,128)S(1)}, f32[8,128]{1,0:T(8,128)S(1)}, u32[]{:S(2)}, u32[]{:S(2)}) collective-permute-start(f32[8,128]{1,0:T(8,128)S(1)} %shard_map.84.s0.stats_ref), channel_id=1, source_target_pairs={{0,48},{2,18},{4,52},{6,22},{8,56},{10,26},{12,60},{14,30},{16,0},... | collective-permute-start | bytes 12296 | tf_op jit(solution)/shard_map/ppermute | solution.py:342
  28.9 5.2 %collective-permute-start.8 = (f32[8,128]{1,0:T(8,128)S(1)}, f32[8,128]{1,0:T(8,128)S(1)}, u32[]{:S(2)}, u32[]{:S(2)}) collective-permute-start(f32[8,128]{1,0:T(8,128)S(1)} %shard_map.84.s0.stats_ref), channel_id=1, source_target_pairs={{0,32},{2,34},{4,36},{6,38},{8,40},{10,42},{12,44},{14,46},{16,48}... | collective-permute-start | bytes 12296 | tf_op jit(solution)/shard_map/ppermute | solution.py:342
  31.8 3.7 %collective-permute-start.7 = (f32[8,128]{1,0:T(8,128)S(1)}, f32[8,128]{1,0:T(8,128)S(1)}, u32[]{:S(2)}, u32[]{:S(2)}) collective-permute-start(f32[8,128]{1,0:T(8,128)S(1)} %shard_map.84.s0.stats_ref), channel_id=1, source_target_pairs={{0,16},{2,50},{4,20},{6,54},{8,24},{10,58},{12,28},{14,62},{16,32}... | collective-permute-start | bytes 12296 | tf_op jit(solution)/shard_map/ppermute | solution.py:342
  31.9 16.8 %collective-permute-start.11 = (bf16[1280,128]{1,0:T(8,128)(2,1)S(1)}, bf16[1280,128]{1,0:T(8,128)(2,1)S(1)}, u32[]{:S(2)}, u32[]{:S(2)}) collective-permute-start(bf16[1280,128]{1,0:T(8,128)(2,1)S(1)} %shard_map.86.refs_1_.refs_2_), channel_id=1, source_target_pairs={{0,48},{2,18},{4,52},{6,22},{8,56},{10,26},{12,60},{14,30},{16,0},... | collective-permute-start | bytes 983048 | tf_op jit(solution)/shard_map/ppermute | solution.py:342
  34.0 15.2 %collective-permute-start.10 = (bf16[1280,128]{1,0:T(8,128)(2,1)S(1)}, bf16[1280,128]{1,0:T(8,128)(2,1)S(1)}, u32[]{:S(2)}, u32[]{:S(2)}) collective-permute-start(bf16[1280,128]{1,0:T(8,128)(2,1)S(1)} %shard_map.86.refs_1_.refs_2_), channel_id=1, source_target_pairs={{0,16},{2,50},{4,20},{6,54},{8,24},{10,58},{12,28},{14,62},{16,32}... | collective-permute-start | bytes 983048 | tf_op jit(solution)/shard_map/ppermute | solution.py:342
  35.5 13.7 %collective-permute-start.12 = (bf16[1280,128]{1,0:T(8,128)(2,1)S(1)}, bf16[1280,128]{1,0:T(8,128)(2,1)S(1)}, u32[]{:S(2)}, u32[]{:S(2)}) collective-permute-start(bf16[1280,128]{1,0:T(8,128)(2,1)S(1)} %shard_map.86.refs_1_.refs_2_), channel_id=1, source_target_pairs={{0,32},{2,34},{4,36},{6,38},{8,40},{10,42},{12,44},{14,46},{16,48}... | collective-permute-start | bytes 983048 | tf_op jit(solution)/shard_map/ppermute | solution.py:342
  40.3 8.3 %collective-permute-start.13 = (bf16[720,128]{1,0:T(8,128)(2,1)S(1)}, bf16[720,128]{1,0:T(8,128)(2,1)S(1)}, u32[]{:S(2)}, u32[]{:S(2)}) collective-permute-start(bf16[720,128]{1,0:T(8,128)(2,1)S(1)} %get-tuple-element.59), channel_id=1, source_target_pairs={{0,4},{2,14},{4,8},{6,2},{8,12},{10,6},{12,0},{14,10},{16,20},{18,... | collective-permute-start | bytes 552968 | tf_op jit(solution)/shard_map/ppermute | solution.py:342
  40.6 11.5 %collective-permute-start.18 = (bf16[720,128]{1,0:T(8,128)(2,1)S(1)}, bf16[720,128]{1,0:T(8,128)(2,1)S(1)}, u32[]{:S(2)}, u32[]{:S(2)}) collective-permute-start(bf16[720,128]{1,0:T(8,128)(2,1)S(1)} %get-tuple-element.64), channel_id=1, source_target_pairs={{0,8},{2,10},{4,12},{6,14},{8,0},{10,2},{12,4},{14,6},{16,24},{18,... | collective-permute-start | bytes 552968 | tf_op jit(solution)/shard_map/ppermute | solution.py:342
  48.6 3.5 %collective-permute-start.14 = (bf16[1280,128]{1,0:T(8,128)(2,1)S(1)}, bf16[1280,128]{1,0:T(8,128)(2,1)S(1)}, u32[]{:S(2)}, u32[]{:S(2)}) collective-permute-start(bf16[1280,128]{1,0:T(8,128)(2,1)S(1)} %shard_map.86.refs_1_.refs_2_), channel_id=1, source_target_pairs={{0,2},{2,0},{4,6},{6,4},{8,10},{10,8},{12,14},{14,12},{16,18},{18,... | collective-permute-start | bytes 983048 | tf_op jit(solution)/shard_map/ppermute | solution.py:342
  48.6 3.5 %collective-permute-start.16 = (bf16[1280,128]{1,0:T(8,128)(2,1)S(1)}, bf16[1280,128]{1,0:T(8,128)(2,1)S(1)}, u32[]{:S(2)}, u32[]{:S(2)}) collective-permute-start(bf16[1280,128]{1,0:T(8,128)(2,1)S(1)} %collective-permute-done.11.refs_3_.refs_4_), channel_id=1, source_target_pairs={{0,2},{2,0},{4,6},{6,4},{8,10},{10,8},{12,14},{14,12},{16,18},{18,... | collective-permute-start | bytes 983048 | tf_op jit(solution)/shard_map/ppermute | solution.py:342
  49.1 3.0 %collective-permute-start.15 = (bf16[1280,128]{1,0:T(8,128)(2,1)S(1)}, bf16[1280,128]{1,0:T(8,128)(2,1)S(1)}, u32[]{:S(2)}, u32[]{:S(2)}) collective-permute-start(bf16[1280,128]{1,0:T(8,128)(2,1)S(1)} %collective-permute-done.10.refs_2_.refs_3_), channel_id=1, source_target_pairs={{0,2},{2,0},{4,6},{6,4},{8,10},{10,8},{12,14},{14,12},{16,18},{18,... | collective-permute-start | bytes 983048 | tf_op jit(solution)/shard_map/ppermute | solution.py:342
  49.2 2.9 %collective-permute-start.17 = (bf16[1280,128]{1,0:T(8,128)(2,1)S(1)}, bf16[1280,128]{1,0:T(8,128)(2,1)S(1)}, u32[]{:S(2)}, u32[]{:S(2)}) collective-permute-start(bf16[1280,128]{1,0:T(8,128)(2,1)S(1)} %collective-permute-done.12.refs_4_.refs_5_), channel_id=1, source_target_pairs={{0,2},{2,0},{4,6},{6,4},{8,10},{10,8},{12,14},{14,12},{16,18},{18,... | collective-permute-start | bytes 983048 | tf_op jit(solution)/shard_map/ppermute | solution.py:342
  52.1 10.7 %collective-permute-start.21 = (bf16[720,128]{1,0:T(8,128)(2,1)S(1)}, bf16[720,128]{1,0:T(8,128)(2,1)S(1)}, u32[]{:S(2)}, u32[]{:S(2)}) collective-permute-start(bf16[720,128]{1,0:T(8,128)(2,1)S(1)} %get-tuple-element.68), channel_id=1, source_target_pairs={{0,12},{2,6},{4,0},{6,10},{8,4},{10,14},{12,8},{14,2},{16,28},{18,... | collective-permute-start | bytes 552968 | tf_op jit(solution)/shard_map/ppermute | solution.py:342
  58.7 11.1 %collective-permute-start.19 = (bf16[640,128]{1,0:T(8,128)(2,1)S(1)}, bf16[640,128]{1,0:T(8,128)(2,1)S(1)}, u32[]{:S(2)}, u32[]{:S(2)}) collective-permute-start(bf16[640,128]{1,0:T(8,128)(2,1)S(1)} %get-tuple-element.65), channel_id=1, source_target_pairs={{0,12},{2,6},{4,0},{6,10},{8,4},{10,14},{12,8},{14,2},{16,28},{18,... | collective-permute-start | bytes 491528 | tf_op jit(solution)/shard_map/ppermute | solution.py:342
  60.8 9.0 %collective-permute-start.20 = (bf16[640,128]{1,0:T(8,128)(2,1)S(1)}, bf16[640,128]{1,0:T(8,128)(2,1)S(1)}, u32[]{:S(2)}, u32[]{:S(2)}) collective-permute-start(bf16[640,128]{1,0:T(8,128)(2,1)S(1)} %get-tuple-element.66), channel_id=1, source_target_pairs={{0,8},{2,10},{4,12},{6,14},{8,0},{10,2},{12,4},{14,6},{16,24},{18,... | collective-permute-start | bytes 491528 | tf_op jit(solution)/shard_map/ppermute | solution.py:342
  66.3 6.6 %collective-permute-start.22 = (bf16[640,128]{1,0:T(8,128)(2,1)S(1)}, bf16[640,128]{1,0:T(8,128)(2,1)S(1)}, u32[]{:S(2)}, u32[]{:S(2)}) collective-permute-start(bf16[640,128]{1,0:T(8,128)(2,1)S(1)} %shard_map.89), channel_id=1, source_target_pairs={{0,4},{2,14},{4,8},{6,2},{8,12},{10,6},{12,0},{14,10},{16,20},{18,... | collective-permute-start | bytes 491528 | tf_op jit(solution)/shard_map/ppermute | solution.py:342

commit v8 on v6

--- a/solution.py
+++ b/solution.py
@@ -399,10 +399,10 @@
     (stats,) = call(stats_kernel, [VMEM] * 4, [((8, LANES), f32)], *parts)
     y_stats = [stats] + [shift(stats, "y", k, cores=(1,)) for k in (1, 2, 3)]
     (piece,) = call(piece_kernel, [VMEM] * 5, [table], stats, *parts)
-    pieces = [piece, shift(piece, "y", 1), shift(piece, "y", 3)]
     (stats,) = call(all_stats_kernel, [VMEM] * 4, [((8, LANES), f32)], *y_stats)
-    pieces.append(shift(after(piece, stats), "y", 2))
-    both_stats = [stats, shift(stats, "core", 1, cores=(1,))]
+    late = after(piece, stats)
+    pieces = [piece] + [shift(late, "y", k) for k in (1, 3, 2)]
+    both_stats = [stats, shift(stats, "core", 1)]
     *queries, fresh = call(
         project_kernel,
         [SMEM] + [VMEM] * 6,

time: 79.9 us -> 81.5 us (1.020)
  starting transfers between devices: 33.8 us -> 39 us
  waiting for transfers between devices: 18 us -> 14 us
    ppermute x24, starting transfers between devices: 33.8 us -> 39 us  [shift(): return lax.ppermute(array, 'patch', pairs)]
    ppermute x24, waiting for transfers between devices: 18 us -> 14 us  [shift(): return lax.ppermute(array, 'patch', pairs)]
  transfers between devices with their start and end apart: 24 -> 24, of which waited for: 7 -> 7; matrix products, arithmetic and copies ran while one was open for 0% -> 0% of each run, Pallas kernels for 27% -> 26%
where the time goes in v8:
time: 81.5 us; the launch traced here: 80.6 us
  starting transfers between devices  39 us (48%)
  Pallas kernels  23.4 us (29%)
  waiting for transfers between devices  14 us (17%)
  local copies, waits for them, and re-layouts  3.36 us (4%)
  between operations  0.84 us (1%)
    ppermute x24, starting transfers between devices, shift(): return lax.ppermute(array, 'patch', pairs)  39 us
    pallas_call x15, Pallas kernels, call(): pl.pallas_call(kernel, in_specs=ins, out_specs=[VMEM] * len(outs), out_sh...  23.4 us
    ppermute x24, waiting for transfers between devices, shift(): return lax.ppermute(array, 'patch', pairs)  14 us
    unnamed x8, local copies, waits for them, and re-layouts  3.36 us
  transfers between devices with their start and end apart: 24, of which 7 were waited for; matrix products, arithmetic and copies ran while one was open for 0% of the time, Pallas kernels for 26%

profile of v8, /device:TPU:32, one launch (start us, length us, event | category | flops | bytes accessed | tf_op | source)
XLA Modules:
  0.0 80.6 jit_solution(16464472733385401746)
XLA Ops:
  0.6 1.1 %copy-done = bf16[1,256,1280]{2,1,0:T(8,128)(2,1)S(1)} copy-done((bf16[1,256,1280]{2,1,0:T(8,128)(2,1)S(1)}, bf16[1,256,1280]{2,1,0:T(8,128)(2,1)}, u32[]{:S(2)}) %copy-start) | copy-done | bytes 655384
  1.7 1.0 %shard_map.77 = (f32[8,128]{1,0:T(8,128)S(1)}, bf16[256,1280]{1,0:T(8,128)(2,1)S(1)}) custom-call(bf16[256,1280]{1,0:T(8,128)(2,1)S(1)} %bitcast.5), custom_call_target="tpu_custom_call" | custom-call | flops 1 | bytes 1 | tf_op jit(solution)/shard_map/pallas_call | solution.py:328
  2.8 0.9 %copy-done.1 = bf16[1,16,2560]{2,1,0:T(8,128)(2,1)S(1)} copy-done((bf16[1,16,2560]{2,1,0:T(8,128)(2,1)S(1)}, bf16[1,16,2560]{2,1,0:T(8,128)(2,1)}, u32[]{:S(2)}) %copy-start.1) | copy-done | bytes 81944
  4.0 1.6 %collective-permute-start.1 = (bf16[96,128]{1,0:T(8,128)(2,1)S(1)}, bf16[96,128]{1,0:T(8,128)(2,1)S(1)}, u32[]{:S(2)}, u32[]{:S(2)}) collective-permute-start(bf16[96,128]{1,0:T(8,128)(2,1)S(1)} %get-tuple-element.39), channel_id=1, source_target_pairs={{0,4},{2,6},{4,8},{6,10},{8,12},{10,14},{12,0},{14,2},{16,20},{18,... | collective-permute-start | bytes 73736 | tf_op jit(solution)/shard_map/ppermute | solution.py:349
  5.5 2.7 %collective-permute-start.2 = (bf16[96,128]{1,0:T(8,128)(2,1)S(1)}, bf16[96,128]{1,0:T(8,128)(2,1)S(1)}, u32[]{:S(2)}, u32[]{:S(2)}) collective-permute-start(bf16[96,128]{1,0:T(8,128)(2,1)S(1)} %get-tuple-element.40), channel_id=1, source_target_pairs={{0,8},{2,10},{4,12},{6,14},{8,0},{10,2},{12,4},{14,6},{16,24},{18,... | collective-permute-start | bytes 73736 | tf_op jit(solution)/shard_map/ppermute | solution.py:349
  8.3 1.4 %collective-permute-start.3 = (bf16[96,128]{1,0:T(8,128)(2,1)S(1)}, bf16[96,128]{1,0:T(8,128)(2,1)S(1)}, u32[]{:S(2)}, u32[]{:S(2)}) collective-permute-start(bf16[96,128]{1,0:T(8,128)(2,1)S(1)} %get-tuple-element.41), channel_id=1, source_target_pairs={{0,12},{2,14},{4,0},{6,2},{8,4},{10,6},{12,8},{14,10},{16,28},{18,... | collective-permute-start | bytes 73736 | tf_op jit(solution)/shard_map/ppermute | solution.py:349
  9.7 0.7 copy-done.2
  10.4 0.7 copy-done.3
  11.1 1.0 %collective-permute-done.3.refs_3_ = bf16[96,128]{1,0:T(8,128)(2,1)S(1)} collective-permute-done((bf16[96,128]{1,0:T(8,128)(2,1)S(1)}, bf16[96,128]{1,0:T(8,128)(2,1)S(1)}, u32[]{:S(2)}, u32[]{:S(2)}) %collective-permute-start.3) | collective-permute-done | bytes 24608 | tf_op jit(solution)/shard_map/ppermute | solution.py:349
  12.1 3.3 %collective-permute-start.6 = (bf16[336,128]{1,0:T(8,128)(2,1)S(1)}, bf16[336,128]{1,0:T(8,128)(2,1)S(1)}, u32[]{:S(2)}, u32[]{:S(2)}) collective-permute-start(bf16[336,128]{1,0:T(8,128)(2,1)S(1)} %shard_map.81.refs_0_), channel_id=1, source_target_pairs={{0,64},{2,66},{4,68},{6,70},{8,72},{10,74},{12,76},{14,78},{16,80}... | collective-permute-start | bytes 258056 | tf_op jit(solution)/shard_map/ppermute | solution.py:349
  15.5 2.2 %collective-permute-start.5 = (bf16[336,128]{1,0:T(8,128)(2,1)S(1)}, bf16[336,128]{1,0:T(8,128)(2,1)S(1)}, u32[]{:S(2)}, u32[]{:S(2)}) collective-permute-start(bf16[336,128]{1,0:T(8,128)(2,1)S(1)} %shard_map.81.refs_0_), channel_id=1, source_target_pairs={{0,192},{2,194},{4,196},{6,198},{8,200},{10,202},{12,204},{14,206}... | collective-permute-start | bytes 258056 | tf_op jit(solution)/shard_map/ppermute | solution.py:349
  17.7 4.9 %collective-permute-start.4 = (bf16[336,128]{1,0:T(8,128)(2,1)S(1)}, bf16[336,128]{1,0:T(8,128)(2,1)S(1)}, u32[]{:S(2)}, u32[]{:S(2)}) collective-permute-start(bf16[336,128]{1,0:T(8,128)(2,1)S(1)} %shard_map.81.refs_0_), channel_id=1, source_target_pairs={{0,128},{2,130},{4,132},{6,134},{8,136},{10,138},{12,140},{14,142}... | collective-permute-start | bytes 258056 | tf_op jit(solution)/shard_map/ppermute | solution.py:349
  22.6 1.9 %shard_map.82.query_ref = bf16[1280,1280]{1,0:T(8,128)(2,1)S(1)} custom-call(bf16[1280,1280]{1,0:T(8,128)(2,1)} %source_hbm), custom_call_target="tpu_custom_call" | custom-call | flops 1 | bytes 1 | tf_op jit(solution)/shard_map/pallas_call | solution.py:328
  24.6 2.9 %shard_map.83.pair_ref = bf16[1280,2560]{1,0:T(8,128)(2,1)S(1)} custom-call(bf16[1280,2560]{1,0:T(8,128)(2,1)} %source_hbm.1), custom_call_target="tpu_custom_call" | custom-call | flops 1 | bytes 1 | tf_op jit(solution)/shard_map/pallas_call | solution.py:328
  27.5 1.2 %collective-permute-done.4.refs_1_ = bf16[336,128]{1,0:T(8,128)(2,1)S(1)} collective-permute-done((bf16[336,128]{1,0:T(8,128)(2,1)S(1)}, bf16[336,128]{1,0:T(8,128)(2,1)S(1)}, u32[]{:S(2)}, u32[]{:S(2)}) %collective-permute-start.4) | collective-permute-done | bytes 86048 | tf_op jit(solution)/shard_map/ppermute | solution.py:349
  29.3 0.7 collective-permute-start.8
  30.7 3.3 %collective-permute-start.13 = (bf16[1280,128]{1,0:T(8,128)(2,1)S(1)}, bf16[1280,128]{1,0:T(8,128)(2,1)S(1)}, u32[]{:S(2)}, u32[]{:S(2)}) collective-permute-start(bf16[1280,128]{1,0:T(8,128)(2,1)S(1)} %shard_map.87.refs_1_.refs_2_), channel_id=1, source_target_pairs={{0,32},{2,34},{4,36},{6,38},{8,40},{10,42},{12,44},{14,46},{16,48}... | collective-permute-start | bytes 983048 | tf_op jit(solution)/shard_map/ppermute | solution.py:349
  34.0 1.1 %collective-permute-start.12 = (bf16[1280,128]{1,0:T(8,128)(2,1)S(1)}, bf16[1280,128]{1,0:T(8,128)(2,1)S(1)}, u32[]{:S(2)}, u32[]{:S(2)}) collective-permute-start(bf16[1280,128]{1,0:T(8,128)(2,1)S(1)} %shard_map.87.refs_1_.refs_2_), channel_id=1, source_target_pairs={{0,48},{2,50},{4,52},{6,54},{8,56},{10,58},{12,60},{14,62},{16,0},... | collective-permute-start | bytes 983048 | tf_op jit(solution)/shard_map/ppermute | solution.py:349
  35.1 1.0 %collective-permute-start.11 = (bf16[1280,128]{1,0:T(8,128)(2,1)S(1)}, bf16[1280,128]{1,0:T(8,128)(2,1)S(1)}, u32[]{:S(2)}, u32[]{:S(2)}) collective-permute-start(bf16[1280,128]{1,0:T(8,128)(2,1)S(1)} %shard_map.87.refs_1_.refs_2_), channel_id=1, source_target_pairs={{0,16},{2,18},{4,20},{6,22},{8,24},{10,26},{12,28},{14,30},{16,32}... | collective-permute-start | bytes 983048 | tf_op jit(solution)/shard_map/ppermute | solution.py:349
  36.0 6.6 %collective-permute-start.10 = (f32[8,128]{1,0:T(8,128)S(1)}, f32[8,128]{1,0:T(8,128)S(1)}, u32[]{:S(2)}, u32[]{:S(2)}) collective-permute-start(f32[8,128]{1,0:T(8,128)S(1)} %shard_map.85.own_ref), channel_id=1, source_target_pairs={{0,2},{2,0},{4,6},{6,4},{8,10},{10,8},{12,14},{14,12},{16,18},{18,... | collective-permute-start | bytes 12296 | tf_op jit(solution)/shard_map/ppermute | solution.py:349
  42.6 0.8 %collective-permute-done.10.other_ref = f32[8,128]{1,0:T(8,128)S(1)} collective-permute-done((f32[8,128]{1,0:T(8,128)S(1)}, f32[8,128]{1,0:T(8,128)S(1)}, u32[]{:S(2)}, u32[]{:S(2)}) %collective-permute-start.10) | collective-permute-done | bytes 4128 | tf_op jit(solution)/shard_map/ppermute | solution.py:349
  43.4 2.9 %shard_map.86 = (bf16[720,128]{1,0:T(8,128)(2,1)S(1)}, bf16[720,128]{1,0:T(8,128)(2,1)S(1)}, bf16[720,128]{1,0:T(8,128)(2,1)S(1)}, bf16[720,128]{1,0:T(8,128)(2,1)S(1)}, bf16[16,2560]{1,0:T(8,128)(2,1)}) custom-call(s32[1]{0:T(128)} %bitcast.place_ref, bf16[256,1280]{1,0:T(8,128)(2,1)S(1)} %get-tuple-element.36.tokens_ref, f32[8,128]{1,0:T(8,128)S(1)} %shard_map.85.own_ref, ...), custom_call_target="tpu_custom_call" | custom-call | flops 1 | bytes 1 | tf_op jit(solution)/shard_map/pallas_call | solution.py:328
  46.7 3.2 %collective-permute-start.19 = (bf16[720,128]{1,0:T(8,128)(2,1)S(1)}, bf16[720,128]{1,0:T(8,128)(2,1)S(1)}, u32[]{:S(2)}, u32[]{:S(2)}) collective-permute-start(bf16[720,128]{1,0:T(8,128)(2,1)S(1)} %get-tuple-element.64), channel_id=1, source_target_pairs={{0,8},{2,10},{4,12},{6,14},{8,0},{10,2},{12,4},{14,6},{16,24},{18,... | collective-permute-start | bytes 552968 | tf_op jit(solution)/shard_map/ppermute | solution.py:349
  50.0 4.7 %collective-permute-done.14.refs_1_ = bf16[720,128]{1,0:T(8,128)(2,1)S(1)} collective-permute-done((bf16[720,128]{1,0:T(8,128)(2,1)S(1)}, bf16[720,128]{1,0:T(8,128)(2,1)S(1)}, u32[]{:S(2)}, u32[]{:S(2)}) %collective-permute-start.14) | collective-permute-done | bytes 184352 | tf_op jit(solution)/shard_map/ppermute | solution.py:349
  55.7 3.1 %collective-permute-done.19.refs_0_ = bf16[720,128]{1,0:T(8,128)(2,1)S(1)} collective-permute-done((bf16[720,128]{1,0:T(8,128)(2,1)S(1)}, bf16[720,128]{1,0:T(8,128)(2,1)S(1)}, u32[]{:S(2)}, u32[]{:S(2)}) %collective-permute-start.19) | collective-permute-done | bytes 184352 | tf_op jit(solution)/shard_map/ppermute | solution.py:349
  58.8 6.5 %shard_map.89 = (bf16[640,128]{1,0:T(8,128)(2,1)S(1)}, bf16[640,128]{1,0:T(8,128)(2,1)S(1)}) custom-call(s32[1]{0:T(128)} %bitcast.place_ref, bf16[720,128]{1,0:T(8,128)(2,1)S(1)} %collective-permute-done.19.refs_0_, bf16[720,128]{1,0:T(8,128)(2,1)S(1)} %collective-permute-done.14.refs_1_, bf16[1280,128]{1,0:T(8,128)(2,1)S(1)} %shard_map.87.refs_1_.refs_2_, ...), custom_call_target="tpu_custom_call" | custom-call | flops 1 | bytes 1 | tf_op jit(solution)/shard_map/pallas_call | solution.py:328
  65.4 0.9 %collective-permute-start.20 = (bf16[640,128]{1,0:T(8,128)(2,1)S(1)}, bf16[640,128]{1,0:T(8,128)(2,1)S(1)}, u32[]{:S(2)}, u32[]{:S(2)}) collective-permute-start(bf16[640,128]{1,0:T(8,128)(2,1)S(1)} %get-tuple-element.65), channel_id=1, source_target_pairs={{0,12},{2,14},{4,0},{6,2},{8,4},{10,6},{12,8},{14,10},{16,28},{18,... | collective-permute-start | bytes 491528 | tf_op jit(solution)/shard_map/ppermute | solution.py:349
  66.3 3.2 %collective-permute-start.21 = (bf16[640,128]{1,0:T(8,128)(2,1)S(1)}, bf16[640,128]{1,0:T(8,128)(2,1)S(1)}, u32[]{:S(2)}, u32[]{:S(2)}) collective-permute-start(bf16[640,128]{1,0:T(8,128)(2,1)S(1)} %get-tuple-element.66), channel_id=1, source_target_pairs={{0,8},{2,10},{4,12},{6,14},{8,0},{10,2},{12,4},{14,6},{16,24},{18,... | collective-permute-start | bytes 491528 | tf_op jit(solution)/shard_map/ppermute | solution.py:349
  69.5 3.5 %shard_map.90 = bf16[640,128]{1,0:T(8,128)(2,1)S(1)} custom-call(s32[1]{0:T(128)} %bitcast.place_ref, bf16[720,128]{1,0:T(8,128)(2,1)S(1)} %collective-permute-done.22.refs_0_, bf16[1280,128]{1,0:T(8,128)(2,1)S(1)} %shard_map.87.refs_1_.refs_2_, bf16[1280,128]{1,0:T(8,128)(2,1)S(1)} %collective-permute-done.11.refs_2_.refs_3_, ...), custom_call_target="tpu_custom_call" | custom-call | flops 1 | bytes 1 | tf_op jit(solution)/shard_map/pallas_call | solution.py:328
  73.1 3.5 %shard_map.88.refs_0_ = bf16[640,128]{1,0:T(8,128)(2,1)S(1)} custom-call(s32[1]{0:T(128)} %bitcast.place_ref, bf16[720,128]{1,0:T(8,128)(2,1)S(1)} %get-tuple-element.57.refs_0_, bf16[1280,128]{1,0:T(8,128)(2,1)S(1)} %shard_map.87.refs_1_.refs_2_, bf16[1280,128]{1,0:T(8,128)(2,1)S(1)} %collective-permute-done.11.refs_2_.refs_3_, ...), custom_call_target="tpu_custom_call" | custom-call | flops 1 | bytes 1 | tf_op jit(solution)/shard_map/pallas_call | solution.py:328
  76.6 3.0 %collective-permute-done.23.refs_3_ = bf16[640,128]{1,0:T(8,128)(2,1)S(1)} collective-permute-done((bf16[640,128]{1,0:T(8,128)(2,1)S(1)}, bf16[640,128]{1,0:T(8,128)(2,1)S(1)}, u32[]{:S(2)}, u32[]{:S(2)}) %collective-permute-start.23) | collective-permute-done | bytes 163872 | tf_op jit(solution)/shard_map/ppermute | solution.py:349
  79.6 1.0 %shard_map.91 = bf16[256,1280]{1,0:T(8,128)(2,1)} custom-call(s32[1]{0:T(128)} %bitcast.place_ref, bf16[640,128]{1,0:T(8,128)(2,1)S(1)} %shard_map.88.refs_0_, bf16[640,128]{1,0:T(8,128)(2,1)S(1)} %collective-permute-done.20.refs_1_, bf16[640,128]{1,0:T(8,128)(2,1)S(1)} %collective-permute-done.21.refs_2_, bf16[640,128]{1,0:T(8,128)(2,1)S(1)} %collective-permute-done.23.refs_3_), custom_call_target="tpu_custom_call" | custom-call | flops 1 | bytes 1 | tf_op jit(solution)/shard_map/pallas_call | solution.py:328
  (39 shorter events, 3.3 us)
Async XLA Ops:
  0.6 1.1 %copy-start = (bf16[1,256,1280]{2,1,0:T(8,128)(2,1)S(1)}, bf16[1,256,1280]{2,1,0:T(8,128)(2,1)}, u32[]{:S(2)}) copy-start(bf16[1,256,1280]{2,1,0:T(8,128)(2,1)} %param.6) | copy-start | bytes 1966084
  2.7 1.2 %collective-permute-start = (f32[8,128]{1,0:T(8,128)S(1)}, f32[8,128]{1,0:T(8,128)S(1)}, u32[]{:S(2)}, u32[]{:S(2)}) collective-permute-start(f32[8,128]{1,0:T(8,128)S(1)} %get-tuple-element.37.stats_ref.own_ref), channel_id=1, source_target_pairs={{0,2},{2,0},{4,6},{6,4},{8,10},{10,8},{12,14},{14,12},{16,18},{18,... | collective-permute-start | bytes 12296 | tf_op jit(solution)/shard_map/ppermute | solution.py:349
  2.8 0.9 %copy-start.1 = (bf16[1,16,2560]{2,1,0:T(8,128)(2,1)S(1)}, bf16[1,16,2560]{2,1,0:T(8,128)(2,1)}, u32[]{:S(2)}) copy-start(bf16[1,16,2560]{2,1,0:T(8,128)(2,1)} %param.7) | copy-start | bytes 245764
  4.0 7.1 %collective-permute-start.1 = (bf16[96,128]{1,0:T(8,128)(2,1)S(1)}, bf16[96,128]{1,0:T(8,128)(2,1)S(1)}, u32[]{:S(2)}, u32[]{:S(2)}) collective-permute-start(bf16[96,128]{1,0:T(8,128)(2,1)S(1)} %get-tuple-element.39), channel_id=1, source_target_pairs={{0,4},{2,6},{4,8},{6,10},{8,12},{10,14},{12,0},{14,2},{16,20},{18,... | collective-permute-start | bytes 73736 | tf_op jit(solution)/shard_map/ppermute | solution.py:349
  5.5 5.6 %collective-permute-start.2 = (bf16[96,128]{1,0:T(8,128)(2,1)S(1)}, bf16[96,128]{1,0:T(8,128)(2,1)S(1)}, u32[]{:S(2)}, u32[]{:S(2)}) collective-permute-start(bf16[96,128]{1,0:T(8,128)(2,1)S(1)} %get-tuple-element.40), channel_id=1, source_target_pairs={{0,8},{2,10},{4,12},{6,14},{8,0},{10,2},{12,4},{14,6},{16,24},{18,... | collective-permute-start | bytes 73736 | tf_op jit(solution)/shard_map/ppermute | solution.py:349
  8.3 3.8 %collective-permute-start.3 = (bf16[96,128]{1,0:T(8,128)(2,1)S(1)}, bf16[96,128]{1,0:T(8,128)(2,1)S(1)}, u32[]{:S(2)}, u32[]{:S(2)}) collective-permute-start(bf16[96,128]{1,0:T(8,128)(2,1)S(1)} %get-tuple-element.41), channel_id=1, source_target_pairs={{0,12},{2,14},{4,0},{6,2},{8,4},{10,6},{12,8},{14,10},{16,28},{18,... | collective-permute-start | bytes 73736 | tf_op jit(solution)/shard_map/ppermute | solution.py:349
  9.7 0.7 copy-start.2
  10.4 0.7 copy-start.3
  12.1 15.3 %collective-permute-start.6 = (bf16[336,128]{1,0:T(8,128)(2,1)S(1)}, bf16[336,128]{1,0:T(8,128)(2,1)S(1)}, u32[]{:S(2)}, u32[]{:S(2)}) collective-permute-start(bf16[336,128]{1,0:T(8,128)(2,1)S(1)} %shard_map.81.refs_0_), channel_id=1, source_target_pairs={{0,64},{2,66},{4,68},{6,70},{8,72},{10,74},{12,76},{14,78},{16,80}... | collective-permute-start | bytes 258056 | tf_op jit(solution)/shard_map/ppermute | solution.py:349
  15.5 12.0 %collective-permute-start.5 = (bf16[336,128]{1,0:T(8,128)(2,1)S(1)}, bf16[336,128]{1,0:T(8,128)(2,1)S(1)}, u32[]{:S(2)}, u32[]{:S(2)}) collective-permute-start(bf16[336,128]{1,0:T(8,128)(2,1)S(1)} %shard_map.81.refs_0_), channel_id=1, source_target_pairs={{0,192},{2,194},{4,196},{6,198},{8,200},{10,202},{12,204},{14,206}... | collective-permute-start | bytes 258056 | tf_op jit(solution)/shard_map/ppermute | solution.py:349
  17.7 10.9 %collective-permute-start.4 = (bf16[336,128]{1,0:T(8,128)(2,1)S(1)}, bf16[336,128]{1,0:T(8,128)(2,1)S(1)}, u32[]{:S(2)}, u32[]{:S(2)}) collective-permute-start(bf16[336,128]{1,0:T(8,128)(2,1)S(1)} %shard_map.81.refs_0_), channel_id=1, source_target_pairs={{0,128},{2,130},{4,132},{6,134},{8,136},{10,138},{12,140},{14,142}... | collective-permute-start | bytes 258056 | tf_op jit(solution)/shard_map/ppermute | solution.py:349
  28.6 2.0 %collective-permute-start.9 = (f32[8,128]{1,0:T(8,128)S(1)}, f32[8,128]{1,0:T(8,128)S(1)}, u32[]{:S(2)}, u32[]{:S(2)}) collective-permute-start(f32[8,128]{1,0:T(8,128)S(1)} %shard_map.84.s0.stats_ref), channel_id=1, source_target_pairs={{2,50},{6,54},{10,58},{14,62},{18,2},{22,6},{26,10},{30,14},{34,18... | collective-permute-start | bytes 12296 | tf_op jit(solution)/shard_map/ppermute | solution.py:349
  29.3 1.4 %collective-permute-start.8 = (f32[8,128]{1,0:T(8,128)S(1)}, f32[8,128]{1,0:T(8,128)S(1)}, u32[]{:S(2)}, u32[]{:S(2)}) collective-permute-start(f32[8,128]{1,0:T(8,128)S(1)} %shard_map.84.s0.stats_ref), channel_id=1, source_target_pairs={{2,34},{6,38},{10,42},{14,46},{18,50},{22,54},{26,58},{30,62},{34,... | collective-permute-start | bytes 12296 | tf_op jit(solution)/shard_map/ppermute | solution.py:349
  30.0 0.7 collective-permute-start.7
  30.7 24.0 %collective-permute-start.13 = (bf16[1280,128]{1,0:T(8,128)(2,1)S(1)}, bf16[1280,128]{1,0:T(8,128)(2,1)S(1)}, u32[]{:S(2)}, u32[]{:S(2)}) collective-permute-start(bf16[1280,128]{1,0:T(8,128)(2,1)S(1)} %shard_map.87.refs_1_.refs_2_), channel_id=1, source_target_pairs={{0,32},{2,34},{4,36},{6,38},{8,40},{10,42},{12,44},{14,46},{16,48}... | collective-permute-start | bytes 983048 | tf_op jit(solution)/shard_map/ppermute | solution.py:349
  34.0 21.2 %collective-permute-start.12 = (bf16[1280,128]{1,0:T(8,128)(2,1)S(1)}, bf16[1280,128]{1,0:T(8,128)(2,1)S(1)}, u32[]{:S(2)}, u32[]{:S(2)}) collective-permute-start(bf16[1280,128]{1,0:T(8,128)(2,1)S(1)} %shard_map.87.refs_1_.refs_2_), channel_id=1, source_target_pairs={{0,48},{2,50},{4,52},{6,54},{8,56},{10,58},{12,60},{14,62},{16,0},... | collective-permute-start | bytes 983048 | tf_op jit(solution)/shard_map/ppermute | solution.py:349
  35.1 20.2 %collective-permute-start.11 = (bf16[1280,128]{1,0:T(8,128)(2,1)S(1)}, bf16[1280,128]{1,0:T(8,128)(2,1)S(1)}, u32[]{:S(2)}, u32[]{:S(2)}) collective-permute-start(bf16[1280,128]{1,0:T(8,128)(2,1)S(1)} %shard_map.87.refs_1_.refs_2_), channel_id=1, source_target_pairs={{0,16},{2,18},{4,20},{6,22},{8,24},{10,26},{12,28},{14,30},{16,32}... | collective-permute-start | bytes 983048 | tf_op jit(solution)/shard_map/ppermute | solution.py:349
  36.0 7.4 %collective-permute-start.10 = (f32[8,128]{1,0:T(8,128)S(1)}, f32[8,128]{1,0:T(8,128)S(1)}, u32[]{:S(2)}, u32[]{:S(2)}) collective-permute-start(f32[8,128]{1,0:T(8,128)S(1)} %shard_map.85.own_ref), channel_id=1, source_target_pairs={{0,2},{2,0},{4,6},{6,4},{8,10},{10,8},{12,14},{14,12},{16,18},{18,... | collective-permute-start | bytes 12296 | tf_op jit(solution)/shard_map/ppermute | solution.py:349
  46.4 8.3 %collective-permute-start.14 = (bf16[720,128]{1,0:T(8,128)(2,1)S(1)}, bf16[720,128]{1,0:T(8,128)(2,1)S(1)}, u32[]{:S(2)}, u32[]{:S(2)}) collective-permute-start(bf16[720,128]{1,0:T(8,128)(2,1)S(1)} %get-tuple-element.59), channel_id=1, source_target_pairs={{0,4},{2,6},{4,8},{6,10},{8,12},{10,14},{12,0},{14,2},{16,20},{18,... | collective-permute-start | bytes 552968 | tf_op jit(solution)/shard_map/ppermute | solution.py:349
  46.7 12.1 %collective-permute-start.19 = (bf16[720,128]{1,0:T(8,128)(2,1)S(1)}, bf16[720,128]{1,0:T(8,128)(2,1)S(1)}, u32[]{:S(2)}, u32[]{:S(2)}) collective-permute-start(bf16[720,128]{1,0:T(8,128)(2,1)S(1)} %get-tuple-element.64), channel_id=1, source_target_pairs={{0,8},{2,10},{4,12},{6,14},{8,0},{10,2},{12,4},{14,6},{16,24},{18,... | collective-permute-start | bytes 552968 | tf_op jit(solution)/shard_map/ppermute | solution.py:349
  54.7 4.1 %collective-permute-start.15 = (bf16[1280,128]{1,0:T(8,128)(2,1)S(1)}, bf16[1280,128]{1,0:T(8,128)(2,1)S(1)}, u32[]{:S(2)}, u32[]{:S(2)}) collective-permute-start(bf16[1280,128]{1,0:T(8,128)(2,1)S(1)} %shard_map.87.refs_1_.refs_2_), channel_id=1, source_target_pairs={{0,2},{2,0},{4,6},{6,4},{8,10},{10,8},{12,14},{14,12},{16,18},{18,... | collective-permute-start | bytes 983048 | tf_op jit(solution)/shard_map/ppermute | solution.py:349
  54.7 4.1 %collective-permute-start.18 = (bf16[1280,128]{1,0:T(8,128)(2,1)S(1)}, bf16[1280,128]{1,0:T(8,128)(2,1)S(1)}, u32[]{:S(2)}, u32[]{:S(2)}) collective-permute-start(bf16[1280,128]{1,0:T(8,128)(2,1)S(1)} %collective-permute-done.13.refs_4_.refs_5_), channel_id=1, source_target_pairs={{0,2},{2,0},{4,6},{6,4},{8,10},{10,8},{12,14},{14,12},{16,18},{18,... | collective-permute-start | bytes 983048 | tf_op jit(solution)/shard_map/ppermute | solution.py:349
  55.2 3.6 %collective-permute-start.17 = (bf16[1280,128]{1,0:T(8,128)(2,1)S(1)}, bf16[1280,128]{1,0:T(8,128)(2,1)S(1)}, u32[]{:S(2)}, u32[]{:S(2)}) collective-permute-start(bf16[1280,128]{1,0:T(8,128)(2,1)S(1)} %collective-permute-done.12.refs_3_.refs_4_), channel_id=1, source_target_pairs={{0,2},{2,0},{4,6},{6,4},{8,10},{10,8},{12,14},{14,12},{16,18},{18,... | collective-permute-start | bytes 983048 | tf_op jit(solution)/shard_map/ppermute | solution.py:349
  55.3 3.5 %collective-permute-start.16 = (bf16[1280,128]{1,0:T(8,128)(2,1)S(1)}, bf16[1280,128]{1,0:T(8,128)(2,1)S(1)}, u32[]{:S(2)}, u32[]{:S(2)}) collective-permute-start(bf16[1280,128]{1,0:T(8,128)(2,1)S(1)} %collective-permute-done.11.refs_2_.refs_3_), channel_id=1, source_target_pairs={{0,2},{2,0},{4,6},{6,4},{8,10},{10,8},{12,14},{14,12},{16,18},{18,... | collective-permute-start | bytes 983048 | tf_op jit(solution)/shard_map/ppermute | solution.py:349
  58.8 10.7 %collective-permute-start.22 = (bf16[720,128]{1,0:T(8,128)(2,1)S(1)}, bf16[720,128]{1,0:T(8,128)(2,1)S(1)}, u32[]{:S(2)}, u32[]{:S(2)}) collective-permute-start(bf16[720,128]{1,0:T(8,128)(2,1)S(1)} %get-tuple-element.68), channel_id=1, source_target_pairs={{0,12},{2,14},{4,0},{6,2},{8,4},{10,6},{12,8},{14,10},{16,28},{18,... | collective-permute-start | bytes 552968 | tf_op jit(solution)/shard_map/ppermute | solution.py:349
  65.4 11.2 %collective-permute-start.20 = (bf16[640,128]{1,0:T(8,128)(2,1)S(1)}, bf16[640,128]{1,0:T(8,128)(2,1)S(1)}, u32[]{:S(2)}, u32[]{:S(2)}) collective-permute-start(bf16[640,128]{1,0:T(8,128)(2,1)S(1)} %get-tuple-element.65), channel_id=1, source_target_pairs={{0,12},{2,14},{4,0},{6,2},{8,4},{10,6},{12,8},{14,10},{16,28},{18,... | collective-permute-start | bytes 491528 | tf_op jit(solution)/shard_map/ppermute | solution.py:349
  66.3 10.3 %collective-permute-start.21 = (bf16[640,128]{1,0:T(8,128)(2,1)S(1)}, bf16[640,128]{1,0:T(8,128)(2,1)S(1)}, u32[]{:S(2)}, u32[]{:S(2)}) collective-permute-start(bf16[640,128]{1,0:T(8,128)(2,1)S(1)} %get-tuple-element.66), channel_id=1, source_target_pairs={{0,8},{2,10},{4,12},{6,14},{8,0},{10,2},{12,4},{14,6},{16,24},{18,... | collective-permute-start | bytes 491528 | tf_op jit(solution)/shard_map/ppermute | solution.py:349
  73.0 6.6 %collective-permute-start.23 = (bf16[640,128]{1,0:T(8,128)(2,1)S(1)}, bf16[640,128]{1,0:T(8,128)(2,1)S(1)}, u32[]{:S(2)}, u32[]{:S(2)}) collective-permute-start(bf16[640,128]{1,0:T(8,128)(2,1)S(1)} %shard_map.90), channel_id=1, source_target_pairs={{0,4},{2,6},{4,8},{6,10},{8,12},{10,14},{12,0},{14,2},{16,20},{18,... | collective-permute-start | bytes 491528 | tf_op jit(solution)/shard_map/ppermute | solution.py:349

commit v9 on v5

--- a/solution.py
+++ b/solution.py
@@ -20,6 +20,7 @@
 SET_ROWS = SET_HEADS * ROWS
 ANSWER_ROWS = SET_HEADS * CELLS // 2
 epsilon = 1e-05
+X_ORDER = (0, 1, 3, 2)
 
 f32 = jnp.float32
 bf16 = jnp.bfloat16
@@ -153,7 +154,7 @@
     *in_refs, out_ref = refs
     stats = [decode(ref[SET_ROWS:, :]) for ref in in_refs]
     mean, squares = combine(stats, 2 * CELLS * GROUP_WIDTH)
-    for k, ref in enumerate(in_refs):
+    for k, ref in zip(X_ORDER, in_refs):
         for h in range(SET_HEADS):
             low = h * 4 * ROWS + k * ROWS
             out_ref[low : low + ROWS, :] = ref[h * ROWS : (h + 1) * ROWS, :]
@@ -368,7 +369,7 @@
         other,
         sets,
     )
-    received = [messages[0]] + [shift(messages[k], "x", k) for k in (1, 2, 3)]
+    received = [messages[0]] + [shift(messages[k], "x", k) for k in X_ORDER[1:]]
     norm_gain, norm_bias, _ = lax.optimization_barrier((norm_gain, norm_bias, messages[0]))
     (affine,) = call(affine_kernel, [VMEM] * 2, [((2, WIDTH), f32)], norm_gain, norm_bias)
     received, affine = lax.optimization_barrier((received, affine))
@@ -389,7 +390,7 @@
     weights = weights[1::-1]
     parts, weights = lax.optimization_barrier((parts, weights))
     (stats,) = call(stats_kernel, [VMEM] * 4, [((8, LANES), f32)], *parts)
-    all_stats = [stats] + [shift(stats, "y", k) for k in (1, 2, 3)]
+    all_stats = [stats] + [shift(stats, "y", k) for k in (2, 3, 1)]
     (piece,) = call(piece_kernel, [VMEM] * 5, [table], stats, *parts)
     pieces = [piece, shift(piece, "y", 1), shift(piece, "y", 3)]
     pieces.append(shift(after(piece, *all_stats), "y", 2))

time: 73.5 us -> 74.3 us (1.011)
  waiting for transfers between devices: 11.3 us -> 14.5 us
  starting transfers between devices: 34.2 us -> 31.9 us
    ppermute x23, waiting for transfers between devices: 11.3 us -> 14.5 us  [permute(): return lax.ppermute(array, 'patch', pairs)]
    ppermute x23, starting transfers between devices: 34.2 us -> 31.9 us  [permute(): return lax.ppermute(array, 'patch', pairs)]
  transfers between devices with their start and end apart: 23 -> 23, of which waited for: 9 -> 10; matrix products, arithmetic and copies ran while one was open for 0% -> 0% of each run, Pallas kernels for 29% -> 29%
where the time goes in v9:
time: 74.3 us; the launch traced here: 74 us
  starting transfers between devices  31.9 us (43%)
  Pallas kernels  23.4 us (31%)
  waiting for transfers between devices  14.5 us (20%)
  local copies, waits for them, and re-layouts  3.36 us (5%)
  between operations  0.8 us (1%)
    ppermute x23, starting transfers between devices, permute(): return lax.ppermute(array, 'patch', pairs)  31.9 us
    pallas_call x14, Pallas kernels, call(): pl.pallas_call(kernel, in_specs=ins, out_specs=[VMEM] * len(outs), out_sh...  23.4 us
    ppermute x23, waiting for transfers between devices, permute(): return lax.ppermute(array, 'patch', pairs)  14.5 us
    unnamed x8, local copies, waits for them, and re-layouts  3.36 us
  transfers between devices with their start and end apart: 23, of which 10 were waited for; matrix products, arithmetic and copies ran while one was open for 0% of the time, Pallas kernels for 29%

profile of v9, /device:TPU:32, one launch (start us, length us, event | category | flops | bytes accessed | tf_op | source)
XLA Modules:
  0.0 74.0 jit_solution(11795298576300110175)
XLA Ops:
  0.6 1.1 %copy-done = bf16[1,256,1280]{2,1,0:T(8,128)(2,1)S(1)} copy-done((bf16[1,256,1280]{2,1,0:T(8,128)(2,1)S(1)}, bf16[1,256,1280]{2,1,0:T(8,128)(2,1)}, u32[]{:S(2)}) %copy-start) | copy-done | bytes 655384
  1.7 1.0 %shard_map.77 = (f32[8,128]{1,0:T(8,128)S(1)}, bf16[256,1280]{1,0:T(8,128)(2,1)S(1)}) custom-call(bf16[256,1280]{1,0:T(8,128)(2,1)S(1)} %bitcast.5), custom_call_target="tpu_custom_call" | custom-call | flops 1 | bytes 1 | tf_op jit(solution)/shard_map/pallas_call | solution.py:319
  2.8 0.9 %copy-done.1 = bf16[1,16,2560]{2,1,0:T(8,128)(2,1)S(1)} copy-done((bf16[1,16,2560]{2,1,0:T(8,128)(2,1)S(1)}, bf16[1,16,2560]{2,1,0:T(8,128)(2,1)}, u32[]{:S(2)}) %copy-start.1) | copy-done | bytes 81944
  4.0 1.6 %collective-permute-start.1 = (bf16[96,128]{1,0:T(8,128)(2,1)S(1)}, bf16[96,128]{1,0:T(8,128)(2,1)S(1)}, u32[]{:S(2)}, u32[]{:S(2)}) collective-permute-start(bf16[96,128]{1,0:T(8,128)(2,1)S(1)} %get-tuple-element.39), channel_id=1, source_target_pairs={{0,4},{2,6},{4,8},{6,10},{8,12},{10,14},{12,0},{14,2},{16,20},{18,... | collective-permute-start | bytes 73736 | tf_op jit(solution)/shard_map/ppermute | solution.py:335
  5.5 1.7 %collective-permute-start.2 = (bf16[96,128]{1,0:T(8,128)(2,1)S(1)}, bf16[96,128]{1,0:T(8,128)(2,1)S(1)}, u32[]{:S(2)}, u32[]{:S(2)}) collective-permute-start(bf16[96,128]{1,0:T(8,128)(2,1)S(1)} %get-tuple-element.40), channel_id=1, source_target_pairs={{0,12},{2,14},{4,0},{6,2},{8,4},{10,6},{12,8},{14,10},{16,28},{18,... | collective-permute-start | bytes 73736 | tf_op jit(solution)/shard_map/ppermute | solution.py:335
  7.3 1.8 %collective-permute-start.3 = (bf16[96,128]{1,0:T(8,128)(2,1)S(1)}, bf16[96,128]{1,0:T(8,128)(2,1)S(1)}, u32[]{:S(2)}, u32[]{:S(2)}) collective-permute-start(bf16[96,128]{1,0:T(8,128)(2,1)S(1)} %get-tuple-element.41), channel_id=1, source_target_pairs={{0,8},{2,10},{4,12},{6,14},{8,0},{10,2},{12,4},{14,6},{16,24},{18,... | collective-permute-start | bytes 73736 | tf_op jit(solution)/shard_map/ppermute | solution.py:335
  9.1 0.7 copy-done.2
  9.8 0.7 copy-done.3
  10.5 2.1 %collective-permute-done.3.refs_3_ = bf16[96,128]{1,0:T(8,128)(2,1)S(1)} collective-permute-done((bf16[96,128]{1,0:T(8,128)(2,1)S(1)}, bf16[96,128]{1,0:T(8,128)(2,1)S(1)}, u32[]{:S(2)}, u32[]{:S(2)}) %collective-permute-start.3) | collective-permute-done | bytes 24608 | tf_op jit(solution)/shard_map/ppermute | solution.py:335
  12.7 3.3 %collective-permute-start.6 = (bf16[336,128]{1,0:T(8,128)(2,1)S(1)}, bf16[336,128]{1,0:T(8,128)(2,1)S(1)}, u32[]{:S(2)}, u32[]{:S(2)}) collective-permute-start(bf16[336,128]{1,0:T(8,128)(2,1)S(1)} %shard_map.81.refs_0_), channel_id=1, source_target_pairs={{0,64},{2,66},{4,68},{6,70},{8,72},{10,74},{12,76},{14,78},{16,80}... | collective-permute-start | bytes 258056 | tf_op jit(solution)/shard_map/ppermute | solution.py:335
  16.0 2.2 %collective-permute-start.5 = (bf16[336,128]{1,0:T(8,128)(2,1)S(1)}, bf16[336,128]{1,0:T(8,128)(2,1)S(1)}, u32[]{:S(2)}, u32[]{:S(2)}) collective-permute-start(bf16[336,128]{1,0:T(8,128)(2,1)S(1)} %shard_map.81.refs_0_), channel_id=1, source_target_pairs={{0,192},{2,194},{4,196},{6,198},{8,200},{10,202},{12,204},{14,206}... | collective-permute-start | bytes 258056 | tf_op jit(solution)/shard_map/ppermute | solution.py:335
  18.2 4.9 %collective-permute-start.4 = (bf16[336,128]{1,0:T(8,128)(2,1)S(1)}, bf16[336,128]{1,0:T(8,128)(2,1)S(1)}, u32[]{:S(2)}, u32[]{:S(2)}) collective-permute-start(bf16[336,128]{1,0:T(8,128)(2,1)S(1)} %shard_map.81.refs_0_), channel_id=1, source_target_pairs={{0,128},{2,130},{4,132},{6,134},{8,136},{10,138},{12,140},{14,142}... | collective-permute-start | bytes 258056 | tf_op jit(solution)/shard_map/ppermute | solution.py:335
  23.2 1.9 %shard_map.82.query_ref = bf16[1280,1280]{1,0:T(8,128)(2,1)S(1)} custom-call(bf16[1280,1280]{1,0:T(8,128)(2,1)} %source_hbm), custom_call_target="tpu_custom_call" | custom-call | flops 1 | bytes 1 | tf_op jit(solution)/shard_map/pallas_call | solution.py:319
  25.1 2.9 %shard_map.83.pair_ref = bf16[1280,2560]{1,0:T(8,128)(2,1)S(1)} custom-call(bf16[1280,2560]{1,0:T(8,128)(2,1)} %source_hbm.1), custom_call_target="tpu_custom_call" | custom-call | flops 1 | bytes 1 | tf_op jit(solution)/shard_map/pallas_call | solution.py:319
  28.0 0.9 %collective-permute-done.4.refs_1_ = bf16[336,128]{1,0:T(8,128)(2,1)S(1)} collective-permute-done((bf16[336,128]{1,0:T(8,128)(2,1)S(1)}, bf16[336,128]{1,0:T(8,128)(2,1)S(1)}, u32[]{:S(2)}, u32[]{:S(2)}) %collective-permute-start.4) | collective-permute-done | bytes 86048 | tf_op jit(solution)/shard_map/ppermute | solution.py:335
  28.9 1.7 %collective-permute-start.9 = (f32[8,128]{1,0:T(8,128)S(1)}, f32[8,128]{1,0:T(8,128)S(1)}, u32[]{:S(2)}, u32[]{:S(2)}) collective-permute-start(f32[8,128]{1,0:T(8,128)S(1)} %shard_map.84.s0.stats_ref), channel_id=1, source_target_pairs={{0,16},{2,18},{4,20},{6,22},{8,24},{10,26},{12,28},{14,30},{16,32}... | collective-permute-start | bytes 12296 | tf_op jit(solution)/shard_map/ppermute | solution.py:335
  30.6 1.7 %collective-permute-start.8 = (f32[8,128]{1,0:T(8,128)S(1)}, f32[8,128]{1,0:T(8,128)S(1)}, u32[]{:S(2)}, u32[]{:S(2)}) collective-permute-start(f32[8,128]{1,0:T(8,128)S(1)} %shard_map.84.s0.stats_ref), channel_id=1, source_target_pairs={{0,48},{2,50},{4,52},{6,54},{8,56},{10,58},{12,60},{14,62},{16,0},... | collective-permute-start | bytes 12296 | tf_op jit(solution)/shard_map/ppermute | solution.py:335
  32.2 2.0 %collective-permute-start.7 = (f32[8,128]{1,0:T(8,128)S(1)}, f32[8,128]{1,0:T(8,128)S(1)}, u32[]{:S(2)}, u32[]{:S(2)}) collective-permute-start(f32[8,128]{1,0:T(8,128)S(1)} %shard_map.84.s0.stats_ref), channel_id=1, source_target_pairs={{0,32},{2,34},{4,36},{6,38},{8,40},{10,42},{12,44},{14,46},{16,48}... | collective-permute-start | bytes 12296 | tf_op jit(solution)/shard_map/ppermute | solution.py:335
  34.2 1.1 %collective-permute-start.11 = (bf16[1280,128]{1,0:T(8,128)(2,1)S(1)}, bf16[1280,128]{1,0:T(8,128)(2,1)S(1)}, u32[]{:S(2)}, u32[]{:S(2)}) collective-permute-start(bf16[1280,128]{1,0:T(8,128)(2,1)S(1)} %shard_map.86.refs_1_.refs_2_), channel_id=1, source_target_pairs={{0,48},{2,50},{4,52},{6,54},{8,56},{10,58},{12,60},{14,62},{16,0},... | collective-permute-start | bytes 983048 | tf_op jit(solution)/shard_map/ppermute | solution.py:335
  35.4 1.0 %collective-permute-start.10 = (bf16[1280,128]{1,0:T(8,128)(2,1)S(1)}, bf16[1280,128]{1,0:T(8,128)(2,1)S(1)}, u32[]{:S(2)}, u32[]{:S(2)}) collective-permute-start(bf16[1280,128]{1,0:T(8,128)(2,1)S(1)} %shard_map.86.refs_1_.refs_2_), channel_id=1, source_target_pairs={{0,16},{2,18},{4,20},{6,22},{8,24},{10,26},{12,28},{14,30},{16,32}... | collective-permute-start | bytes 983048 | tf_op jit(solution)/shard_map/ppermute | solution.py:335
  36.4 1.1 %collective-permute-done.7.s1 = f32[8,128]{1,0:T(8,128)S(1)} collective-permute-done((f32[8,128]{1,0:T(8,128)S(1)}, f32[8,128]{1,0:T(8,128)S(1)}, u32[]{:S(2)}, u32[]{:S(2)}) %collective-permute-start.7) | collective-permute-done | bytes 4128 | tf_op jit(solution)/shard_map/ppermute | solution.py:335
  37.5 2.0 %collective-permute-start.12 = (bf16[1280,128]{1,0:T(8,128)(2,1)S(1)}, bf16[1280,128]{1,0:T(8,128)(2,1)S(1)}, u32[]{:S(2)}, u32[]{:S(2)}) collective-permute-start(bf16[1280,128]{1,0:T(8,128)(2,1)S(1)} %shard_map.86.refs_1_.refs_2_), channel_id=1, source_target_pairs={{0,32},{2,34},{4,36},{6,38},{8,40},{10,42},{12,44},{14,46},{16,48}... | collective-permute-start | bytes 983048 | tf_op jit(solution)/shard_map/ppermute | solution.py:335
  39.4 3.0 %shard_map.85 = (bf16[720,128]{1,0:T(8,128)(2,1)S(1)}, bf16[720,128]{1,0:T(8,128)(2,1)S(1)}, bf16[720,128]{1,0:T(8,128)(2,1)S(1)}, bf16[720,128]{1,0:T(8,128)(2,1)S(1)}, bf16[16,2560]{1,0:T(8,128)(2,1)}) custom-call(s32[1]{0:T(128)} %bitcast.place_ref, bf16[256,1280]{1,0:T(8,128)(2,1)S(1)} %get-tuple-element.36.tokens_ref, ...), custom_call_target="tpu_custom_call" | custom-call | flops 1 | bytes 1 | tf_op jit(solution)/shard_map/pallas_call | solution.py:319
  42.7 2.7 %collective-permute-start.18 = (bf16[720,128]{1,0:T(8,128)(2,1)S(1)}, bf16[720,128]{1,0:T(8,128)(2,1)S(1)}, u32[]{:S(2)}, u32[]{:S(2)}) collective-permute-start(bf16[720,128]{1,0:T(8,128)(2,1)S(1)} %get-tuple-element.64), channel_id=1, source_target_pairs={{0,8},{2,10},{4,12},{6,14},{8,0},{10,2},{12,4},{14,6},{16,24},{18,... | collective-permute-start | bytes 552968 | tf_op jit(solution)/shard_map/ppermute | solution.py:335
  45.4 5.7 %collective-permute-done.13.refs_1_ = bf16[720,128]{1,0:T(8,128)(2,1)S(1)} collective-permute-done((bf16[720,128]{1,0:T(8,128)(2,1)S(1)}, bf16[720,128]{1,0:T(8,128)(2,1)S(1)}, u32[]{:S(2)}, u32[]{:S(2)}) %collective-permute-start.13) | collective-permute-done | bytes 184352 | tf_op jit(solution)/shard_map/ppermute | solution.py:335
  52.2 0.5 collective-permute-start.21
  54.2 6.5 %shard_map.88 = (bf16[640,128]{1,0:T(8,128)(2,1)S(1)}, bf16[640,128]{1,0:T(8,128)(2,1)S(1)}) custom-call(s32[1]{0:T(128)} %bitcast.place_ref, bf16[720,128]{1,0:T(8,128)(2,1)S(1)} %collective-permute-done.18.refs_0_, bf16[720,128]{1,0:T(8,128)(2,1)S(1)} %collective-permute-done.13.refs_1_, bf16[1280,128]{1,0:T(8,128)(2,1)S(1)} %shard_map.86.refs_1_.refs_2_, ...), custom_call_target="tpu_custom_call" | custom-call | flops 1 | bytes 1 | tf_op jit(solution)/shard_map/pallas_call | solution.py:319
  60.8 2.1 %collective-permute-start.20 = (bf16[640,128]{1,0:T(8,128)(2,1)S(1)}, bf16[640,128]{1,0:T(8,128)(2,1)S(1)}, u32[]{:S(2)}, u32[]{:S(2)}) collective-permute-start(bf16[640,128]{1,0:T(8,128)(2,1)S(1)} %get-tuple-element.66), channel_id=1, source_target_pairs={{0,8},{2,10},{4,12},{6,14},{8,0},{10,2},{12,4},{14,6},{16,24},{18,... | collective-permute-start | bytes 491528 | tf_op jit(solution)/shard_map/ppermute | solution.py:335
  62.9 3.5 %shard_map.89 = bf16[640,128]{1,0:T(8,128)(2,1)S(1)} custom-call(s32[1]{0:T(128)} %bitcast.place_ref, bf16[720,128]{1,0:T(8,128)(2,1)S(1)} %collective-permute-done.21.refs_0_, bf16[1280,128]{1,0:T(8,128)(2,1)S(1)} %shard_map.86.refs_1_.refs_2_, bf16[1280,128]{1,0:T(8,128)(2,1)S(1)} %collective-permute-done.10.refs_2_.refs_3_, ...), custom_call_target="tpu_custom_call" | custom-call | flops 1 | bytes 1 | tf_op jit(solution)/shard_map/pallas_call | solution.py:319
  66.5 3.5 %shard_map.87.refs_0_ = bf16[640,128]{1,0:T(8,128)(2,1)S(1)} custom-call(s32[1]{0:T(128)} %bitcast.place_ref, bf16[720,128]{1,0:T(8,128)(2,1)S(1)} %get-tuple-element.57.refs_0_, bf16[1280,128]{1,0:T(8,128)(2,1)S(1)} %shard_map.86.refs_1_.refs_2_, bf16[1280,128]{1,0:T(8,128)(2,1)S(1)} %collective-permute-done.10.refs_2_.refs_3_, ...), custom_call_target="tpu_custom_call" | custom-call | flops 1 | bytes 1 | tf_op jit(solution)/shard_map/pallas_call | solution.py:319
  70.0 3.0 %collective-permute-done.22.refs_3_ = bf16[640,128]{1,0:T(8,128)(2,1)S(1)} collective-permute-done((bf16[640,128]{1,0:T(8,128)(2,1)S(1)}, bf16[640,128]{1,0:T(8,128)(2,1)S(1)}, u32[]{:S(2)}, u32[]{:S(2)}) %collective-permute-start.22) | collective-permute-done | bytes 163872 | tf_op jit(solution)/shard_map/ppermute | solution.py:335
  73.0 1.0 %shard_map.90 = bf16[256,1280]{1,0:T(8,128)(2,1)} custom-call(s32[1]{0:T(128)} %bitcast.place_ref, bf16[640,128]{1,0:T(8,128)(2,1)S(1)} %shard_map.87.refs_0_, bf16[640,128]{1,0:T(8,128)(2,1)S(1)} %collective-permute-done.19.refs_1_, bf16[640,128]{1,0:T(8,128)(2,1)S(1)} %collective-permute-done.20.refs_2_, bf16[640,128]{1,0:T(8,128)(2,1)S(1)} %collective-permute-done.22.refs_3_), custom_call_target="tpu_custom_call" | custom-call | flops 1 | bytes 1 | tf_op jit(solution)/shard_map/pallas_call | solution.py:319
  (36 shorter events, 3.4 us)
Async XLA Ops:
  0.6 1.1 %copy-start = (bf16[1,256,1280]{2,1,0:T(8,128)(2,1)S(1)}, bf16[1,256,1280]{2,1,0:T(8,128)(2,1)}, u32[]{:S(2)}) copy-start(bf16[1,256,1280]{2,1,0:T(8,128)(2,1)} %param.6) | copy-start | bytes 1966084
  2.7 1.2 %collective-permute-start = (f32[8,128]{1,0:T(8,128)S(1)}, f32[8,128]{1,0:T(8,128)S(1)}, u32[]{:S(2)}, u32[]{:S(2)}) collective-permute-start(f32[8,128]{1,0:T(8,128)S(1)} %get-tuple-element.37.stats_ref.own_ref), channel_id=1, source_target_pairs={{0,2},{2,0},{4,6},{6,4},{8,10},{10,8},{12,14},{14,12},{16,18},{18,... | collective-permute-start | bytes 12296 | tf_op jit(solution)/shard_map/ppermute | solution.py:335
  2.8 0.9 %copy-start.1 = (bf16[1,16,2560]{2,1,0:T(8,128)(2,1)S(1)}, bf16[1,16,2560]{2,1,0:T(8,128)(2,1)}, u32[]{:S(2)}) copy-start(bf16[1,16,2560]{2,1,0:T(8,128)(2,1)} %param.7) | copy-start | bytes 245764
  4.0 6.5 %collective-permute-start.1 = (bf16[96,128]{1,0:T(8,128)(2,1)S(1)}, bf16[96,128]{1,0:T(8,128)(2,1)S(1)}, u32[]{:S(2)}, u32[]{:S(2)}) collective-permute-start(bf16[96,128]{1,0:T(8,128)(2,1)S(1)} %get-tuple-element.39), channel_id=1, source_target_pairs={{0,4},{2,6},{4,8},{6,10},{8,12},{10,14},{12,0},{14,2},{16,20},{18,... | collective-permute-start | bytes 73736 | tf_op jit(solution)/shard_map/ppermute | solution.py:335
  5.5 5.0 %collective-permute-start.2 = (bf16[96,128]{1,0:T(8,128)(2,1)S(1)}, bf16[96,128]{1,0:T(8,128)(2,1)S(1)}, u32[]{:S(2)}, u32[]{:S(2)}) collective-permute-start(bf16[96,128]{1,0:T(8,128)(2,1)S(1)} %get-tuple-element.40), channel_id=1, source_target_pairs={{0,12},{2,14},{4,0},{6,2},{8,4},{10,6},{12,8},{14,10},{16,28},{18,... | collective-permute-start | bytes 73736 | tf_op jit(solution)/shard_map/ppermute | solution.py:335
  7.3 5.3 %collective-permute-start.3 = (bf16[96,128]{1,0:T(8,128)(2,1)S(1)}, bf16[96,128]{1,0:T(8,128)(2,1)S(1)}, u32[]{:S(2)}, u32[]{:S(2)}) collective-permute-start(bf16[96,128]{1,0:T(8,128)(2,1)S(1)} %get-tuple-element.41), channel_id=1, source_target_pairs={{0,8},{2,10},{4,12},{6,14},{8,0},{10,2},{12,4},{14,6},{16,24},{18,... | collective-permute-start | bytes 73736 | tf_op jit(solution)/shard_map/ppermute | solution.py:335
  9.1 0.7 copy-start.2
  9.8 0.7 copy-start.3
  12.7 15.3 %collective-permute-start.6 = (bf16[336,128]{1,0:T(8,128)(2,1)S(1)}, bf16[336,128]{1,0:T(8,128)(2,1)S(1)}, u32[]{:S(2)}, u32[]{:S(2)}) collective-permute-start(bf16[336,128]{1,0:T(8,128)(2,1)S(1)} %shard_map.81.refs_0_), channel_id=1, source_target_pairs={{0,64},{2,66},{4,68},{6,70},{8,72},{10,74},{12,76},{14,78},{16,80}... | collective-permute-start | bytes 258056 | tf_op jit(solution)/shard_map/ppermute | solution.py:335
  16.0 12.0 %collective-permute-start.5 = (bf16[336,128]{1,0:T(8,128)(2,1)S(1)}, bf16[336,128]{1,0:T(8,128)(2,1)S(1)}, u32[]{:S(2)}, u32[]{:S(2)}) collective-permute-start(bf16[336,128]{1,0:T(8,128)(2,1)S(1)} %shard_map.81.refs_0_), channel_id=1, source_target_pairs={{0,192},{2,194},{4,196},{6,198},{8,200},{10,202},{12,204},{14,206}... | collective-permute-start | bytes 258056 | tf_op jit(solution)/shard_map/ppermute | solution.py:335
  18.2 10.7 %collective-permute-start.4 = (bf16[336,128]{1,0:T(8,128)(2,1)S(1)}, bf16[336,128]{1,0:T(8,128)(2,1)S(1)}, u32[]{:S(2)}, u32[]{:S(2)}) collective-permute-start(bf16[336,128]{1,0:T(8,128)(2,1)S(1)} %shard_map.81.refs_0_), channel_id=1, source_target_pairs={{0,128},{2,130},{4,132},{6,134},{8,136},{10,138},{12,140},{14,142}... | collective-permute-start | bytes 258056 | tf_op jit(solution)/shard_map/ppermute | solution.py:335
  28.9 7.4 %collective-permute-start.9 = (f32[8,128]{1,0:T(8,128)S(1)}, f32[8,128]{1,0:T(8,128)S(1)}, u32[]{:S(2)}, u32[]{:S(2)}) collective-permute-start(f32[8,128]{1,0:T(8,128)S(1)} %shard_map.84.s0.stats_ref), channel_id=1, source_target_pairs={{0,16},{2,18},{4,20},{6,22},{8,24},{10,26},{12,28},{14,30},{16,32}... | collective-permute-start | bytes 12296 | tf_op jit(solution)/shard_map/ppermute | solution.py:335
  30.6 5.8 %collective-permute-start.8 = (f32[8,128]{1,0:T(8,128)S(1)}, f32[8,128]{1,0:T(8,128)S(1)}, u32[]{:S(2)}, u32[]{:S(2)}) collective-permute-start(f32[8,128]{1,0:T(8,128)S(1)} %shard_map.84.s0.stats_ref), channel_id=1, source_target_pairs={{0,48},{2,50},{4,52},{6,54},{8,56},{10,58},{12,60},{14,62},{16,0},... | collective-permute-start | bytes 12296 | tf_op jit(solution)/shard_map/ppermute | solution.py:335
  32.2 5.2 %collective-permute-start.7 = (f32[8,128]{1,0:T(8,128)S(1)}, f32[8,128]{1,0:T(8,128)S(1)}, u32[]{:S(2)}, u32[]{:S(2)}) collective-permute-start(f32[8,128]{1,0:T(8,128)S(1)} %shard_map.84.s0.stats_ref), channel_id=1, source_target_pairs={{0,32},{2,34},{4,36},{6,38},{8,40},{10,42},{12,44},{14,46},{16,48}... | collective-permute-start | bytes 12296 | tf_op jit(solution)/shard_map/ppermute | solution.py:335
  34.2 16.9 %collective-permute-start.11 = (bf16[1280,128]{1,0:T(8,128)(2,1)S(1)}, bf16[1280,128]{1,0:T(8,128)(2,1)S(1)}, u32[]{:S(2)}, u32[]{:S(2)}) collective-permute-start(bf16[1280,128]{1,0:T(8,128)(2,1)S(1)} %shard_map.86.refs_1_.refs_2_), channel_id=1, source_target_pairs={{0,48},{2,50},{4,52},{6,54},{8,56},{10,58},{12,60},{14,62},{16,0},... | collective-permute-start | bytes 983048 | tf_op jit(solution)/shard_map/ppermute | solution.py:335
  35.4 16.3 %collective-permute-start.10 = (bf16[1280,128]{1,0:T(8,128)(2,1)S(1)}, bf16[1280,128]{1,0:T(8,128)(2,1)S(1)}, u32[]{:S(2)}, u32[]{:S(2)}) collective-permute-start(bf16[1280,128]{1,0:T(8,128)(2,1)S(1)} %shard_map.86.refs_1_.refs_2_), channel_id=1, source_target_pairs={{0,16},{2,18},{4,20},{6,22},{8,24},{10,26},{12,28},{14,30},{16,32}... | collective-permute-start | bytes 983048 | tf_op jit(solution)/shard_map/ppermute | solution.py:335
  37.5 14.3 %collective-permute-start.12 = (bf16[1280,128]{1,0:T(8,128)(2,1)S(1)}, bf16[1280,128]{1,0:T(8,128)(2,1)S(1)}, u32[]{:S(2)}, u32[]{:S(2)}) collective-permute-start(bf16[1280,128]{1,0:T(8,128)(2,1)S(1)} %shard_map.86.refs_1_.refs_2_), channel_id=1, source_target_pairs={{0,32},{2,34},{4,36},{6,38},{8,40},{10,42},{12,44},{14,46},{16,48}... | collective-permute-start | bytes 983048 | tf_op jit(solution)/shard_map/ppermute | solution.py:335
  42.4 8.7 %collective-permute-start.13 = (bf16[720,128]{1,0:T(8,128)(2,1)S(1)}, bf16[720,128]{1,0:T(8,128)(2,1)S(1)}, u32[]{:S(2)}, u32[]{:S(2)}) collective-permute-start(bf16[720,128]{1,0:T(8,128)(2,1)S(1)} %get-tuple-element.59), channel_id=1, source_target_pairs={{0,4},{2,6},{4,8},{6,10},{8,12},{10,14},{12,0},{14,2},{16,20},{18,... | collective-permute-start | bytes 552968 | tf_op jit(solution)/shard_map/ppermute | solution.py:335
  42.7 9.4 %collective-permute-start.18 = (bf16[720,128]{1,0:T(8,128)(2,1)S(1)}, bf16[720,128]{1,0:T(8,128)(2,1)S(1)}, u32[]{:S(2)}, u32[]{:S(2)}) collective-permute-start(bf16[720,128]{1,0:T(8,128)(2,1)S(1)} %get-tuple-element.64), channel_id=1, source_target_pairs={{0,8},{2,10},{4,12},{6,14},{8,0},{10,2},{12,4},{14,6},{16,24},{18,... | collective-permute-start | bytes 552968 | tf_op jit(solution)/shard_map/ppermute | solution.py:335
  51.1 1.6 %collective-permute-start.14 = (bf16[1280,128]{1,0:T(8,128)(2,1)S(1)}, bf16[1280,128]{1,0:T(8,128)(2,1)S(1)}, u32[]{:S(2)}, u32[]{:S(2)}) collective-permute-start(bf16[1280,128]{1,0:T(8,128)(2,1)S(1)} %shard_map.86.refs_1_.refs_2_), channel_id=1, source_target_pairs={{0,2},{2,0},{4,6},{6,4},{8,10},{10,8},{12,14},{14,12},{16,18},{18,... | collective-permute-start | bytes 983048 | tf_op jit(solution)/shard_map/ppermute | solution.py:335
  51.1 2.1 %collective-permute-start.16 = (bf16[1280,128]{1,0:T(8,128)(2,1)S(1)}, bf16[1280,128]{1,0:T(8,128)(2,1)S(1)}, u32[]{:S(2)}, u32[]{:S(2)}) collective-permute-start(bf16[1280,128]{1,0:T(8,128)(2,1)S(1)} %collective-permute-done.11.refs_3_.refs_4_), channel_id=1, source_target_pairs={{0,2},{2,0},{4,6},{6,4},{8,10},{10,8},{12,14},{14,12},{16,18},{18,... | collective-permute-start | bytes 983048 | tf_op jit(solution)/shard_map/ppermute | solution.py:335
  51.6 2.0 %collective-permute-start.15 = (bf16[1280,128]{1,0:T(8,128)(2,1)S(1)}, bf16[1280,128]{1,0:T(8,128)(2,1)S(1)}, u32[]{:S(2)}, u32[]{:S(2)}) collective-permute-start(bf16[1280,128]{1,0:T(8,128)(2,1)S(1)} %collective-permute-done.10.refs_2_.refs_3_), channel_id=1, source_target_pairs={{0,2},{2,0},{4,6},{6,4},{8,10},{10,8},{12,14},{14,12},{16,18},{18,... | collective-permute-start | bytes 983048 | tf_op jit(solution)/shard_map/ppermute | solution.py:335
  51.7 2.4 %collective-permute-start.17 = (bf16[1280,128]{1,0:T(8,128)(2,1)S(1)}, bf16[1280,128]{1,0:T(8,128)(2,1)S(1)}, u32[]{:S(2)}, u32[]{:S(2)}) collective-permute-start(bf16[1280,128]{1,0:T(8,128)(2,1)S(1)} %collective-permute-done.12.refs_4_.refs_5_), channel_id=1, source_target_pairs={{0,2},{2,0},{4,6},{6,4},{8,10},{10,8},{12,14},{14,12},{16,18},{18,... | collective-permute-start | bytes 983048 | tf_op jit(solution)/shard_map/ppermute | solution.py:335
  52.2 10.7 %collective-permute-start.21 = (bf16[720,128]{1,0:T(8,128)(2,1)S(1)}, bf16[720,128]{1,0:T(8,128)(2,1)S(1)}, u32[]{:S(2)}, u32[]{:S(2)}) collective-permute-start(bf16[720,128]{1,0:T(8,128)(2,1)S(1)} %get-tuple-element.68), channel_id=1, source_target_pairs={{0,12},{2,14},{4,0},{6,2},{8,4},{10,6},{12,8},{14,10},{16,28},{18,... | collective-permute-start | bytes 552968 | tf_op jit(solution)/shard_map/ppermute | solution.py:335
  60.7 9.3 %collective-permute-start.19 = (bf16[640,128]{1,0:T(8,128)(2,1)S(1)}, bf16[640,128]{1,0:T(8,128)(2,1)S(1)}, u32[]{:S(2)}, u32[]{:S(2)}) collective-permute-start(bf16[640,128]{1,0:T(8,128)(2,1)S(1)} %get-tuple-element.65), channel_id=1, source_target_pairs={{0,12},{2,14},{4,0},{6,2},{8,4},{10,6},{12,8},{14,10},{16,28},{18,... | collective-permute-start | bytes 491528 | tf_op jit(solution)/shard_map/ppermute | solution.py:335
  60.8 9.2 %collective-permute-start.20 = (bf16[640,128]{1,0:T(8,128)(2,1)S(1)}, bf16[640,128]{1,0:T(8,128)(2,1)S(1)}, u32[]{:S(2)}, u32[]{:S(2)}) collective-permute-start(bf16[640,128]{1,0:T(8,128)(2,1)S(1)} %get-tuple-element.66), channel_id=1, source_target_pairs={{0,8},{2,10},{4,12},{6,14},{8,0},{10,2},{12,4},{14,6},{16,24},{18,... | collective-permute-start | bytes 491528 | tf_op jit(solution)/shard_map/ppermute | solution.py:335
  66.4 6.6 %collective-permute-start.22 = (bf16[640,128]{1,0:T(8,128)(2,1)S(1)}, bf16[640,128]{1,0:T(8,128)(2,1)S(1)}, u32[]{:S(2)}, u32[]{:S(2)}) collective-permute-start(bf16[640,128]{1,0:T(8,128)(2,1)S(1)} %shard_map.89), channel_id=1, source_target_pairs={{0,4},{2,6},{4,8},{6,10},{8,12},{10,14},{12,0},{14,2},{16,20},{18,... | collective-permute-start | bytes 491528 | tf_op jit(solution)/shard_map/ppermute | solution.py:335

commit v10 on v9

--- a/solution.py
+++ b/solution.py
@@ -20,7 +20,7 @@
 SET_ROWS = SET_HEADS * ROWS
 ANSWER_ROWS = SET_HEADS * CELLS // 2
 epsilon = 1e-05
-X_ORDER = (0, 1, 3, 2)
+X_ORDER = (0, 2, 1, 3)
 
 f32 = jnp.float32
 bf16 = jnp.bfloat16
@@ -390,7 +390,7 @@
     weights = weights[1::-1]
     parts, weights = lax.optimization_barrier((parts, weights))
     (stats,) = call(stats_kernel, [VMEM] * 4, [((8, LANES), f32)], *parts)
-    all_stats = [stats] + [shift(stats, "y", k) for k in (2, 3, 1)]
+    all_stats = [stats] + [shift(stats, "y", k) for k in (1, 2, 3)]
     (piece,) = call(piece_kernel, [VMEM] * 5, [table], stats, *parts)
     pieces = [piece, shift(piece, "y", 1), shift(piece, "y", 3)]
     pieces.append(shift(after(piece, *all_stats), "y", 2))

time: 74.3 us -> 74.1 us (level)
  waiting for transfers between devices: 14.5 us -> 11.1 us
  starting transfers between devices: 31.9 us -> 35.1 us
    ppermute x23, waiting for transfers between devices: 14.5 us -> 11.1 us  [permute(): return lax.ppermute(array, 'patch', pairs)]
    ppermute x23, starting transfers between devices: 31.9 us -> 35.1 us  [permute(): return lax.ppermute(array, 'patch', pairs)]
  transfers between devices with their start and end apart: 23 -> 23, of which waited for: 10 -> 9; matrix products, arithmetic and copies ran while one was open for 0% -> 0% of each run, Pallas kernels for 29% -> 29%
where the time goes in v10:
time: 74.1 us; the launch traced here: 73.8 us
  starting transfers between devices  35.1 us (47%)
  Pallas kernels  23.4 us (32%)
  waiting for transfers between devices  11.1 us (15%)
  local copies, waits for them, and re-layouts  3.36 us (5%)
  between operations  0.79 us (1%)
    ppermute x23, starting transfers between devices, permute(): return lax.ppermute(array, 'patch', pairs)  35.1 us
    pallas_call x14, Pallas kernels, call(): pl.pallas_call(kernel, in_specs=ins, out_specs=[VMEM] * len(outs), out_sh...  23.4 us
    ppermute x23, waiting for transfers between devices, permute(): return lax.ppermute(array, 'patch', pairs)  11.1 us
    unnamed x8, local copies, waits for them, and re-layouts  3.36 us
  transfers between devices with their start and end apart: 23, of which 9 were waited for; matrix products, arithmetic and copies ran while one was open for 0% of the time, Pallas kernels for 29%

profile of v10, /device:TPU:32, one launch (start us, length us, event | category | flops | bytes accessed | tf_op | source)
XLA Modules:
  0.0 73.8 jit_solution(10965583061097749901)
XLA Ops:
  0.6 1.1 %copy-done = bf16[1,256,1280]{2,1,0:T(8,128)(2,1)S(1)} copy-done((bf16[1,256,1280]{2,1,0:T(8,128)(2,1)S(1)}, bf16[1,256,1280]{2,1,0:T(8,128)(2,1)}, u32[]{:S(2)}) %copy-start) | copy-done | bytes 655384
  1.7 1.0 %shard_map.77 = (f32[8,128]{1,0:T(8,128)S(1)}, bf16[256,1280]{1,0:T(8,128)(2,1)S(1)}) custom-call(bf16[256,1280]{1,0:T(8,128)(2,1)S(1)} %bitcast.5), custom_call_target="tpu_custom_call" | custom-call | flops 1 | bytes 1 | tf_op jit(solution)/shard_map/pallas_call | solution.py:319
  2.8 0.9 %copy-done.1 = bf16[1,16,2560]{2,1,0:T(8,128)(2,1)S(1)} copy-done((bf16[1,16,2560]{2,1,0:T(8,128)(2,1)S(1)}, bf16[1,16,2560]{2,1,0:T(8,128)(2,1)}, u32[]{:S(2)}) %copy-start.1) | copy-done | bytes 81944
  4.0 3.1 %collective-permute-start.1 = (bf16[96,128]{1,0:T(8,128)(2,1)S(1)}, bf16[96,128]{1,0:T(8,128)(2,1)S(1)}, u32[]{:S(2)}, u32[]{:S(2)}) collective-permute-start(bf16[96,128]{1,0:T(8,128)(2,1)S(1)} %get-tuple-element.39), channel_id=1, source_target_pairs={{0,8},{2,10},{4,12},{6,14},{8,0},{10,2},{12,4},{14,6},{16,24},{18,... | collective-permute-start | bytes 73736 | tf_op jit(solution)/shard_map/ppermute | solution.py:335
  7.1 0.6 collective-permute-start.2
  7.7 2.6 %collective-permute-start.3 = (bf16[96,128]{1,0:T(8,128)(2,1)S(1)}, bf16[96,128]{1,0:T(8,128)(2,1)S(1)}, u32[]{:S(2)}, u32[]{:S(2)}) collective-permute-start(bf16[96,128]{1,0:T(8,128)(2,1)S(1)} %get-tuple-element.41), channel_id=1, source_target_pairs={{0,12},{2,14},{4,0},{6,2},{8,4},{10,6},{12,8},{14,10},{16,28},{18,... | collective-permute-start | bytes 73736 | tf_op jit(solution)/shard_map/ppermute | solution.py:335
  10.3 0.7 copy-done.2
  11.0 0.7 copy-done.3
  12.2 3.3 %collective-permute-start.6 = (bf16[336,128]{1,0:T(8,128)(2,1)S(1)}, bf16[336,128]{1,0:T(8,128)(2,1)S(1)}, u32[]{:S(2)}, u32[]{:S(2)}) collective-permute-start(bf16[336,128]{1,0:T(8,128)(2,1)S(1)} %shard_map.81.refs_0_), channel_id=1, source_target_pairs={{0,64},{2,66},{4,68},{6,70},{8,72},{10,74},{12,76},{14,78},{16,80}... | collective-permute-start | bytes 258056 | tf_op jit(solution)/shard_map/ppermute | solution.py:335
  15.5 2.2 %collective-permute-start.5 = (bf16[336,128]{1,0:T(8,128)(2,1)S(1)}, bf16[336,128]{1,0:T(8,128)(2,1)S(1)}, u32[]{:S(2)}, u32[]{:S(2)}) collective-permute-start(bf16[336,128]{1,0:T(8,128)(2,1)S(1)} %shard_map.81.refs_0_), channel_id=1, source_target_pairs={{0,192},{2,194},{4,196},{6,198},{8,200},{10,202},{12,204},{14,206}... | collective-permute-start | bytes 258056 | tf_op jit(solution)/shard_map/ppermute | solution.py:335
  17.7 4.9 %collective-permute-start.4 = (bf16[336,128]{1,0:T(8,128)(2,1)S(1)}, bf16[336,128]{1,0:T(8,128)(2,1)S(1)}, u32[]{:S(2)}, u32[]{:S(2)}) collective-permute-start(bf16[336,128]{1,0:T(8,128)(2,1)S(1)} %shard_map.81.refs_0_), channel_id=1, source_target_pairs={{0,128},{2,130},{4,132},{6,134},{8,136},{10,138},{12,140},{14,142}... | collective-permute-start | bytes 258056 | tf_op jit(solution)/shard_map/ppermute | solution.py:335
  22.7 1.9 %shard_map.82.query_ref = bf16[1280,1280]{1,0:T(8,128)(2,1)S(1)} custom-call(bf16[1280,1280]{1,0:T(8,128)(2,1)} %source_hbm), custom_call_target="tpu_custom_call" | custom-call | flops 1 | bytes 1 | tf_op jit(solution)/shard_map/pallas_call | solution.py:319
  24.6 2.9 %shard_map.83.pair_ref = bf16[1280,2560]{1,0:T(8,128)(2,1)S(1)} custom-call(bf16[1280,2560]{1,0:T(8,128)(2,1)} %source_hbm.1), custom_call_target="tpu_custom_call" | custom-call | flops 1 | bytes 1 | tf_op jit(solution)/shard_map/pallas_call | solution.py:319
  27.5 1.4 %collective-permute-done.4.refs_1_ = bf16[336,128]{1,0:T(8,128)(2,1)S(1)} collective-permute-done((bf16[336,128]{1,0:T(8,128)(2,1)S(1)}, bf16[336,128]{1,0:T(8,128)(2,1)S(1)}, u32[]{:S(2)}, u32[]{:S(2)}) %collective-permute-start.4) | collective-permute-done | bytes 86048 | tf_op jit(solution)/shard_map/ppermute | solution.py:335
  28.9 3.1 %collective-permute-start.9 = (f32[8,128]{1,0:T(8,128)S(1)}, f32[8,128]{1,0:T(8,128)S(1)}, u32[]{:S(2)}, u32[]{:S(2)}) collective-permute-start(f32[8,128]{1,0:T(8,128)S(1)} %shard_map.84.s0.stats_ref), channel_id=1, source_target_pairs={{0,48},{2,50},{4,52},{6,54},{8,56},{10,58},{12,60},{14,62},{16,0},... | collective-permute-start | bytes 12296 | tf_op jit(solution)/shard_map/ppermute | solution.py:335
  32.0 0.6 collective-permute-start.8
  32.6 1.0 %collective-permute-start.7 = (f32[8,128]{1,0:T(8,128)S(1)}, f32[8,128]{1,0:T(8,128)S(1)}, u32[]{:S(2)}, u32[]{:S(2)}) collective-permute-start(f32[8,128]{1,0:T(8,128)S(1)} %shard_map.84.s0.stats_ref), channel_id=1, source_target_pairs={{0,16},{2,18},{4,20},{6,22},{8,24},{10,26},{12,28},{14,30},{16,32}... | collective-permute-start | bytes 12296 | tf_op jit(solution)/shard_map/ppermute | solution.py:335
  33.6 2.3 %collective-permute-start.11 = (bf16[1280,128]{1,0:T(8,128)(2,1)S(1)}, bf16[1280,128]{1,0:T(8,128)(2,1)S(1)}, u32[]{:S(2)}, u32[]{:S(2)}) collective-permute-start(bf16[1280,128]{1,0:T(8,128)(2,1)S(1)} %shard_map.86.refs_1_.refs_2_), channel_id=1, source_target_pairs={{0,48},{2,50},{4,52},{6,54},{8,56},{10,58},{12,60},{14,62},{16,0},... | collective-permute-start | bytes 983048 | tf_op jit(solution)/shard_map/ppermute | solution.py:335
  36.0 1.2 %collective-permute-done.8.s2 = f32[8,128]{1,0:T(8,128)S(1)} collective-permute-done((f32[8,128]{1,0:T(8,128)S(1)}, f32[8,128]{1,0:T(8,128)S(1)}, u32[]{:S(2)}, u32[]{:S(2)}) %collective-permute-start.8) | collective-permute-done | bytes 4128 | tf_op jit(solution)/shard_map/ppermute | solution.py:335
  37.5 1.7 %collective-permute-start.12 = (bf16[1280,128]{1,0:T(8,128)(2,1)S(1)}, bf16[1280,128]{1,0:T(8,128)(2,1)S(1)}, u32[]{:S(2)}, u32[]{:S(2)}) collective-permute-start(bf16[1280,128]{1,0:T(8,128)(2,1)S(1)} %shard_map.86.refs_1_.refs_2_), channel_id=1, source_target_pairs={{0,32},{2,34},{4,36},{6,38},{8,40},{10,42},{12,44},{14,46},{16,48}... | collective-permute-start | bytes 983048 | tf_op jit(solution)/shard_map/ppermute | solution.py:335
  39.2 3.0 %shard_map.85 = (bf16[720,128]{1,0:T(8,128)(2,1)S(1)}, bf16[720,128]{1,0:T(8,128)(2,1)S(1)}, bf16[720,128]{1,0:T(8,128)(2,1)S(1)}, bf16[720,128]{1,0:T(8,128)(2,1)S(1)}, bf16[16,2560]{1,0:T(8,128)(2,1)}) custom-call(s32[1]{0:T(128)} %bitcast.place_ref, bf16[256,1280]{1,0:T(8,128)(2,1)S(1)} %get-tuple-element.36.tokens_ref, ...), custom_call_target="tpu_custom_call" | custom-call | flops 1 | bytes 1 | tf_op jit(solution)/shard_map/pallas_call | solution.py:319
  42.2 4.2 %collective-permute-start.18 = (bf16[720,128]{1,0:T(8,128)(2,1)S(1)}, bf16[720,128]{1,0:T(8,128)(2,1)S(1)}, u32[]{:S(2)}, u32[]{:S(2)}) collective-permute-start(bf16[720,128]{1,0:T(8,128)(2,1)S(1)} %get-tuple-element.64), channel_id=1, source_target_pairs={{0,8},{2,10},{4,12},{6,14},{8,0},{10,2},{12,4},{14,6},{16,24},{18,... | collective-permute-start | bytes 552968 | tf_op jit(solution)/shard_map/ppermute | solution.py:335
  46.4 2.5 %collective-permute-done.13.refs_1_ = bf16[720,128]{1,0:T(8,128)(2,1)S(1)} collective-permute-done((bf16[720,128]{1,0:T(8,128)(2,1)S(1)}, bf16[720,128]{1,0:T(8,128)(2,1)S(1)}, u32[]{:S(2)}, u32[]{:S(2)}) %collective-permute-start.13) | collective-permute-done | bytes 184352 | tf_op jit(solution)/shard_map/ppermute | solution.py:335
  49.5 1.9 %collective-permute-done.10.refs_2_.refs_3_ = bf16[1280,128]{1,0:T(8,128)(2,1)S(1)} collective-permute-done((bf16[1280,128]{1,0:T(8,128)(2,1)S(1)}, bf16[1280,128]{1,0:T(8,128)(2,1)S(1)}, u32[]{:S(2)}, u32[]{:S(2)}) %collective-permute-start.10) | collective-permute-done | bytes 327712 | tf_op jit(solution)/shard_map/ppermute | solution.py:335
  51.9 1.4 %collective-permute-start.21 = (bf16[720,128]{1,0:T(8,128)(2,1)S(1)}, bf16[720,128]{1,0:T(8,128)(2,1)S(1)}, u32[]{:S(2)}, u32[]{:S(2)}) collective-permute-start(bf16[720,128]{1,0:T(8,128)(2,1)S(1)} %get-tuple-element.68), channel_id=1, source_target_pairs={{0,12},{2,14},{4,0},{6,2},{8,4},{10,6},{12,8},{14,10},{16,28},{18,... | collective-permute-start | bytes 552968 | tf_op jit(solution)/shard_map/ppermute | solution.py:335
  53.5 6.5 %shard_map.88 = (bf16[640,128]{1,0:T(8,128)(2,1)S(1)}, bf16[640,128]{1,0:T(8,128)(2,1)S(1)}) custom-call(s32[1]{0:T(128)} %bitcast.place_ref, bf16[720,128]{1,0:T(8,128)(2,1)S(1)} %collective-permute-done.18.refs_0_, bf16[720,128]{1,0:T(8,128)(2,1)S(1)} %collective-permute-done.13.refs_1_, bf16[1280,128]{1,0:T(8,128)(2,1)S(1)} %shard_map.86.refs_1_.refs_2_, ...), custom_call_target="tpu_custom_call" | custom-call | flops 1 | bytes 1 | tf_op jit(solution)/shard_map/pallas_call | solution.py:319
  60.0 1.5 %collective-permute-start.19 = (bf16[640,128]{1,0:T(8,128)(2,1)S(1)}, bf16[640,128]{1,0:T(8,128)(2,1)S(1)}, u32[]{:S(2)}, u32[]{:S(2)}) collective-permute-start(bf16[640,128]{1,0:T(8,128)(2,1)S(1)} %get-tuple-element.65), channel_id=1, source_target_pairs={{0,12},{2,14},{4,0},{6,2},{8,4},{10,6},{12,8},{14,10},{16,28},{18,... | collective-permute-start | bytes 491528 | tf_op jit(solution)/shard_map/ppermute | solution.py:335
  61.5 1.2 %collective-permute-start.20 = (bf16[640,128]{1,0:T(8,128)(2,1)S(1)}, bf16[640,128]{1,0:T(8,128)(2,1)S(1)}, u32[]{:S(2)}, u32[]{:S(2)}) collective-permute-start(bf16[640,128]{1,0:T(8,128)(2,1)S(1)} %get-tuple-element.66), channel_id=1, source_target_pairs={{0,8},{2,10},{4,12},{6,14},{8,0},{10,2},{12,4},{14,6},{16,24},{18,... | collective-permute-start | bytes 491528 | tf_op jit(solution)/shard_map/ppermute | solution.py:335
  62.7 3.5 %shard_map.89 = bf16[640,128]{1,0:T(8,128)(2,1)S(1)} custom-call(s32[1]{0:T(128)} %bitcast.place_ref, bf16[720,128]{1,0:T(8,128)(2,1)S(1)} %collective-permute-done.21.refs_0_, bf16[1280,128]{1,0:T(8,128)(2,1)S(1)} %shard_map.86.refs_1_.refs_2_, bf16[1280,128]{1,0:T(8,128)(2,1)S(1)} %collective-permute-done.10.refs_2_.refs_3_, ...), custom_call_target="tpu_custom_call" | custom-call | flops 1 | bytes 1 | tf_op jit(solution)/shard_map/pallas_call | solution.py:319
  66.2 3.5 %shard_map.87.refs_0_ = bf16[640,128]{1,0:T(8,128)(2,1)S(1)} custom-call(s32[1]{0:T(128)} %bitcast.place_ref, bf16[720,128]{1,0:T(8,128)(2,1)S(1)} %get-tuple-element.57.refs_0_, bf16[1280,128]{1,0:T(8,128)(2,1)S(1)} %shard_map.86.refs_1_.refs_2_, bf16[1280,128]{1,0:T(8,128)(2,1)S(1)} %collective-permute-done.10.refs_2_.refs_3_, ...), custom_call_target="tpu_custom_call" | custom-call | flops 1 | bytes 1 | tf_op jit(solution)/shard_map/pallas_call | solution.py:319
  69.8 3.0 %collective-permute-done.22.refs_3_ = bf16[640,128]{1,0:T(8,128)(2,1)S(1)} collective-permute-done((bf16[640,128]{1,0:T(8,128)(2,1)S(1)}, bf16[640,128]{1,0:T(8,128)(2,1)S(1)}, u32[]{:S(2)}, u32[]{:S(2)}) %collective-permute-start.22) | collective-permute-done | bytes 163872 | tf_op jit(solution)/shard_map/ppermute | solution.py:335
  72.8 1.0 %shard_map.90 = bf16[256,1280]{1,0:T(8,128)(2,1)} custom-call(s32[1]{0:T(128)} %bitcast.place_ref, bf16[640,128]{1,0:T(8,128)(2,1)S(1)} %shard_map.87.refs_0_, bf16[640,128]{1,0:T(8,128)(2,1)S(1)} %collective-permute-done.19.refs_1_, bf16[640,128]{1,0:T(8,128)(2,1)S(1)} %collective-permute-done.20.refs_2_, bf16[640,128]{1,0:T(8,128)(2,1)S(1)} %collective-permute-done.22.refs_3_), custom_call_target="tpu_custom_call" | custom-call | flops 1 | bytes 1 | tf_op jit(solution)/shard_map/pallas_call | solution.py:319
  (36 shorter events, 2.5 us)
Async XLA Ops:
  0.6 1.1 %copy-start = (bf16[1,256,1280]{2,1,0:T(8,128)(2,1)S(1)}, bf16[1,256,1280]{2,1,0:T(8,128)(2,1)}, u32[]{:S(2)}) copy-start(bf16[1,256,1280]{2,1,0:T(8,128)(2,1)} %param.6) | copy-start | bytes 1966084
  2.7 1.2 %collective-permute-start = (f32[8,128]{1,0:T(8,128)S(1)}, f32[8,128]{1,0:T(8,128)S(1)}, u32[]{:S(2)}, u32[]{:S(2)}) collective-permute-start(f32[8,128]{1,0:T(8,128)S(1)} %get-tuple-element.37.stats_ref.own_ref), channel_id=1, source_target_pairs={{0,2},{2,0},{4,6},{6,4},{8,10},{10,8},{12,14},{14,12},{16,18},{18,... | collective-permute-start | bytes 12296 | tf_op jit(solution)/shard_map/ppermute | solution.py:335
  2.8 0.9 %copy-start.1 = (bf16[1,16,2560]{2,1,0:T(8,128)(2,1)S(1)}, bf16[1,16,2560]{2,1,0:T(8,128)(2,1)}, u32[]{:S(2)}) copy-start(bf16[1,16,2560]{2,1,0:T(8,128)(2,1)} %param.7) | copy-start | bytes 245764
  4.0 7.8 %collective-permute-start.1 = (bf16[96,128]{1,0:T(8,128)(2,1)S(1)}, bf16[96,128]{1,0:T(8,128)(2,1)S(1)}, u32[]{:S(2)}, u32[]{:S(2)}) collective-permute-start(bf16[96,128]{1,0:T(8,128)(2,1)S(1)} %get-tuple-element.39), channel_id=1, source_target_pairs={{0,8},{2,10},{4,12},{6,14},{8,0},{10,2},{12,4},{14,6},{16,24},{18,... | collective-permute-start | bytes 73736 | tf_op jit(solution)/shard_map/ppermute | solution.py:335
  7.1 5.0 %collective-permute-start.2 = (bf16[96,128]{1,0:T(8,128)(2,1)S(1)}, bf16[96,128]{1,0:T(8,128)(2,1)S(1)}, u32[]{:S(2)}, u32[]{:S(2)}) collective-permute-start(bf16[96,128]{1,0:T(8,128)(2,1)S(1)} %get-tuple-element.40), channel_id=1, source_target_pairs={{0,4},{2,6},{4,8},{6,10},{8,12},{10,14},{12,0},{14,2},{16,20},{18,... | collective-permute-start | bytes 73736 | tf_op jit(solution)/shard_map/ppermute | solution.py:335
  7.7 4.4 %collective-permute-start.3 = (bf16[96,128]{1,0:T(8,128)(2,1)S(1)}, bf16[96,128]{1,0:T(8,128)(2,1)S(1)}, u32[]{:S(2)}, u32[]{:S(2)}) collective-permute-start(bf16[96,128]{1,0:T(8,128)(2,1)S(1)} %get-tuple-element.41), channel_id=1, source_target_pairs={{0,12},{2,14},{4,0},{6,2},{8,4},{10,6},{12,8},{14,10},{16,28},{18,... | collective-permute-start | bytes 73736 | tf_op jit(solution)/shard_map/ppermute | solution.py:335
  10.3 0.7 copy-start.2
  11.0 0.7 copy-start.3
  12.2 15.3 %collective-permute-start.6 = (bf16[336,128]{1,0:T(8,128)(2,1)S(1)}, bf16[336,128]{1,0:T(8,128)(2,1)S(1)}, u32[]{:S(2)}, u32[]{:S(2)}) collective-permute-start(bf16[336,128]{1,0:T(8,128)(2,1)S(1)} %shard_map.81.refs_0_), channel_id=1, source_target_pairs={{0,64},{2,66},{4,68},{6,70},{8,72},{10,74},{12,76},{14,78},{16,80}... | collective-permute-start | bytes 258056 | tf_op jit(solution)/shard_map/ppermute | solution.py:335
  15.5 12.0 %collective-permute-start.5 = (bf16[336,128]{1,0:T(8,128)(2,1)S(1)}, bf16[336,128]{1,0:T(8,128)(2,1)S(1)}, u32[]{:S(2)}, u32[]{:S(2)}) collective-permute-start(bf16[336,128]{1,0:T(8,128)(2,1)S(1)} %shard_map.81.refs_0_), channel_id=1, source_target_pairs={{0,192},{2,194},{4,196},{6,198},{8,200},{10,202},{12,204},{14,206}... | collective-permute-start | bytes 258056 | tf_op jit(solution)/shard_map/ppermute | solution.py:335
  17.7 11.2 %collective-permute-start.4 = (bf16[336,128]{1,0:T(8,128)(2,1)S(1)}, bf16[336,128]{1,0:T(8,128)(2,1)S(1)}, u32[]{:S(2)}, u32[]{:S(2)}) collective-permute-start(bf16[336,128]{1,0:T(8,128)(2,1)S(1)} %shard_map.81.refs_0_), channel_id=1, source_target_pairs={{0,128},{2,130},{4,132},{6,134},{8,136},{10,138},{12,140},{14,142}... | collective-permute-start | bytes 258056 | tf_op jit(solution)/shard_map/ppermute | solution.py:335
  28.9 7.1 %collective-permute-start.9 = (f32[8,128]{1,0:T(8,128)S(1)}, f32[8,128]{1,0:T(8,128)S(1)}, u32[]{:S(2)}, u32[]{:S(2)}) collective-permute-start(f32[8,128]{1,0:T(8,128)S(1)} %shard_map.84.s0.stats_ref), channel_id=1, source_target_pairs={{0,48},{2,50},{4,52},{6,54},{8,56},{10,58},{12,60},{14,62},{16,0},... | collective-permute-start | bytes 12296 | tf_op jit(solution)/shard_map/ppermute | solution.py:335
  32.0 5.2 %collective-permute-start.8 = (f32[8,128]{1,0:T(8,128)S(1)}, f32[8,128]{1,0:T(8,128)S(1)}, u32[]{:S(2)}, u32[]{:S(2)}) collective-permute-start(f32[8,128]{1,0:T(8,128)S(1)} %shard_map.84.s0.stats_ref), channel_id=1, source_target_pairs={{0,32},{2,34},{4,36},{6,38},{8,40},{10,42},{12,44},{14,46},{16,48}... | collective-permute-start | bytes 12296 | tf_op jit(solution)/shard_map/ppermute | solution.py:335
  32.6 4.9 %collective-permute-start.7 = (f32[8,128]{1,0:T(8,128)S(1)}, f32[8,128]{1,0:T(8,128)S(1)}, u32[]{:S(2)}, u32[]{:S(2)}) collective-permute-start(f32[8,128]{1,0:T(8,128)S(1)} %shard_map.84.s0.stats_ref), channel_id=1, source_target_pairs={{0,16},{2,18},{4,20},{6,22},{8,24},{10,26},{12,28},{14,30},{16,32}... | collective-permute-start | bytes 12296 | tf_op jit(solution)/shard_map/ppermute | solution.py:335
  33.6 15.3 %collective-permute-start.11 = (bf16[1280,128]{1,0:T(8,128)(2,1)S(1)}, bf16[1280,128]{1,0:T(8,128)(2,1)S(1)}, u32[]{:S(2)}, u32[]{:S(2)}) collective-permute-start(bf16[1280,128]{1,0:T(8,128)(2,1)S(1)} %shard_map.86.refs_1_.refs_2_), channel_id=1, source_target_pairs={{0,48},{2,50},{4,52},{6,54},{8,56},{10,58},{12,60},{14,62},{16,0},... | collective-permute-start | bytes 983048 | tf_op jit(solution)/shard_map/ppermute | solution.py:335
  36.0 15.4 %collective-permute-start.10 = (bf16[1280,128]{1,0:T(8,128)(2,1)S(1)}, bf16[1280,128]{1,0:T(8,128)(2,1)S(1)}, u32[]{:S(2)}, u32[]{:S(2)}) collective-permute-start(bf16[1280,128]{1,0:T(8,128)(2,1)S(1)} %shard_map.86.refs_1_.refs_2_), channel_id=1, source_target_pairs={{0,16},{2,18},{4,20},{6,22},{8,24},{10,26},{12,28},{14,30},{16,32}... | collective-permute-start | bytes 983048 | tf_op jit(solution)/shard_map/ppermute | solution.py:335
  37.5 13.9 %collective-permute-start.12 = (bf16[1280,128]{1,0:T(8,128)(2,1)S(1)}, bf16[1280,128]{1,0:T(8,128)(2,1)S(1)}, u32[]{:S(2)}, u32[]{:S(2)}) collective-permute-start(bf16[1280,128]{1,0:T(8,128)(2,1)S(1)} %shard_map.86.refs_1_.refs_2_), channel_id=1, source_target_pairs={{0,32},{2,34},{4,36},{6,38},{8,40},{10,42},{12,44},{14,46},{16,48}... | collective-permute-start | bytes 983048 | tf_op jit(solution)/shard_map/ppermute | solution.py:335
  42.2 6.7 %collective-permute-start.13 = (bf16[720,128]{1,0:T(8,128)(2,1)S(1)}, bf16[720,128]{1,0:T(8,128)(2,1)S(1)}, u32[]{:S(2)}, u32[]{:S(2)}) collective-permute-start(bf16[720,128]{1,0:T(8,128)(2,1)S(1)} %get-tuple-element.59), channel_id=1, source_target_pairs={{0,4},{2,6},{4,8},{6,10},{8,12},{10,14},{12,0},{14,2},{16,20},{18,... | collective-permute-start | bytes 552968 | tf_op jit(solution)/shard_map/ppermute | solution.py:335
  42.2 9.7 %collective-permute-start.18 = (bf16[720,128]{1,0:T(8,128)(2,1)S(1)}, bf16[720,128]{1,0:T(8,128)(2,1)S(1)}, u32[]{:S(2)}, u32[]{:S(2)}) collective-permute-start(bf16[720,128]{1,0:T(8,128)(2,1)S(1)} %get-tuple-element.64), channel_id=1, source_target_pairs={{0,8},{2,10},{4,12},{6,14},{8,0},{10,2},{12,4},{14,6},{16,24},{18,... | collective-permute-start | bytes 552968 | tf_op jit(solution)/shard_map/ppermute | solution.py:335
  48.9 4.4 %collective-permute-start.14 = (bf16[1280,128]{1,0:T(8,128)(2,1)S(1)}, bf16[1280,128]{1,0:T(8,128)(2,1)S(1)}, u32[]{:S(2)}, u32[]{:S(2)}) collective-permute-start(bf16[1280,128]{1,0:T(8,128)(2,1)S(1)} %shard_map.86.refs_1_.refs_2_), channel_id=1, source_target_pairs={{0,2},{2,0},{4,6},{6,4},{8,10},{10,8},{12,14},{14,12},{16,18},{18,... | collective-permute-start | bytes 983048 | tf_op jit(solution)/shard_map/ppermute | solution.py:335
  49.0 4.4 %collective-permute-start.16 = (bf16[1280,128]{1,0:T(8,128)(2,1)S(1)}, bf16[1280,128]{1,0:T(8,128)(2,1)S(1)}, u32[]{:S(2)}, u32[]{:S(2)}) collective-permute-start(bf16[1280,128]{1,0:T(8,128)(2,1)S(1)} %collective-permute-done.11.refs_3_.refs_4_), channel_id=1, source_target_pairs={{0,2},{2,0},{4,6},{6,4},{8,10},{10,8},{12,14},{14,12},{16,18},{18,... | collective-permute-start | bytes 983048 | tf_op jit(solution)/shard_map/ppermute | solution.py:335
  51.4 1.9 %collective-permute-start.15 = (bf16[1280,128]{1,0:T(8,128)(2,1)S(1)}, bf16[1280,128]{1,0:T(8,128)(2,1)S(1)}, u32[]{:S(2)}, u32[]{:S(2)}) collective-permute-start(bf16[1280,128]{1,0:T(8,128)(2,1)S(1)} %collective-permute-done.10.refs_2_.refs_3_), channel_id=1, source_target_pairs={{0,2},{2,0},{4,6},{6,4},{8,10},{10,8},{12,14},{14,12},{16,18},{18,... | collective-permute-start | bytes 983048 | tf_op jit(solution)/shard_map/ppermute | solution.py:335
  51.4 2.1 %collective-permute-start.17 = (bf16[1280,128]{1,0:T(8,128)(2,1)S(1)}, bf16[1280,128]{1,0:T(8,128)(2,1)S(1)}, u32[]{:S(2)}, u32[]{:S(2)}) collective-permute-start(bf16[1280,128]{1,0:T(8,128)(2,1)S(1)} %collective-permute-done.12.refs_4_.refs_5_), channel_id=1, source_target_pairs={{0,2},{2,0},{4,6},{6,4},{8,10},{10,8},{12,14},{14,12},{16,18},{18,... | collective-permute-start | bytes 983048 | tf_op jit(solution)/shard_map/ppermute | solution.py:335
  51.9 10.7 %collective-permute-start.21 = (bf16[720,128]{1,0:T(8,128)(2,1)S(1)}, bf16[720,128]{1,0:T(8,128)(2,1)S(1)}, u32[]{:S(2)}, u32[]{:S(2)}) collective-permute-start(bf16[720,128]{1,0:T(8,128)(2,1)S(1)} %get-tuple-element.68), channel_id=1, source_target_pairs={{0,12},{2,14},{4,0},{6,2},{8,4},{10,6},{12,8},{14,10},{16,28},{18,... | collective-permute-start | bytes 552968 | tf_op jit(solution)/shard_map/ppermute | solution.py:335
  60.0 9.7 %collective-permute-start.19 = (bf16[640,128]{1,0:T(8,128)(2,1)S(1)}, bf16[640,128]{1,0:T(8,128)(2,1)S(1)}, u32[]{:S(2)}, u32[]{:S(2)}) collective-permute-start(bf16[640,128]{1,0:T(8,128)(2,1)S(1)} %get-tuple-element.65), channel_id=1, source_target_pairs={{0,12},{2,14},{4,0},{6,2},{8,4},{10,6},{12,8},{14,10},{16,28},{18,... | collective-permute-start | bytes 491528 | tf_op jit(solution)/shard_map/ppermute | solution.py:335
  61.5 8.2 %collective-permute-start.20 = (bf16[640,128]{1,0:T(8,128)(2,1)S(1)}, bf16[640,128]{1,0:T(8,128)(2,1)S(1)}, u32[]{:S(2)}, u32[]{:S(2)}) collective-permute-start(bf16[640,128]{1,0:T(8,128)(2,1)S(1)} %get-tuple-element.66), channel_id=1, source_target_pairs={{0,8},{2,10},{4,12},{6,14},{8,0},{10,2},{12,4},{14,6},{16,24},{18,... | collective-permute-start | bytes 491528 | tf_op jit(solution)/shard_map/ppermute | solution.py:335
  66.1 6.6 %collective-permute-start.22 = (bf16[640,128]{1,0:T(8,128)(2,1)S(1)}, bf16[640,128]{1,0:T(8,128)(2,1)S(1)}, u32[]{:S(2)}, u32[]{:S(2)}) collective-permute-start(bf16[640,128]{1,0:T(8,128)(2,1)S(1)} %shard_map.89), channel_id=1, source_target_pairs={{0,4},{2,6},{4,8},{6,10},{8,12},{10,14},{12,0},{14,2},{16,20},{18,... | collective-permute-start | bytes 491528 | tf_op jit(solution)/shard_map/ppermute | solution.py:335

commit v11 on v5

--- a/solution.py
+++ b/solution.py
@@ -345,6 +345,17 @@
     return lax.optimization_barrier((array, *others))[0]
 
 
+def load(weight, limit):
+    return call(
+        load_kernel,
+        [HBM],
+        [(weight.shape, bf16)],
+        weight,
+        scratch=[pltpu.SemaphoreType.DMA],
+        limit=limit,
+    )[0]
+
+
 def per_device(tokens, stale_keys, norm_gain, norm_bias, query_weight, pair_weight):
     place = (lax.axis_index("patch") // 2 % 4).astype(jnp.int32).reshape(1)
     table = ((SET_HEADS * CELLS, LANES), bf16)
@@ -369,24 +380,15 @@
         sets,
     )
     received = [messages[0]] + [shift(messages[k], "x", k) for k in (1, 2, 3)]
-    norm_gain, norm_bias, _ = lax.optimization_barrier((norm_gain, norm_bias, messages[0]))
+    norm_gain, norm_bias, query_weight, _ = lax.optimization_barrier(
+        (norm_gain, norm_bias, query_weight, messages[0])
+    )
     (affine,) = call(affine_kernel, [VMEM] * 2, [((2, WIDTH), f32)], norm_gain, norm_bias)
-    received, affine = lax.optimization_barrier((received, affine))
+    query_weight = load(query_weight, 49)
+    received, affine, query_weight = lax.optimization_barrier((received, affine, query_weight))
     (part,) = call(z_kernel, [VMEM] * 4, [((4 * SET_ROWS + ROWS, LANES), bf16)], *received)
     parts = [part] + [shift(part, "z", k) for k in (2, 3, 1)]
-    weights = [part]
-    for weight, limit in ((query_weight, 49), (pair_weight, 43)):
-        weight = after(weight, weights[0])
-        loaded = call(
-            load_kernel,
-            [HBM],
-            [(weight.shape, bf16)],
-            weight,
-            scratch=[pltpu.SemaphoreType.DMA],
-            limit=limit,
-        )
-        weights = [*loaded, *weights]
-    weights = weights[1::-1]
+    weights = [query_weight, load(after(pair_weight, part), 43)]
     parts, weights = lax.optimization_barrier((parts, weights))
     (stats,) = call(stats_kernel, [VMEM] * 4, [((8, LANES), f32)], *parts)
     all_stats = [stats] + [shift(stats, "y", k) for k in (1, 2, 3)]

time: 73.5 us -> 74.6 us (1.015)
  waiting for transfers between devices: 11.3 us -> 14.6 us
  local copies, waits for them, and re-layouts: 3.36 us -> 1.97 us
    ppermute x23, waiting for transfers between devices: 11.3 us -> 14.6 us  [permute(): return lax.ppermute(array, 'patch', pairs)]
    unnamed x8, local copies, waits for them, and re-layouts: 3.36 us -> 1.97 us
  transfers between devices with their start and end apart: 23 -> 23, of which waited for: 9 -> 10; matrix products, arithmetic and copies ran while one was open for 0% -> 0% of each run, Pallas kernels for 29% -> 29%
where the time goes in v11:
time: 74.6 us; the launch traced here: 74.4 us
  starting transfers between devices  33.6 us (45%)
  Pallas kernels  23.4 us (31%)
  waiting for transfers between devices  14.6 us (20%)
  local copies, waits for them, and re-layouts  1.97 us (3%)
  between operations  0.83 us (1%)
    ppermute x23, starting transfers between devices, permute(): return lax.ppermute(array, 'patch', pairs)  33.6 us
    pallas_call x14, Pallas kernels, call(): pl.pallas_call(kernel, in_specs=ins, out_specs=[VMEM] * len(outs), out_sh...  23.4 us
    ppermute x23, waiting for transfers between devices, permute(): return lax.ppermute(array, 'patch', pairs)  14.6 us
    unnamed x8, local copies, waits for them, and re-layouts  1.97 us
  transfers between devices with their start and end apart: 23, of which 10 were waited for; matrix products, arithmetic and copies ran while one was open for 0% of the time, Pallas kernels for 29%

profile of v11, /device:TPU:32, one launch (start us, length us, event | category | flops | bytes accessed | tf_op | source)
XLA Modules:
  0.0 74.4 jit_solution(11789545017077097615)
XLA Ops:
  0.6 1.1 %copy-done = bf16[1,256,1280]{2,1,0:T(8,128)(2,1)S(1)} copy-done((bf16[1,256,1280]{2,1,0:T(8,128)(2,1)S(1)}, bf16[1,256,1280]{2,1,0:T(8,128)(2,1)}, u32[]{:S(2)}) %copy-start) | copy-done | bytes 655384
  1.7 1.0 %shard_map.77 = (f32[8,128]{1,0:T(8,128)S(1)}, bf16[256,1280]{1,0:T(8,128)(2,1)S(1)}) custom-call(bf16[256,1280]{1,0:T(8,128)(2,1)S(1)} %bitcast.5), custom_call_target="tpu_custom_call" | custom-call | flops 1 | bytes 1 | tf_op jit(solution)/shard_map/pallas_call | solution.py:318
  2.8 0.9 %copy-done.1 = bf16[1,16,2560]{2,1,0:T(8,128)(2,1)S(1)} copy-done((bf16[1,16,2560]{2,1,0:T(8,128)(2,1)S(1)}, bf16[1,16,2560]{2,1,0:T(8,128)(2,1)}, u32[]{:S(2)}) %copy-start.1) | copy-done | bytes 81944
  4.0 1.6 %collective-permute-start.1 = (bf16[96,128]{1,0:T(8,128)(2,1)S(1)}, bf16[96,128]{1,0:T(8,128)(2,1)S(1)}, u32[]{:S(2)}, u32[]{:S(2)}) collective-permute-start(bf16[96,128]{1,0:T(8,128)(2,1)S(1)} %get-tuple-element.40), channel_id=1, source_target_pairs={{0,4},{2,6},{4,8},{6,10},{8,12},{10,14},{12,0},{14,2},{16,20},{18,... | collective-permute-start | bytes 73736 | tf_op jit(solution)/shard_map/ppermute | solution.py:334
  5.5 2.7 %collective-permute-start.2 = (bf16[96,128]{1,0:T(8,128)(2,1)S(1)}, bf16[96,128]{1,0:T(8,128)(2,1)S(1)}, u32[]{:S(2)}, u32[]{:S(2)}) collective-permute-start(bf16[96,128]{1,0:T(8,128)(2,1)S(1)} %get-tuple-element.41), channel_id=1, source_target_pairs={{0,8},{2,10},{4,12},{6,14},{8,0},{10,2},{12,4},{14,6},{16,24},{18,... | collective-permute-start | bytes 73736 | tf_op jit(solution)/shard_map/ppermute | solution.py:334
  8.3 1.4 %collective-permute-start.3 = (bf16[96,128]{1,0:T(8,128)(2,1)S(1)}, bf16[96,128]{1,0:T(8,128)(2,1)S(1)}, u32[]{:S(2)}, u32[]{:S(2)}) collective-permute-start(bf16[96,128]{1,0:T(8,128)(2,1)S(1)} %get-tuple-element.42), channel_id=1, source_target_pairs={{0,12},{2,14},{4,0},{6,2},{8,4},{10,6},{12,8},{14,10},{16,28},{18,... | collective-permute-start | bytes 73736 | tf_op jit(solution)/shard_map/ppermute | solution.py:334
  9.7 1.9 %shard_map.81.query_ref = bf16[1280,1280]{1,0:T(8,128)(2,1)S(1)} custom-call(bf16[1280,1280]{1,0:T(8,128)(2,1)} %source_hbm), custom_call_target="tpu_custom_call" | custom-call | flops 1 | bytes 1 | tf_op jit(solution)/shard_map/pallas_call | solution.py:318
  12.1 3.3 %collective-permute-start.6 = (bf16[336,128]{1,0:T(8,128)(2,1)S(1)}, bf16[336,128]{1,0:T(8,128)(2,1)S(1)}, u32[]{:S(2)}, u32[]{:S(2)}) collective-permute-start(bf16[336,128]{1,0:T(8,128)(2,1)S(1)} %shard_map.82.refs_0_), channel_id=1, source_target_pairs={{0,64},{2,66},{4,68},{6,70},{8,72},{10,74},{12,76},{14,78},{16,80}... | collective-permute-start | bytes 258056 | tf_op jit(solution)/shard_map/ppermute | solution.py:334
  15.5 2.2 %collective-permute-start.5 = (bf16[336,128]{1,0:T(8,128)(2,1)S(1)}, bf16[336,128]{1,0:T(8,128)(2,1)S(1)}, u32[]{:S(2)}, u32[]{:S(2)}) collective-permute-start(bf16[336,128]{1,0:T(8,128)(2,1)S(1)} %shard_map.82.refs_0_), channel_id=1, source_target_pairs={{0,192},{2,194},{4,196},{6,198},{8,200},{10,202},{12,204},{14,206}... | collective-permute-start | bytes 258056 | tf_op jit(solution)/shard_map/ppermute | solution.py:334
  17.7 4.9 %collective-permute-start.4 = (bf16[336,128]{1,0:T(8,128)(2,1)S(1)}, bf16[336,128]{1,0:T(8,128)(2,1)S(1)}, u32[]{:S(2)}, u32[]{:S(2)}) collective-permute-start(bf16[336,128]{1,0:T(8,128)(2,1)S(1)} %shard_map.82.refs_0_), channel_id=1, source_target_pairs={{0,128},{2,130},{4,132},{6,134},{8,136},{10,138},{12,140},{14,142}... | collective-permute-start | bytes 258056 | tf_op jit(solution)/shard_map/ppermute | solution.py:334
  22.6 2.9 %shard_map.83.pair_ref = bf16[1280,2560]{1,0:T(8,128)(2,1)S(1)} custom-call(bf16[1280,2560]{1,0:T(8,128)(2,1)} %source_hbm.1), custom_call_target="tpu_custom_call" | custom-call | flops 1 | bytes 1 | tf_op jit(solution)/shard_map/pallas_call | solution.py:318
  25.5 3.3 %collective-permute-done.4.refs_1_ = bf16[336,128]{1,0:T(8,128)(2,1)S(1)} collective-permute-done((bf16[336,128]{1,0:T(8,128)(2,1)S(1)}, bf16[336,128]{1,0:T(8,128)(2,1)S(1)}, u32[]{:S(2)}, u32[]{:S(2)}) %collective-permute-start.4) | collective-permute-done | bytes 86048 | tf_op jit(solution)/shard_map/ppermute | solution.py:334
  28.9 3.1 %collective-permute-start.9 = (f32[8,128]{1,0:T(8,128)S(1)}, f32[8,128]{1,0:T(8,128)S(1)}, u32[]{:S(2)}, u32[]{:S(2)}) collective-permute-start(f32[8,128]{1,0:T(8,128)S(1)} %shard_map.84.s0.stats_ref), channel_id=1, source_target_pairs={{0,48},{2,50},{4,52},{6,54},{8,56},{10,58},{12,60},{14,62},{16,0},... | collective-permute-start | bytes 12296 | tf_op jit(solution)/shard_map/ppermute | solution.py:334
  32.0 0.6 collective-permute-start.8
  32.6 1.0 %collective-permute-start.7 = (f32[8,128]{1,0:T(8,128)S(1)}, f32[8,128]{1,0:T(8,128)S(1)}, u32[]{:S(2)}, u32[]{:S(2)}) collective-permute-start(f32[8,128]{1,0:T(8,128)S(1)} %shard_map.84.s0.stats_ref), channel_id=1, source_target_pairs={{0,16},{2,18},{4,20},{6,22},{8,24},{10,26},{12,28},{14,30},{16,32}... | collective-permute-start | bytes 12296 | tf_op jit(solution)/shard_map/ppermute | solution.py:334
  33.6 2.3 %collective-permute-start.11 = (bf16[1280,128]{1,0:T(8,128)(2,1)S(1)}, bf16[1280,128]{1,0:T(8,128)(2,1)S(1)}, u32[]{:S(2)}, u32[]{:S(2)}) collective-permute-start(bf16[1280,128]{1,0:T(8,128)(2,1)S(1)} %shard_map.86.refs_1_.refs_2_), channel_id=1, source_target_pairs={{0,48},{2,50},{4,52},{6,54},{8,56},{10,58},{12,60},{14,62},{16,0},... | collective-permute-start | bytes 983048 | tf_op jit(solution)/shard_map/ppermute | solution.py:334
  36.0 1.2 %collective-permute-done.8.s2 = f32[8,128]{1,0:T(8,128)S(1)} collective-permute-done((f32[8,128]{1,0:T(8,128)S(1)}, f32[8,128]{1,0:T(8,128)S(1)}, u32[]{:S(2)}, u32[]{:S(2)}) %collective-permute-start.8) | collective-permute-done | bytes 4128 | tf_op jit(solution)/shard_map/ppermute | solution.py:334
  37.5 1.7 %collective-permute-start.12 = (bf16[1280,128]{1,0:T(8,128)(2,1)S(1)}, bf16[1280,128]{1,0:T(8,128)(2,1)S(1)}, u32[]{:S(2)}, u32[]{:S(2)}) collective-permute-start(bf16[1280,128]{1,0:T(8,128)(2,1)S(1)} %shard_map.86.refs_1_.refs_2_), channel_id=1, source_target_pairs={{0,32},{2,34},{4,36},{6,38},{8,40},{10,42},{12,44},{14,46},{16,48}... | collective-permute-start | bytes 983048 | tf_op jit(solution)/shard_map/ppermute | solution.py:334
  39.2 3.0 %shard_map.85 = (bf16[720,128]{1,0:T(8,128)(2,1)S(1)}, bf16[720,128]{1,0:T(8,128)(2,1)S(1)}, bf16[720,128]{1,0:T(8,128)(2,1)S(1)}, bf16[720,128]{1,0:T(8,128)(2,1)S(1)}, bf16[16,2560]{1,0:T(8,128)(2,1)}) custom-call(s32[1]{0:T(128)} %bitcast.place_ref, bf16[256,1280]{1,0:T(8,128)(2,1)S(1)} %get-tuple-element.37.tokens_ref, ...), custom_call_target="tpu_custom_call" | custom-call | flops 1 | bytes 1 | tf_op jit(solution)/shard_map/pallas_call | solution.py:318
  42.2 0.6 collective-permute-start.13
  42.7 3.1 %collective-permute-start.18 = (bf16[720,128]{1,0:T(8,128)(2,1)S(1)}, bf16[720,128]{1,0:T(8,128)(2,1)S(1)}, u32[]{:S(2)}, u32[]{:S(2)}) collective-permute-start(bf16[720,128]{1,0:T(8,128)(2,1)S(1)} %get-tuple-element.66), channel_id=1, source_target_pairs={{0,8},{2,10},{4,12},{6,14},{8,0},{10,2},{12,4},{14,6},{16,24},{18,... | collective-permute-start | bytes 552968 | tf_op jit(solution)/shard_map/ppermute | solution.py:334
  45.8 3.1 %collective-permute-done.13.refs_1_ = bf16[720,128]{1,0:T(8,128)(2,1)S(1)} collective-permute-done((bf16[720,128]{1,0:T(8,128)(2,1)S(1)}, bf16[720,128]{1,0:T(8,128)(2,1)S(1)}, u32[]{:S(2)}, u32[]{:S(2)}) %collective-permute-start.13) | collective-permute-done | bytes 184352 | tf_op jit(solution)/shard_map/ppermute | solution.py:334
  49.4 2.0 %collective-permute-done.10.refs_2_.refs_3_ = bf16[1280,128]{1,0:T(8,128)(2,1)S(1)} collective-permute-done((bf16[1280,128]{1,0:T(8,128)(2,1)S(1)}, bf16[1280,128]{1,0:T(8,128)(2,1)S(1)}, u32[]{:S(2)}, u32[]{:S(2)}) %collective-permute-start.10) | collective-permute-done | bytes 327712 | tf_op jit(solution)/shard_map/ppermute | solution.py:334
  51.4 0.5 collective-permute-start.17
  51.9 0.8 %collective-permute-start.21 = (bf16[720,128]{1,0:T(8,128)(2,1)S(1)}, bf16[720,128]{1,0:T(8,128)(2,1)S(1)}, u32[]{:S(2)}, u32[]{:S(2)}) collective-permute-start(bf16[720,128]{1,0:T(8,128)(2,1)S(1)} %get-tuple-element.70), channel_id=1, source_target_pairs={{0,12},{2,14},{4,0},{6,2},{8,4},{10,6},{12,8},{14,10},{16,28},{18,... | collective-permute-start | bytes 552968 | tf_op jit(solution)/shard_map/ppermute | solution.py:334
  53.5 6.5 %shard_map.88 = (bf16[640,128]{1,0:T(8,128)(2,1)S(1)}, bf16[640,128]{1,0:T(8,128)(2,1)S(1)}) custom-call(s32[1]{0:T(128)} %bitcast.place_ref, bf16[720,128]{1,0:T(8,128)(2,1)S(1)} %collective-permute-done.18.refs_0_, bf16[720,128]{1,0:T(8,128)(2,1)S(1)} %collective-permute-done.13.refs_1_, bf16[1280,128]{1,0:T(8,128)(2,1)S(1)} %shard_map.86.refs_1_.refs_2_, ...), custom_call_target="tpu_custom_call" | custom-call | flops 1 | bytes 1 | tf_op jit(solution)/shard_map/pallas_call | solution.py:318
  60.0 0.9 %collective-permute-start.19 = (bf16[640,128]{1,0:T(8,128)(2,1)S(1)}, bf16[640,128]{1,0:T(8,128)(2,1)S(1)}, u32[]{:S(2)}, u32[]{:S(2)}) collective-permute-start(bf16[640,128]{1,0:T(8,128)(2,1)S(1)} %get-tuple-element.67), channel_id=1, source_target_pairs={{0,12},{2,14},{4,0},{6,2},{8,4},{10,6},{12,8},{14,10},{16,28},{18,... | collective-permute-start | bytes 491528 | tf_op jit(solution)/shard_map/ppermute | solution.py:334
  60.9 2.0 %collective-permute-start.20 = (bf16[640,128]{1,0:T(8,128)(2,1)S(1)}, bf16[640,128]{1,0:T(8,128)(2,1)S(1)}, u32[]{:S(2)}, u32[]{:S(2)}) collective-permute-start(bf16[640,128]{1,0:T(8,128)(2,1)S(1)} %get-tuple-element.68), channel_id=1, source_target_pairs={{0,8},{2,10},{4,12},{6,14},{8,0},{10,2},{12,4},{14,6},{16,24},{18,... | collective-permute-start | bytes 491528 | tf_op jit(solution)/shard_map/ppermute | solution.py:334
  62.9 3.5 %shard_map.89 = bf16[640,128]{1,0:T(8,128)(2,1)S(1)} custom-call(s32[1]{0:T(128)} %bitcast.place_ref, bf16[720,128]{1,0:T(8,128)(2,1)S(1)} %collective-permute-done.21.refs_0_, bf16[1280,128]{1,0:T(8,128)(2,1)S(1)} %shard_map.86.refs_1_.refs_2_, bf16[1280,128]{1,0:T(8,128)(2,1)S(1)} %collective-permute-done.10.refs_2_.refs_3_, ...), custom_call_target="tpu_custom_call" | custom-call | flops 1 | bytes 1 | tf_op jit(solution)/shard_map/pallas_call | solution.py:318
  66.5 3.5 %shard_map.87.refs_0_ = bf16[640,128]{1,0:T(8,128)(2,1)S(1)} custom-call(s32[1]{0:T(128)} %bitcast.place_ref, bf16[720,128]{1,0:T(8,128)(2,1)S(1)} %get-tuple-element.59.refs_0_, bf16[1280,128]{1,0:T(8,128)(2,1)S(1)} %shard_map.86.refs_1_.refs_2_, bf16[1280,128]{1,0:T(8,128)(2,1)S(1)} %collective-permute-done.10.refs_2_.refs_3_, ...), custom_call_target="tpu_custom_call" | custom-call | flops 1 | bytes 1 | tf_op jit(solution)/shard_map/pallas_call | solution.py:318
  70.0 3.4 %collective-permute-done.22.refs_3_ = bf16[640,128]{1,0:T(8,128)(2,1)S(1)} collective-permute-done((bf16[640,128]{1,0:T(8,128)(2,1)S(1)}, bf16[640,128]{1,0:T(8,128)(2,1)S(1)}, u32[]{:S(2)}, u32[]{:S(2)}) %collective-permute-start.22) | collective-permute-done | bytes 163872 | tf_op jit(solution)/shard_map/ppermute | solution.py:334
  73.4 1.0 %shard_map.90 = bf16[256,1280]{1,0:T(8,128)(2,1)} custom-call(s32[1]{0:T(128)} %bitcast.place_ref, bf16[640,128]{1,0:T(8,128)(2,1)S(1)} %shard_map.87.refs_0_, bf16[640,128]{1,0:T(8,128)(2,1)S(1)} %collective-permute-done.19.refs_1_, bf16[640,128]{1,0:T(8,128)(2,1)S(1)} %collective-permute-done.20.refs_2_, bf16[640,128]{1,0:T(8,128)(2,1)S(1)} %collective-permute-done.22.refs_3_), custom_call_target="tpu_custom_call" | custom-call | flops 1 | bytes 1 | tf_op jit(solution)/shard_map/pallas_call | solution.py:318
  (36 shorter events, 2.6 us)
Async XLA Ops:
  0.6 1.1 %copy-start = (bf16[1,256,1280]{2,1,0:T(8,128)(2,1)S(1)}, bf16[1,256,1280]{2,1,0:T(8,128)(2,1)}, u32[]{:S(2)}) copy-start(bf16[1,256,1280]{2,1,0:T(8,128)(2,1)} %param.6) | copy-start | bytes 1966084
  1.7 9.9 %copy-start.2 = (f32[1280]{0:T(1024)S(1)}, f32[1280]{0:T(1024)}, u32[]{:S(2)}) copy-start(f32[1280]{0:T(1024)} %gain_ref) | copy-start | bytes 15364
  1.7 9.9 %copy-start.3 = (f32[1280]{0:T(1024)S(1)}, f32[1280]{0:T(1024)}, u32[]{:S(2)}) copy-start(f32[1280]{0:T(1024)} %bias_ref) | copy-start | bytes 15364
  2.7 1.2 %collective-permute-start = (f32[8,128]{1,0:T(8,128)S(1)}, f32[8,128]{1,0:T(8,128)S(1)}, u32[]{:S(2)}, u32[]{:S(2)}) collective-permute-start(f32[8,128]{1,0:T(8,128)S(1)} %get-tuple-element.38.stats_ref.own_ref), channel_id=1, source_target_pairs={{0,2},{2,0},{4,6},{6,4},{8,10},{10,8},{12,14},{14,12},{16,18},{18,... | collective-permute-start | bytes 12296 | tf_op jit(solution)/shard_map/ppermute | solution.py:334
  2.8 0.9 %copy-start.1 = (bf16[1,16,2560]{2,1,0:T(8,128)(2,1)S(1)}, bf16[1,16,2560]{2,1,0:T(8,128)(2,1)}, u32[]{:S(2)}) copy-start(bf16[1,16,2560]{2,1,0:T(8,128)(2,1)} %param.7) | copy-start | bytes 245764
  4.0 7.7 %collective-permute-start.1 = (bf16[96,128]{1,0:T(8,128)(2,1)S(1)}, bf16[96,128]{1,0:T(8,128)(2,1)S(1)}, u32[]{:S(2)}, u32[]{:S(2)}) collective-permute-start(bf16[96,128]{1,0:T(8,128)(2,1)S(1)} %get-tuple-element.40), channel_id=1, source_target_pairs={{0,4},{2,6},{4,8},{6,10},{8,12},{10,14},{12,0},{14,2},{16,20},{18,... | collective-permute-start | bytes 73736 | tf_op jit(solution)/shard_map/ppermute | solution.py:334
  5.5 6.2 %collective-permute-start.2 = (bf16[96,128]{1,0:T(8,128)(2,1)S(1)}, bf16[96,128]{1,0:T(8,128)(2,1)S(1)}, u32[]{:S(2)}, u32[]{:S(2)}) collective-permute-start(bf16[96,128]{1,0:T(8,128)(2,1)S(1)} %get-tuple-element.41), channel_id=1, source_target_pairs={{0,8},{2,10},{4,12},{6,14},{8,0},{10,2},{12,4},{14,6},{16,24},{18,... | collective-permute-start | bytes 73736 | tf_op jit(solution)/shard_map/ppermute | solution.py:334
  8.3 3.8 %collective-permute-start.3 = (bf16[96,128]{1,0:T(8,128)(2,1)S(1)}, bf16[96,128]{1,0:T(8,128)(2,1)S(1)}, u32[]{:S(2)}, u32[]{:S(2)}) collective-permute-start(bf16[96,128]{1,0:T(8,128)(2,1)S(1)} %get-tuple-element.42), channel_id=1, source_target_pairs={{0,12},{2,14},{4,0},{6,2},{8,4},{10,6},{12,8},{14,10},{16,28},{18,... | collective-permute-start | bytes 73736 | tf_op jit(solution)/shard_map/ppermute | solution.py:334
  12.1 13.4 %collective-permute-start.6 = (bf16[336,128]{1,0:T(8,128)(2,1)S(1)}, bf16[336,128]{1,0:T(8,128)(2,1)S(1)}, u32[]{:S(2)}, u32[]{:S(2)}) collective-permute-start(bf16[336,128]{1,0:T(8,128)(2,1)S(1)} %shard_map.82.refs_0_), channel_id=1, source_target_pairs={{0,64},{2,66},{4,68},{6,70},{8,72},{10,74},{12,76},{14,78},{16,80}... | collective-permute-start | bytes 258056 | tf_op jit(solution)/shard_map/ppermute | solution.py:334
  15.5 10.0 %collective-permute-start.5 = (bf16[336,128]{1,0:T(8,128)(2,1)S(1)}, bf16[336,128]{1,0:T(8,128)(2,1)S(1)}, u32[]{:S(2)}, u32[]{:S(2)}) collective-permute-start(bf16[336,128]{1,0:T(8,128)(2,1)S(1)} %shard_map.82.refs_0_), channel_id=1, source_target_pairs={{0,192},{2,194},{4,196},{6,198},{8,200},{10,202},{12,204},{14,206}... | collective-permute-start | bytes 258056 | tf_op jit(solution)/shard_map/ppermute | solution.py:334
  17.7 11.2 %collective-permute-start.4 = (bf16[336,128]{1,0:T(8,128)(2,1)S(1)}, bf16[336,128]{1,0:T(8,128)(2,1)S(1)}, u32[]{:S(2)}, u32[]{:S(2)}) collective-permute-start(bf16[336,128]{1,0:T(8,128)(2,1)S(1)} %shard_map.82.refs_0_), channel_id=1, source_target_pairs={{0,128},{2,130},{4,132},{6,134},{8,136},{10,138},{12,140},{14,142}... | collective-permute-start | bytes 258056 | tf_op jit(solution)/shard_map/ppermute | solution.py:334
  28.9 7.1 %collective-permute-start.9 = (f32[8,128]{1,0:T(8,128)S(1)}, f32[8,128]{1,0:T(8,128)S(1)}, u32[]{:S(2)}, u32[]{:S(2)}) collective-permute-start(f32[8,128]{1,0:T(8,128)S(1)} %shard_map.84.s0.stats_ref), channel_id=1, source_target_pairs={{0,48},{2,50},{4,52},{6,54},{8,56},{10,58},{12,60},{14,62},{16,0},... | collective-permute-start | bytes 12296 | tf_op jit(solution)/shard_map/ppermute | solution.py:334
  32.0 5.2 %collective-permute-start.8 = (f32[8,128]{1,0:T(8,128)S(1)}, f32[8,128]{1,0:T(8,128)S(1)}, u32[]{:S(2)}, u32[]{:S(2)}) collective-permute-start(f32[8,128]{1,0:T(8,128)S(1)} %shard_map.84.s0.stats_ref), channel_id=1, source_target_pairs={{0,32},{2,34},{4,36},{6,38},{8,40},{10,42},{12,44},{14,46},{16,48}... | collective-permute-start | bytes 12296 | tf_op jit(solution)/shard_map/ppermute | solution.py:334
  32.6 4.9 %collective-permute-start.7 = (f32[8,128]{1,0:T(8,128)S(1)}, f32[8,128]{1,0:T(8,128)S(1)}, u32[]{:S(2)}, u32[]{:S(2)}) collective-permute-start(f32[8,128]{1,0:T(8,128)S(1)} %shard_map.84.s0.stats_ref), channel_id=1, source_target_pairs={{0,16},{2,18},{4,20},{6,22},{8,24},{10,26},{12,28},{14,30},{16,32}... | collective-permute-start | bytes 12296 | tf_op jit(solution)/shard_map/ppermute | solution.py:334
  33.6 15.3 %collective-permute-start.11 = (bf16[1280,128]{1,0:T(8,128)(2,1)S(1)}, bf16[1280,128]{1,0:T(8,128)(2,1)S(1)}, u32[]{:S(2)}, u32[]{:S(2)}) collective-permute-start(bf16[1280,128]{1,0:T(8,128)(2,1)S(1)} %shard_map.86.refs_1_.refs_2_), channel_id=1, source_target_pairs={{0,48},{2,50},{4,52},{6,54},{8,56},{10,58},{12,60},{14,62},{16,0},... | collective-permute-start | bytes 983048 | tf_op jit(solution)/shard_map/ppermute | solution.py:334
  36.0 15.4 %collective-permute-start.10 = (bf16[1280,128]{1,0:T(8,128)(2,1)S(1)}, bf16[1280,128]{1,0:T(8,128)(2,1)S(1)}, u32[]{:S(2)}, u32[]{:S(2)}) collective-permute-start(bf16[1280,128]{1,0:T(8,128)(2,1)S(1)} %shard_map.86.refs_1_.refs_2_), channel_id=1, source_target_pairs={{0,16},{2,18},{4,20},{6,22},{8,24},{10,26},{12,28},{14,30},{16,32}... | collective-permute-start | bytes 983048 | tf_op jit(solution)/shard_map/ppermute | solution.py:334
  37.5 13.9 %collective-permute-start.12 = (bf16[1280,128]{1,0:T(8,128)(2,1)S(1)}, bf16[1280,128]{1,0:T(8,128)(2,1)S(1)}, u32[]{:S(2)}, u32[]{:S(2)}) collective-permute-start(bf16[1280,128]{1,0:T(8,128)(2,1)S(1)} %shard_map.86.refs_1_.refs_2_), channel_id=1, source_target_pairs={{0,32},{2,34},{4,36},{6,38},{8,40},{10,42},{12,44},{14,46},{16,48}... | collective-permute-start | bytes 983048 | tf_op jit(solution)/shard_map/ppermute | solution.py:334
  42.2 6.7 %collective-permute-start.13 = (bf16[720,128]{1,0:T(8,128)(2,1)S(1)}, bf16[720,128]{1,0:T(8,128)(2,1)S(1)}, u32[]{:S(2)}, u32[]{:S(2)}) collective-permute-start(bf16[720,128]{1,0:T(8,128)(2,1)S(1)} %get-tuple-element.61), channel_id=1, source_target_pairs={{0,4},{2,6},{4,8},{6,10},{8,12},{10,14},{12,0},{14,2},{16,20},{18,... | collective-permute-start | bytes 552968 | tf_op jit(solution)/shard_map/ppermute | solution.py:334
  42.7 9.2 %collective-permute-start.18 = (bf16[720,128]{1,0:T(8,128)(2,1)S(1)}, bf16[720,128]{1,0:T(8,128)(2,1)S(1)}, u32[]{:S(2)}, u32[]{:S(2)}) collective-permute-start(bf16[720,128]{1,0:T(8,128)(2,1)S(1)} %get-tuple-element.66), channel_id=1, source_target_pairs={{0,8},{2,10},{4,12},{6,14},{8,0},{10,2},{12,4},{14,6},{16,24},{18,... | collective-permute-start | bytes 552968 | tf_op jit(solution)/shard_map/ppermute | solution.py:334
  48.9 3.8 %collective-permute-start.14 = (bf16[1280,128]{1,0:T(8,128)(2,1)S(1)}, bf16[1280,128]{1,0:T(8,128)(2,1)S(1)}, u32[]{:S(2)}, u32[]{:S(2)}) collective-permute-start(bf16[1280,128]{1,0:T(8,128)(2,1)S(1)} %shard_map.86.refs_1_.refs_2_), channel_id=1, source_target_pairs={{0,2},{2,0},{4,6},{6,4},{8,10},{10,8},{12,14},{14,12},{16,18},{18,... | collective-permute-start | bytes 983048 | tf_op jit(solution)/shard_map/ppermute | solution.py:334
  48.9 3.8 %collective-permute-start.16 = (bf16[1280,128]{1,0:T(8,128)(2,1)S(1)}, bf16[1280,128]{1,0:T(8,128)(2,1)S(1)}, u32[]{:S(2)}, u32[]{:S(2)}) collective-permute-start(bf16[1280,128]{1,0:T(8,128)(2,1)S(1)} %collective-permute-done.11.refs_3_.refs_4_), channel_id=1, source_target_pairs={{0,2},{2,0},{4,6},{6,4},{8,10},{10,8},{12,14},{14,12},{16,18},{18,... | collective-permute-start | bytes 983048 | tf_op jit(solution)/shard_map/ppermute | solution.py:334
  51.4 1.6 %collective-permute-start.15 = (bf16[1280,128]{1,0:T(8,128)(2,1)S(1)}, bf16[1280,128]{1,0:T(8,128)(2,1)S(1)}, u32[]{:S(2)}, u32[]{:S(2)}) collective-permute-start(bf16[1280,128]{1,0:T(8,128)(2,1)S(1)} %collective-permute-done.10.refs_2_.refs_3_), channel_id=1, source_target_pairs={{0,2},{2,0},{4,6},{6,4},{8,10},{10,8},{12,14},{14,12},{16,18},{18,... | collective-permute-start | bytes 983048 | tf_op jit(solution)/shard_map/ppermute | solution.py:334
  51.4 2.1 %collective-permute-start.17 = (bf16[1280,128]{1,0:T(8,128)(2,1)S(1)}, bf16[1280,128]{1,0:T(8,128)(2,1)S(1)}, u32[]{:S(2)}, u32[]{:S(2)}) collective-permute-start(bf16[1280,128]{1,0:T(8,128)(2,1)S(1)} %collective-permute-done.12.refs_4_.refs_5_), channel_id=1, source_target_pairs={{0,2},{2,0},{4,6},{6,4},{8,10},{10,8},{12,14},{14,12},{16,18},{18,... | collective-permute-start | bytes 983048 | tf_op jit(solution)/shard_map/ppermute | solution.py:334
  51.9 11.0 %collective-permute-start.21 = (bf16[720,128]{1,0:T(8,128)(2,1)S(1)}, bf16[720,128]{1,0:T(8,128)(2,1)S(1)}, u32[]{:S(2)}, u32[]{:S(2)}) collective-permute-start(bf16[720,128]{1,0:T(8,128)(2,1)S(1)} %get-tuple-element.70), channel_id=1, source_target_pairs={{0,12},{2,14},{4,0},{6,2},{8,4},{10,6},{12,8},{14,10},{16,28},{18,... | collective-permute-start | bytes 552968 | tf_op jit(solution)/shard_map/ppermute | solution.py:334
  60.0 10.0 %collective-permute-start.19 = (bf16[640,128]{1,0:T(8,128)(2,1)S(1)}, bf16[640,128]{1,0:T(8,128)(2,1)S(1)}, u32[]{:S(2)}, u32[]{:S(2)}) collective-permute-start(bf16[640,128]{1,0:T(8,128)(2,1)S(1)} %get-tuple-element.67), channel_id=1, source_target_pairs={{0,12},{2,14},{4,0},{6,2},{8,4},{10,6},{12,8},{14,10},{16,28},{18,... | collective-permute-start | bytes 491528 | tf_op jit(solution)/shard_map/ppermute | solution.py:334
  60.9 9.1 %collective-permute-start.20 = (bf16[640,128]{1,0:T(8,128)(2,1)S(1)}, bf16[640,128]{1,0:T(8,128)(2,1)S(1)}, u32[]{:S(2)}, u32[]{:S(2)}) collective-permute-start(bf16[640,128]{1,0:T(8,128)(2,1)S(1)} %get-tuple-element.68), channel_id=1, source_target_pairs={{0,8},{2,10},{4,12},{6,14},{8,0},{10,2},{12,4},{14,6},{16,24},{18,... | collective-permute-start | bytes 491528 | tf_op jit(solution)/shard_map/ppermute | solution.py:334
  66.4 7.0 %collective-permute-start.22 = (bf16[640,128]{1,0:T(8,128)(2,1)S(1)}, bf16[640,128]{1,0:T(8,128)(2,1)S(1)}, u32[]{:S(2)}, u32[]{:S(2)}) collective-permute-start(bf16[640,128]{1,0:T(8,128)(2,1)S(1)} %shard_map.89), channel_id=1, source_target_pairs={{0,4},{2,6},{4,8},{6,10},{8,12},{10,14},{12,0},{14,2},{16,20},{18,... | collective-permute-start | bytes 491528 | tf_op jit(solution)/shard_map/ppermute | solution.py:334

commit v12 on v5

--- a/solution.py
+++ b/solution.py
@@ -391,8 +391,8 @@
     (stats,) = call(stats_kernel, [VMEM] * 4, [((8, LANES), f32)], *parts)
     all_stats = [stats] + [shift(stats, "y", k) for k in (1, 2, 3)]
     (piece,) = call(piece_kernel, [VMEM] * 5, [table], stats, *parts)
-    pieces = [piece, shift(piece, "y", 1), shift(piece, "y", 3)]
-    pieces.append(shift(after(piece, *all_stats), "y", 2))
+    pieces = [piece, shift(piece, "y", 1), shift(piece, "y", 2)]
+    pieces.append(shift(after(piece, *all_stats), "y", 3))
     *queries, fresh = call(
         project_kernel,
         [SMEM] + [VMEM] * 8,

time: 73.5 us -> 73.2 us (level)
  transfers between devices with their start and end apart: 23 -> 23, of which waited for: 9 -> 8; matrix products, arithmetic and copies ran while one was open for 0% -> 0% of each run, Pallas kernels for 29% -> 29%
where the time goes in v12:
time: 73.2 us; the launch traced here: 72.9 us
  starting transfers between devices  34.1 us (47%)
  Pallas kernels  23.4 us (32%)
  waiting for transfers between devices  11.1 us (15%)
  local copies, waits for them, and re-layouts  3.36 us (5%)
  between operations  0.81 us (1%)
    ppermute x23, starting transfers between devices, permute(): return lax.ppermute(array, 'patch', pairs)  34.1 us
    pallas_call x14, Pallas kernels, call(): pl.pallas_call(kernel, in_specs=ins, out_specs=[VMEM] * len(outs), out_sh...  23.4 us
    ppermute x23, waiting for transfers between devices, permute(): return lax.ppermute(array, 'patch', pairs)  11.1 us
    unnamed x8, local copies, waits for them, and re-layouts  3.36 us
  transfers between devices with their start and end apart: 23, of which 8 were waited for; matrix products, arithmetic and copies ran while one was open for 0% of the time, Pallas kernels for 29%

profile of v12, /device:TPU:32, one launch (start us, length us, event | category | flops | bytes accessed | tf_op | source)
XLA Modules:
  0.0 72.9 jit_solution(13008513890127265717)
XLA Ops:
  0.6 1.1 %copy-done = bf16[1,256,1280]{2,1,0:T(8,128)(2,1)S(1)} copy-done((bf16[1,256,1280]{2,1,0:T(8,128)(2,1)S(1)}, bf16[1,256,1280]{2,1,0:T(8,128)(2,1)}, u32[]{:S(2)}) %copy-start) | copy-done | bytes 655384
  1.7 1.0 %shard_map.77 = (f32[8,128]{1,0:T(8,128)S(1)}, bf16[256,1280]{1,0:T(8,128)(2,1)S(1)}) custom-call(bf16[256,1280]{1,0:T(8,128)(2,1)S(1)} %bitcast.5), custom_call_target="tpu_custom_call" | custom-call | flops 1 | bytes 1 | tf_op jit(solution)/shard_map/pallas_call | solution.py:318
  2.8 0.9 %copy-done.1 = bf16[1,16,2560]{2,1,0:T(8,128)(2,1)S(1)} copy-done((bf16[1,16,2560]{2,1,0:T(8,128)(2,1)S(1)}, bf16[1,16,2560]{2,1,0:T(8,128)(2,1)}, u32[]{:S(2)}) %copy-start.1) | copy-done | bytes 81944
  4.0 1.6 %collective-permute-start.1 = (bf16[96,128]{1,0:T(8,128)(2,1)S(1)}, bf16[96,128]{1,0:T(8,128)(2,1)S(1)}, u32[]{:S(2)}, u32[]{:S(2)}) collective-permute-start(bf16[96,128]{1,0:T(8,128)(2,1)S(1)} %get-tuple-element.39), channel_id=1, source_target_pairs={{0,4},{2,6},{4,8},{6,10},{8,12},{10,14},{12,0},{14,2},{16,20},{18,... | collective-permute-start | bytes 73736 | tf_op jit(solution)/shard_map/ppermute | solution.py:334
  5.5 2.7 %collective-permute-start.2 = (bf16[96,128]{1,0:T(8,128)(2,1)S(1)}, bf16[96,128]{1,0:T(8,128)(2,1)S(1)}, u32[]{:S(2)}, u32[]{:S(2)}) collective-permute-start(bf16[96,128]{1,0:T(8,128)(2,1)S(1)} %get-tuple-element.40), channel_id=1, source_target_pairs={{0,8},{2,10},{4,12},{6,14},{8,0},{10,2},{12,4},{14,6},{16,24},{18,... | collective-permute-start | bytes 73736 | tf_op jit(solution)/shard_map/ppermute | solution.py:334
  8.3 1.4 %collective-permute-start.3 = (bf16[96,128]{1,0:T(8,128)(2,1)S(1)}, bf16[96,128]{1,0:T(8,128)(2,1)S(1)}, u32[]{:S(2)}, u32[]{:S(2)}) collective-permute-start(bf16[96,128]{1,0:T(8,128)(2,1)S(1)} %get-tuple-element.41), channel_id=1, source_target_pairs={{0,12},{2,14},{4,0},{6,2},{8,4},{10,6},{12,8},{14,10},{16,28},{18,... | collective-permute-start | bytes 73736 | tf_op jit(solution)/shard_map/ppermute | solution.py:334
  9.7 0.7 copy-done.2
  11.1 1.0 %collective-permute-done.3.refs_3_ = bf16[96,128]{1,0:T(8,128)(2,1)S(1)} collective-permute-done((bf16[96,128]{1,0:T(8,128)(2,1)S(1)}, bf16[96,128]{1,0:T(8,128)(2,1)S(1)}, u32[]{:S(2)}, u32[]{:S(2)}) %collective-permute-start.3) | collective-permute-done | bytes 24608 | tf_op jit(solution)/shard_map/ppermute | solution.py:334
  12.1 3.3 %collective-permute-start.6 = (bf16[336,128]{1,0:T(8,128)(2,1)S(1)}, bf16[336,128]{1,0:T(8,128)(2,1)S(1)}, u32[]{:S(2)}, u32[]{:S(2)}) collective-permute-start(bf16[336,128]{1,0:T(8,128)(2,1)S(1)} %shard_map.81.refs_0_), channel_id=1, source_target_pairs={{0,64},{2,66},{4,68},{6,70},{8,72},{10,74},{12,76},{14,78},{16,80}... | collective-permute-start | bytes 258056 | tf_op jit(solution)/shard_map/ppermute | solution.py:334
  15.5 2.2 %collective-permute-start.5 = (bf16[336,128]{1,0:T(8,128)(2,1)S(1)}, bf16[336,128]{1,0:T(8,128)(2,1)S(1)}, u32[]{:S(2)}, u32[]{:S(2)}) collective-permute-start(bf16[336,128]{1,0:T(8,128)(2,1)S(1)} %shard_map.81.refs_0_), channel_id=1, source_target_pairs={{0,192},{2,194},{4,196},{6,198},{8,200},{10,202},{12,204},{14,206}... | collective-permute-start | bytes 258056 | tf_op jit(solution)/shard_map/ppermute | solution.py:334
  17.7 4.9 %collective-permute-start.4 = (bf16[336,128]{1,0:T(8,128)(2,1)S(1)}, bf16[336,128]{1,0:T(8,128)(2,1)S(1)}, u32[]{:S(2)}, u32[]{:S(2)}) collective-permute-start(bf16[336,128]{1,0:T(8,128)(2,1)S(1)} %shard_map.81.refs_0_), channel_id=1, source_target_pairs={{0,128},{2,130},{4,132},{6,134},{8,136},{10,138},{12,140},{14,142}... | collective-permute-start | bytes 258056 | tf_op jit(solution)/shard_map/ppermute | solution.py:334
  22.6 1.9 %shard_map.82.query_ref = bf16[1280,1280]{1,0:T(8,128)(2,1)S(1)} custom-call(bf16[1280,1280]{1,0:T(8,128)(2,1)} %source_hbm), custom_call_target="tpu_custom_call" | custom-call | flops 1 | bytes 1 | tf_op jit(solution)/shard_map/pallas_call | solution.py:318
  24.6 2.9 %shard_map.83.pair_ref = bf16[1280,2560]{1,0:T(8,128)(2,1)S(1)} custom-call(bf16[1280,2560]{1,0:T(8,128)(2,1)} %source_hbm.1), custom_call_target="tpu_custom_call" | custom-call | flops 1 | bytes 1 | tf_op jit(solution)/shard_map/pallas_call | solution.py:318
  27.5 1.2 %collective-permute-done.4.refs_1_ = bf16[336,128]{1,0:T(8,128)(2,1)S(1)} collective-permute-done((bf16[336,128]{1,0:T(8,128)(2,1)S(1)}, bf16[336,128]{1,0:T(8,128)(2,1)S(1)}, u32[]{:S(2)}, u32[]{:S(2)}) %collective-permute-start.4) | collective-permute-done | bytes 86048 | tf_op jit(solution)/shard_map/ppermute | solution.py:334
  28.7 3.1 %collective-permute-start.9 = (f32[8,128]{1,0:T(8,128)S(1)}, f32[8,128]{1,0:T(8,128)S(1)}, u32[]{:S(2)}, u32[]{:S(2)}) collective-permute-start(f32[8,128]{1,0:T(8,128)S(1)} %shard_map.84.s0.stats_ref), channel_id=1, source_target_pairs={{0,48},{2,50},{4,52},{6,54},{8,56},{10,58},{12,60},{14,62},{16,0},... | collective-permute-start | bytes 12296 | tf_op jit(solution)/shard_map/ppermute | solution.py:334
  32.4 1.0 %collective-permute-start.7 = (f32[8,128]{1,0:T(8,128)S(1)}, f32[8,128]{1,0:T(8,128)S(1)}, u32[]{:S(2)}, u32[]{:S(2)}) collective-permute-start(f32[8,128]{1,0:T(8,128)S(1)} %shard_map.84.s0.stats_ref), channel_id=1, source_target_pairs={{0,16},{2,18},{4,20},{6,22},{8,24},{10,26},{12,28},{14,30},{16,32}... | collective-permute-start | bytes 12296 | tf_op jit(solution)/shard_map/ppermute | solution.py:334
  33.4 2.0 %collective-permute-start.11 = (bf16[1280,128]{1,0:T(8,128)(2,1)S(1)}, bf16[1280,128]{1,0:T(8,128)(2,1)S(1)}, u32[]{:S(2)}, u32[]{:S(2)}) collective-permute-start(bf16[1280,128]{1,0:T(8,128)(2,1)S(1)} %shard_map.86.refs_1_.refs_2_), channel_id=1, source_target_pairs={{0,32},{2,34},{4,36},{6,38},{8,40},{10,42},{12,44},{14,46},{16,48}... | collective-permute-start | bytes 983048 | tf_op jit(solution)/shard_map/ppermute | solution.py:334
  35.4 1.2 %collective-permute-start.10 = (bf16[1280,128]{1,0:T(8,128)(2,1)S(1)}, bf16[1280,128]{1,0:T(8,128)(2,1)S(1)}, u32[]{:S(2)}, u32[]{:S(2)}) collective-permute-start(bf16[1280,128]{1,0:T(8,128)(2,1)S(1)} %shard_map.86.refs_1_.refs_2_), channel_id=1, source_target_pairs={{0,16},{2,18},{4,20},{6,22},{8,24},{10,26},{12,28},{14,30},{16,32}... | collective-permute-start | bytes 983048 | tf_op jit(solution)/shard_map/ppermute | solution.py:334
  37.1 0.9 %collective-permute-done.7.s1 = f32[8,128]{1,0:T(8,128)S(1)} collective-permute-done((f32[8,128]{1,0:T(8,128)S(1)}, f32[8,128]{1,0:T(8,128)S(1)}, u32[]{:S(2)}, u32[]{:S(2)}) %collective-permute-start.7) | collective-permute-done | bytes 4128 | tf_op jit(solution)/shard_map/ppermute | solution.py:334
  37.9 0.8 %collective-permute-start.12 = (bf16[1280,128]{1,0:T(8,128)(2,1)S(1)}, bf16[1280,128]{1,0:T(8,128)(2,1)S(1)}, u32[]{:S(2)}, u32[]{:S(2)}) collective-permute-start(bf16[1280,128]{1,0:T(8,128)(2,1)S(1)} %shard_map.86.refs_1_.refs_2_), channel_id=1, source_target_pairs={{0,48},{2,50},{4,52},{6,54},{8,56},{10,58},{12,60},{14,62},{16,0},... | collective-permute-start | bytes 983048 | tf_op jit(solution)/shard_map/ppermute | solution.py:334
  38.7 3.0 %shard_map.85 = (bf16[720,128]{1,0:T(8,128)(2,1)S(1)}, bf16[720,128]{1,0:T(8,128)(2,1)S(1)}, bf16[720,128]{1,0:T(8,128)(2,1)S(1)}, bf16[720,128]{1,0:T(8,128)(2,1)S(1)}, bf16[16,2560]{1,0:T(8,128)(2,1)}) custom-call(s32[1]{0:T(128)} %bitcast.place_ref, bf16[256,1280]{1,0:T(8,128)(2,1)S(1)} %get-tuple-element.36.tokens_ref, ...), custom_call_target="tpu_custom_call" | custom-call | flops 1 | bytes 1 | tf_op jit(solution)/shard_map/pallas_call | solution.py:318
  42.0 3.6 %collective-permute-start.18 = (bf16[720,128]{1,0:T(8,128)(2,1)S(1)}, bf16[720,128]{1,0:T(8,128)(2,1)S(1)}, u32[]{:S(2)}, u32[]{:S(2)}) collective-permute-start(bf16[720,128]{1,0:T(8,128)(2,1)S(1)} %get-tuple-element.64), channel_id=1, source_target_pairs={{0,8},{2,10},{4,12},{6,14},{8,0},{10,2},{12,4},{14,6},{16,24},{18,... | collective-permute-start | bytes 552968 | tf_op jit(solution)/shard_map/ppermute | solution.py:334
  45.5 2.9 %collective-permute-done.13.refs_1_ = bf16[720,128]{1,0:T(8,128)(2,1)S(1)} collective-permute-done((bf16[720,128]{1,0:T(8,128)(2,1)S(1)}, bf16[720,128]{1,0:T(8,128)(2,1)S(1)}, u32[]{:S(2)}, u32[]{:S(2)}) %collective-permute-start.13) | collective-permute-done | bytes 184352 | tf_op jit(solution)/shard_map/ppermute | solution.py:334
  49.5 1.6 %collective-permute-done.18.refs_0_ = bf16[720,128]{1,0:T(8,128)(2,1)S(1)} collective-permute-done((bf16[720,128]{1,0:T(8,128)(2,1)S(1)}, bf16[720,128]{1,0:T(8,128)(2,1)S(1)}, u32[]{:S(2)}, u32[]{:S(2)}) %collective-permute-start.18) | collective-permute-done | bytes 184352 | tf_op jit(solution)/shard_map/ppermute | solution.py:334
  51.0 0.9 %collective-permute-start.21 = (bf16[720,128]{1,0:T(8,128)(2,1)S(1)}, bf16[720,128]{1,0:T(8,128)(2,1)S(1)}, u32[]{:S(2)}, u32[]{:S(2)}) collective-permute-start(bf16[720,128]{1,0:T(8,128)(2,1)S(1)} %get-tuple-element.68), channel_id=1, source_target_pairs={{0,12},{2,14},{4,0},{6,2},{8,4},{10,6},{12,8},{14,10},{16,28},{18,... | collective-permute-start | bytes 552968 | tf_op jit(solution)/shard_map/ppermute | solution.py:334
  52.0 6.5 %shard_map.88 = (bf16[640,128]{1,0:T(8,128)(2,1)S(1)}, bf16[640,128]{1,0:T(8,128)(2,1)S(1)}) custom-call(s32[1]{0:T(128)} %bitcast.place_ref, bf16[720,128]{1,0:T(8,128)(2,1)S(1)} %collective-permute-done.18.refs_0_, bf16[720,128]{1,0:T(8,128)(2,1)S(1)} %collective-permute-done.13.refs_1_, bf16[1280,128]{1,0:T(8,128)(2,1)S(1)} %shard_map.86.refs_1_.refs_2_, ...), custom_call_target="tpu_custom_call" | custom-call | flops 1 | bytes 1 | tf_op jit(solution)/shard_map/pallas_call | solution.py:318
  58.5 1.3 %collective-permute-start.19 = (bf16[640,128]{1,0:T(8,128)(2,1)S(1)}, bf16[640,128]{1,0:T(8,128)(2,1)S(1)}, u32[]{:S(2)}, u32[]{:S(2)}) collective-permute-start(bf16[640,128]{1,0:T(8,128)(2,1)S(1)} %get-tuple-element.65), channel_id=1, source_target_pairs={{0,12},{2,14},{4,0},{6,2},{8,4},{10,6},{12,8},{14,10},{16,28},{18,... | collective-permute-start | bytes 491528 | tf_op jit(solution)/shard_map/ppermute | solution.py:334
  59.8 2.0 %collective-permute-start.20 = (bf16[640,128]{1,0:T(8,128)(2,1)S(1)}, bf16[640,128]{1,0:T(8,128)(2,1)S(1)}, u32[]{:S(2)}, u32[]{:S(2)}) collective-permute-start(bf16[640,128]{1,0:T(8,128)(2,1)S(1)} %get-tuple-element.66), channel_id=1, source_target_pairs={{0,8},{2,10},{4,12},{6,14},{8,0},{10,2},{12,4},{14,6},{16,24},{18,... | collective-permute-start | bytes 491528 | tf_op jit(solution)/shard_map/ppermute | solution.py:334
  61.8 3.5 %shard_map.89 = bf16[640,128]{1,0:T(8,128)(2,1)S(1)} custom-call(s32[1]{0:T(128)} %bitcast.place_ref, bf16[720,128]{1,0:T(8,128)(2,1)S(1)} %collective-permute-done.21.refs_0_, bf16[1280,128]{1,0:T(8,128)(2,1)S(1)} %shard_map.86.refs_1_.refs_2_, bf16[1280,128]{1,0:T(8,128)(2,1)S(1)} %collective-permute-done.10.refs_2_.refs_3_, ...), custom_call_target="tpu_custom_call" | custom-call | flops 1 | bytes 1 | tf_op jit(solution)/shard_map/pallas_call | solution.py:318
  65.3 3.5 %shard_map.87.refs_0_ = bf16[640,128]{1,0:T(8,128)(2,1)S(1)} custom-call(s32[1]{0:T(128)} %bitcast.place_ref, bf16[720,128]{1,0:T(8,128)(2,1)S(1)} %get-tuple-element.57.refs_0_, bf16[1280,128]{1,0:T(8,128)(2,1)S(1)} %shard_map.86.refs_1_.refs_2_, bf16[1280,128]{1,0:T(8,128)(2,1)S(1)} %collective-permute-done.10.refs_2_.refs_3_, ...), custom_call_target="tpu_custom_call" | custom-call | flops 1 | bytes 1 | tf_op jit(solution)/shard_map/pallas_call | solution.py:318
  68.8 3.0 %collective-permute-done.22.refs_3_ = bf16[640,128]{1,0:T(8,128)(2,1)S(1)} collective-permute-done((bf16[640,128]{1,0:T(8,128)(2,1)S(1)}, bf16[640,128]{1,0:T(8,128)(2,1)S(1)}, u32[]{:S(2)}, u32[]{:S(2)}) %collective-permute-start.22) | collective-permute-done | bytes 163872 | tf_op jit(solution)/shard_map/ppermute | solution.py:334
  71.8 1.0 %shard_map.90 = bf16[256,1280]{1,0:T(8,128)(2,1)} custom-call(s32[1]{0:T(128)} %bitcast.place_ref, bf16[640,128]{1,0:T(8,128)(2,1)S(1)} %shard_map.87.refs_0_, bf16[640,128]{1,0:T(8,128)(2,1)S(1)} %collective-permute-done.19.refs_1_, bf16[640,128]{1,0:T(8,128)(2,1)S(1)} %collective-permute-done.20.refs_2_, bf16[640,128]{1,0:T(8,128)(2,1)S(1)} %collective-permute-done.22.refs_3_), custom_call_target="tpu_custom_call" | custom-call | flops 1 | bytes 1 | tf_op jit(solution)/shard_map/pallas_call | solution.py:318
  (36 shorter events, 3.7 us)
Async XLA Ops:
  0.6 1.1 %copy-start = (bf16[1,256,1280]{2,1,0:T(8,128)(2,1)S(1)}, bf16[1,256,1280]{2,1,0:T(8,128)(2,1)}, u32[]{:S(2)}) copy-start(bf16[1,256,1280]{2,1,0:T(8,128)(2,1)} %param.6) | copy-start | bytes 1966084
  2.7 1.2 %collective-permute-start = (f32[8,128]{1,0:T(8,128)S(1)}, f32[8,128]{1,0:T(8,128)S(1)}, u32[]{:S(2)}, u32[]{:S(2)}) collective-permute-start(f32[8,128]{1,0:T(8,128)S(1)} %get-tuple-element.37.stats_ref.own_ref), channel_id=1, source_target_pairs={{0,2},{2,0},{4,6},{6,4},{8,10},{10,8},{12,14},{14,12},{16,18},{18,... | collective-permute-start | bytes 12296 | tf_op jit(solution)/shard_map/ppermute | solution.py:334
  2.8 0.9 %copy-start.1 = (bf16[1,16,2560]{2,1,0:T(8,128)(2,1)S(1)}, bf16[1,16,2560]{2,1,0:T(8,128)(2,1)}, u32[]{:S(2)}) copy-start(bf16[1,16,2560]{2,1,0:T(8,128)(2,1)} %param.7) | copy-start | bytes 245764
  4.0 7.1 %collective-permute-start.1 = (bf16[96,128]{1,0:T(8,128)(2,1)S(1)}, bf16[96,128]{1,0:T(8,128)(2,1)S(1)}, u32[]{:S(2)}, u32[]{:S(2)}) collective-permute-start(bf16[96,128]{1,0:T(8,128)(2,1)S(1)} %get-tuple-element.39), channel_id=1, source_target_pairs={{0,4},{2,6},{4,8},{6,10},{8,12},{10,14},{12,0},{14,2},{16,20},{18,... | collective-permute-start | bytes 73736 | tf_op jit(solution)/shard_map/ppermute | solution.py:334
  5.5 5.6 %collective-permute-start.2 = (bf16[96,128]{1,0:T(8,128)(2,1)S(1)}, bf16[96,128]{1,0:T(8,128)(2,1)S(1)}, u32[]{:S(2)}, u32[]{:S(2)}) collective-permute-start(bf16[96,128]{1,0:T(8,128)(2,1)S(1)} %get-tuple-element.40), channel_id=1, source_target_pairs={{0,8},{2,10},{4,12},{6,14},{8,0},{10,2},{12,4},{14,6},{16,24},{18,... | collective-permute-start | bytes 73736 | tf_op jit(solution)/shard_map/ppermute | solution.py:334
  8.3 3.8 %collective-permute-start.3 = (bf16[96,128]{1,0:T(8,128)(2,1)S(1)}, bf16[96,128]{1,0:T(8,128)(2,1)S(1)}, u32[]{:S(2)}, u32[]{:S(2)}) collective-permute-start(bf16[96,128]{1,0:T(8,128)(2,1)S(1)} %get-tuple-element.41), channel_id=1, source_target_pairs={{0,12},{2,14},{4,0},{6,2},{8,4},{10,6},{12,8},{14,10},{16,28},{18,... | collective-permute-start | bytes 73736 | tf_op jit(solution)/shard_map/ppermute | solution.py:334
  9.7 0.7 copy-start.2
  10.4 0.7 copy-start.3
  12.1 15.3 %collective-permute-start.6 = (bf16[336,128]{1,0:T(8,128)(2,1)S(1)}, bf16[336,128]{1,0:T(8,128)(2,1)S(1)}, u32[]{:S(2)}, u32[]{:S(2)}) collective-permute-start(bf16[336,128]{1,0:T(8,128)(2,1)S(1)} %shard_map.81.refs_0_), channel_id=1, source_target_pairs={{0,64},{2,66},{4,68},{6,70},{8,72},{10,74},{12,76},{14,78},{16,80}... | collective-permute-start | bytes 258056 | tf_op jit(solution)/shard_map/ppermute | solution.py:334
  15.5 12.0 %collective-permute-start.5 = (bf16[336,128]{1,0:T(8,128)(2,1)S(1)}, bf16[336,128]{1,0:T(8,128)(2,1)S(1)}, u32[]{:S(2)}, u32[]{:S(2)}) collective-permute-start(bf16[336,128]{1,0:T(8,128)(2,1)S(1)} %shard_map.81.refs_0_), channel_id=1, source_target_pairs={{0,192},{2,194},{4,196},{6,198},{8,200},{10,202},{12,204},{14,206}... | collective-permute-start | bytes 258056 | tf_op jit(solution)/shard_map/ppermute | solution.py:334
  17.7 10.9 %collective-permute-start.4 = (bf16[336,128]{1,0:T(8,128)(2,1)S(1)}, bf16[336,128]{1,0:T(8,128)(2,1)S(1)}, u32[]{:S(2)}, u32[]{:S(2)}) collective-permute-start(bf16[336,128]{1,0:T(8,128)(2,1)S(1)} %shard_map.81.refs_0_), channel_id=1, source_target_pairs={{0,128},{2,130},{4,132},{6,134},{8,136},{10,138},{12,140},{14,142}... | collective-permute-start | bytes 258056 | tf_op jit(solution)/shard_map/ppermute | solution.py:334
  28.7 7.9 %collective-permute-start.9 = (f32[8,128]{1,0:T(8,128)S(1)}, f32[8,128]{1,0:T(8,128)S(1)}, u32[]{:S(2)}, u32[]{:S(2)}) collective-permute-start(f32[8,128]{1,0:T(8,128)S(1)} %shard_map.84.s0.stats_ref), channel_id=1, source_target_pairs={{0,48},{2,50},{4,52},{6,54},{8,56},{10,58},{12,60},{14,62},{16,0},... | collective-permute-start | bytes 12296 | tf_op jit(solution)/shard_map/ppermute | solution.py:334
  31.7 5.3 %collective-permute-start.8 = (f32[8,128]{1,0:T(8,128)S(1)}, f32[8,128]{1,0:T(8,128)S(1)}, u32[]{:S(2)}, u32[]{:S(2)}) collective-permute-start(f32[8,128]{1,0:T(8,128)S(1)} %shard_map.84.s0.stats_ref), channel_id=1, source_target_pairs={{0,32},{2,34},{4,36},{6,38},{8,40},{10,42},{12,44},{14,46},{16,48}... | collective-permute-start | bytes 12296 | tf_op jit(solution)/shard_map/ppermute | solution.py:334
  32.4 5.6 %collective-permute-start.7 = (f32[8,128]{1,0:T(8,128)S(1)}, f32[8,128]{1,0:T(8,128)S(1)}, u32[]{:S(2)}, u32[]{:S(2)}) collective-permute-start(f32[8,128]{1,0:T(8,128)S(1)} %shard_map.84.s0.stats_ref), channel_id=1, source_target_pairs={{0,16},{2,18},{4,20},{6,22},{8,24},{10,26},{12,28},{14,30},{16,32}... | collective-permute-start | bytes 12296 | tf_op jit(solution)/shard_map/ppermute | solution.py:334
  33.4 15.1 %collective-permute-start.11 = (bf16[1280,128]{1,0:T(8,128)(2,1)S(1)}, bf16[1280,128]{1,0:T(8,128)(2,1)S(1)}, u32[]{:S(2)}, u32[]{:S(2)}) collective-permute-start(bf16[1280,128]{1,0:T(8,128)(2,1)S(1)} %shard_map.86.refs_1_.refs_2_), channel_id=1, source_target_pairs={{0,32},{2,34},{4,36},{6,38},{8,40},{10,42},{12,44},{14,46},{16,48}... | collective-permute-start | bytes 983048 | tf_op jit(solution)/shard_map/ppermute | solution.py:334
  35.4 13.6 %collective-permute-start.10 = (bf16[1280,128]{1,0:T(8,128)(2,1)S(1)}, bf16[1280,128]{1,0:T(8,128)(2,1)S(1)}, u32[]{:S(2)}, u32[]{:S(2)}) collective-permute-start(bf16[1280,128]{1,0:T(8,128)(2,1)S(1)} %shard_map.86.refs_1_.refs_2_), channel_id=1, source_target_pairs={{0,16},{2,18},{4,20},{6,22},{8,24},{10,26},{12,28},{14,30},{16,32}... | collective-permute-start | bytes 983048 | tf_op jit(solution)/shard_map/ppermute | solution.py:334
  37.9 11.1 %collective-permute-start.12 = (bf16[1280,128]{1,0:T(8,128)(2,1)S(1)}, bf16[1280,128]{1,0:T(8,128)(2,1)S(1)}, u32[]{:S(2)}, u32[]{:S(2)}) collective-permute-start(bf16[1280,128]{1,0:T(8,128)(2,1)S(1)} %shard_map.86.refs_1_.refs_2_), channel_id=1, source_target_pairs={{0,48},{2,50},{4,52},{6,54},{8,56},{10,58},{12,60},{14,62},{16,0},... | collective-permute-start | bytes 983048 | tf_op jit(solution)/shard_map/ppermute | solution.py:334
  41.7 6.7 %collective-permute-start.13 = (bf16[720,128]{1,0:T(8,128)(2,1)S(1)}, bf16[720,128]{1,0:T(8,128)(2,1)S(1)}, u32[]{:S(2)}, u32[]{:S(2)}) collective-permute-start(bf16[720,128]{1,0:T(8,128)(2,1)S(1)} %get-tuple-element.59), channel_id=1, source_target_pairs={{0,4},{2,6},{4,8},{6,10},{8,12},{10,14},{12,0},{14,2},{16,20},{18,... | collective-permute-start | bytes 552968 | tf_op jit(solution)/shard_map/ppermute | solution.py:334
  42.0 9.1 %collective-permute-start.18 = (bf16[720,128]{1,0:T(8,128)(2,1)S(1)}, bf16[720,128]{1,0:T(8,128)(2,1)S(1)}, u32[]{:S(2)}, u32[]{:S(2)}) collective-permute-start(bf16[720,128]{1,0:T(8,128)(2,1)S(1)} %get-tuple-element.64), channel_id=1, source_target_pairs={{0,8},{2,10},{4,12},{6,14},{8,0},{10,2},{12,4},{14,6},{16,24},{18,... | collective-permute-start | bytes 552968 | tf_op jit(solution)/shard_map/ppermute | solution.py:334
  48.4 3.5 %collective-permute-start.14 = (bf16[1280,128]{1,0:T(8,128)(2,1)S(1)}, bf16[1280,128]{1,0:T(8,128)(2,1)S(1)}, u32[]{:S(2)}, u32[]{:S(2)}) collective-permute-start(bf16[1280,128]{1,0:T(8,128)(2,1)S(1)} %shard_map.86.refs_1_.refs_2_), channel_id=1, source_target_pairs={{0,2},{2,0},{4,6},{6,4},{8,10},{10,8},{12,14},{14,12},{16,18},{18,... | collective-permute-start | bytes 983048 | tf_op jit(solution)/shard_map/ppermute | solution.py:334
  48.4 3.5 %collective-permute-start.16 = (bf16[1280,128]{1,0:T(8,128)(2,1)S(1)}, bf16[1280,128]{1,0:T(8,128)(2,1)S(1)}, u32[]{:S(2)}, u32[]{:S(2)}) collective-permute-start(bf16[1280,128]{1,0:T(8,128)(2,1)S(1)} %collective-permute-done.11.refs_3_.refs_4_), channel_id=1, source_target_pairs={{0,2},{2,0},{4,6},{6,4},{8,10},{10,8},{12,14},{14,12},{16,18},{18,... | collective-permute-start | bytes 983048 | tf_op jit(solution)/shard_map/ppermute | solution.py:334
  48.9 3.0 %collective-permute-start.15 = (bf16[1280,128]{1,0:T(8,128)(2,1)S(1)}, bf16[1280,128]{1,0:T(8,128)(2,1)S(1)}, u32[]{:S(2)}, u32[]{:S(2)}) collective-permute-start(bf16[1280,128]{1,0:T(8,128)(2,1)S(1)} %collective-permute-done.10.refs_2_.refs_3_), channel_id=1, source_target_pairs={{0,2},{2,0},{4,6},{6,4},{8,10},{10,8},{12,14},{14,12},{16,18},{18,... | collective-permute-start | bytes 983048 | tf_op jit(solution)/shard_map/ppermute | solution.py:334
  49.0 2.9 %collective-permute-start.17 = (bf16[1280,128]{1,0:T(8,128)(2,1)S(1)}, bf16[1280,128]{1,0:T(8,128)(2,1)S(1)}, u32[]{:S(2)}, u32[]{:S(2)}) collective-permute-start(bf16[1280,128]{1,0:T(8,128)(2,1)S(1)} %collective-permute-done.12.refs_4_.refs_5_), channel_id=1, source_target_pairs={{0,2},{2,0},{4,6},{6,4},{8,10},{10,8},{12,14},{14,12},{16,18},{18,... | collective-permute-start | bytes 983048 | tf_op jit(solution)/shard_map/ppermute | solution.py:334
  51.0 10.7 %collective-permute-start.21 = (bf16[720,128]{1,0:T(8,128)(2,1)S(1)}, bf16[720,128]{1,0:T(8,128)(2,1)S(1)}, u32[]{:S(2)}, u32[]{:S(2)}) collective-permute-start(bf16[720,128]{1,0:T(8,128)(2,1)S(1)} %get-tuple-element.68), channel_id=1, source_target_pairs={{0,12},{2,14},{4,0},{6,2},{8,4},{10,6},{12,8},{14,10},{16,28},{18,... | collective-permute-start | bytes 552968 | tf_op jit(solution)/shard_map/ppermute | solution.py:334
  58.5 10.3 %collective-permute-start.19 = (bf16[640,128]{1,0:T(8,128)(2,1)S(1)}, bf16[640,128]{1,0:T(8,128)(2,1)S(1)}, u32[]{:S(2)}, u32[]{:S(2)}) collective-permute-start(bf16[640,128]{1,0:T(8,128)(2,1)S(1)} %get-tuple-element.65), channel_id=1, source_target_pairs={{0,12},{2,14},{4,0},{6,2},{8,4},{10,6},{12,8},{14,10},{16,28},{18,... | collective-permute-start | bytes 491528 | tf_op jit(solution)/shard_map/ppermute | solution.py:334
  59.8 9.1 %collective-permute-start.20 = (bf16[640,128]{1,0:T(8,128)(2,1)S(1)}, bf16[640,128]{1,0:T(8,128)(2,1)S(1)}, u32[]{:S(2)}, u32[]{:S(2)}) collective-permute-start(bf16[640,128]{1,0:T(8,128)(2,1)S(1)} %get-tuple-element.66), channel_id=1, source_target_pairs={{0,8},{2,10},{4,12},{6,14},{8,0},{10,2},{12,4},{14,6},{16,24},{18,... | collective-permute-start | bytes 491528 | tf_op jit(solution)/shard_map/ppermute | solution.py:334
  65.2 6.6 %collective-permute-start.22 = (bf16[640,128]{1,0:T(8,128)(2,1)S(1)}, bf16[640,128]{1,0:T(8,128)(2,1)S(1)}, u32[]{:S(2)}, u32[]{:S(2)}) collective-permute-start(bf16[640,128]{1,0:T(8,128)(2,1)S(1)} %shard_map.89), channel_id=1, source_target_pairs={{0,4},{2,6},{4,8},{6,10},{8,12},{10,14},{12,0},{14,2},{16,20},{18,... | collective-permute-start | bytes 491528 | tf_op jit(solution)/shard_map/ppermute | solution.py:334
